TPU v7x, 32 devices: a whole 2x2x4 slice. The times are simulated.
32 devices in a mesh: bank: 4 (over z), freq: 8 (over y, x, core).
Axes of the slice: x: 2, y: 2, z: 4, core: 2. Of those that a mesh axis runs over, the one named last changes fastest.
Arguments:
- strain: float32 [3, 2, 512, 2048], P(None, None, 'freq', 'bank'), may hold values from -6 to 6
- templates: float32 [8, 2, 512, 2048], P('bank', None, 'freq'), may hold values from -6 to 6
- coinc_tmpl: int32 [4], P('bank'), may hold values from 0 to 1
- coinc_det: int32 [4], P('bank'), may hold values from 0 to 2
- bin_edges: int32 [8, 15], P('bank'), may hold values from 1 to 31, as said below
Outputs:
- snr: float32 [8, 3, 2, 2048, 512], P('bank', None, None, 'freq')
- chi_sq: float32 [4, 2048, 512], P('bank', 'freq')
Inputs may be any that keep to these rules, and one draw needn't show every extreme that they name: `coinc_tmpl`: the entries of shard j // 1 of bank name templates of that shard. `bin_edges`: each row is strictly increasing.
All inputs are finite; a program needn't handle non-finite values.
Results may differ from a plain program's by a relative error of at most 0.0003.
Values sent between devices are 32-bit elements; how exact they have to be, the bound alone decides.
No kernel may reach another device: no remote copies, remote signals or barrier semaphores. Data moves between devices by JAX's collectives and lax.ppermute only.
A program may use at most 192 MiB of HBM per device.

v0:
```python
import math

import jax
import jax.numpy as jnp
from jax import lax
from jax.sharding import PartitionSpec as P

N1 = 2048
N2 = 512
NBLK = 32
BINS = 16


def phase(row_index, col_index, length):
    product = row_index[:, None] * col_index[None, :] % length
    angle = product.astype(jnp.float32) * (2.0 * math.pi / length)
    return (jnp.cos(angle), jnp.sin(angle))


def per_device(strain, templates, coinc_tmpl, coinc_det, bin_edges):
    highest = lax.Precision.HIGHEST
    strain_all = lax.all_gather(strain, "bank", axis=3, tiled=True)
    strain_re = strain_all[:, 0]
    strain_im = strain_all[:, 1]
    tmpl_re = templates[:, 0]
    tmpl_im = templates[:, 1]
    tmpl_count, col_count, row_total = tmpl_re.shape
    det_count = strain_re.shape[0]
    prod_re = tmpl_re[:, None] * strain_re[None] + tmpl_im[:, None] * strain_im[None]
    prod_im = tmpl_re[:, None] * strain_im[None] - tmpl_im[:, None] * strain_re[None]
    block_rows = N1 // NBLK
    local_power = (
        (tmpl_re * tmpl_re + tmpl_im * tmpl_im)
        .reshape(tmpl_count, col_count, NBLK, block_rows)
        .sum(axis=(1, 3))
    )
    block_power = lax.psum(local_power, "freq")
    sigma_sq = block_power.sum(axis=1)
    inv_sigma = lax.rsqrt(sigma_sq)
    row_index = jnp.arange(N1, dtype=jnp.int32)
    first_cos, first_sin = phase(row_index, row_index, N1)
    form = "tdck,kn->tdcn"
    section_re = jnp.einsum(form, prod_re, first_cos, precision=highest) - jnp.einsum(
        form, prod_im, first_sin, precision=highest
    )
    section_im = jnp.einsum(form, prod_re, first_sin, precision=highest) + jnp.einsum(
        form, prod_im, first_cos, precision=highest
    )
    col_global = lax.axis_index("freq") * col_count + jnp.arange(col_count, dtype=jnp.int32)
    twist_cos, twist_sin = phase(col_global, row_index, N1 * N2)
    scaling = inv_sigma[:, None, None, None]
    whole_re = (section_re * twist_cos - section_im * twist_sin) * scaling
    whole_im = (section_re * twist_sin + section_im * twist_cos) * scaling
    bin_of = jnp.sum(
        jnp.arange(NBLK, dtype=jnp.int32)[None, :, None] >= bin_edges[:, None, :], axis=2
    )
    bin_mask = (bin_of[:, :, None] == jnp.arange(BINS, dtype=jnp.int32)[None, None, :]).astype(
        jnp.float32
    )
    weights = jnp.einsum("tb,tbl->tl", block_power, bin_mask, precision=highest) / sigma_sq[:, None]
    pick_tmpl = (coinc_tmpl[:, None] == jnp.arange(tmpl_count, dtype=jnp.int32)[None, :]).astype(
        jnp.float32
    )
    pick_det = (coinc_det[:, None] == jnp.arange(det_count, dtype=jnp.int32)[None, :]).astype(
        jnp.float32
    )
    picked = pick_tmpl[:, :, None] * pick_det[:, None, :]
    entry_re = jnp.einsum("jtd,tdck->jck", picked, prod_re, precision=highest)
    entry_im = jnp.einsum("jtd,tdck->jck", picked, prod_im, precision=highest)
    slot_count = entry_re.shape[0]
    entry_re = entry_re.reshape(slot_count, col_count, NBLK, block_rows)
    entry_im = entry_im.reshape(slot_count, col_count, NBLK, block_rows)
    block_cos = first_cos.reshape(NBLK, block_rows, N1)
    block_sin = first_sin.reshape(NBLK, block_rows, N1)
    form_block = "jcbk,bkn->jbcn"
    block_re = jnp.einsum(form_block, entry_re, block_cos, precision=highest) - jnp.einsum(
        form_block, entry_im, block_sin, precision=highest
    )
    block_im = jnp.einsum(form_block, entry_re, block_sin, precision=highest) + jnp.einsum(
        form_block, entry_im, block_cos, precision=highest
    )
    slot_bins = jnp.einsum("jt,tbl->jbl", pick_tmpl, bin_mask, precision=highest)
    slot_inv = jnp.einsum("jt,t->j", pick_tmpl, inv_sigma, precision=highest)
    slot_weights = jnp.einsum("jt,tl->jl", pick_tmpl, weights, precision=highest)
    raw_re = jnp.einsum("jbcn,jbl->jlcn", block_re, slot_bins, precision=highest)
    raw_im = jnp.einsum("jbcn,jbl->jlcn", block_im, slot_bins, precision=highest)
    slot_scale = slot_inv[:, None, None, None]
    bins_re = (raw_re * twist_cos - raw_im * twist_sin) * slot_scale
    bins_im = (raw_re * twist_sin + raw_im * twist_cos) * slot_scale
    col_index = jnp.arange(N2, dtype=jnp.int32)
    second_cos, second_sin = phase(col_index, col_index, N2)
    series_count = tmpl_count * det_count
    joint_re = jnp.concatenate(
        [
            whole_re.reshape(series_count, col_count, N1),
            bins_re.reshape(slot_count * BINS, col_count, N1),
        ],
        0,
    )
    joint_im = jnp.concatenate(
        [
            whole_im.reshape(series_count, col_count, N1),
            bins_im.reshape(slot_count * BINS, col_count, N1),
        ],
        0,
    )
    part_re = lax.all_to_all(joint_re, "freq", split_axis=2, concat_axis=1, tiled=True)
    part_im = lax.all_to_all(joint_im, "freq", split_axis=2, concat_axis=1, tiled=True)
    form_two = "...cn,cm->...nm"
    out_re = jnp.einsum(form_two, part_re, second_cos, precision=highest) - jnp.einsum(
        form_two, part_im, second_sin, precision=highest
    )
    out_im = jnp.einsum(form_two, part_re, second_sin, precision=highest) + jnp.einsum(
        form_two, part_im, second_cos, precision=highest
    )
    time_rows = out_re.shape[1]
    snr_re = out_re[:series_count].reshape(tmpl_count, det_count, time_rows, N2)
    snr_im = out_im[:series_count].reshape(tmpl_count, det_count, time_rows, N2)
    snr = jnp.stack([snr_re, snr_im], 2)
    level_re = out_re[series_count:].reshape(slot_count, BINS, time_rows, N2)
    level_im = out_im[series_count:].reshape(slot_count, BINS, time_rows, N2)
    total_re = level_re.sum(axis=1)
    total_im = level_im.sum(axis=1)
    spread = slot_weights[:, :, None, None]
    dev_re = level_re - spread * total_re[:, None]
    dev_im = level_im - spread * total_im[:, None]
    chi_sq = jnp.sum((dev_re * dev_re + dev_im * dev_im) / spread, axis=1)
    return (snr, chi_sq)


def solution(mesh):
    placed = (
        P(None, None, "freq", "bank"),
        P("bank", None, "freq", None),
        P("bank"),
        P("bank"),
        P("bank", None),
    )
    return jax.shard_map(
        per_device,
        mesh=mesh,
        in_specs=placed,
        out_specs=(P("bank", None, None, "freq", None), P("bank", "freq", None)),
        check_vma=False,
    )
```

profile of v0, /device:TPU:0, one launch (start us, length us, event | category | flops | bytes accessed | tf_op | source)
XLA Modules:
  0.0 1372.1 jit_solution(1766728740631755142)
XLA Ops:
  7.2 0.7 all-gather.2.cloned.1.call-update
  9.2 0.8 copy.77
  10.0 3.1 slice_bitcast_fusion.7
  13.0 0.1 reduce_sum.64
  13.1 0.1 reduce_sum.65
  13.2 15.5 %psum.7 = f32[2,32]{1,0:T(2,128)S(1)} all-reduce(f32[2,32]{1,0:T(2,128)S(1)} %reduce_sum.65), channel_id=1, replica_groups=mesh['bank'=4,'freq'=8] {'freq'}, use_global_device_ids=true, to_apply=%region_2.0 | all-reduce | flops 64 | bytes 512 | tf_op jit(solution)/shard_map/psum | solution.py:37
  28.7 0.1 reduce_sum.66
  28.9 3.0 mul.458
  31.9 2.2 mul.465
  34.1 0.6 multiply_add_fusion.6
  34.8 0.7 select_reduce_fusion
  35.4 0.7 fusion.163
  36.2 3.2 fusion.104
  39.4 36.4 %all-gather.2.cloned.1.call-done = f32[3,2,64,2048]{3,2,1,0:T(8,128)} async-done(((f32[3,2,64,512]{3,2,1,0:T(8,128)}), f32[3,2,64,2048]{3,2,1,0:T(8,128)}) %all-gather.2.cloned.1.call-update) | async-done | bytes 3145744 | tf_op jit(solution)/shard_map/all_gather | solution.py:22
  75.8 4.0 slice_bitcast_fusion.3
  79.7 2.2 multiply_subtract_fusion.13
  82.0 2.3 multiply_subtract_fusion.12
  84.2 2.2 multiply_add_fusion.5.clone.5
  86.5 2.2 multiply_add_fusion.10
  88.7 2.7 mul.461
  91.4 3.6 mul.468
  95.0 5.4 multiply_add_fusion
  100.5 18.3 %fusion.26 = f32[1,64,32,64,1]{3,0,4,2,1:T(1,128)} fusion(f32[2,3,1,1,1]{1,2,0,4,3:T(1,128)S(1)} %bitcast.172, f32[64,32,64,3,2]{2,1,4,3,0:T(8,128)S(1)} %get-tuple-element.4), kind=kOutput, calls=%fused_computation.36 | convolution fusion | flops 9437184 | bytes 3670040 | tf_op jit(solution)/shard_map/jtd,tdck->jck/dot_general | solution.py:68
  118.8 17.1 %fusion.24 = f32[1,64,32,64,1]{3,0,4,2,1:T(1,128)S(1)} fusion(f32[2,3,1,1,1]{1,2,0,4,3:T(1,128)S(1)} %bitcast.173, f32[64,32,64,3,2]{2,1,4,3,0:T(8,128)S(1)} %get-tuple-element.5), kind=kOutput, calls=%fused_computation.34 | convolution fusion | flops 9437184 | bytes 3670040 | tf_op jit(solution)/shard_map/jtd,tdck->jck/dot_general | solution.py:69
  135.9 82.4 %fusion.6 = f32[2,3,64,2048]{3,2,1,0:T(8,128)S(1)} fusion(f32[2,3,64,2048]{3,2,1,0:T(8,128)S(1)} %copy-done.4), kind=kOutput, calls=%fused_computation.12 | convolution fusion | flops 19386073088 | bytes 6291456 | tf_op jit(solution)/shard_map/tdck,kn->tdcn/dot_general | solution.py:46
  218.3 82.6 %fusion.8 = f32[2,3,64,2048]{3,2,1,0:T(8,128)S(1)} fusion(f32[2,3,64,2048]{3,2,1,0:T(8,128)S(1)} %copy-done.5), kind=kOutput, calls=%fused_computation.14 | convolution fusion | flops 19386073088 | bytes 6291456 | tf_op jit(solution)/shard_map/tdck,kn->tdcn/dot_general | solution.py:43
  301.0 82.8 %fusion.49 = f32[2,3,64,2048]{3,2,1,0:T(8,128)S(1)} fusion(f32[2,3,64,2048]{3,2,1,0:T(8,128)S(1)} %fusion.8, f32[2,3,64,2048]{3,2,1,0:T(8,128)S(1)} %copy-done.3), kind=kOutput, calls=%fused_computation.61 | convolution fusion | flops 19386859520 | bytes 9437184 | tf_op jit(solution)/shard_map/tdck,kn->tdcn/dot_general | solution.py:43
  383.8 84.0 %add_multiply_fusion.1 = (f32[2,3,64,2048]{3,2,1,0:T(8,128)S(1)}, f32[2,3,64,2048]{3,2,1,0:T(8,128)S(1)}) fusion(f32[2,3,64,2048]{3,2,1,0:T(8,128)S(1)} %fusion.49, f32[2]{0:T(128)S(1)} %get-tuple-element.17, f32[64,2048]{1,0:T(8,128)S(1)} %copy-done.7, f32[64,2048]{1,0:T(8,128)S(1)} %copy-done.6, f32[2,3,64,2048]{3,2,1,0:T(8,128)S(1)} %fusion.6, ...), kind=kOutput, calls=%fused_computation.57 | convolution fusion | flops 19393150976 | bytes 16777224 | tf_op jit(solution)/shard_map/tdck,kn->tdcn/dot_general | solution.py:46
  467.8 3.9 copy.84
  471.7 3.8 copy.89
  475.5 83.3 %fusion.30 = f32[32,2048,64]{1,2,0:T(8,128)S(1)} fusion(s32[32,64]{1,0:T(8,128)S(1)} %copy-done.10, f32[1,64,32,64,1]{3,0,4,2,1:T(1,128)S(1)} %fusion.24), kind=kOutput, calls=%fused_computation.43 | convolution fusion | flops 3279945728 | bytes 17309696 | tf_op jit(solution)/shard_map/jcbk,bkn->jbcn/dot_general | solution.py:79
  558.9 83.4 %fusion.32 = f32[32,2048,64]{1,2,0:T(8,128)S(1)} fusion(s32[32,64]{1,0:T(8,128)S(1)} %copy-done.10, f32[1,64,32,64,1]{3,0,4,2,1:T(1,128)S(1)} %copy-done.8), kind=kOutput, calls=%fused_computation.44 | convolution fusion | flops 3279945728 | bytes 17309696 | tf_op jit(solution)/shard_map/jcbk,bkn->jbcn/dot_general | solution.py:76
  642.3 85.3 %add_bitcast_fusion = f32[32,64,2048]{2,1,0:T(8,128)} fusion(f32[32,2048,64]{1,2,0:T(8,128)S(1)} %fusion.30, s32[32,64]{1,0:T(8,128)S(1)} %copy-done.10, f32[1,64,32,64,1]{3,0,4,2,1:T(1,128)S(1)} %copy-done.8), kind=kOutput, calls=%fused_computation.24 | convolution fusion | flops 3284140032 | bytes 34086912 | tf_op jit(solution)/shard_map/jcbk,bkn->jbcn/dot_general | solution.py:79
  727.6 84.3 %subtract_bitcast_fusion = f32[32,64,2048]{2,1,0:T(8,128)S(1)} fusion(f32[32,2048,64]{1,2,0:T(8,128)S(1)} %fusion.32, s32[32,64]{1,0:T(8,128)S(1)} %copy-done.10, f32[1,64,32,64,1]{3,0,4,2,1:T(1,128)S(1)} %fusion.24), kind=kOutput, calls=%fused_computation.25 | convolution fusion | flops 3284140032 | bytes 34086912 | tf_op jit(solution)/shard_map/jcbk,bkn->jbcn/dot_general | solution.py:76
  811.9 18.3 %fusion.16 = f32[16,64,2048]{2,0,1:T(8,128)S(1)} fusion(f32[32,64,2048]{2,1,0:T(8,128)S(1)} %subtract_bitcast_fusion, f32[32,16]{1,0:T(8,128)S(1)} %copy-done.9), kind=kOutput, calls=%fused_computation.22 | convolution fusion | flops 805306368 | bytes 25167872 | tf_op jit(solution)/shard_map/jbcn,jbl->jlcn/dot_general | solution.py:85
  830.3 24.7 %add_multiply_fusion = (f32[16,64,2048]{2,0,1:T(8,128)S(1)}, f32[16,64,2048]{2,0,1:T(8,128)S(1)}) fusion(f32[16,64,2048]{2,0,1:T(8,128)S(1)} %fusion.16, f32[]{:T(128)} %get-tuple-element.18, f32[64,2048]{1,0:T(8,128)S(1)} %copy-done.7, f32[64,2048]{1,0:T(8,128)S(1)} %copy-done.6, f32[32,64,2048]{2,1,0:T(8,128)} %add_bitcast_fusion, f32[32,16]{1,0:T(8,128)S(1)} %copy-done.9), kind=kOutput, calls=%fused_computation.39 | convolution fusion | flops 822083584 | bytes 42993668 | tf_op jit(solution)/shard_map/jbcn,jbl->jlcn/dot_general | solution.py:86
  854.9 13.0 pad_maximum_fusion
  867.9 19.3 %copy.85 = f32[22,64,2048]{1,0,2:T(8,128)} copy(f32[22,64,2048]{2,0,1:T(8,128)} %get-tuple-element.21) | data formatting | bytes 23068672 | tf_op jit(solution)/shard_map/concatenate | solution.py:93
  887.3 19.7 %reshape.245 = f32[8,1,360448]{2,1,0:T(1,128)} reshape(f32[2048,22,64]{2,1,0:T(8,128)} %bitcast.161) | data formatting | bytes 23068672
  906.9 5.6 all-to-all-start
  912.6 19.4 %copy.90 = f32[22,64,2048]{1,0,2:T(8,128)} copy(f32[22,64,2048]{2,0,1:T(8,128)} %get-tuple-element.22) | data formatting | bytes 23068672 | tf_op jit(solution)/shard_map/concatenate | solution.py:100
  931.9 19.6 %reshape.247 = f32[8,1,360448]{2,1,0:T(1,128)} reshape(f32[2048,22,64]{2,1,0:T(8,128)} %bitcast.162) | data formatting | bytes 23068672
  951.6 88.8 %all-to-all-done = f32[8,1,360448]{2,1,0:T(1,128)} async-done(((f32[8,1,360448]{2,1,0:T(1,128)}), f32[8,1,360448]{2,1,0:T(1,128)}, u32[]{:S(2)}, u32[]{:S(2)}) %all-to-all-start) | async-done | bytes 11534368 | tf_op jit(solution)/shard_map/all_to_all | solution.py:107
  1040.4 5.3 all-to-all-start.1
  1045.7 0.2 fusion.105
  1045.9 0.2 convolution_bitcast_fusion
  1046.1 0.5 broadcast.242
  1046.6 33.7 %reduce.12 = f32[8,360448]{1,0:T(8,128)} reduce(f32[8,1,360448]{2,1,0:T(1,128)} %all-to-all-done, f32[]{:T(128)} %broadcast.242), dimensions={1}, to_apply=%all_to_all.26.reduce_sub_computation | reduce | bytes 23068676 | tf_op jit(solution)/shard_map/all_to_all | solution.py:107
  1080.3 23.8 %reshape.246 = f32[2048,22,64]{2,1,0:T(8,128)} reshape(f32[8,360448]{1,0:T(8,128)} %reduce.12) | data formatting | bytes 23068672
  1104.1 18.4 %copy.87 = f32[22,8,64,256]{3,2,1,0:T(8,128)} copy(f32[22,8,64,256]{2,0,3,1:T(8,128)} %bitcast.163) | data formatting | bytes 23068672 | tf_op jit(solution)/shard_map/all_to_all | solution.py:107
  1122.5 31.4 %fusion.74 = f32[22,256,512]{2,1,0:T(8,128)} fusion(f32[22,512,256]{2,1,0:T(8,128)} %bitcast.159), kind=kOutput, calls=%fused_computation.90 | convolution fusion | flops 17720410112 | bytes 23068672 | tf_op jit(solution)/shard_map/...cn,cm->...nm/dot_general | solution.py:113
  1153.9 30.0 %fusion.78 = f32[22,256,512]{2,1,0:T(8,128)} fusion(f32[22,512,256]{2,1,0:T(8,128)S(1)} %bitcast.160), kind=kOutput, calls=%fused_computation.94 | convolution fusion | flops 17720410112 | bytes 23068672 | tf_op jit(solution)/shard_map/...cn,cm->...nm/dot_general | solution.py:110
  1183.9 33.8 %reduce.13 = f32[8,360448]{1,0:T(8,128)} reduce(f32[8,1,360448]{2,1,0:T(1,128)} %all-to-all-done.1, f32[]{:T(128)} %broadcast.242), dimensions={1}, to_apply=%all_to_all.30.reduce_sub_computation | reduce | bytes 23068676 | tf_op jit(solution)/shard_map/all_to_all | solution.py:108
  1217.7 23.8 %reshape.248 = f32[2048,22,64]{2,1,0:T(8,128)} reshape(f32[8,360448]{1,0:T(8,128)} %reduce.13) | data formatting | bytes 23068672
  1241.4 18.5 %copy.92 = f32[22,8,64,256]{3,2,1,0:T(8,128)} copy(f32[22,8,64,256]{2,0,3,1:T(8,128)} %bitcast.164) | data formatting | bytes 23068672 | tf_op jit(solution)/shard_map/all_to_all | solution.py:108
  1259.9 33.5 %convolution_subtract_fusion = f32[22,256,512]{2,1,0:T(8,128)} fusion(f32[22,256,512]{2,1,0:T(8,128)} %fusion.78, f32[22,512,256]{2,1,0:T(8,128)} %bitcast.157), kind=kOutput, calls=%fused_computation.56 | convolution fusion | flops 17723293696 | bytes 34603008 | tf_op jit(solution)/shard_map/...cn,cm->...nm/dot_general | solution.py:110
  1293.4 4.6 slice_reduce_fusion.1
  1298.0 2.0 copy-done
  1300.0 48.4 %convolution_add_fusion = f32[22,256,512]{2,1,0:T(8,128)} fusion(f32[22,256,512]{2,1,0:T(8,128)} %fusion.74, f32[22,512,256]{2,1,0:T(8,128)S(1)} %bitcast.158), kind=kOutput, calls=%fused_computation.55 | convolution fusion | flops 17723293696 | bytes 34603008 | tf_op jit(solution)/shard_map/...cn,cm->...nm/dot_general | solution.py:113
  1348.4 4.6 slice_reduce_fusion
  1353.1 0.6 slice-done.4
  1353.6 4.0 pad_maximum_fusion.2
  1357.7 1.7 slice-done.2
  1359.4 5.6 fusion.44
  (49 shorter events, 0.4 us)
Async XLA Ops:
  7.2 68.6 %all-gather.2.cloned.1.call-start = ((), (), s32[]{:S(2)}) async-start(), calls=%async_computation.2 | async-start | bytes 3932160 | tf_op jit(solution)/shard_map/all_gather | solution.py:22
  28.7 53.2 %copy-start.13 = (f32[2,32]{1,0:T(2,128)}, f32[2,32]{1,0:T(2,128)S(1)}, u32[]{:S(2)}) copy-start(f32[2,32]{1,0:T(2,128)S(1)} %psum.7) | copy-start | bytes 772
  28.9 53.1 %copy-start.15 = (f32[2]{0:T(128)}, f32[2]{0:T(128)S(1)}, u32[]{:S(2)}) copy-start(f32[2]{0:T(128)S(1)} %reduce_sum.66) | copy-start | bytes 28
  34.8 49.5 %copy-start.11 = (s32[2,32]{1,0:T(2,128)}, s32[2,32]{1,0:T(2,128)S(1)}, u32[]{:S(2)}) copy-start(s32[2,32]{1,0:T(2,128)S(1)} %fusion.109) | copy-start | bytes 772
  100.5 35.4 %copy-start.4 = (f32[2,3,64,2048]{3,2,1,0:T(8,128)S(1)}, f32[2,3,64,2048]{3,2,1,0:T(8,128)}, u32[]{:S(2)}) copy-start(f32[2,3,64,2048]{3,2,1,0:T(8,128)} %multiply_subtract_fusion.12) | copy-start | bytes 9437188
  135.9 82.4 %copy-start.5 = (f32[2,3,64,2048]{3,2,1,0:T(8,128)S(1)}, f32[2,3,64,2048]{3,2,1,0:T(8,128)}, u32[]{:S(2)}) copy-start(f32[2,3,64,2048]{3,2,1,0:T(8,128)} %multiply_add_fusion.10) | copy-start | bytes 9437188
  218.3 82.6 %copy-start.3 = (f32[2,3,64,2048]{3,2,1,0:T(8,128)S(1)}, f32[2,3,64,2048]{3,2,1,0:T(8,128)}, u32[]{:S(2)}) copy-start(f32[2,3,64,2048]{3,2,1,0:T(8,128)} %multiply_subtract_fusion.13) | copy-start | bytes 9437188
  301.0 82.8 %copy-start.2 = (f32[2,3,64,2048]{3,2,1,0:T(8,128)S(1)}, f32[2,3,64,2048]{3,2,1,0:T(8,128)}, u32[]{:S(2)}) copy-start(f32[2,3,64,2048]{3,2,1,0:T(8,128)} %multiply_add_fusion.5.clone.5) | copy-start | bytes 9437188
  301.0 82.8 %copy-start.6 = (f32[64,2048]{1,0:T(8,128)S(1)}, f32[64,2048]{1,0:T(8,128)}, u32[]{:S(2)}) copy-start(f32[64,2048]{1,0:T(8,128)} %get-tuple-element.19) | copy-start | bytes 1572868
  301.0 82.8 %copy-start.7 = (f32[64,2048]{1,0:T(8,128)S(1)}, f32[64,2048]{1,0:T(8,128)}, u32[]{:S(2)}) copy-start(f32[64,2048]{1,0:T(8,128)} %get-tuple-element.20) | copy-start | bytes 1572868
  467.8 7.7 copy-start.10
  475.5 83.3 %copy-start.8 = (f32[1,64,32,64,1]{3,0,4,2,1:T(1,128)S(1)}, f32[1,64,32,64,1]{3,0,4,2,1:T(1,128)}, u32[]{:S(2)}) copy-start(f32[1,64,32,64,1]{3,0,4,2,1:T(1,128)} %fusion.26) | copy-start | bytes 1572868
  727.5 84.4 %copy-start.9 = (f32[32,16]{1,0:T(8,128)S(1)}, f32[32,16]{1,0:T(8,128)}, u32[]{:S(2)}) copy-start(f32[32,16]{1,0:T(8,128)} %select_reduce_fusion) | copy-start | bytes 6148
  906.9 133.4 %all-to-all-start = ((f32[8,1,360448]{2,1,0:T(1,128)}), f32[8,1,360448]{2,1,0:T(1,128)}, u32[]{:S(2)}, u32[]{:S(2)}) async-start(f32[8,1,360448]{2,1,0:T(1,128)} %reshape.245), calls=%async_computation | async-start | bytes 23068672 | tf_op jit(solution)/shard_map/all_to_all | solution.py:107
  951.6 94.1 %copy-start.12 = (s32[2,32]{1,0:T(2,128)S(1)}, s32[2,32]{1,0:T(2,128)}, u32[]{:S(2)}) copy-start(s32[2,32]{1,0:T(2,128)} %copy-done.11) | copy-start | bytes 772
  951.6 94.1 %copy-start.14 = (f32[2,32]{1,0:T(2,128)S(1)}, f32[2,32]{1,0:T(2,128)}, u32[]{:S(2)}) copy-start(f32[2,32]{1,0:T(2,128)} %copy-done.13) | copy-start | bytes 772
  951.6 94.3 %copy-start.16 = (f32[2]{0:T(128)S(1)}, f32[2]{0:T(128)}, u32[]{:S(2)}) copy-start(f32[2]{0:T(128)} %copy-done.15) | copy-start | bytes 28
  1040.4 143.5 %all-to-all-start.1 = ((f32[8,1,360448]{2,1,0:T(1,128)}), f32[8,1,360448]{2,1,0:T(1,128)}, u32[]{:S(2)}, u32[]{:S(2)}) async-start(f32[8,1,360448]{2,1,0:T(1,128)} %reshape.247), calls=%async_computation.1 | async-start | bytes 23068672 | tf_op jit(solution)/shard_map/all_to_all | solution.py:108
  1122.5 31.4 %copy-start.1 = (f32[22,8,64,256]{3,2,1,0:T(8,128)S(1)}, f32[22,8,64,256]{3,2,1,0:T(8,128)}, u32[]{:S(2)}) copy-start(f32[22,8,64,256]{3,2,1,0:T(8,128)} %copy.87) | copy-start | bytes 34603012
  1293.4 6.7 copy-start
  1348.4 4.7 slice-start.3
  1348.4 5.2 slice-start.4
  1348.4 9.2 slice-start
  1353.1 4.7 slice-start.1
  1353.6 5.7 slice-start.2
Sparse Core Ops, SparseCore 0:
  9.6 66.1 all-gather.1
where the time goes:
time: 1380 us; the launch traced here: 1370 us
  matrix products  890 us (64%)
  local copies, waits for them, and re-layouts  191 us (14%)
  waiting for transfers between devices  126 us (9%)
  other arithmetic  122 us (9%)
  between operations  15.9 us (1%)
  blocking collectives  15.5 us (1%)
    unnamed x45, local copies, waits for them, and re-layouts  91.4 us
    all_to_all x1, waiting for transfers between devices, per_device(): lax.all_to_all(joint_re, 'freq', split_axis=2, concat_axis=1, tiled=True)  88.8 us
    dot_general x1, matrix products, per_device(): jnp.einsum(form_block, entry_re, block_sin, precision=highest)  85.3 us
    dot_general x1, matrix products, per_device(): jnp.einsum(form_block, entry_im, block_sin, precision=highest)  84.3 us
    dot_general x1, matrix products, per_device(): jnp.einsum(form, prod_re, first_sin, precision=highest)  84 us
    dot_general x1, matrix products, per_device(): jnp.einsum(form_block, entry_re, block_cos, precision=highest)  83.4 us
    dot_general x1, matrix products, per_device(): jnp.einsum(form_block, entry_im, block_cos, precision=highest)  83.3 us
    dot_general x1, matrix products, per_device(): jnp.einsum(form, prod_im, first_sin, precision=highest)  82.8 us
  transfers between devices with their start and end apart: 3, of which 2 were waited for; matrix products, arithmetic and copies ran while one was open for 14% of the time, Pallas kernels for 0%

commit v1 on v0

v1 whole, which is shorter than its diff:
```python
import functools

import jax
import jax.numpy as jnp
import ml_dtypes
import numpy as np
from jax import lax
from jax.experimental import pallas as pl
from jax.experimental.pallas import tpu as pltpu
from jax.sharding import PartitionSpec as P

N1 = 2048
N2 = 512
NBLK = 32
BLOCK = N1 // NBLK
BINS = 16
LANES = 128
COARSE = N1 // LANES
FOUR = N2 // LANES
F32 = jnp.float32
BF16 = jnp.bfloat16
MIB = 1 << 20


def split_table(table):
    high = table.astype(ml_dtypes.bfloat16)
    low = (table - high.astype(np.float64)).astype(ml_dtypes.bfloat16)
    return high, low


def first_table():
    angle = 2 * np.pi * (np.outer(np.arange(LANES), np.arange(LANES)) % LANES) / LANES
    cos, sin = np.cos(angle), np.sin(angle)
    return split_table(np.block([[cos, sin], [-sin, cos]]))


def stage_table():
    angle = 2 * np.pi * np.outer(np.arange(COARSE), np.arange(LANES)) / N1
    return np.concatenate([np.cos(angle), np.sin(angle)]).astype(np.float32)


def second_table():
    blocks = []
    for a in range(FOUR):
        n2 = a + FOUR * np.arange(LANES)
        angle = 2 * np.pi * (np.outer(n2, np.arange(LANES)) % N2) / N2
        cos, sin = np.cos(angle), np.sin(angle)
        blocks.append(np.block([[cos, -sin], [sin, cos]]))
    return split_table(np.concatenate(blocks))


def split(x):
    high = x.astype(BF16)
    return high, (x - high.astype(F32)).astype(BF16)


def phase(index, length):
    angle = (index % length).astype(F32) * (2.0 * np.pi / length)
    return jnp.cos(angle), jnp.sin(angle)


def times_i(z):
    return (-z[1], z[0])


def plus(x, y):
    return (x[0] + y[0], x[1] + y[1])


def minus(x, y):
    return (x[0] - y[0], x[1] - y[1])


def dft4(x):
    s0, s1 = plus(x[0], x[2]), minus(x[0], x[2])
    s2, s3 = plus(x[1], x[3]), times_i(minus(x[1], x[3]))
    return [plus(s0, s2), plus(s1, s3), minus(s0, s2), minus(s1, s3)]


def turn(z, step):
    step %= 16
    if step == 0:
        return z
    if step == 4:
        return times_i(z)
    if step == 8:
        return (-z[0], -z[1])
    half = float(np.sqrt(0.5))
    if step == 2:
        return ((z[0] - z[1]) * half, (z[0] + z[1]) * half)
    if step == 6:
        return ((z[0] + z[1]) * -half, (z[0] - z[1]) * half)
    cos, sin = float(np.cos(np.pi * step / 8)), float(np.sin(np.pi * step / 8))
    return (z[0] * cos - z[1] * sin, z[0] * sin + z[1] * cos)


def dft16(x):
    columns = [dft4([x[4 * u1 + u0] for u1 in range(4)]) for u0 in range(4)]
    out = [None] * 16
    for a0 in range(4):
        ys = dft4([turn(columns[u0][a0], u0 * a0) for u0 in range(4)])
        for a1 in range(4):
            out[a0 + 4 * a1] = ys[a1]
    return out


def dot3(left, right):
    (lh, ll), (rh, rl) = left, right
    d = functools.partial(jnp.dot, preferred_element_type=F32)
    return d(lh, rh) + (d(lh, rl) + d(ll, rh))


def first_kernel(
    freq, tmpl_ref, strain_ref, wh_ref, wl_ref, stage_ref, tw_ref, out_ref, gh, gl
):
    tmpls, _, rows, _ = tmpl_ref.shape
    per_piece = COARSE // strain_ref.shape[0]
    for t in range(tmpls):
        x = []
        for u in range(COARSE):
            at = slice(u * LANES, (u + 1) * LANES)
            off = u % per_piece
            there = slice(off * LANES, (off + 1) * LANES)
            hr, hi = tmpl_ref[t, 0, :, at], tmpl_ref[t, 1, :, at]
            sr = strain_ref[u // per_piece, 0, :, there]
            si = strain_ref[u // per_piece, 1, :, there]
            x.append((hr * sr + hi * si, hr * si - hi * sr))
        y = dft16(x)
        for a in range(COARSE):
            cos, sin = stage_ref[a : a + 1, :], stage_ref[COARSE + a : COARSE + a + 1, :]
            yr, yi = y[a]
            at = pl.ds((a * tmpls + t) * rows, rows)
            gh[at, :LANES], gl[at, :LANES] = split(yr * cos - yi * sin)
            gh[at, LANES:], gl[at, LANES:] = split(yr * sin + yi * cos)
    z = dot3((gh[...], gl[...]), (wh_ref[...], wl_ref[...]))
    width = LANES // freq
    slot = lax.broadcasted_iota(jnp.int32, (rows, LANES), 1) // width
    for t in range(tmpls):
        for group in range(COARSE // freq):
            turned = []
            for i in range(freq):
                a = group * freq + i
                at = slice((a * tmpls + t) * rows, (a * tmpls + t + 1) * rows)
                zr, zi = z[at, :LANES], z[at, LANES:]
                lane = slice(a * LANES, (a + 1) * LANES)
                cos, sin = tw_ref[0, :, lane], tw_ref[1, :, lane]
                pair = (zr * cos - zi * sin, zr * sin + zi * cos)
                if i:
                    pair = tuple(pltpu.roll(v, i * width, 1) for v in pair)
                turned.append(pair)
            for q in range(freq):
                for p in range(2):
                    value = turned[(0 - q) % freq][p]
                    for s in range(1, freq):
                        value = jnp.where(slot == s, turned[(s - q) % freq][p], value)
                    out_ref[q, t, p, group] = value


def first_section(freq, templates, strain, first, stage, twist):
    tmpls, _, cols, _ = templates.shape
    pieces, _, _, piece_len = strain.shape
    groups = COARSE // freq
    rows = 16
    whole = lambda shape: pl.BlockSpec(shape, lambda c: (0,) * len(shape))
    return pl.pallas_call(
        functools.partial(first_kernel, freq),
        grid=(cols // rows,),
        in_specs=[
            pl.BlockSpec((tmpls, 2, rows, N1), lambda c: (0, 0, c, 0)),
            pl.BlockSpec((pieces, 2, rows, piece_len), lambda c: (0, 0, c, 0)),
            whole((2 * LANES, 2 * LANES)),
            whole((2 * LANES, 2 * LANES)),
            whole((2 * COARSE, LANES)),
            pl.BlockSpec((2, rows, N1), lambda c: (0, c, 0)),
        ],
        out_specs=pl.BlockSpec(
            (freq, tmpls, 2, groups, rows, LANES), lambda c: (0, 0, 0, 0, c, 0)
        ),
        out_shape=jax.ShapeDtypeStruct((freq, tmpls, 2, groups, cols, LANES), F32),
        scratch_shapes=[pltpu.VMEM((COARSE * tmpls * rows, 2 * LANES), BF16)] * 2,
        compiler_params=pltpu.CompilerParams(vmem_limit_bytes=32 * MIB),
        cost_estimate=pl.CostEstimate(
            flops=6 * tmpls * cols * N1 * 4 * LANES,
            bytes_accessed=4 * MIB,
            transcendentals=0,
        ),
        name="first_section",
    )(templates, strain, first[0], first[1], stage, twist)


def entry_kernel(which_ref, tmpl_ref, *refs):
    strain_refs, out_ref = refs[:-1], refs[-1]
    rows = out_ref.shape[0]
    lane = lax.broadcasted_iota(jnp.int32, (rows, LANES), 1)
    first_half = lane < BLOCK
    t = which_ref[0]
    for d, strain_ref in enumerate(strain_refs):

        @pl.when(which_ref[1] == d)
        def _():
            per_piece = COARSE // strain_ref.shape[0]
            for u in range(COARSE):
                at = slice(u * LANES, (u + 1) * LANES)
                off = u % per_piece
                there = slice(off * LANES, (off + 1) * LANES)
                hr, hi = tmpl_ref[t, 0, :, at], tmpl_ref[t, 1, :, at]
                sr = strain_ref[u // per_piece, 0, :, there]
                si = strain_ref[u // per_piece, 1, :, there]
                re, im = hr * sr + hi * si, hr * si - hi * sr
                lane0 = slice(2 * u * LANES, (2 * u + 1) * LANES)
                lane1 = slice((2 * u + 1) * LANES, (2 * u + 2) * LANES)
                out_ref[:, lane0] = jnp.where(first_half, re, pltpu.roll(im, BLOCK, 1))
                out_ref[:, lane1] = jnp.where(first_half, pltpu.roll(re, BLOCK, 1), im)


def entry_product(which, templates, strains):
    tmpls, _, cols, _ = templates.shape
    pieces, _, _, piece_len = strains[0].shape
    rows = 16
    return pl.pallas_call(
        entry_kernel,
        grid_spec=pltpu.PrefetchScalarGridSpec(
            num_scalar_prefetch=1,
            grid=(cols // rows,),
            in_specs=[pl.BlockSpec((tmpls, 2, rows, N1), lambda c, w: (0, 0, c, 0))]
            + [pl.BlockSpec((pieces, 2, rows, piece_len), lambda c, w: (0, 0, c, 0))]
            * len(strains),
            out_specs=pl.BlockSpec((rows, 2 * N1), lambda c, w: (c, 0)),
        ),
        out_shape=jax.ShapeDtypeStruct((cols, 2 * N1), F32),
        compiler_params=pltpu.CompilerParams(vmem_limit_bytes=32 * MIB),
        cost_estimate=pl.CostEstimate(
            flops=8 * cols * N1, bytes_accessed=6 * MIB, transcendentals=0
        ),
        name="entry_product",
    )(which, templates, *strains)


def second_points(x, w2h_ref, w2l_ref, use):
    for a, (yr, yi) in enumerate(dft4(x)):
        y = jnp.concatenate([yr, yi], axis=0)
        at = slice(a * 2 * LANES, (a + 1) * 2 * LANES)
        z = dot3((w2h_ref[at, :], w2l_ref[at, :]), split(y))
        use(a, z[:LANES], z[LANES:])


def second_kernel(freq, place_ref, scale_ref, part_ref, w2h_ref, w2l_ref, *refs):
    out_ref, hold, order = refs[-3:]
    groups, cols = part_ref.shape[3], part_ref.shape[4]
    per = LANES // cols
    width = LANES // freq
    scale = scale_ref[pl.program_id(0)]

    def rows_of(p, u):
        tiles = [
            jnp.concatenate(
                [part_ref[u * per + f, 0, p, g] for f in range(per)], axis=0
            )
            for g in range(groups)
        ]
        return jnp.concatenate(tiles, axis=1)

    x = [(rows_of(0, u), rows_of(1, u)) for u in range(FOUR)]

    def keep(a, re, im):
        for p, value in enumerate((re, im)):
            for g in range(groups):
                hold[p, g, pl.ds(a, LANES, stride=FOUR), :] = (
                    value[:, g * LANES : (g + 1) * LANES] * scale
                )

    second_points(x, w2h_ref, w2l_ref, keep)
    for p in range(2):
        for g in range(groups):
            turned = hold[p, g].T
            for s in range(freq):
                a = g * freq + lax.rem(s - place_ref[0] + freq, freq)
                for j in range(FOUR):
                    order[p, j, pl.ds(a, width, stride=COARSE), :] = turned[
                        s * width : (s + 1) * width, j * LANES : (j + 1) * LANES
                    ]
        for j in range(FOUR):
            out_ref[0, 0, p, :, j * LANES : (j + 1) * LANES] = order[p, j]


def second_section(freq, det, place, scale, parts, second, dets, earlier):
    _, tmpls, _, groups, cols, _ = parts.shape
    times = groups * LANES
    smem = pl.BlockSpec(memory_space=pltpu.SMEM)
    table = pl.BlockSpec((FOUR * 2 * LANES, 2 * LANES), lambda t: (0, 0))
    operands = [place, scale, parts, second[0], second[1]]
    in_specs = [
        smem,
        smem,
        pl.BlockSpec(
            (freq, 1, 2, groups, cols, LANES), lambda t: (0, t, 0, 0, 0, 0)
        ),
        table,
        table,
    ]
    aliases = {}
    if earlier is not None:
        operands.append(earlier)
        in_specs.append(pl.BlockSpec(memory_space=pl.ANY))
        aliases = {5: 0}
    return pl.pallas_call(
        functools.partial(second_kernel, freq),
        grid=(tmpls,),
        in_specs=in_specs,
        out_specs=pl.BlockSpec((1, 1, 2, times, N2), lambda t: (t, det, 0, 0, 0)),
        out_shape=jax.ShapeDtypeStruct((tmpls, dets, 2, times, N2), F32),
        scratch_shapes=[
            pltpu.VMEM((2, groups, N2, LANES), F32),
            pltpu.VMEM((2, FOUR, times, LANES), F32),
        ],
        input_output_aliases=aliases,
        compiler_params=pltpu.CompilerParams(vmem_limit_bytes=32 * MIB),
        cost_estimate=pl.CostEstimate(
            flops=6 * tmpls * times * FOUR * 4 * LANES * LANES,
            bytes_accessed=8 * MIB,
            transcendentals=0,
        ),
        name="second_section",
    )(*operands)


def bins_kernel(
    edge_ref, gain_ref, share_ref, entry_ref, wh_ref, wl_ref, tw_ref, w2h_ref, w2l_ref,
    out_ref, xh, xl, acc, levels, total, chi, hold,
):
    times = out_ref.shape[0]

    def cut(i, carry):
        at = pl.ds(pl.multiple_of(i * 2 * LANES, 2 * LANES), 2 * LANES)
        xh[:, at], xl[:, at] = split(entry_ref[:, at])
        return carry

    lax.fori_loop(0, 2 * N1 // (2 * LANES), cut, 0)
    total[...] = jnp.zeros_like(total)

    def add(block, blocks):
        at = pl.ds(pl.multiple_of(block * LANES, LANES), blocks * LANES)
        acc[...] += dot3((xh[:, at], xl[:, at]), (wh_ref[at, :], wl_ref[at, :]))

    def first(level, carry):
        start, end = edge_ref[level], edge_ref[level + 1]
        acc[...] = jnp.zeros_like(acc)

        def two(i, inner):
            add(start + 2 * i, 2)
            return inner

        lax.fori_loop(0, (end - start) // 2, two, 0)

        @pl.when((end - start) % 2 == 1)
        def _():
            add(end - 1, 1)

        for u in range(FOUR):
            at = slice(u * LANES, (u + 1) * LANES)
            re, im = acc[at, :times], acc[at, times:]
            cos, sin = tw_ref[0, at, :], tw_ref[1, at, :]
            vr, vi = re * cos - im * sin, re * sin + im * cos
            levels[level, 0, at, :] = vr
            levels[level, 1, at, :] = vi
            total[0, at, :] += vr
            total[1, at, :] += vi
        return carry

    lax.fori_loop(0, BINS, first, 0)
    chi[...] = jnp.zeros_like(chi)

    def second(level, carry):
        gain, share = gain_ref[level], share_ref[level]

        def rows_of(p, u):
            at = slice(u * LANES, (u + 1) * LANES)
            return levels[level, p, at, :] * gain - total[p, at, :] * share

        def keep(a, re, im):
            chi[a] += re * re + im * im

        x = [(rows_of(0, u), rows_of(1, u)) for u in range(FOUR)]
        second_points(x, w2h_ref, w2l_ref, keep)
        return carry

    lax.fori_loop(0, BINS, second, 0)
    for g in range(times // LANES):
        lane = slice(g * LANES, (g + 1) * LANES)
        for a in range(FOUR):
            hold[pl.ds(a, LANES, stride=FOUR), :] = chi[a, :, lane]
        out_ref[lane, :] = hold[...].T


def bins_section(edges, gain, share, entry, bank_table, twist, second):
    times = twist.shape[2]
    smem = pl.BlockSpec(memory_space=pltpu.SMEM)
    vmem = pl.BlockSpec(memory_space=pltpu.VMEM)
    return pl.pallas_call(
        bins_kernel,
        in_specs=[smem] * 3 + [vmem] * 6,
        out_specs=vmem,
        out_shape=jax.ShapeDtypeStruct((times, N2), F32),
        scratch_shapes=[
            pltpu.VMEM((N2, 2 * N1), BF16),
            pltpu.VMEM((N2, 2 * N1), BF16),
            pltpu.VMEM((N2, 2 * times), F32),
            pltpu.VMEM((BINS, 2, N2, times), F32),
            pltpu.VMEM((2, N2, times), F32),
            pltpu.VMEM((FOUR, LANES, times), F32),
            pltpu.VMEM((N2, LANES), F32),
        ],
        compiler_params=pltpu.CompilerParams(vmem_limit_bytes=58 * MIB),
        cost_estimate=pl.CostEstimate(
            flops=6 * 24 * N2 * 4 * LANES * times + 6 * BINS * FOUR * 4 * LANES**2 * times,
            bytes_accessed=20 * MIB,
            transcendentals=0,
        ),
        name="bins",
    )(edges, gain, share, entry, bank_table[0], bank_table[1], twist, *second)


def time_table(place, times):
    block = jnp.arange(NBLK, dtype=jnp.int32)[:, None, None]
    inner = jnp.arange(BLOCK, dtype=jnp.int32)[None, :, None]
    time = place * times + jnp.arange(times, dtype=jnp.int32)[None, None, :]
    cos, sin = phase((block * BLOCK + inner) * time, N1)
    real = jnp.concatenate([cos, sin], axis=2)
    imag = jnp.concatenate([-sin, cos], axis=2)
    table = jnp.concatenate([real, imag], axis=1).reshape(2 * N1, 2 * times)
    high = lax.reduce_precision(table, 8, 7)
    low = lax.reduce_precision(table - high, 8, 7)
    return high.astype(BF16), low.astype(BF16)


def per_device(strain, templates, coinc_tmpl, coinc_det, bin_edges):
    freq = lax.axis_size("freq")
    place = lax.axis_index("freq").astype(jnp.int32)
    tmpls, _, cols, _ = templates.shape
    dets = strain.shape[0]
    times = N1 // freq

    strains = [lax.all_gather(strain[d], "bank", axis=0, tiled=False) for d in range(dets)]

    first = tuple(jnp.asarray(t) for t in first_table())
    second = tuple(jnp.asarray(t) for t in second_table())
    stage = jnp.asarray(stage_table())

    power = (templates[:, 0] ** 2 + templates[:, 1] ** 2).sum(axis=1)
    local_power = power.reshape(tmpls, NBLK, BLOCK).sum(axis=2)
    block_power = lax.psum(local_power, "freq")
    sigma_sq = block_power.sum(axis=1)
    inv_sigma = lax.rsqrt(sigma_sq)
    bin_of = jnp.sum(
        jnp.arange(NBLK, dtype=jnp.int32)[None, :, None] >= bin_edges[:, None, :], axis=2
    )
    inside = bin_of[:, None, :] == jnp.arange(BINS, dtype=jnp.int32)[None, :, None]
    weights = jnp.where(inside, block_power[:, None, :], 0.0).sum(axis=2) / sigma_sq[:, None]

    column = place * cols + jnp.arange(cols, dtype=jnp.int32)
    lane = jnp.arange(N1, dtype=jnp.int32)
    time_of_lane = lane // LANES + COARSE * (lane % LANES)
    twist = jnp.stack(phase(column[:, None] * time_of_lane[None, :], N1 * N2))
    own_time = place * times + jnp.arange(times, dtype=jnp.int32)
    all_columns = jnp.arange(N2, dtype=jnp.int32)
    own_twist = jnp.stack(phase(all_columns[:, None] * own_time[None, :], N1 * N2))
    bank_table = time_table(place, times)

    parts = []
    for d in range(dets):
        sent = first_section(freq, templates, strains[d], first, stage, twist)
        shape = sent.shape
        got = lax.all_to_all(
            sent.reshape(freq, -1, LANES), "freq", split_axis=0, concat_axis=0, tiled=True
        )
        parts.append(got.reshape(shape))

    chi = []
    for j in range(coinc_tmpl.shape[0]):
        which = jnp.stack([coinc_tmpl[j], coinc_det[j]])
        product = entry_product(which, templates, strains)
        entry = lax.all_gather(product, "freq", axis=0, tiled=True)
        t = coinc_tmpl[j]
        edges = jnp.concatenate(
            [jnp.zeros((1,), jnp.int32), bin_edges[t], jnp.full((1,), NBLK, jnp.int32)]
        )
        gain = inv_sigma[t] * lax.rsqrt(weights[t])
        chi.append(
            bins_section(edges, gain, gain * weights[t], entry, bank_table, own_twist, second)
        )

    snr = None
    for d in range(dets):
        snr = second_section(
            freq, d, place.reshape(1), inv_sigma, parts[d], second, dets, snr
        )
    return (snr, jnp.stack(chi))


def solution(mesh):
    placed = (
        P(None, None, "freq", "bank"),
        P("bank", None, "freq", None),
        P("bank"),
        P("bank"),
        P("bank", None),
    )
    return jax.shard_map(
        per_device,
        mesh=mesh,
        in_specs=placed,
        out_specs=(P("bank", None, None, "freq", None), P("bank", "freq", None)),
        check_vma=False,
    )
```

time: 1380 us -> 282 us (0.20)
  matrix products: 890 us -> 0 us
  local copies, waits for them, and re-layouts: 191 us -> 13.2 us
  other arithmetic: 122 us -> 28.1 us
  Pallas kernels: 0 us -> 66.7 us
  blocking collectives: 15.5 us -> 38.5 us
  waiting for transfers between devices: 126 us -> 107 us
    dot_general x18 -> x0, matrix products: 890 us -> none  [the longest x1 85.3 us: per_device(): jnp.einsum(form_block, entry_re, block_sin, precision=highest)]
    unnamed x45 -> x35, local copies, waits for them, and re-layouts: 91.4 us -> 10.3 us
    all_to_all x2 -> x3, waiting for transfers between devices: 88.8 us -> 18.2 us  [per_device(): lax.all_to_all(sent.reshape(freq, -1, LANES), 'freq', split_axis=0, conca...]
    all_to_all x2 -> x0, other arithmetic: 67.5 us -> none  [the longest x1 33.8 us: per_device(): lax.all_to_all(joint_im, 'freq', split_axis=2, concat_axis=1, tiled=True)]
    pallas_call x0 -> x8, Pallas kernels: none -> 66.7 us  [the longest x1 38.7 us: bins_section(): pl.pallas_call(bins_kernel, in_specs=[smem] * 3 + [vmem] * 6, out_specs=v...]
    all_gather x1 -> x4, waiting for transfers between devices: 36.4 us -> 87.2 us  [the longest x3 87.2 us: per_device(): lax.all_gather(strain[d], 'bank', axis=0, tiled=False)]
    concatenate x2 -> x0, local copies, waits for them, and re-layouts: 38.7 us -> none  [the longest x1 19.4 us: per_device(): jnp.concatenate([whole_im.reshape(series_count, col_count, N1), bins_im.r...]
    all_to_all x3 -> x0, local copies, waits for them, and re-layouts: 37.4 us -> none  [the longest x2 19 us: per_device(): lax.all_to_all(joint_re, 'freq', split_axis=2, concat_axis=1, tiled=True)]
  transfers between devices with their start and end apart: 3 -> 7, of which waited for: 2 -> 5; matrix products, arithmetic and copies ran while one was open for 14% -> 10% of each run, Pallas kernels for 0% -> 9%
where the time goes in v1:
time: 282 us
  waiting for transfers between devices  107 us (38%)
  Pallas kernels  66.7 us (24%)
  blocking collectives  38.5 us (14%)
  other arithmetic  28.1 us (10%)
  between operations  15.3 us (5%)
  starting transfers between devices  13.5 us (5%)
  local copies, waits for them, and re-layouts  13.2 us (5%)
    all_gather x3, waiting for transfers between devices, per_device(): lax.all_gather(strain[d], 'bank', axis=0, tiled=False)  87.2 us
    pallas_call x1, Pallas kernels, bins_section(): pl.pallas_call(bins_kernel, in_specs=[smem] * 3 + [vmem] * 6, out_specs=v...  38.7 us
    psum x1, blocking collectives, per_device(): block_power = lax.psum(local_power, 'freq')  38.5 us
    all_to_all x3, waiting for transfers between devices, per_device(): lax.all_to_all(sent.reshape(freq, -1, LANES), 'freq', split_axis=0, conca...  18.2 us
    pallas_call x3, Pallas kernels, second_section(): pl.pallas_call(functools.partial(second_kernel, freq), grid=(tmpls,), in_...  15.4 us
    all_to_all x3, starting transfers between devices, per_device(): lax.all_to_all(sent.reshape(freq, -1, LANES), 'freq', split_axis=0, conca...  13.4 us
    sin x1, other arithmetic, phase(): return (jnp.cos(angle), jnp.sin(angle))  10.7 us
    unnamed x35, local copies, waits for them, and re-layouts  10.3 us
  transfers between devices with their start and end apart: 7, of which 5 were waited for; matrix products, arithmetic and copies ran while one was open for 10% of the time, Pallas kernels for 9%

profile of v1, /device:TPU:0, one launch (start us, length us, event | category | flops | bytes accessed | tf_op | source)
XLA Modules:
  0.0 282.1 jit_solution(13496097295585201561)
XLA Ops:
  7.2 0.0 copy-start
  7.2 0.0 all-gather.5.cloned.1.call-start
  7.2 2.1 fusion.33
  9.4 0.0 all-gather.5.cloned.1.call-update
  9.4 0.0 all-gather.7.cloned.1.call-start
  9.4 0.7 all-gather.7.cloned.1.call-update
  10.1 0.0 all-gather.9.cloned.1.call-start
  10.2 0.7 all-gather.9.cloned.1.call-update
  10.9 0.0 all-gather.11.cloned.1.call-start
  12.2 0.1 pad_add_fusion.1.which_ref
  12.3 28.5 %all-gather.5.cloned.1.call-done.strain_ref.refs_2_ = f32[4,2,64,512]{3,2,1,0:T(8,128)} async-done(((f32[1,2,64,512]{3,2,1,0:T(8,128)}), f32[4,2,64,512]{3,2,1,0:T(8,128)}) %all-gather.5.cloned.1.call-update) | async-done | bytes 1048592 | tf_op jit(solution)/shard_map/all_gather | solution.py:443
  40.8 29.0 %all-gather.7.cloned.1.call-done.strain_ref.refs_1_ = f32[4,2,64,512]{3,2,1,0:T(8,128)} async-done(((f32[1,2,64,512]{3,2,1,0:T(8,128)}), f32[4,2,64,512]{3,2,1,0:T(8,128)}) %all-gather.7.cloned.1.call-update) | async-done | bytes 1048592 | tf_op jit(solution)/shard_map/all_gather | solution.py:443
  69.8 29.6 %all-gather.9.cloned.1.call-done.strain_ref.refs_0_ = f32[4,2,64,512]{3,2,1,0:T(8,128)} async-done(((f32[1,2,64,512]{3,2,1,0:T(8,128)}), f32[4,2,64,512]{3,2,1,0:T(8,128)}) %all-gather.9.cloned.1.call-update) | async-done | bytes 1048592 | tf_op jit(solution)/shard_map/all_gather | solution.py:443
  99.4 0.0 copy-done
  99.5 1.2 copy-done.6
  100.7 1.2 copy-done.8
  101.9 1.2 copy-done.10
  103.1 2.7 entry_product.1
  105.9 0.0 all-gather.11.cloned.1.call-update
  105.9 2.1 fusion.20
  108.0 0.1 pad_maximum_fusion.tw_ref
  108.1 0.0 copy-done.12
  108.1 0.0 copy-done.13
  108.1 0.0 copy-done.14
  108.2 1.2 copy-done.11
  109.4 3.3 %first_section.5 = f32[8,2,2,2,64,128]{5,4,3,2,1,0:T(8,128)S(1)} custom-call(f32[2,2,64,2048]{3,2,1,0:T(8,128)S(1)} %copy-done, f32[4,2,64,512]{3,2,1,0:T(8,128)S(1)} %copy-done.11, bf16[256,256]{1,0:T(8,128)(2,1)S(1)} %copy-done.12, bf16[256,256]{1,0:T(8,128)(2,1)S(1)} %copy-done.13, f32[32,128]{1,0:T(8,128)S(1)} %copy-done.14, ...), custom_call_target="tpu_custom_call" | custom-call | flops 805306368 | bytes 4194304 | tf_op jit(solution)/shard_map/first_section/pallas_call | solution.py:165
  112.7 1.4 copy-done.3
  114.1 4.4 %all-to-all-start.2 = ((f32[8,512,128]{2,1,0:T(8,128)}), f32[8,512,128]{2,1,0:T(8,128)}, u32[]{:S(2)}, u32[]{:S(2)}) async-start(f32[8,512,128]{2,1,0:T(8,128)} %bitcast.26), calls=%async_computation.2 | async-start | bytes 4194304 | tf_op jit(solution)/shard_map/all_to_all | solution.py:473
  118.4 0.0 copy-start.16
  118.5 0.2 add_reduce_fusion
  118.7 0.1 reshape.332
  118.7 0.1 reduce_sum.46
  118.8 38.5 %psum.7 = f32[2,32]{1,0:T(2,128)S(1)} all-reduce(f32[2,32]{1,0:T(2,128)S(1)} %reduce_sum.46), channel_id=1, replica_groups=mesh['bank'=4,'freq'=8] {'freq'}, use_global_device_ids=true, to_apply=%region_2.0 | all-reduce | flops 64 | bytes 512 | tf_op jit(solution)/shard_map/psum | solution.py:451
  157.4 0.1 reduce_sum.47
  157.5 0.1 copy.14
  157.6 0.6 dynamic_slice.11
  158.2 1.2 copy-done.9
  159.4 3.3 %first_section.4 = f32[8,2,2,2,64,128]{5,4,3,2,1,0:T(8,128)S(1)} custom-call(f32[2,2,64,2048]{3,2,1,0:T(8,128)S(1)} %copy-done, f32[4,2,64,512]{3,2,1,0:T(8,128)S(1)} %copy-done.9, bf16[256,256]{1,0:T(8,128)(2,1)S(1)} %copy-done.12, bf16[256,256]{1,0:T(8,128)(2,1)S(1)} %copy-done.13, f32[32,128]{1,0:T(8,128)S(1)} %copy-done.14, ...), custom_call_target="tpu_custom_call" | custom-call | flops 805306368 | bytes 4194304 | tf_op jit(solution)/shard_map/first_section/pallas_call | solution.py:165
  162.7 0.0 copy-start.1
  162.7 1.3 copy-done.1
  164.1 0.0 all-to-all-done.2
  164.1 4.4 %all-to-all-start.1 = ((f32[8,512,128]{2,1,0:T(8,128)}), f32[8,512,128]{2,1,0:T(8,128)}, u32[]{:S(2)}, u32[]{:S(2)}) async-start(f32[8,512,128]{2,1,0:T(8,128)} %bitcast.24), calls=%async_computation.1 | async-start | bytes 4194304 | tf_op jit(solution)/shard_map/all_to_all | solution.py:473
  168.5 0.1 fusion.25
  168.5 0.1 select_reduce_fusion
  168.6 0.1 broadcast_divide_fusion
  168.7 1.2 bitcast_multiply_fusion
  169.9 2.1 fusion.18
  172.0 1.1 pad_maximum_fusion.1.tw_ref
  173.0 0.1 iota_add_fusion
  173.1 10.7 %fusion.5 = (f32[32,64,256]{2,1,0:T(8,128)}, f32[32,64,256]{2,1,0:T(8,128)}, f32[32,64,256]{2,1,0:T(8,128)}) fusion(s32[256]{0:T(256)S(1)} %iota_add_fusion.1, s32[32,64]{1,0:T(8,128)S(1)} %iota_add_fusion), kind=kLoop, calls=%fused_computation.15 | loop fusion | flops 7864320 | bytes 6300672 | tf_op jit(solution)/shard_map/sin | solution.py:59
  183.8 3.3 %first_section.3 = f32[8,2,2,2,64,128]{5,4,3,2,1,0:T(8,128)S(1)} custom-call(f32[2,2,64,2048]{3,2,1,0:T(8,128)S(1)} %copy-done, f32[4,2,64,512]{3,2,1,0:T(8,128)S(1)} %copy-done.7, bf16[256,256]{1,0:T(8,128)(2,1)S(1)} %copy-done.12, bf16[256,256]{1,0:T(8,128)(2,1)S(1)} %copy-done.13, f32[32,128]{1,0:T(8,128)S(1)} %copy-done.14, ...), custom_call_target="tpu_custom_call" | custom-call | flops 805306368 | bytes 4194304 | tf_op jit(solution)/shard_map/first_section/pallas_call | solution.py:165
  187.2 1.4 copy-done.2
  188.5 12.1 %all-to-all-done.1 = f32[8,512,128]{2,1,0:T(8,128)} async-done(((f32[8,512,128]{2,1,0:T(8,128)}), f32[8,512,128]{2,1,0:T(8,128)}, u32[]{:S(2)}, u32[]{:S(2)}) %all-to-all-start.1) | async-done | bytes 2097184 | tf_op jit(solution)/shard_map/all_to_all | solution.py:473
  200.6 4.7 %all-to-all-start = ((f32[8,512,128]{2,1,0:T(8,128)}), f32[8,512,128]{2,1,0:T(8,128)}, u32[]{:S(2)}, u32[]{:S(2)}) async-start(f32[8,512,128]{2,1,0:T(8,128)} %bitcast.25), calls=%async_computation | async-start | bytes 4194304 | tf_op jit(solution)/shard_map/all_to_all | solution.py:473
  205.3 0.7 pad_add_fusion.edge_ref
  205.9 3.7 %maximum_maximum_fusion = f32[32,128,512]{2,1,0:T(8,128)S(1)} fusion(f32[32,64,256]{2,1,0:T(8,128)} %get-tuple-element.11, f32[32,64,256]{2,1,0:T(8,128)} %get-tuple-element.10, f32[32,64,256]{2,1,0:T(8,128)S(1)} %copy-done.15), kind=kLoop, calls=%fused_computation.4 | loop fusion | flops 6291456 | bytes 14680064 | tf_op jit(solution)/shard_map/concatenate | solution.py:430
  209.6 0.0 copy-start.4
  209.6 0.0 copy-start.5
  209.6 5.7 %fusion.1 = (bf16[4096,512]{1,0:T(8,128)(2,1)}, bf16[4096,512]{1,0:T(8,128)(2,1)}) fusion(f32[32,128,512]{2,1,0:T(8,128)S(1)} %maximum_maximum_fusion), kind=kLoop, calls=%fused_computation.3 | loop fusion | flops 10485760 | bytes 16777216 | tf_op jit(solution)/shard_map/convert_element_type | solution.py:433
  215.3 5.1 %second_section.3.refs_0_ = f32[2,3,2,256,512]{4,3,2,1,0:T(8,128)} custom-call(s32[1]{0:T(128)} %bitcast.place_ref, f32[2]{0:T(128)S(1)} %rsqrt.6.scale_ref, f32[8,2,2,2,64,128]{5,4,3,2,1,0:T(8,128)} %bitcast.6.part_ref, bf16[1024,256]{1,0:T(8,128)(2,1)S(1)} %copy-done.4, bf16[1024,256]{1,0:T(8,128)(2,1)S(1)} %copy-done.5), custom_call_target="tpu_custom_call" | custom-call | flops 805306368 | bytes 8388608 | tf_op jit(solution)/shard_map/second_section/pallas_call | solution.py:306
  220.5 5.1 %second_section.4.refs_0_ = f32[2,3,2,256,512]{4,3,2,1,0:T(8,128)} custom-call(s32[1]{0:T(128)} %bitcast.place_ref, f32[2]{0:T(128)S(1)} %rsqrt.6.scale_ref, f32[8,2,2,2,64,128]{5,4,3,2,1,0:T(8,128)} %bitcast.4.part_ref, bf16[1024,256]{1,0:T(8,128)(2,1)S(1)} %copy-done.4, bf16[1024,256]{1,0:T(8,128)(2,1)S(1)} %copy-done.5, ...), custom_call_target="tpu_custom_call", output_to_operand_aliasing={{}: (5, {})} | custom-call | flops 805306368 | bytes 8388608 | tf_op jit(solution)/shard_map/second_section/pallas_call | solution.py:306
  225.6 6.1 %all-to-all-done = f32[8,512,128]{2,1,0:T(8,128)} async-done(((f32[8,512,128]{2,1,0:T(8,128)}), f32[8,512,128]{2,1,0:T(8,128)}, u32[]{:S(2)}, u32[]{:S(2)}) %all-to-all-start) | async-done | bytes 2097184 | tf_op jit(solution)/shard_map/all_to_all | solution.py:473
  231.7 5.1 %second_section.5 = f32[2,3,2,256,512]{4,3,2,1,0:T(8,128)} custom-call(s32[1]{0:T(128)} %bitcast.place_ref, f32[2]{0:T(128)S(1)} %rsqrt.6.scale_ref, f32[8,2,2,2,64,128]{5,4,3,2,1,0:T(8,128)} %bitcast.2.part_ref, bf16[1024,256]{1,0:T(8,128)(2,1)S(1)} %copy-done.4, bf16[1024,256]{1,0:T(8,128)(2,1)S(1)} %copy-done.5, ...), custom_call_target="tpu_custom_call", output_to_operand_aliasing={{}: (5, {})} | custom-call | flops 805306368 | bytes 8388608 | tf_op jit(solution)/shard_map/second_section/pallas_call | solution.py:306
  236.9 38.7 %bins.1 = f32[256,512]{1,0:T(8,128)} custom-call(s32[17]{0:T(128)} %pad_add_fusion.edge_ref, f32[16]{0:T(128)} %get-tuple-element.3.gain_ref, f32[16]{0:T(128)} %get-tuple-element.2.share_ref, f32[512,4096]{1,0:T(8,128)} %all-gather.11.cloned.1.call-done.entry_ref, bf16[4096,512]{1,0:T(8,128)(2,1)} %get-tuple-element.5.wh_ref, ...), custom_call_target="tpu_custom_call" | custom-call | flops 16106127360 | bytes 20971520 | tf_op jit(solution)/shard_map/bins/pallas_call | solution.py:399
  (24 shorter events, 0.1 us)
Async XLA Ops:
  7.2 92.3 %copy-start = (f32[2,2,64,2048]{3,2,1,0:T(8,128)S(1)}, f32[2,2,64,2048]{3,2,1,0:T(8,128)}, u32[]{:S(2)}) copy-start(f32[2,2,64,2048]{3,2,1,0:T(8,128)} %tmpl_ref.7) | copy-start | bytes 6291460
  7.2 33.6 %all-gather.5.cloned.1.call-start = ((), (), s32[]{:S(2)}) async-start(), calls=%async_computation.3 | async-start | bytes 1310720 | tf_op jit(solution)/shard_map/all_gather | solution.py:443
  9.4 60.5 %all-gather.7.cloned.1.call-start = ((), (), s32[]{:S(2)}) async-start(), calls=%async_computation.4 | async-start | bytes 1310720 | tf_op jit(solution)/shard_map/all_gather | solution.py:443
  10.1 89.3 %all-gather.9.cloned.1.call-start = ((), (), s32[]{:S(2)}) async-start(), calls=%async_computation.5 | async-start | bytes 1310720 | tf_op jit(solution)/shard_map/all_gather | solution.py:443
  10.9 226.0 %all-gather.11.cloned.1.call-start = ((), (), s32[]{:S(2)}) async-start(), calls=%async_computation.6 | async-start | bytes 9437184 | tf_op jit(solution)/shard_map/all_gather | solution.py:482
  99.5 1.2 copy-start.6
  100.7 1.2 copy-start.8
  101.9 1.2 copy-start.10
  105.9 2.3 copy-start.12
  105.9 2.3 copy-start.13
  105.9 2.3 copy-start.14
  108.2 1.2 copy-start.11
  112.7 1.4 copy-start.3
  114.1 50.0 %all-to-all-start.2 = ((f32[8,512,128]{2,1,0:T(8,128)}), f32[8,512,128]{2,1,0:T(8,128)}, u32[]{:S(2)}, u32[]{:S(2)}) async-start(f32[8,512,128]{2,1,0:T(8,128)} %bitcast.26), calls=%async_computation.2 | async-start | bytes 4194304 | tf_op jit(solution)/shard_map/all_to_all | solution.py:473
  118.4 39.0 %copy-start.16 = (s32[2,15]{1,0:T(2,128)S(1)}, s32[2,15]{1,0:T(2,128)}, u32[]{:S(2)}) copy-start(s32[2,15]{1,0:T(2,128)} %param.14) | copy-start | bytes 364
  158.2 1.2 copy-start.9
  162.7 1.3 copy-start.1
  164.1 36.5 %all-to-all-start.1 = ((f32[8,512,128]{2,1,0:T(8,128)}), f32[8,512,128]{2,1,0:T(8,128)}, u32[]{:S(2)}, u32[]{:S(2)}) async-start(f32[8,512,128]{2,1,0:T(8,128)} %bitcast.24), calls=%async_computation.1 | async-start | bytes 4194304 | tf_op jit(solution)/shard_map/all_to_all | solution.py:473
  173.1 10.7 %copy-start.7 = (f32[4,2,64,512]{3,2,1,0:T(8,128)S(1)}, f32[4,2,64,512]{3,2,1,0:T(8,128)}, u32[]{:S(2)}) copy-start(f32[4,2,64,512]{3,2,1,0:T(8,128)} %all-gather.5.cloned.1.call-done.strain_ref.refs_2_) | copy-start | bytes 3145732
  187.1 1.4 copy-start.2
  200.6 5.3 %copy-start.15 = (f32[32,64,256]{2,1,0:T(8,128)S(1)}, f32[32,64,256]{2,1,0:T(8,128)}, u32[]{:S(2)}) copy-start(f32[32,64,256]{2,1,0:T(8,128)} %get-tuple-element.9) | copy-start | bytes 6291460
  200.6 31.1 %all-to-all-start = ((f32[8,512,128]{2,1,0:T(8,128)}), f32[8,512,128]{2,1,0:T(8,128)}, u32[]{:S(2)}, u32[]{:S(2)}) async-start(f32[8,512,128]{2,1,0:T(8,128)} %bitcast.25), calls=%async_computation | async-start | bytes 4194304 | tf_op jit(solution)/shard_map/all_to_all | solution.py:473
  209.6 5.7 %copy-start.4 = (bf16[1024,256]{1,0:T(8,128)(2,1)S(1)}, bf16[1024,256]{1,0:T(8,128)(2,1)}, u32[]{:S(2)}) copy-start(bf16[1024,256]{1,0:T(8,128)(2,1)} %constant.104.clone.w2h_ref) | copy-start | bytes 1572868
  209.6 5.7 %copy-start.5 = (bf16[1024,256]{1,0:T(8,128)(2,1)S(1)}, bf16[1024,256]{1,0:T(8,128)(2,1)}, u32[]{:S(2)}) copy-start(bf16[1024,256]{1,0:T(8,128)(2,1)} %constant.105.clone.w2l_ref) | copy-start | bytes 1572868
Sparse Core Ops, SparseCore 0:
  10.1 30.6 all-gather.4
  42.4 27.4 all-gather.6
  72.0 27.4 all-gather.8
  106.0 78.5 all-gather.10

commit v2 on v1

v2 whole, which is shorter than its diff:
```python
import functools

import jax
import jax.numpy as jnp
import ml_dtypes
import numpy as np
from jax import lax
from jax.experimental import pallas as pl
from jax.experimental.pallas import tpu as pltpu
from jax.sharding import PartitionSpec as P

N1 = 2048
N2 = 512
NBLK = 32
BLOCK = N1 // NBLK
BINS = 16
LANES = 128
COARSE = N1 // LANES
FOUR = N2 // LANES
F32 = jnp.float32
BF16 = jnp.bfloat16
MIB = 1 << 20
VMEM_LIMIT = 56 * MIB
ANY = pl.BlockSpec(memory_space=pl.ANY)


def split_table(table):
    high = table.astype(ml_dtypes.bfloat16)
    low = (table - high.astype(np.float64)).astype(ml_dtypes.bfloat16)
    return high, low


def first_table():
    angle = 2 * np.pi * (np.outer(np.arange(LANES), np.arange(LANES)) % LANES) / LANES
    cos, sin = np.cos(angle), np.sin(angle)
    return split_table(np.block([[cos, sin], [-sin, cos]]))


def stage_table():
    angle = 2 * np.pi * np.outer(np.arange(COARSE), np.arange(LANES)) / N1
    return np.concatenate([np.cos(angle), np.sin(angle)]).astype(np.float32)


def second_table(cols, halves):
    order = np.arange(LANES).reshape(LANES // cols, halves, cols // halves)
    order = order.transpose(1, 0, 2).reshape(-1)
    blocks = []
    for a in range(FOUR):
        n2 = a + FOUR * np.arange(LANES)
        angle = 2 * np.pi * (np.outer(n2, order) % N2) / N2
        cos, sin = np.cos(angle), np.sin(angle)
        blocks.append(np.block([[cos, -sin], [sin, cos]]))
    return split_table(np.concatenate(blocks))


def split(x):
    high = x.astype(BF16)
    return high, (x - high.astype(F32)).astype(BF16)


def phase(index, length):
    angle = (index % length).astype(F32) * (2.0 * np.pi / length)
    return jnp.cos(angle), jnp.sin(angle)


def times_i(z):
    return (-z[1], z[0])


def plus(x, y):
    return (x[0] + y[0], x[1] + y[1])


def minus(x, y):
    return (x[0] - y[0], x[1] - y[1])


def dft4(x):
    s0, s1 = plus(x[0], x[2]), minus(x[0], x[2])
    s2, s3 = plus(x[1], x[3]), times_i(minus(x[1], x[3]))
    return [plus(s0, s2), plus(s1, s3), minus(s0, s2), minus(s1, s3)]


def turn(z, step):
    step %= 16
    if step == 0:
        return z
    if step == 4:
        return times_i(z)
    if step == 8:
        return (-z[0], -z[1])
    half = float(np.sqrt(0.5))
    if step == 2:
        return ((z[0] - z[1]) * half, (z[0] + z[1]) * half)
    if step == 6:
        return ((z[0] + z[1]) * -half, (z[0] - z[1]) * half)
    cos, sin = float(np.cos(np.pi * step / 8)), float(np.sin(np.pi * step / 8))
    return (z[0] * cos - z[1] * sin, z[0] * sin + z[1] * cos)


def dft16(x):
    columns = [dft4([x[4 * u1 + u0] for u1 in range(4)]) for u0 in range(4)]
    out = [None] * 16
    for a0 in range(4):
        ys = dft4([turn(columns[u0][a0], u0 * a0) for u0 in range(4)])
        for a1 in range(4):
            out[a0 + 4 * a1] = ys[a1]
    return out


def dot3(left, right):
    (lh, ll), (rh, rl) = left, right
    d = functools.partial(jnp.dot, preferred_element_type=F32)
    return d(lh, rh) + (d(lh, rl) + d(ll, rh))


def products(tmpl, strain_ref, where):
    per_piece = COARSE // strain_ref.shape[0]
    for u in range(COARSE):
        off = u % per_piece
        there = slice(off * LANES, (off + 1) * LANES)
        hr, hi = tmpl(0, u), tmpl(1, u)
        sr = strain_ref[(u // per_piece,) + where + (0, slice(None), there)]
        si = strain_ref[(u // per_piece,) + where + (1, slice(None), there)]
        yield u, hr * sr + hi * si, hr * si - hi * sr


def tile(u):
    return slice(u * LANES, (u + 1) * LANES)


def first_kernel(
    freq, tmpl_ref, strain_ref, wh_ref, wl_ref, stage_ref, tw_ref, *refs
):
    out_ref, gh, gl = refs[-3:]
    tmpls, _, rows, _ = tmpl_ref.shape
    for t in range(tmpls):
        got = products(lambda p, u: tmpl_ref[t, p, :, tile(u)], strain_ref, (0,))
        y = dft16([(re, im) for _, re, im in got])
        for a in range(COARSE):
            cos, sin = stage_ref[a : a + 1, :], stage_ref[COARSE + a : COARSE + a + 1, :]
            yr, yi = y[a]
            at = pl.ds((a * tmpls + t) * rows, rows)
            gh[at, :LANES], gl[at, :LANES] = split(yr * cos - yi * sin)
            gh[at, LANES:], gl[at, LANES:] = split(yr * sin + yi * cos)
    z = dot3((gh[...], gl[...]), (wh_ref[...], wl_ref[...]))
    width = LANES // freq
    slot = lax.broadcasted_iota(jnp.int32, (rows, LANES), 1) // width
    for t in range(tmpls):
        for group in range(COARSE // freq):
            turned = []
            for i in range(freq):
                a = group * freq + i
                at = slice((a * tmpls + t) * rows, (a * tmpls + t + 1) * rows)
                zr, zi = z[at, :LANES], z[at, LANES:]
                cos, sin = tw_ref[0, :, tile(a)], tw_ref[1, :, tile(a)]
                pair = (zr * cos - zi * sin, zr * sin + zi * cos)
                if i:
                    pair = tuple(pltpu.roll(v, i * width, 1) for v in pair)
                turned.append(pair)
            for q in range(freq):
                for p in range(2):
                    value = turned[(0 - q) % freq][p]
                    for s in range(1, freq):
                        value = jnp.where(slot == s, turned[(s - q) % freq][p], value)
                    out_ref[q, 0, t, p, group] = value


ROWS = 16


def first_section(freq, half, templates, strain, first, stage, twist, after):
    tmpls = templates.shape[0]
    pieces, dets, _, cols, piece_len = strain.shape
    groups = COARSE // freq
    steps = cols // ROWS
    table = pl.BlockSpec((2 * LANES, 2 * LANES), lambda c, d: (0, 0))
    return pl.pallas_call(
        functools.partial(first_kernel, freq),
        grid=(steps, dets),
        in_specs=[
            pl.BlockSpec((tmpls, 2, ROWS, N1), lambda c, d: (0, 0, half * steps + c, 0)),
            pl.BlockSpec((pieces, 1, 2, ROWS, piece_len), lambda c, d: (0, d, 0, c, 0)),
            table,
            table,
            pl.BlockSpec((2 * COARSE, LANES), lambda c, d: (0, 0)),
            pl.BlockSpec((2, ROWS, N1), lambda c, d: (0, half * steps + c, 0)),
        ]
        + [ANY] * len(after),
        out_specs=pl.BlockSpec(
            (freq, 1, tmpls, 2, groups, ROWS, LANES), lambda c, d: (0, d, 0, 0, 0, c, 0)
        ),
        out_shape=jax.ShapeDtypeStruct((freq, dets, tmpls, 2, groups, cols, LANES), F32),
        scratch_shapes=[pltpu.VMEM((COARSE * tmpls * ROWS, 2 * LANES), BF16)] * 2,
        compiler_params=pltpu.CompilerParams(vmem_limit_bytes=VMEM_LIMIT),
        cost_estimate=pl.CostEstimate(
            flops=60 * dets * tmpls * cols * N1 * LANES,
            bytes_accessed=12 * MIB,
            transcendentals=0,
        ),
        name="first_section",
    )(templates, strain, first[0], first[1], stage, twist, *after)


def entry_kernel(which_ref, tmpl_ref, strain_ref, *refs):
    out_ref = refs[-1]
    first_half = lax.broadcasted_iota(jnp.int32, (ROWS, LANES), 1) < BLOCK
    got = products(lambda p, u: tmpl_ref[0, p, :, tile(u)], strain_ref, (0,))
    for u, re, im in got:
        out_ref[:, tile(2 * u)] = jnp.where(first_half, re, pltpu.roll(im, BLOCK, 1))
        out_ref[:, tile(2 * u + 1)] = jnp.where(first_half, pltpu.roll(re, BLOCK, 1), im)


def entry_product(which, half, templates, strain, after):
    pieces, _, _, cols, piece_len = strain.shape
    steps = cols // ROWS
    return pl.pallas_call(
        entry_kernel,
        grid_spec=pltpu.PrefetchScalarGridSpec(
            num_scalar_prefetch=1,
            grid=(steps,),
            in_specs=[
                pl.BlockSpec((1, 2, ROWS, N1), lambda c, w: (w[0], 0, half * steps + c, 0)),
                pl.BlockSpec((pieces, 1, 2, ROWS, piece_len), lambda c, w: (0, w[1], 0, c, 0)),
            ]
            + [ANY] * len(after),
            out_specs=pl.BlockSpec((ROWS, 2 * N1), lambda c, w: (c, 0)),
        ),
        out_shape=jax.ShapeDtypeStruct((cols, 2 * N1), F32),
        compiler_params=pltpu.CompilerParams(vmem_limit_bytes=VMEM_LIMIT),
        cost_estimate=pl.CostEstimate(
            flops=8 * cols * N1, bytes_accessed=2 * MIB, transcendentals=0
        ),
        name="entry_product",
    )(which, templates, strain, *after)


def second_points(x, w2h_ref, w2l_ref, use):
    for a, (yr, yi) in enumerate(dft4(x)):
        y = jnp.concatenate([yr, yi], axis=0)
        at = slice(a * 2 * LANES, (a + 1) * 2 * LANES)
        z = dot3((w2h_ref[at, :], w2l_ref[at, :]), split(y))
        use(a, z[:LANES], z[LANES:])


def second_kernel(freq, halves, place_ref, scale_ref, *refs):
    part_refs, (w2h_ref, w2l_ref), rest = refs[:halves], refs[halves : halves + 2], refs[-3:]
    out_ref, hold, order = rest
    groups, cols = part_refs[0].shape[4:6]
    per = LANES // (halves * cols)
    width = LANES // freq
    scale = scale_ref[pl.program_id(0)]

    def rows_of(p, u):
        tiles = [
            jnp.concatenate(
                [ref[u * per + f, 0, 0, p, g] for ref in part_refs for f in range(per)],
                axis=0,
            )
            for g in range(groups)
        ]
        return jnp.concatenate(tiles, axis=1)

    x = [(rows_of(0, u), rows_of(1, u)) for u in range(FOUR)]

    def keep(a, re, im):
        for p, value in enumerate((re, im)):
            for g in range(groups):
                hold[p, g, pl.ds(a, LANES, stride=FOUR), :] = value[:, tile(g)] * scale

    second_points(x, w2h_ref, w2l_ref, keep)
    for p in range(2):
        for g in range(groups):
            turned = hold[p, g].T
            for s in range(freq):
                a = g * freq + lax.rem(s - place_ref[0] + freq, freq)
                for j in range(FOUR):
                    order[p, j, pl.ds(a, width, stride=COARSE), :] = turned[
                        s * width : (s + 1) * width, tile(j)
                    ]
        for j in range(FOUR):
            out_ref[0, 0, p, :, tile(j)] = order[p, j]


def second_section(place, scale, parts, second, after):
    freq, dets, tmpls, _, groups, cols, _ = parts[0].shape
    halves = len(parts)
    times = groups * LANES
    smem = pl.BlockSpec(memory_space=pltpu.SMEM)
    table = pl.BlockSpec((FOUR * 2 * LANES, 2 * LANES), lambda t, d: (0, 0))
    part = pl.BlockSpec(
        (freq, 1, 1, 2, groups, cols, LANES), lambda t, d: (0, d, t, 0, 0, 0, 0)
    )
    return pl.pallas_call(
        functools.partial(second_kernel, freq, halves),
        grid=(tmpls, dets),
        in_specs=[smem, smem] + [part] * halves + [table, table] + [ANY] * len(after),
        out_specs=pl.BlockSpec((1, 1, 2, times, N2), lambda t, d: (t, d, 0, 0, 0)),
        out_shape=jax.ShapeDtypeStruct((tmpls, dets, 2, times, N2), F32),
        scratch_shapes=[
            pltpu.VMEM((2, groups, N2, LANES), F32),
            pltpu.VMEM((2, FOUR, times, LANES), F32),
        ],
        compiler_params=pltpu.CompilerParams(vmem_limit_bytes=VMEM_LIMIT),
        cost_estimate=pl.CostEstimate(
            flops=60 * dets * tmpls * times * FOUR * LANES * LANES,
            bytes_accessed=24 * MIB,
            transcendentals=0,
        ),
        name="second_section",
    )(place, scale, *parts, *second, *after)


def bank_kernel(block_ref, inner_ref, high_ref, low_ref):
    times = block_ref.shape[-1]
    bc, bs = block_ref[0, 0:1, :], block_ref[0, 1:2, :]
    rc, rs = inner_ref[0], inner_ref[1]
    cos, sin = bc * rc - bs * rs, bc * rs + bs * rc
    cos, sin = split(cos), split(sin)
    for ref, c, s in zip((high_ref, low_ref), cos, sin):
        ref[:BLOCK, :times] = c
        ref[:BLOCK, times:] = s
        ref[BLOCK:, :times] = -s
        ref[BLOCK:, times:] = c


def bank_table(own_time):
    times = own_time.shape[0]
    block = jnp.arange(NBLK, dtype=jnp.int32)[:, None] * own_time[None, :]
    block = jnp.stack(phase(block, NBLK), axis=1)
    inner = jnp.arange(BLOCK, dtype=jnp.int32)[:, None] * own_time[None, :]
    inner = jnp.stack(phase(inner, N1))
    return pl.pallas_call(
        bank_kernel,
        grid=(NBLK,),
        in_specs=[
            pl.BlockSpec((1, 2, times), lambda b: (b, 0, 0)),
            pl.BlockSpec((2, BLOCK, times), lambda b: (0, 0, 0)),
        ],
        out_specs=[pl.BlockSpec((2 * BLOCK, 2 * times), lambda b: (b, 0))] * 2,
        out_shape=[jax.ShapeDtypeStruct((2 * N1, 2 * times), BF16)] * 2,
        compiler_params=pltpu.CompilerParams(vmem_limit_bytes=VMEM_LIMIT),
        cost_estimate=pl.CostEstimate(
            flops=8 * N1 * times, bytes_accessed=8 * MIB, transcendentals=0
        ),
        name="bank_table",
    )(block, inner)


def bins_first_kernel(pieces, place_ref, edge_ref, *refs):
    piece_refs = refs[:pieces]
    wh_ref, wl_ref, tw_ref = refs[pieces : pieces + 3]
    level_ref, total_ref, xh, xl, acc = refs[-5:]
    times = total_ref.shape[-1]
    cols = piece_refs[0].shape[0]
    level = pl.program_id(0)

    @pl.when(level == 0)
    def _():
        for k, ref in enumerate(piece_refs):
            row = pl.multiple_of((place_ref[0] ^ k) * cols, cols)

            def cut(i, carry):
                at = pl.ds(pl.multiple_of(i * FOUR * LANES, FOUR * LANES), FOUR * LANES)
                xh[pl.ds(row, cols), at], xl[pl.ds(row, cols), at] = split(ref[:, at])
                return carry

            lax.fori_loop(0, 2 * N1 // (FOUR * LANES), cut, 0)
        total_ref[...] = jnp.zeros_like(total_ref)

    def add(block, blocks):
        at = pl.ds(pl.multiple_of(block * LANES, LANES), blocks * LANES)
        acc[...] += dot3((xh[:, at], xl[:, at]), (wh_ref[at, :], wl_ref[at, :]))

    start, end = edge_ref[level], edge_ref[level + 1]
    acc[...] = jnp.zeros_like(acc)

    def two(i, carry):
        add(start + 2 * i, 2)
        return carry

    lax.fori_loop(0, (end - start) // 2, two, 0)

    @pl.when((end - start) % 2 == 1)
    def _():
        add(end - 1, 1)

    for u in range(pieces * cols // LANES):
        at = tile(u)
        re, im = acc[at, :times], acc[at, times:]
        cos, sin = tw_ref[0, at, :], tw_ref[1, at, :]
        vr, vi = re * cos - im * sin, re * sin + im * cos
        level_ref[0, 0, at, :] = vr
        level_ref[0, 1, at, :] = vi
        total_ref[0, at, :] += vr
        total_ref[1, at, :] += vi


def bins_first(place, edges, pieces, table, twist, after):
    cols = pieces[0].shape[0]
    rows, times = twist.shape[1:]
    smem = pl.BlockSpec(memory_space=pltpu.SMEM)
    fixed = lambda shape: pl.BlockSpec(shape, lambda i: (0,) * len(shape))
    return pl.pallas_call(
        functools.partial(bins_first_kernel, len(pieces)),
        grid=(BINS,),
        in_specs=[smem, smem]
        + [fixed((cols, 2 * N1))] * len(pieces)
        + [fixed((2 * N1, 2 * times))] * 2
        + [fixed((2, rows, times))]
        + [ANY] * len(after),
        out_specs=[
            pl.BlockSpec((1, 2, rows, times), lambda i: (i, 0, 0, 0)),
            fixed((2, rows, times)),
        ],
        out_shape=[
            jax.ShapeDtypeStruct((BINS, 2, rows, times), F32),
            jax.ShapeDtypeStruct((2, rows, times), F32),
        ],
        scratch_shapes=[
            pltpu.VMEM((rows, 2 * N1), BF16),
            pltpu.VMEM((rows, 2 * N1), BF16),
            pltpu.VMEM((rows, 2 * times), F32),
        ],
        compiler_params=pltpu.CompilerParams(vmem_limit_bytes=VMEM_LIMIT),
        cost_estimate=pl.CostEstimate(
            flops=600 * rows * LANES * times * BINS,
            bytes_accessed=20 * MIB,
            transcendentals=0,
        ),
        name="bins_first",
    )(place, edges, *pieces, *table, twist, *after)


def bins_second_kernel(halves, gain_ref, share_ref, *refs):
    level_refs, total_refs = refs[:halves], refs[halves : 2 * halves]
    w2h_ref, w2l_ref, out_ref, chi, hold = refs[2 * halves :]
    times = out_ref.shape[0]
    part_rows = LANES // halves
    level = pl.program_id(0)
    gain, share = gain_ref[level], share_ref[level]

    @pl.when(level == 0)
    def _():
        chi[...] = jnp.zeros_like(chi)

    def rows_of(p, u):
        at = slice(u * part_rows, (u + 1) * part_rows)
        return jnp.concatenate(
            [
                one[0, p, at, :] * gain - whole[p, at, :] * share
                for one, whole in zip(level_refs, total_refs)
            ],
            axis=0,
        )

    def keep(a, re, im):
        chi[a] += re * re + im * im

    x = [(rows_of(0, u), rows_of(1, u)) for u in range(FOUR)]
    second_points(x, w2h_ref, w2l_ref, keep)

    @pl.when(level == BINS - 1)
    def _():
        for g in range(times // LANES):
            for a in range(FOUR):
                hold[pl.ds(a, LANES, stride=FOUR), :] = chi[a, :, tile(g)]
            out_ref[tile(g), :] = hold[...].T


def bins_second(gain, share, levels, totals, second):
    _, _, rows, times = levels[0].shape
    halves = len(levels)
    smem = pl.BlockSpec(memory_space=pltpu.SMEM)
    fixed = lambda shape: pl.BlockSpec(shape, lambda i: (0,) * len(shape))
    return pl.pallas_call(
        functools.partial(bins_second_kernel, halves),
        grid=(BINS,),
        in_specs=[smem, smem]
        + [pl.BlockSpec((1, 2, rows, times), lambda i: (i, 0, 0, 0))] * halves
        + [fixed((2, rows, times))] * halves
        + [fixed((FOUR * 2 * LANES, 2 * LANES))] * 2,
        out_specs=fixed((times, N2)),
        out_shape=jax.ShapeDtypeStruct((times, N2), F32),
        scratch_shapes=[
            pltpu.VMEM((FOUR, LANES, times), F32),
            pltpu.VMEM((N2, LANES), F32),
        ],
        compiler_params=pltpu.CompilerParams(vmem_limit_bytes=VMEM_LIMIT),
        cost_estimate=pl.CostEstimate(
            flops=60 * BINS * FOUR * LANES**2 * times,
            bytes_accessed=20 * MIB,
            transcendentals=0,
        ),
        name="bins_second",
    )(gain, share, *levels, *totals, *second)


def spread_pieces(own, freq):
    def swap(x, k):
        return lax.ppermute(x, "freq", [(i, i ^ k) for i in range(freq)])

    pieces = [own] + [None] * (freq - 1)
    for k in range(2, freq, 2):
        pieces[k] = swap(own, k)
    for k in range(1, freq, 2):
        pieces[k] = swap(pieces[k - 1], 1)
    return pieces


HALVES = 2


def per_device(strain, templates, coinc_tmpl, coinc_det, bin_edges):
    freq = lax.axis_size("freq")
    place = lax.axis_index("freq").astype(jnp.int32)
    tmpls, _, cols, _ = templates.shape
    slots = coinc_tmpl.shape[0]
    times = N1 // freq
    part = cols // HALVES

    strains = [
        lax.all_gather(strain[:, :, h * part : (h + 1) * part], "bank", axis=0, tiled=False)
        for h in range(HALVES)
    ]
    first = tuple(jnp.asarray(t) for t in first_table())
    second = tuple(jnp.asarray(t) for t in second_table(cols, HALVES))
    stage = jnp.asarray(stage_table())

    power = (templates[:, 0] ** 2 + templates[:, 1] ** 2).sum(axis=1)
    local_power = power.reshape(tmpls, NBLK, BLOCK).sum(axis=2)
    block_power = lax.psum(local_power, "freq")
    sigma_sq = block_power.sum(axis=1)
    inv_sigma = lax.rsqrt(sigma_sq)
    bin_of = jnp.sum(
        jnp.arange(NBLK, dtype=jnp.int32)[None, :, None] >= bin_edges[:, None, :], axis=2
    )
    inside = bin_of[:, None, :] == jnp.arange(BINS, dtype=jnp.int32)[None, :, None]
    weights = jnp.where(inside, block_power[:, None, :], 0.0).sum(axis=2) / sigma_sq[:, None]

    column = place * cols + jnp.arange(cols, dtype=jnp.int32)
    lane = jnp.arange(N1, dtype=jnp.int32)
    time_of_lane = lane // LANES + COARSE * (lane % LANES)
    twist = jnp.stack(phase(column[:, None] * time_of_lane[None, :], N1 * N2))
    own_time = place * times + jnp.arange(times, dtype=jnp.int32)
    table = bank_table(own_time)
    own_twist = []
    for h in range(HALVES):
        rows = jnp.arange(freq * part, dtype=jnp.int32)
        rows = rows // part * cols + h * part + rows % part
        own_twist.append(jnp.stack(phase(rows[:, None] * own_time[None, :], N1 * N2)))

    which = [jnp.stack([coinc_tmpl[j], coinc_det[j]]) for j in range(slots)]
    which, inv_sigma, weights, twist, table, own_twist = lax.optimization_barrier(
        (which, inv_sigma, weights, twist, table, own_twist)
    )
    here = place.reshape(1)
    pieces, sent, parts = [], [], []
    for h in range(HALVES):
        after = [x for entry in pieces for x in entry[2::2]] + sent
        half = [entry_product(w, h, templates, strains[h], after) for w in which]
        pieces = [spread_pieces(x, freq) for x in half]
        if h == 0:
            early = pieces
        sent = [first_section(freq, h, templates, strains[h], first, stage, twist, half)]
        got = lax.all_to_all(
            sent[0].reshape(freq, -1, LANES), "freq", split_axis=0, concat_axis=0, tiled=True
        )
        parts.append(got.reshape(sent[0].shape))

    chi = []
    for j in range(slots):
        t = coinc_tmpl[j]
        ends = jnp.zeros((1,), jnp.int32), jnp.full((1,), NBLK, jnp.int32)
        edges = jnp.concatenate([ends[0], bin_edges[t], ends[1]])
        halves = [
            bins_first(here, edges, entry[j], table, own_twist[h], sent)
            for h, entry in enumerate((early, pieces))
        ]
        levels, totals = zip(*halves)
        gain = inv_sigma[t] * lax.rsqrt(weights[t])
        chi.append(bins_second(gain, gain * weights[t], levels, totals, second))
    snr = second_section(here, inv_sigma, parts, second, chi)
    return (snr, jnp.stack(chi))


def solution(mesh):
    placed = (
        P(None, None, "freq", "bank"),
        P("bank", None, "freq", None),
        P("bank"),
        P("bank"),
        P("bank", None),
    )
    return jax.shard_map(
        per_device,
        mesh=mesh,
        in_specs=placed,
        out_specs=(P("bank", None, None, "freq", None), P("bank", "freq", None)),
        check_vma=False,
    )
```

time: 282 us -> 225 us (0.80)
  waiting for transfers between devices: 107 us -> 54.6 us
  Pallas kernels: 66.7 us -> 102 us
  blocking collectives: 38.5 us -> 15.5 us
  other arithmetic: 28.1 us -> 12.1 us
  local copies, waits for them, and re-layouts: 13.2 us -> 5.85 us
  starting transfers between devices: 13.5 us -> 17 us
    all_gather x4 -> x2, waiting for transfers between devices: 87.2 us -> 20.6 us  [per_device(): lax.all_gather(strain[:, :, h * part:(h + 1) * part], 'bank', axis=0, til...]
    pallas_call x7, Pallas kernels: 64 us -> 97 us  [the longest x2 35.7 us: bins_first(): pl.pallas_call(functools.partial(bins_first_kernel, len(pieces)), grid=(B...]
    psum x1, blocking collectives: 38.5 us -> 15.5 us  [per_device(): block_power = lax.psum(local_power, 'freq')]
    ppermute x0 -> x14, waiting for transfers between devices: none -> 21.1 us  [swap(): return lax.ppermute(x, 'freq', [(i, i ^ k) for i in range(freq)])]
    sin x1 -> x0, other arithmetic: 10.7 us -> none  [phase(): return (jnp.cos(angle), jnp.sin(angle))]
    ppermute x0 -> x14, starting transfers between devices: none -> 8.56 us  [swap(): return lax.ppermute(x, 'freq', [(i, i ^ k) for i in range(freq)])]
    unnamed x35 -> x17, local copies, waits for them, and re-layouts: 10.3 us -> 3.02 us
    all_to_all x3 -> x2, waiting for transfers between devices: 18.2 us -> 12.2 us  [per_device(): lax.all_to_all(sent[0].reshape(freq, -1, LANES), 'freq', split_axis=0, co...]
  transfers between devices with their start and end apart: 7 -> 18, of which waited for: 5 -> 4; matrix products, arithmetic and copies ran while one was open for 10% -> 6% of each run, Pallas kernels for 9% -> 41%
where the time goes in v2:
time: 225 us; the launch traced here: 223 us
  Pallas kernels  102 us (45%)
  waiting for transfers between devices  54.6 us (24%)
  starting transfers between devices  17 us (8%)
  blocking collectives  15.5 us (7%)
  between operations  15.5 us (7%)
  other arithmetic  12.1 us (5%)
  local copies, waits for them, and re-layouts  5.85 us (3%)
    pallas_call x2, Pallas kernels, bins_first(): pl.pallas_call(functools.partial(bins_first_kernel, len(pieces)), grid=(B...  35.7 us
    ppermute x14, waiting for transfers between devices, swap(): return lax.ppermute(x, 'freq', [(i, i ^ k) for i in range(freq)])  21.1 us
    all_gather x2, waiting for transfers between devices, per_device(): lax.all_gather(strain[:, :, h * part:(h + 1) * part], 'bank', axis=0, til...  20.6 us
    pallas_call x1, Pallas kernels, bins_second(): pl.pallas_call(functools.partial(bins_second_kernel, halves), grid=(BINS,...  19 us
    pallas_call x1, Pallas kernels, bank_table(): pl.pallas_call(bank_kernel, grid=(NBLK,), in_specs=[pl.BlockSpec((1, 2, t...  15.6 us
    psum x1, blocking collectives, per_device(): block_power = lax.psum(local_power, 'freq')  15.5 us
    pallas_call x2, Pallas kernels, first_section(): pl.pallas_call(functools.partial(first_kernel, freq), grid=(steps, dets),...  15.2 us
    all_to_all x2, waiting for transfers between devices, per_device(): lax.all_to_all(sent[0].reshape(freq, -1, LANES), 'freq', split_axis=0, co...  12.2 us
  transfers between devices with their start and end apart: 18, of which 4 were waited for; matrix products, arithmetic and copies ran while one was open for 6% of the time, Pallas kernels for 41%

profile of v2, /device:TPU:0, one launch (start us, length us, event | category | flops | bytes accessed | tf_op | source)
XLA Modules:
  0.0 223.1 jit_solution(16275031192269078908)
XLA Ops:
  7.2 0.0 copy-start
  7.2 0.0 all-gather.5.cloned.1.call-start
  7.2 2.2 fusion.46
  9.4 0.0 all-gather.5.cloned.1.call-update
  9.4 0.0 all-gather.7.cloned.1.call-start
  9.5 0.7 all-gather.7.cloned.1.call-update
  10.2 0.3 fusion.24
  10.5 1.0 fusion.39
  11.6 0.2 add_reduce_fusion
  13.1 0.7 pad_maximum_fusion.3.inner_ref
  13.7 0.7 pad_maximum_fusion.4.block_ref
  14.4 0.6 pad_add_fusion.which_ref
  15.0 0.1 reshape.662
  15.1 0.1 reduce_sum.46
  15.2 15.5 %psum.7 = f32[2,32]{1,0:T(2,128)S(1)} all-reduce(f32[2,32]{1,0:T(2,128)S(1)} %reduce_sum.46), channel_id=1, replica_groups=mesh['bank'=4,'freq'=8] {'freq'}, use_global_device_ids=true, to_apply=%region_2.0 | all-reduce | flops 64 | bytes 512 | tf_op jit(solution)/shard_map/psum | solution.py:532
  30.7 0.1 reduce_sum.47
  30.8 0.1 copy.13
  30.9 15.6 %bank_table.1 = (bf16[4096,512]{1,0:T(8,128)(2,1)}, bf16[4096,512]{1,0:T(8,128)(2,1)}) custom-call(f32[32,2,256]{2,1,0:T(2,128)} %pad_maximum_fusion.4.block_ref, f32[2,64,256]{2,1,0:T(8,128)} %pad_maximum_fusion.3.inner_ref), custom_call_target="tpu_custom_call" | custom-call | flops 4194304 | bytes 8388608 | tf_op jit(solution)/shard_map/bank_table/pallas_call | solution.py:333
  46.6 0.1 fusion.32
  46.6 0.1 select_reduce_fusion
  46.7 2.1 fusion.12
  48.9 1.1 pad_maximum_fusion.1
  49.9 0.1 broadcast_divide_fusion
  50.0 2.1 fusion.10
  52.1 1.1 pad_maximum_fusion.tw_ref
  53.2 2.7 %entry_product.2.refs_0_ = f32[32,4096]{1,0:T(8,128)} custom-call(s32[2]{0:T(128)} %pad_add_fusion.which_ref, f32[2,2,64,2048]{3,2,1,0:T(8,128)} %tmpl_ref.7, f32[4,3,2,32,512]{4,3,2,1,0:T(8,128)} %bitcast.25), custom_call_target="tpu_custom_call" | custom-call | flops 524288 | bytes 2097152 | tf_op jit(solution)/shard_map/entry_product/pallas_call | solution.py:217
  55.9 0.0 collective-permute-start
  55.9 0.5 collective-permute-start.1
  56.5 3.0 %collective-permute-start.2 = (f32[32,4096]{1,0:T(8,128)}, f32[32,4096]{1,0:T(8,128)S(1)}, u32[]{:S(2)}, u32[]{:S(2)}) collective-permute-start(f32[32,4096]{1,0:T(8,128)} %entry_product.2.refs_0_), channel_id=1, source_target_pairs={{0,6},{1,7},{2,4},{3,5},{4,2},{5,3},{6,0},{7,1},{8,14},{9,15},{10,... | collective-permute-start | bytes 1572872 | tf_op jit(solution)/shard_map/ppermute | solution.py:501
  59.4 7.6 %first_section.2.refs_3_ = f32[8,3,2,2,2,32,128]{6,5,4,3,2,1,0:T(8,128)} custom-call(f32[2,2,64,2048]{3,2,1,0:T(8,128)} %tmpl_ref.7, f32[4,3,2,32,512]{4,3,2,1,0:T(8,128)} %bitcast.26, bf16[256,256]{1,0:T(8,128)(2,1)} %constant.153.clone.wh_ref, bf16[256,256]{1,0:T(8,128)(2,1)} %constant.154.clone.wl_ref, f32[32,128]{1,0:T(8,128)} %constant.157.clone.stage_ref, ...), custom_call_target="tpu_custom_call" | custom-call | flops 3019898880 | bytes 12582912 | tf_op jit(solution)/shard_map/first_section/pallas_call | solution.py:178
  67.0 20.5 %all-gather.7.cloned.1.call-done = f32[12,2,32,512]{3,2,1,0:T(8,128)} async-done(((f32[3,2,32,512]{3,2,1,0:T(8,128)}), f32[12,2,32,512]{3,2,1,0:T(8,128)}) %all-gather.7.cloned.1.call-update) | async-done | bytes 1572880 | tf_op jit(solution)/shard_map/all_gather | solution.py:523
  87.6 0.0 collective-permute-done.refs_0_.refs_2_
  87.6 0.0 collective-permute-done.1.refs_1_.refs_4_
  87.6 0.0 collective-permute-done.2.refs_2_.refs_6_
  87.6 0.8 copy-done.2
  88.3 0.2 copy-done.3
  88.6 0.2 copy-done.4
  88.7 2.8 %entry_product.3.refs_0_ = f32[32,4096]{1,0:T(8,128)} custom-call(s32[2]{0:T(128)} %pad_add_fusion.which_ref, f32[2,2,64,2048]{3,2,1,0:T(8,128)} %tmpl_ref.7, f32[4,3,2,32,512]{4,3,2,1,0:T(8,128)} %bitcast.23, f32[32,4096]{1,0:T(8,128)} %copy-done.2, f32[32,4096]{1,0:T(8,128)} %copy-done.3, f32[32,4096]{1,0:T(8,128)} %copy-done.4, ...), custom_call_target="tpu_custom_call" | custom-call | flops 524288 | bytes 2097152 | tf_op jit(solution)/shard_map/entry_product/pallas_call | solution.py:217
  91.5 1.5 collective-permute-start.10
  92.9 1.5 collective-permute-start.12
  94.4 0.6 collective-permute-start.8
  94.9 0.0 collective-permute-start.4
  95.0 0.5 collective-permute-start.5
  95.5 21.1 %collective-permute-done.10.refs_4_ = f32[32,4096]{1,0:T(8,128)} collective-permute-done((f32[32,4096]{1,0:T(8,128)}, f32[32,4096]{1,0:T(8,128)}, u32[]{:S(2)}, u32[]{:S(2)}) %collective-permute-start.10) | collective-permute-done | bytes 524320 | tf_op jit(solution)/shard_map/ppermute | solution.py:501
  116.6 0.6 dynamic_slice.10
  117.1 0.7 pad_add_fusion.1.edge_ref
  117.8 1.1 bitcast_multiply_fusion
  118.9 3.8 %all-to-all-start = ((f32[8,768,128]{2,1,0:T(8,128)}), f32[8,768,128]{2,1,0:T(8,128)S(1)}, u32[]{:S(2)}, u32[]{:S(2)}) async-start(f32[8,768,128]{2,1,0:T(8,128)} %bitcast.2), calls=%async_computation | async-start | bytes 6291456 | tf_op jit(solution)/shard_map/all_to_all | solution.py:566
  122.6 7.6 %first_section.3.refs_11_ = f32[8,3,2,2,2,32,128]{6,5,4,3,2,1,0:T(8,128)} custom-call(f32[2,2,64,2048]{3,2,1,0:T(8,128)} %tmpl_ref.7, f32[4,3,2,32,512]{4,3,2,1,0:T(8,128)} %bitcast.24, bf16[256,256]{1,0:T(8,128)(2,1)} %constant.153.clone.wh_ref, bf16[256,256]{1,0:T(8,128)(2,1)} %constant.154.clone.wl_ref, f32[32,128]{1,0:T(8,128)} %constant.157.clone.stage_ref, ...), custom_call_target="tpu_custom_call" | custom-call | flops 3019898880 | bytes 12582912 | tf_op jit(solution)/shard_map/first_section/pallas_call | solution.py:178
  130.2 0.5 collective-permute-start.7
  130.7 0.0 collective-permute-done.8.refs_2_
  130.7 0.1 collective-permute-start.11
  130.8 0.0 collective-permute-done.4.refs_3_
  130.8 0.4 collective-permute-start.13
  131.2 0.0 collective-permute-done.5.refs_5_
  131.2 0.1 collective-permute-start.9
  131.3 17.8 %bins_first.2 = (f32[16,2,256,256]{3,2,1,0:T(8,128)}, f32[2,256,256]{2,1,0:T(8,128)}) custom-call(s32[1]{0:T(128)} %bitcast.place_ref, s32[17]{0:T(128)} %pad_add_fusion.1.edge_ref, f32[32,4096]{1,0:T(8,128)} %entry_product.2.refs_0_, f32[32,4096]{1,0:T(8,128)} %copy-done.6, f32[32,4096]{1,0:T(8,128)} %copy-done.2, ...), custom_call_target="tpu_custom_call" | custom-call | flops 80530636800 | bytes 20971520 | tf_op jit(solution)/shard_map/bins_first/pallas_call | solution.py:404
  149.1 11.4 %all-to-all-done = f32[8,768,128]{2,1,0:T(8,128)S(1)} async-done(((f32[8,768,128]{2,1,0:T(8,128)}), f32[8,768,128]{2,1,0:T(8,128)S(1)}, u32[]{:S(2)}, u32[]{:S(2)}) %all-to-all-start) | async-done | bytes 3145760 | tf_op jit(solution)/shard_map/all_to_all | solution.py:566
  160.5 1.8 copy-done.1
  162.3 4.6 %all-to-all-start.1 = ((f32[8,768,128]{2,1,0:T(8,128)}), f32[8,768,128]{2,1,0:T(8,128)}, u32[]{:S(2)}, u32[]{:S(2)}) async-start(f32[8,768,128]{2,1,0:T(8,128)} %bitcast.22), calls=%async_computation.1 | async-start | bytes 6291456 | tf_op jit(solution)/shard_map/all_to_all | solution.py:566
  167.0 17.8 %bins_first.3 = (f32[16,2,256,256]{3,2,1,0:T(8,128)}, f32[2,256,256]{2,1,0:T(8,128)}) custom-call(s32[1]{0:T(128)} %bitcast.place_ref, s32[17]{0:T(128)} %pad_add_fusion.1.edge_ref, f32[32,4096]{1,0:T(8,128)} %entry_product.3.refs_0_, f32[32,4096]{1,0:T(8,128)} %collective-permute-done.7.refs_1_, f32[32,4096]{1,0:T(8,128)} %collective-permute-done.8.refs_2_, ...), custom_call_target="tpu_custom_call" | custom-call | flops 80530636800 | bytes 20971520 | tf_op jit(solution)/shard_map/bins_first/pallas_call | solution.py:404
  184.8 19.0 %bins_second.1.refs_4_ = f32[256,512]{1,0:T(8,128)} custom-call(f32[16]{0:T(128)} %get-tuple-element.31.gain_ref, f32[16]{0:T(128)} %get-tuple-element.30.share_ref, f32[16,2,256,256]{3,2,1,0:T(8,128)} %get-tuple-element.25.refs_0_, f32[16,2,256,256]{3,2,1,0:T(8,128)} %get-tuple-element.27.refs_1_, f32[2,256,256]{2,1,0:T(8,128)} %get-tuple-element.28.refs_2_, ...), custom_call_target="tpu_custom_call" | custom-call | flops 16106127360 | bytes 20971520 | tf_op jit(solution)/shard_map/bins_second/pallas_call | solution.py:476
  203.8 0.9 all-to-all-done.1
  204.7 11.6 %second_section.1 = f32[2,3,2,256,512]{4,3,2,1,0:T(8,128)} custom-call(s32[1]{0:T(128)} %bitcast.place_ref, f32[2]{0:T(128)} %copy-done.7, f32[8,3,2,2,2,32,128]{6,5,4,3,2,1,0:T(8,128)} %bitcast.21, f32[8,3,2,2,2,32,128]{6,5,4,3,2,1,0:T(8,128)} %bitcast.6.refs_1_, bf16[1024,256]{1,0:T(8,128)(2,1)} %constant.155.clone.refs_4_.refs_2_, ...), custom_call_target="tpu_custom_call" | custom-call | flops 6039797760 | bytes 25165824 | tf_op jit(solution)/shard_map/second_section/pallas_call | solution.py:294
  (29 shorter events, 0.1 us)
Async XLA Ops:
  7.2 4.4 %copy-start = (f32[2,2,64,2048]{3,2,1,0:T(8,128)S(1)}, f32[2,2,64,2048]{3,2,1,0:T(8,128)}, u32[]{:S(2)}) copy-start(f32[2,2,64,2048]{3,2,1,0:T(8,128)} %tmpl_ref.7) | copy-start | bytes 6291460
  7.2 23.7 %copy-start.5 = (s32[2,15]{1,0:T(2,128)S(1)}, s32[2,15]{1,0:T(2,128)}, u32[]{:S(2)}) copy-start(s32[2,15]{1,0:T(2,128)} %param.14) | copy-start | bytes 364
  7.2 46.0 %all-gather.5.cloned.1.call-start = ((), (), s32[]{:S(2)}) async-start(), calls=%async_computation.2 | async-start | bytes 1966080 | tf_op jit(solution)/shard_map/all_gather | solution.py:523
  9.4 78.1 %all-gather.7.cloned.1.call-start = ((), (), s32[]{:S(2)}) async-start(), calls=%async_computation.3 | async-start | bytes 1966080 | tf_op jit(solution)/shard_map/all_gather | solution.py:523
  30.9 85.6 %copy-start.7 = (f32[2]{0:T(128)}, f32[2]{0:T(128)S(1)}, u32[]{:S(2)}) copy-start(f32[2]{0:T(128)S(1)} %rsqrt.6.scale_ref) | copy-start | bytes 28
  55.9 31.6 %collective-permute-start = (f32[32,4096]{1,0:T(8,128)}, f32[32,4096]{1,0:T(8,128)S(1)}, u32[]{:S(2)}, u32[]{:S(2)}) collective-permute-start(f32[32,4096]{1,0:T(8,128)} %entry_product.2.refs_0_), channel_id=1, source_target_pairs={{0,2},{1,3},{2,0},{3,1},{4,6},{5,7},{6,4},{7,5},{8,10},{9,11},{10,... | collective-permute-start | bytes 1572872 | tf_op jit(solution)/shard_map/ppermute | solution.py:501
  55.9 31.6 %collective-permute-start.1 = (f32[32,4096]{1,0:T(8,128)}, f32[32,4096]{1,0:T(8,128)S(1)}, u32[]{:S(2)}, u32[]{:S(2)}) collective-permute-start(f32[32,4096]{1,0:T(8,128)} %entry_product.2.refs_0_), channel_id=1, source_target_pairs={{0,4},{1,5},{2,6},{3,7},{4,0},{5,1},{6,2},{7,3},{8,12},{9,13},{10,... | collective-permute-start | bytes 1572872 | tf_op jit(solution)/shard_map/ppermute | solution.py:501
  56.5 31.1 %collective-permute-start.2 = (f32[32,4096]{1,0:T(8,128)}, f32[32,4096]{1,0:T(8,128)S(1)}, u32[]{:S(2)}, u32[]{:S(2)}) collective-permute-start(f32[32,4096]{1,0:T(8,128)} %entry_product.2.refs_0_), channel_id=1, source_target_pairs={{0,6},{1,7},{2,4},{3,5},{4,2},{5,3},{6,0},{7,1},{8,14},{9,15},{10,... | collective-permute-start | bytes 1572872 | tf_op jit(solution)/shard_map/ppermute | solution.py:501
  59.4 35.5 %collective-permute-start.3 = (f32[32,4096]{1,0:T(8,128)}, f32[32,4096]{1,0:T(8,128)S(1)}, u32[]{:S(2)}, u32[]{:S(2)}) collective-permute-start(f32[32,4096]{1,0:T(8,128)} %entry_product.2.refs_0_), channel_id=1, source_target_pairs={{0,1},{1,0},{2,3},{3,2},{4,5},{5,4},{6,7},{7,6},{8,9},{9,8},{10,11... | collective-permute-start | bytes 1572872 | tf_op jit(solution)/shard_map/ppermute | solution.py:501
  87.6 0.8 copy-start.2
  87.6 1.0 copy-start.3
  87.6 1.1 copy-start.4
  91.5 25.1 %collective-permute-start.10 = (f32[32,4096]{1,0:T(8,128)}, f32[32,4096]{1,0:T(8,128)}, u32[]{:S(2)}, u32[]{:S(2)}) collective-permute-start(f32[32,4096]{1,0:T(8,128)} %entry_product.3.refs_0_), channel_id=1, source_target_pairs={{0,4},{1,5},{2,6},{3,7},{4,0},{5,1},{6,2},{7,3},{8,12},{9,13},{10,... | collective-permute-start | bytes 1572872 | tf_op jit(solution)/shard_map/ppermute | solution.py:501
  92.9 37.3 %collective-permute-start.12 = (f32[32,4096]{1,0:T(8,128)}, f32[32,4096]{1,0:T(8,128)}, u32[]{:S(2)}, u32[]{:S(2)}) collective-permute-start(f32[32,4096]{1,0:T(8,128)} %entry_product.3.refs_0_), channel_id=1, source_target_pairs={{0,6},{1,7},{2,4},{3,5},{4,2},{5,3},{6,0},{7,1},{8,14},{9,15},{10,... | collective-permute-start | bytes 1572872 | tf_op jit(solution)/shard_map/ppermute | solution.py:501
  94.4 36.3 %collective-permute-start.8 = (f32[32,4096]{1,0:T(8,128)}, f32[32,4096]{1,0:T(8,128)}, u32[]{:S(2)}, u32[]{:S(2)}) collective-permute-start(f32[32,4096]{1,0:T(8,128)} %entry_product.3.refs_0_), channel_id=1, source_target_pairs={{0,2},{1,3},{2,0},{3,1},{4,6},{5,7},{6,4},{7,5},{8,10},{9,11},{10,... | collective-permute-start | bytes 1572872 | tf_op jit(solution)/shard_map/ppermute | solution.py:501
  94.9 35.9 %collective-permute-start.4 = (f32[32,4096]{1,0:T(8,128)}, f32[32,4096]{1,0:T(8,128)}, u32[]{:S(2)}, u32[]{:S(2)}) collective-permute-start(f32[32,4096]{1,0:T(8,128)} %copy-done.2), channel_id=1, source_target_pairs={{0,1},{1,0},{2,3},{3,2},{4,5},{5,4},{6,7},{7,6},{8,9},{9,8},{10,11... | collective-permute-start | bytes 1572872 | tf_op jit(solution)/shard_map/ppermute | solution.py:501
  95.0 21.6 %copy-start.6 = (f32[32,4096]{1,0:T(8,128)}, f32[32,4096]{1,0:T(8,128)S(1)}, u32[]{:S(2)}) copy-start(f32[32,4096]{1,0:T(8,128)S(1)} %collective-permute-done.3.refs_1_) | copy-start | bytes 1572868
  95.0 36.3 %collective-permute-start.5 = (f32[32,4096]{1,0:T(8,128)}, f32[32,4096]{1,0:T(8,128)}, u32[]{:S(2)}, u32[]{:S(2)}) collective-permute-start(f32[32,4096]{1,0:T(8,128)} %copy-done.3), channel_id=1, source_target_pairs={{0,1},{1,0},{2,3},{3,2},{4,5},{5,4},{6,7},{7,6},{8,9},{9,8},{10,11... | collective-permute-start | bytes 1572872 | tf_op jit(solution)/shard_map/ppermute | solution.py:501
  116.6 14.8 %collective-permute-start.6 = (f32[32,4096]{1,0:T(8,128)}, f32[32,4096]{1,0:T(8,128)}, u32[]{:S(2)}, u32[]{:S(2)}) collective-permute-start(f32[32,4096]{1,0:T(8,128)} %copy-done.4), channel_id=1, source_target_pairs={{0,1},{1,0},{2,3},{3,2},{4,5},{5,4},{6,7},{7,6},{8,9},{9,8},{10,11... | collective-permute-start | bytes 1572872 | tf_op jit(solution)/shard_map/ppermute | solution.py:501
  118.9 41.6 %all-to-all-start = ((f32[8,768,128]{2,1,0:T(8,128)}), f32[8,768,128]{2,1,0:T(8,128)S(1)}, u32[]{:S(2)}, u32[]{:S(2)}) async-start(f32[8,768,128]{2,1,0:T(8,128)} %bitcast.2), calls=%async_computation | async-start | bytes 6291456 | tf_op jit(solution)/shard_map/all_to_all | solution.py:566
  130.2 36.7 %collective-permute-start.7 = (f32[32,4096]{1,0:T(8,128)}, f32[32,4096]{1,0:T(8,128)}, u32[]{:S(2)}, u32[]{:S(2)}) collective-permute-start(f32[32,4096]{1,0:T(8,128)} %entry_product.3.refs_0_), channel_id=1, source_target_pairs={{0,1},{1,0},{2,3},{3,2},{4,5},{5,4},{6,7},{7,6},{8,9},{9,8},{10,11... | collective-permute-start | bytes 1572872 | tf_op jit(solution)/shard_map/ppermute | solution.py:501
  130.7 36.2 %collective-permute-start.11 = (f32[32,4096]{1,0:T(8,128)}, f32[32,4096]{1,0:T(8,128)}, u32[]{:S(2)}, u32[]{:S(2)}) collective-permute-start(f32[32,4096]{1,0:T(8,128)} %collective-permute-done.10.refs_4_), channel_id=1, source_target_pairs={{0,1},{1,0},{2,3},{3,2},{4,5},{5,4},{6,7},{7,6},{8,9},{9,8},{10,11... | collective-permute-start | bytes 1572872 | tf_op jit(solution)/shard_map/ppermute | solution.py:501
  130.8 36.2 %collective-permute-start.13 = (f32[32,4096]{1,0:T(8,128)}, f32[32,4096]{1,0:T(8,128)}, u32[]{:S(2)}, u32[]{:S(2)}) collective-permute-start(f32[32,4096]{1,0:T(8,128)} %collective-permute-done.12.refs_6_), channel_id=1, source_target_pairs={{0,1},{1,0},{2,3},{3,2},{4,5},{5,4},{6,7},{7,6},{8,9},{9,8},{10,11... | collective-permute-start | bytes 1572872 | tf_op jit(solution)/shard_map/ppermute | solution.py:501
  131.2 35.7 %collective-permute-start.9 = (f32[32,4096]{1,0:T(8,128)}, f32[32,4096]{1,0:T(8,128)}, u32[]{:S(2)}, u32[]{:S(2)}) collective-permute-start(f32[32,4096]{1,0:T(8,128)} %collective-permute-done.8.refs_2_), channel_id=1, source_target_pairs={{0,1},{1,0},{2,3},{3,2},{4,5},{5,4},{6,7},{7,6},{8,9},{9,8},{10,11... | collective-permute-start | bytes 1572872 | tf_op jit(solution)/shard_map/ppermute | solution.py:501
  160.5 1.8 copy-start.1
  162.3 42.3 %all-to-all-start.1 = ((f32[8,768,128]{2,1,0:T(8,128)}), f32[8,768,128]{2,1,0:T(8,128)}, u32[]{:S(2)}, u32[]{:S(2)}) async-start(f32[8,768,128]{2,1,0:T(8,128)} %bitcast.22), calls=%async_computation.1 | async-start | bytes 6291456 | tf_op jit(solution)/shard_map/all_to_all | solution.py:566
Sparse Core Ops, SparseCore 0:
  10.2 39.7 all-gather.4
  51.6 35.9 all-gather.6

commit v3 on v2

--- a/solution.py
+++ b/solution.py
@@ -22,6 +22,7 @@
 MIB = 1 << 20
 VMEM_LIMIT = 56 * MIB
 ANY = pl.BlockSpec(memory_space=pl.ANY)
+COST = pl.CostEstimate(flops=MIB, bytes_accessed=MIB, transcendentals=0)
 
 
 def split_table(table):
@@ -130,76 +131,82 @@
 
 
 def first_kernel(
-    freq, tmpl_ref, strain_ref, wh_ref, wl_ref, stage_ref, tw_ref, *refs
+    freq, info_ref, tmpl_ref, strain_ref, wh_ref, wl_ref, stage_ref, tw_ref, *refs
 ):
     out_ref, gh, gl = refs[-3:]
-    tmpls, _, rows, _ = tmpl_ref.shape
-    for t in range(tmpls):
-        got = products(lambda p, u: tmpl_ref[t, p, :, tile(u)], strain_ref, (0,))
-        y = dft16([(re, im) for _, re, im in got])
-        for a in range(COARSE):
-            cos, sin = stage_ref[a : a + 1, :], stage_ref[COARSE + a : COARSE + a + 1, :]
-            yr, yi = y[a]
-            at = pl.ds((a * tmpls + t) * rows, rows)
-            gh[at, :LANES], gl[at, :LANES] = split(yr * cos - yi * sin)
-            gh[at, LANES:], gl[at, LANES:] = split(yr * sin + yi * cos)
+    rows = tmpl_ref.shape[2]
+    got = products(lambda p, u: tmpl_ref[0, p, :, tile(u)], strain_ref, (0,))
+    y = dft16([(re, im) for _, re, im in got])
+    for a in range(COARSE):
+        cos, sin = stage_ref[a : a + 1, :], stage_ref[COARSE + a : COARSE + a + 1, :]
+        yr, yi = y[a]
+        at = pl.ds(a * rows, rows)
+        gh[at, :LANES], gl[at, :LANES] = split(yr * cos - yi * sin)
+        gh[at, LANES:], gl[at, LANES:] = split(yr * sin + yi * cos)
     z = dot3((gh[...], gl[...]), (wh_ref[...], wl_ref[...]))
     width = LANES // freq
     slot = lax.broadcasted_iota(jnp.int32, (rows, LANES), 1) // width
-    for t in range(tmpls):
-        for group in range(COARSE // freq):
-            turned = []
-            for i in range(freq):
-                a = group * freq + i
-                at = slice((a * tmpls + t) * rows, (a * tmpls + t + 1) * rows)
-                zr, zi = z[at, :LANES], z[at, LANES:]
-                cos, sin = tw_ref[0, :, tile(a)], tw_ref[1, :, tile(a)]
-                pair = (zr * cos - zi * sin, zr * sin + zi * cos)
-                if i:
-                    pair = tuple(pltpu.roll(v, i * width, 1) for v in pair)
-                turned.append(pair)
-            for q in range(freq):
-                for p in range(2):
-                    value = turned[(0 - q) % freq][p]
-                    for s in range(1, freq):
-                        value = jnp.where(slot == s, turned[(s - q) % freq][p], value)
-                    out_ref[q, 0, t, p, group] = value
+    for group in range(COARSE // freq):
+        turned = []
+        for i in range(freq):
+            a = group * freq + i
+            at = slice(a * rows, (a + 1) * rows)
+            zr, zi = z[at, :LANES], z[at, LANES:]
+            cos, sin = tw_ref[0, :, tile(a)], tw_ref[1, :, tile(a)]
+            pair = (zr * cos - zi * sin, zr * sin + zi * cos)
+            if i:
+                pair = tuple(pltpu.roll(v, i * width, 1) for v in pair)
+            turned.append(pair)
+        for q in range(freq):
+            for p in range(2):
+                value = turned[(0 - q) % freq][p]
+                for s in range(1, freq):
+                    value = jnp.where(slot == s, turned[(s - q) % freq][p], value)
+                out_ref[q, 0, p, group] = value
 
 
 ROWS = 16
 
 
-def first_section(freq, half, templates, strain, first, stage, twist, after):
+def first_section(freq, half, info, templates, strain, first, stage, twist, after):
     tmpls = templates.shape[0]
     pieces, dets, _, cols, piece_len = strain.shape
+    series = tmpls * dets - 1
     groups = COARSE // freq
     steps = cols // ROWS
-    table = pl.BlockSpec((2 * LANES, 2 * LANES), lambda c, d: (0, 0))
+    table = pl.BlockSpec((2 * LANES, 2 * LANES), lambda c, i, n: (0, 0))
+    out = (freq, series, 2, groups, cols, LANES)
     return pl.pallas_call(
         functools.partial(first_kernel, freq),
-        grid=(steps, dets),
-        in_specs=[
-            pl.BlockSpec((tmpls, 2, ROWS, N1), lambda c, d: (0, 0, half * steps + c, 0)),
-            pl.BlockSpec((pieces, 1, 2, ROWS, piece_len), lambda c, d: (0, d, 0, c, 0)),
-            table,
-            table,
-            pl.BlockSpec((2 * COARSE, LANES), lambda c, d: (0, 0)),
-            pl.BlockSpec((2, ROWS, N1), lambda c, d: (0, half * steps + c, 0)),
-        ]
-        + [ANY] * len(after),
-        out_specs=pl.BlockSpec(
-            (freq, 1, tmpls, 2, groups, ROWS, LANES), lambda c, d: (0, d, 0, 0, 0, c, 0)
+        grid_spec=pltpu.PrefetchScalarGridSpec(
+            num_scalar_prefetch=1,
+            grid=(steps, series),
+            in_specs=[
+                pl.BlockSpec(
+                    (1, 2, ROWS, N1), lambda c, i, n: (n[1 + 2 * i], 0, half * steps + c, 0)
+                ),
+                pl.BlockSpec(
+                    (pieces, 1, 2, ROWS, piece_len), lambda c, i, n: (0, n[2 + 2 * i], 0, c, 0)
+                ),
+                table,
+                table,
+                pl.BlockSpec((2 * COARSE, LANES), lambda c, i, n: (0, 0)),
+                pl.BlockSpec((2, ROWS, N1), lambda c, i, n: (0, half * steps + c, 0)),
+            ]
+            + [ANY] * len(after),
+            out_specs=pl.BlockSpec(
+                (freq, 1, 2, groups, ROWS, LANES), lambda c, i, n: (0, i, 0, 0, c, 0)
+            ),
+            scratch_shapes=[
+                pltpu.VMEM((COARSE * ROWS, 2 * LANES), BF16),
+                pltpu.VMEM((COARSE * ROWS, 2 * LANES), BF16),
+            ],
         ),
-        out_shape=jax.ShapeDtypeStruct((freq, dets, tmpls, 2, groups, cols, LANES), F32),
-        scratch_shapes=[pltpu.VMEM((COARSE * tmpls * ROWS, 2 * LANES), BF16)] * 2,
+        out_shape=jax.ShapeDtypeStruct(out, F32),
         compiler_params=pltpu.CompilerParams(vmem_limit_bytes=VMEM_LIMIT),
-        cost_estimate=pl.CostEstimate(
-            flops=60 * dets * tmpls * cols * N1 * LANES,
-            bytes_accessed=12 * MIB,
-            transcendentals=0,
-        ),
+        cost_estimate=COST,
         name="first_section",
-    )(templates, strain, first[0], first[1], stage, twist, *after)
+    )(info, templates, strain, first[0], first[1], stage, twist, *after)
 
 
 def entry_kernel(which_ref, tmpl_ref, strain_ref, *refs):
@@ -228,9 +235,7 @@
         ),
         out_shape=jax.ShapeDtypeStruct((cols, 2 * N1), F32),
         compiler_params=pltpu.CompilerParams(vmem_limit_bytes=VMEM_LIMIT),
-        cost_estimate=pl.CostEstimate(
-            flops=8 * cols * N1, bytes_accessed=2 * MIB, transcendentals=0
-        ),
+        cost_estimate=COST,
         name="entry_product",
     )(which, templates, strain, *after)
 
@@ -243,18 +248,19 @@
         use(a, z[:LANES], z[LANES:])
 
 
-def second_kernel(freq, halves, place_ref, scale_ref, *refs):
-    part_refs, (w2h_ref, w2l_ref), rest = refs[:halves], refs[halves : halves + 2], refs[-3:]
-    out_ref, hold, order = rest
-    groups, cols = part_refs[0].shape[4:6]
+def second_kernel(freq, halves, info_ref, scale_ref, *refs):
+    part_refs, (w2h_ref, w2l_ref) = refs[:halves], refs[halves : halves + 2]
+    out_ref, hold, order = refs[-3:]
+    place = info_ref[0]
+    groups, cols = part_refs[0].shape[3:5]
     per = LANES // (halves * cols)
     width = LANES // freq
-    scale = scale_ref[pl.program_id(0)]
+    scale = scale_ref[info_ref[1 + 2 * pl.program_id(0)]]
 
     def rows_of(p, u):
         tiles = [
             jnp.concatenate(
-                [ref[u * per + f, 0, 0, p, g] for ref in part_refs for f in range(per)],
+                [ref[u * per + f, 0, p, g] for ref in part_refs for f in range(per)],
                 axis=0,
             )
             for g in range(groups)
@@ -273,7 +279,7 @@
         for g in range(groups):
             turned = hold[p, g].T
             for s in range(freq):
-                a = g * freq + lax.rem(s - place_ref[0] + freq, freq)
+                a = g * freq + lax.rem(s - place + freq, freq)
                 for j in range(FOUR):
                     order[p, j, pl.ds(a, width, stride=COARSE), :] = turned[
                         s * width : (s + 1) * width, tile(j)
@@ -282,46 +288,97 @@
             out_ref[0, 0, p, :, tile(j)] = order[p, j]
 
 
-def second_section(place, scale, parts, second, after):
-    freq, dets, tmpls, _, groups, cols, _ = parts[0].shape
+def second_section(freq, info, scale, parts, second, snr, after):
+    _, series, _, groups, cols, _ = parts[0].shape
     halves = len(parts)
     times = groups * LANES
     smem = pl.BlockSpec(memory_space=pltpu.SMEM)
-    table = pl.BlockSpec((FOUR * 2 * LANES, 2 * LANES), lambda t, d: (0, 0))
+    table = pl.BlockSpec((FOUR * 2 * LANES, 2 * LANES), lambda i, n: (0, 0))
     part = pl.BlockSpec(
-        (freq, 1, 1, 2, groups, cols, LANES), lambda t, d: (0, d, t, 0, 0, 0, 0)
+        (freq, 1, 2, groups, cols, LANES), lambda i, n: (0, i, 0, 0, 0, 0)
     )
     return pl.pallas_call(
         functools.partial(second_kernel, freq, halves),
-        grid=(tmpls, dets),
-        in_specs=[smem, smem] + [part] * halves + [table, table] + [ANY] * len(after),
-        out_specs=pl.BlockSpec((1, 1, 2, times, N2), lambda t, d: (t, d, 0, 0, 0)),
+        grid_spec=pltpu.PrefetchScalarGridSpec(
+            num_scalar_prefetch=1,
+            grid=(series,),
+            in_specs=[smem] + [part] * halves + [table, table, ANY] + [ANY] * len(after),
+            out_specs=pl.BlockSpec(
+                (1, 1, 2, times, N2), lambda i, n: (n[1 + 2 * i], n[2 + 2 * i], 0, 0, 0)
+            ),
+            scratch_shapes=[
+                pltpu.VMEM((2, groups, N2, LANES), F32),
+                pltpu.VMEM((2, FOUR, times, LANES), F32),
+            ],
+        ),
+        out_shape=jax.ShapeDtypeStruct(snr.shape, F32),
+        input_output_aliases={4 + halves: 0},
+        compiler_params=pltpu.CompilerParams(vmem_limit_bytes=VMEM_LIMIT),
+        cost_estimate=COST,
+        name="second_section",
+    )(info, scale, *parts, *second, snr, *after)
+
+
+def sum_kernel(halves, which_ref, scale_ref, *refs):
+    total_refs, (w2h_ref, w2l_ref, out_ref, hold) = refs[:halves], refs[halves:]
+    times = out_ref.shape[3]
+    part_rows = LANES // halves
+    scale = scale_ref[which_ref[0]]
+
+    def rows_of(p, u):
+        at = slice(u * part_rows, (u + 1) * part_rows)
+        return jnp.concatenate([ref[p, at, :] for ref in total_refs], axis=0)
+
+    def keep(a, re, im):
+        for p, value in enumerate((re, im)):
+            for g in range(times // LANES):
+                hold[p, g, pl.ds(a, LANES, stride=FOUR), :] = value[:, tile(g)] * scale
+
+    x = [(rows_of(0, u), rows_of(1, u)) for u in range(FOUR)]
+    second_points(x, w2h_ref, w2l_ref, keep)
+    for p in range(2):
+        for g in range(times // LANES):
+            out_ref[0, 0, p, tile(g), :] = hold[p, g].T
+
+
+def entry_series(which, scale, totals, second, tmpls, dets):
+    _, rows, times = totals[0].shape
+    halves = len(totals)
+    smem = pl.BlockSpec(memory_space=pltpu.SMEM)
+    return pl.pallas_call(
+        functools.partial(sum_kernel, halves),
+        grid_spec=pltpu.PrefetchScalarGridSpec(
+            num_scalar_prefetch=1,
+            grid=(1,),
+            in_specs=[smem]
+            + [pl.BlockSpec((2, rows, times), lambda i, w: (0, 0, 0))] * halves
+            + [pl.BlockSpec((FOUR * 2 * LANES, 2 * LANES), lambda i, w: (0, 0))] * 2,
+            out_specs=pl.BlockSpec((1, 1, 2, times, N2), lambda i, w: (w[0], w[1], 0, 0, 0)),
+            scratch_shapes=[pltpu.VMEM((2, times // LANES, N2, LANES), F32)],
+        ),
         out_shape=jax.ShapeDtypeStruct((tmpls, dets, 2, times, N2), F32),
-        scratch_shapes=[
-            pltpu.VMEM((2, groups, N2, LANES), F32),
-            pltpu.VMEM((2, FOUR, times, LANES), F32),
-        ],
         compiler_params=pltpu.CompilerParams(vmem_limit_bytes=VMEM_LIMIT),
-        cost_estimate=pl.CostEstimate(
-            flops=60 * dets * tmpls * times * FOUR * LANES * LANES,
-            bytes_accessed=24 * MIB,
-            transcendentals=0,
-        ),
-        name="second_section",
-    )(place, scale, *parts, *second, *after)
+        cost_estimate=COST,
+        name="entry_series",
+    )(which, scale, *totals, *second)
+
+
+BLOCKS = 4
 
 
 def bank_kernel(block_ref, inner_ref, high_ref, low_ref):
     times = block_ref.shape[-1]
-    bc, bs = block_ref[0, 0:1, :], block_ref[0, 1:2, :]
     rc, rs = inner_ref[0], inner_ref[1]
-    cos, sin = bc * rc - bs * rs, bc * rs + bs * rc
-    cos, sin = split(cos), split(sin)
-    for ref, c, s in zip((high_ref, low_ref), cos, sin):
-        ref[:BLOCK, :times] = c
-        ref[:BLOCK, times:] = s
-        ref[BLOCK:, :times] = -s
-        ref[BLOCK:, times:] = c
+    for b in range(BLOCKS):
+        bc, bs = block_ref[b, 0:1, :], block_ref[b, 1:2, :]
+        cos, sin = split(bc * rc - bs * rs), split(bc * rs + bs * rc)
+        top = slice(2 * b * BLOCK, (2 * b + 1) * BLOCK)
+        low = slice((2 * b + 1) * BLOCK, (2 * b + 2) * BLOCK)
+        for ref, c, s in zip((high_ref, low_ref), cos, sin):
+            ref[top, :times] = c
+            ref[top, times:] = s
+            ref[low, :times] = -s
+            ref[low, times:] = c
 
 
 def bank_table(own_time):
@@ -332,17 +389,15 @@
     inner = jnp.stack(phase(inner, N1))
     return pl.pallas_call(
         bank_kernel,
-        grid=(NBLK,),
+        grid=(NBLK // BLOCKS,),
         in_specs=[
-            pl.BlockSpec((1, 2, times), lambda b: (b, 0, 0)),
+            pl.BlockSpec((BLOCKS, 2, times), lambda b: (b, 0, 0)),
             pl.BlockSpec((2, BLOCK, times), lambda b: (0, 0, 0)),
         ],
-        out_specs=[pl.BlockSpec((2 * BLOCK, 2 * times), lambda b: (b, 0))] * 2,
+        out_specs=[pl.BlockSpec((BLOCKS * 2 * BLOCK, 2 * times), lambda b: (b, 0))] * 2,
         out_shape=[jax.ShapeDtypeStruct((2 * N1, 2 * times), BF16)] * 2,
         compiler_params=pltpu.CompilerParams(vmem_limit_bytes=VMEM_LIMIT),
-        cost_estimate=pl.CostEstimate(
-            flops=8 * N1 * times, bytes_accessed=8 * MIB, transcendentals=0
-        ),
+        cost_estimate=COST,
         name="bank_table",
     )(block, inner)
 
@@ -423,11 +478,7 @@
             pltpu.VMEM((rows, 2 * times), F32),
         ],
         compiler_params=pltpu.CompilerParams(vmem_limit_bytes=VMEM_LIMIT),
-        cost_estimate=pl.CostEstimate(
-            flops=600 * rows * LANES * times * BINS,
-            bytes_accessed=20 * MIB,
-            transcendentals=0,
-        ),
+        cost_estimate=COST,
         name="bins_first",
     )(place, edges, *pieces, *table, twist, *after)
 
@@ -487,24 +538,21 @@
             pltpu.VMEM((N2, LANES), F32),
         ],
         compiler_params=pltpu.CompilerParams(vmem_limit_bytes=VMEM_LIMIT),
-        cost_estimate=pl.CostEstimate(
-            flops=60 * BINS * FOUR * LANES**2 * times,
-            bytes_accessed=20 * MIB,
-            transcendentals=0,
-        ),
+        cost_estimate=COST,
         name="bins_second",
     )(gain, share, *levels, *totals, *second)
 
 
+def swap(x, freq, k):
+    return lax.ppermute(x, "freq", [(i, i ^ k) for i in range(freq)])
+
+
 def spread_pieces(own, freq):
-    def swap(x, k):
-        return lax.ppermute(x, "freq", [(i, i ^ k) for i in range(freq)])
-
     pieces = [own] + [None] * (freq - 1)
     for k in range(2, freq, 2):
-        pieces[k] = swap(own, k)
+        pieces[k] = swap(own, freq, k)
     for k in range(1, freq, 2):
-        pieces[k] = swap(pieces[k - 1], 1)
+        pieces[k] = swap(pieces[k - 1], freq, 1)
     return pieces
 
 
@@ -515,7 +563,7 @@
     freq = lax.axis_size("freq")
     place = lax.axis_index("freq").astype(jnp.int32)
     tmpls, _, cols, _ = templates.shape
-    slots = coinc_tmpl.shape[0]
+    slots, dets = coinc_tmpl.shape[0], strain.shape[0]
     times = N1 // freq
     part = cols // HALVES
 
@@ -551,36 +599,40 @@
         own_twist.append(jnp.stack(phase(rows[:, None] * own_time[None, :], N1 * N2)))
 
     which = [jnp.stack([coinc_tmpl[j], coinc_det[j]]) for j in range(slots)]
-    which, inv_sigma, weights, twist, table, own_twist = lax.optimization_barrier(
-        (which, inv_sigma, weights, twist, table, own_twist)
+    series = jnp.arange(tmpls * dets - 1, dtype=jnp.int32)
+    series = series + (series >= which[0][0] * dets + which[0][1])
+    info = jnp.stack([series // dets, series % dets], axis=1).reshape(-1)
+    info = jnp.concatenate([place.reshape(1), info])
+    which, inv_sigma, weights, table, twist, own_twist, info = lax.optimization_barrier(
+        (which, inv_sigma, weights, table, twist, own_twist, info)
     )
     here = place.reshape(1)
-    pieces, sent, parts = [], [], []
+    pieces, sent, parts, after = [], [], [], []
     for h in range(HALVES):
-        after = [x for entry in pieces for x in entry[2::2]] + sent
         half = [entry_product(w, h, templates, strains[h], after) for w in which]
-        pieces = [spread_pieces(x, freq) for x in half]
-        if h == 0:
-            early = pieces
-        sent = [first_section(freq, h, templates, strains[h], first, stage, twist, half)]
+        early, pieces = pieces, [spread_pieces(x, freq) for x in half]
+        sent = first_section(freq, h, info, templates, strains[h], first, stage, twist, half)
         got = lax.all_to_all(
-            sent[0].reshape(freq, -1, LANES), "freq", split_axis=0, concat_axis=0, tiled=True
+            sent.reshape(freq, -1, LANES), "freq", split_axis=0, concat_axis=0, tiled=True
         )
-        parts.append(got.reshape(sent[0].shape))
-
-    chi = []
+        parts.append(got.reshape(sent.shape))
+        after = [x for entry in pieces for x in entry[2::2]] + [sent]
+
+    chi, totals = [], []
     for j in range(slots):
         t = coinc_tmpl[j]
         ends = jnp.zeros((1,), jnp.int32), jnp.full((1,), NBLK, jnp.int32)
         edges = jnp.concatenate([ends[0], bin_edges[t], ends[1]])
         halves = [
-            bins_first(here, edges, entry[j], table, own_twist[h], sent)
+            bins_first(here, edges, entry[j], table, own_twist[h], [sent, parts[0]])
             for h, entry in enumerate((early, pieces))
         ]
-        levels, totals = zip(*halves)
+        levels, total = zip(*halves)
+        totals.append(total)
         gain = inv_sigma[t] * lax.rsqrt(weights[t])
-        chi.append(bins_second(gain, gain * weights[t], levels, totals, second))
-    snr = second_section(here, inv_sigma, parts, second, chi)
+        chi.append(bins_second(gain, gain * weights[t], levels, total, second))
+    snr = entry_series(which[0], inv_sigma, totals[0], second, tmpls, dets)
+    snr = second_section(freq, info, inv_sigma, parts, second, snr, chi)
     return (snr, jnp.stack(chi))
 
 

time: 225 us -> 281 us (1.25)
  waiting for transfers between devices: 54.6 us -> 110 us
    ppermute x14, waiting for transfers between devices: 21.1 us -> 86.1 us  [swap(): return lax.ppermute(x, 'freq', [(i, i ^ k) for i in range(freq)])]
    all_to_all x2, waiting for transfers between devices: 12.2 us -> 0.01 us  [per_device(): lax.all_to_all(sent.reshape(freq, -1, LANES), 'freq', split_axis=0, conca...]
    pallas_call x2, Pallas kernels: 35.7 us -> 38.7 us  [bins_first(): pl.pallas_call(functools.partial(bins_first_kernel, len(pieces)), grid=(B...]
    pallas_call x4 -> x5, Pallas kernels: 42.3 us -> 41.2 us  [the longest x2 20.2 us: first_section(): pl.pallas_call(functools.partial(first_kernel, freq), grid_spec=pltpu.Pre...]
  transfers between devices with their start and end apart: 18 -> 18, of which waited for: 4 -> 7; matrix products, arithmetic and copies ran while one was open for 6% -> 5% of each run, Pallas kernels for 41% -> 33%
where the time goes in v3:
time: 281 us
  waiting for transfers between devices  110 us (39%)
  Pallas kernels  104 us (37%)
  starting transfers between devices  16.9 us (6%)
  blocking collectives  15.5 us (6%)
  between operations  15.5 us (6%)
  other arithmetic  12.7 us (5%)
  local copies, waits for them, and re-layouts  6.11 us (2%)
    ppermute x14, waiting for transfers between devices, swap(): return lax.ppermute(x, 'freq', [(i, i ^ k) for i in range(freq)])  86.1 us
    pallas_call x2, Pallas kernels, bins_first(): pl.pallas_call(functools.partial(bins_first_kernel, len(pieces)), grid=(B...  38.7 us
    all_gather x2, waiting for transfers between devices, per_device(): lax.all_gather(strain[:, :, h * part:(h + 1) * part], 'bank', axis=0, til...  22.8 us
    pallas_call x2, Pallas kernels, first_section(): pl.pallas_call(functools.partial(first_kernel, freq), grid_spec=pltpu.Pre...  20.2 us
    pallas_call x1, Pallas kernels, bins_second(): pl.pallas_call(functools.partial(bins_second_kernel, halves), grid=(BINS,...  19 us
    psum x1, blocking collectives, per_device(): block_power = lax.psum(local_power, 'freq')  15.5 us
    pallas_call x1, Pallas kernels, second_section(): pl.pallas_call(functools.partial(second_kernel, freq, halves), grid_spec=...  10.7 us
    ppermute x14, starting transfers between devices, swap(): return lax.ppermute(x, 'freq', [(i, i ^ k) for i in range(freq)])  8.48 us
  transfers between devices with their start and end apart: 18, of which 7 were waited for; matrix products, arithmetic and copies ran while one was open for 5% of the time, Pallas kernels for 33%

profile of v3, /device:TPU:0, one launch (start us, length us, event | category | flops | bytes accessed | tf_op | source)
XLA Modules:
  0.0 280.7 jit_solution(4979535024478238927)
XLA Ops:
  7.2 0.0 copy-start
  7.2 0.0 all-gather.5.cloned.1.call-start
  7.2 2.2 fusion.48
  9.4 0.0 all-gather.5.cloned.1.call-update
  9.4 0.0 all-gather.7.cloned.1.call-start
  9.5 0.7 all-gather.7.cloned.1.call-update
  10.2 0.3 fusion.24
  10.6 1.0 fusion.39
  12.9 0.6 pad_add_fusion.1.which_ref
  13.5 0.1 copy.18
  13.6 0.1 reshape.720
  13.7 0.2 add_reduce_fusion
  13.9 0.1 reshape.718
  14.0 0.1 reduce_sum.46
  14.1 15.5 %psum.7 = f32[2,32]{1,0:T(2,128)S(1)} all-reduce(f32[2,32]{1,0:T(2,128)S(1)} %reduce_sum.46), channel_id=1, replica_groups=mesh['bank'=4,'freq'=8] {'freq'}, use_global_device_ids=true, to_apply=%region_2.0 | all-reduce | flops 64 | bytes 512 | tf_op jit(solution)/shard_map/psum | solution.py:580
  29.6 0.1 reduce_sum.47
  29.7 0.1 copy.16
  29.8 0.1 fusion.32
  29.9 0.1 select_reduce_fusion
  30.0 0.1 broadcast_divide_fusion
  30.0 2.1 fusion.12
  32.2 0.7 pad_maximum_fusion.3.inner_ref
  32.8 0.7 pad_maximum_fusion.4.block_ref
  33.5 6.1 %bank_table.1 = (bf16[4096,512]{1,0:T(8,128)(2,1)}, bf16[4096,512]{1,0:T(8,128)(2,1)}) custom-call(f32[32,2,256]{2,1,0:T(2,128)} %pad_maximum_fusion.4.block_ref, f32[2,64,256]{2,1,0:T(8,128)} %pad_maximum_fusion.3.inner_ref), custom_call_target="tpu_custom_call" | custom-call | flops 1048576 | bytes 1048576 | tf_op jit(solution)/shard_map/bank_table/pallas_call | solution.py:390
  39.6 2.1 fusion.10
  41.7 1.1 pad_maximum_fusion.tw_ref
  42.8 1.1 pad_maximum_fusion.1
  43.9 0.6 pad_add_fusion.2.info_ref
  44.5 5.5 %all-gather.5.cloned.1.call-done = f32[12,2,32,512]{3,2,1,0:T(8,128)} async-done(((f32[3,2,32,512]{3,2,1,0:T(8,128)}), f32[12,2,32,512]{3,2,1,0:T(8,128)}) %all-gather.5.cloned.1.call-update) | async-done | bytes 1572880 | tf_op jit(solution)/shard_map/all_gather | solution.py:571
  50.0 2.7 entry_product.2.refs_0_
  52.7 10.2 %first_section.2.refs_3_ = f32[8,5,2,2,32,128]{5,4,3,2,1,0:T(8,128)} custom-call(s32[11]{0:T(128)} %pad_add_fusion.2.info_ref, f32[2,2,64,2048]{3,2,1,0:T(8,128)} %tmpl_ref.7, f32[4,3,2,32,512]{4,3,2,1,0:T(8,128)} %bitcast.32, bf16[256,256]{1,0:T(8,128)(2,1)} %constant.170.clone.wh_ref, bf16[256,256]{1,0:T(8,128)(2,1)} %constant.171.clone.wl_ref, ...), custom_call_target="tpu_custom_call" | custom-call | flops 1048576 | bytes 1048576 | tf_op jit(solution)/shard_map/first_section/pallas_call | solution.py:179
  62.9 3.8 %all-to-all-start = ((f32[8,640,128]{2,1,0:T(8,128)}), f32[8,640,128]{2,1,0:T(8,128)S(1)}, u32[]{:S(2)}, u32[]{:S(2)}) async-start(f32[8,640,128]{2,1,0:T(8,128)} %bitcast.28), calls=%async_computation | async-start | bytes 5242880 | tf_op jit(solution)/shard_map/all_to_all | solution.py:615
  66.7 2.0 collective-permute-start
  68.7 1.5 collective-permute-start.1
  70.1 0.1 collective-permute-start.2
  70.2 17.3 %all-gather.7.cloned.1.call-done = f32[12,2,32,512]{3,2,1,0:T(8,128)} async-done(((f32[3,2,32,512]{3,2,1,0:T(8,128)}), f32[12,2,32,512]{3,2,1,0:T(8,128)}) %all-gather.7.cloned.1.call-update) | async-done | bytes 1572880 | tf_op jit(solution)/shard_map/all_gather | solution.py:571
  87.5 22.3 %collective-permute-done.refs_0_.refs_2_ = f32[32,4096]{1,0:T(8,128)} collective-permute-done((f32[32,4096]{1,0:T(8,128)S(1)}, f32[32,4096]{1,0:T(8,128)}, u32[]{:S(2)}, u32[]{:S(2)}) %collective-permute-start) | collective-permute-done | bytes 524320 | tf_op jit(solution)/shard_map/ppermute | solution.py:547
  109.9 11.7 %collective-permute-done.2.refs_2_.refs_6_ = f32[32,4096]{1,0:T(8,128)} collective-permute-done((f32[32,4096]{1,0:T(8,128)S(1)}, f32[32,4096]{1,0:T(8,128)}, u32[]{:S(2)}, u32[]{:S(2)}) %collective-permute-start.2) | collective-permute-done | bytes 524320 | tf_op jit(solution)/shard_map/ppermute | solution.py:547
  121.5 2.7 entry_product.3.refs_0_
  124.3 10.1 %first_section.3.refs_11_ = f32[8,5,2,2,32,128]{5,4,3,2,1,0:T(8,128)} custom-call(s32[11]{0:T(128)} %pad_add_fusion.2.info_ref, f32[2,2,64,2048]{3,2,1,0:T(8,128)} %tmpl_ref.7, f32[4,3,2,32,512]{4,3,2,1,0:T(8,128)} %bitcast.30, bf16[256,256]{1,0:T(8,128)(2,1)} %constant.170.clone.wh_ref, bf16[256,256]{1,0:T(8,128)(2,1)} %constant.171.clone.wl_ref, ...), custom_call_target="tpu_custom_call" | custom-call | flops 1048576 | bytes 1048576 | tf_op jit(solution)/shard_map/first_section/pallas_call | solution.py:179
  134.4 1.5 copy-done.1
  135.8 4.6 %all-to-all-start.1 = ((f32[8,640,128]{2,1,0:T(8,128)}), f32[8,640,128]{2,1,0:T(8,128)}, u32[]{:S(2)}, u32[]{:S(2)}) async-start(f32[8,640,128]{2,1,0:T(8,128)} %bitcast.27), calls=%async_computation.1 | async-start | bytes 5242880 | tf_op jit(solution)/shard_map/all_to_all | solution.py:615
  140.4 1.7 collective-permute-start.10
  142.1 1.4 collective-permute-start.12
  143.6 0.4 collective-permute-start.8
  144.0 49.9 %collective-permute-done.10.refs_4_ = f32[32,4096]{1,0:T(8,128)S(1)} collective-permute-done((f32[32,4096]{1,0:T(8,128)}, f32[32,4096]{1,0:T(8,128)S(1)}, u32[]{:S(2)}, u32[]{:S(2)}) %collective-permute-start.10) | collective-permute-done | bytes 524320 | tf_op jit(solution)/shard_map/ppermute | solution.py:547
  193.9 0.5 collective-permute-start.13
  194.4 0.1 collective-permute-start.9
  194.5 0.4 collective-permute-start.3
  195.0 0.1 collective-permute-start.4
  195.0 0.8 collective-permute-done.11.refs_5_
  195.8 0.1 collective-permute-start.5
  196.0 1.4 collective-permute-done.13.refs_7_
  197.3 0.1 collective-permute-start.6
  197.5 0.7 copy-done.9
  198.2 0.6 dynamic_slice.11
  198.8 0.6 pad_add_fusion.3.edge_ref
  199.3 1.1 bitcast_multiply_fusion
  200.5 19.4 %bins_first.3 = (f32[16,2,256,256]{3,2,1,0:T(8,128)}, f32[2,256,256]{2,1,0:T(8,128)}) custom-call(s32[1]{0:T(128)} %bitcast.place_ref, s32[17]{0:T(128)} %pad_add_fusion.3.edge_ref, f32[32,4096]{1,0:T(8,128)} %entry_product.3.refs_0_, f32[32,4096]{1,0:T(8,128)} %copy-done.7, f32[32,4096]{1,0:T(8,128)} %copy-done.5, ...), custom_call_target="tpu_custom_call" | custom-call | flops 1048576 | bytes 1048576 | tf_op jit(solution)/shard_map/bins_first/pallas_call | solution.py:459
  219.9 0.8 copy-done.6
  220.7 19.3 %bins_first.2 = (f32[16,2,256,256]{3,2,1,0:T(8,128)}, f32[2,256,256]{2,1,0:T(8,128)}) custom-call(s32[1]{0:T(128)} %bitcast.place_ref, s32[17]{0:T(128)} %pad_add_fusion.3.edge_ref, f32[32,4096]{1,0:T(8,128)} %entry_product.2.refs_0_, f32[32,4096]{1,0:T(8,128)} %copy-done.6, f32[32,4096]{1,0:T(8,128)} %collective-permute-done.refs_0_.refs_2_, ...), custom_call_target="tpu_custom_call" | custom-call | flops 1048576 | bytes 1048576 | tf_op jit(solution)/shard_map/bins_first/pallas_call | solution.py:459
  240.0 4.1 %entry_series.1.refs_4_ = f32[2,3,2,256,512]{4,3,2,1,0:T(8,128)} custom-call(s32[2]{0:T(128)} %pad_add_fusion.1.which_ref, f32[2]{0:T(128)} %copy-done.10, f32[2,256,256]{2,1,0:T(8,128)} %get-tuple-element.26.refs_0_.refs_2_, f32[2,256,256]{2,1,0:T(8,128)} %get-tuple-element.28.refs_1_.refs_3_, bf16[1024,256]{1,0:T(8,128)(2,1)} %constant.172.clone.refs_2_.refs_4_, ...), custom_call_target="tpu_custom_call" | custom-call | flops 1048576 | bytes 1048576 | tf_op jit(solution)/shard_map/entry_series/pallas_call | solution.py:348
  244.1 19.0 %bins_second.1.refs_5_ = f32[256,512]{1,0:T(8,128)} custom-call(f32[16]{0:T(128)} %get-tuple-element.33.gain_ref, f32[16]{0:T(128)} %get-tuple-element.32.share_ref, f32[16,2,256,256]{3,2,1,0:T(8,128)} %get-tuple-element.30.refs_0_, f32[16,2,256,256]{3,2,1,0:T(8,128)} %get-tuple-element.31.refs_1_, f32[2,256,256]{2,1,0:T(8,128)} %get-tuple-element.26.refs_0_.refs_2_, ...), custom_call_target="tpu_custom_call" | custom-call | flops 1048576 | bytes 1048576 | tf_op jit(solution)/shard_map/bins_second/pallas_call | solution.py:527
  263.1 10.7 %second_section.1 = f32[2,3,2,256,512]{4,3,2,1,0:T(8,128)} custom-call(s32[11]{0:T(128)} %pad_add_fusion.2.info_ref, f32[2]{0:T(128)} %copy-done.10, f32[8,5,2,2,32,128]{5,4,3,2,1,0:T(8,128)} %bitcast.26, f32[8,5,2,2,32,128]{5,4,3,2,1,0:T(8,128)} %bitcast.8.refs_1_, ...), custom_call_target="tpu_custom_call", output_to_operand_aliasing={{}: (6, {})} | custom-call | flops 1048576 | bytes 1048576 | tf_op jit(solution)/shard_map/second_section/pallas_call | solution.py:300
  (43 shorter events, 0.2 us)
Async XLA Ops:
  7.2 6.5 %copy-start = (f32[2,2,64,2048]{3,2,1,0:T(8,128)S(1)}, f32[2,2,64,2048]{3,2,1,0:T(8,128)}, u32[]{:S(2)}) copy-start(f32[2,2,64,2048]{3,2,1,0:T(8,128)} %tmpl_ref.7) | copy-start | bytes 6291460
  7.2 22.5 %copy-start.11 = (s32[2,15]{1,0:T(2,128)S(1)}, s32[2,15]{1,0:T(2,128)}, u32[]{:S(2)}) copy-start(s32[2,15]{1,0:T(2,128)} %param.14) | copy-start | bytes 364
  7.2 42.8 %all-gather.5.cloned.1.call-start = ((), (), s32[]{:S(2)}) async-start(), calls=%async_computation.2 | async-start | bytes 1966080 | tf_op jit(solution)/shard_map/all_gather | solution.py:571
  9.4 78.1 %all-gather.7.cloned.1.call-start = ((), (), s32[]{:S(2)}) async-start(), calls=%async_computation.3 | async-start | bytes 1966080 | tf_op jit(solution)/shard_map/all_gather | solution.py:571
  30.0 168.2 %copy-start.10 = (f32[2]{0:T(128)}, f32[2]{0:T(128)S(1)}, u32[]{:S(2)}) copy-start(f32[2]{0:T(128)S(1)} %rsqrt.6.scale_ref) | copy-start | bytes 28
  62.9 3.8 %copy-start.2 = (f32[32,4096]{1,0:T(8,128)S(1)}, f32[32,4096]{1,0:T(8,128)}, u32[]{:S(2)}) copy-start(f32[32,4096]{1,0:T(8,128)} %entry_product.2.refs_0_) | copy-start | bytes 1572868
  62.9 71.5 %all-to-all-start = ((f32[8,640,128]{2,1,0:T(8,128)}), f32[8,640,128]{2,1,0:T(8,128)S(1)}, u32[]{:S(2)}, u32[]{:S(2)}) async-start(f32[8,640,128]{2,1,0:T(8,128)} %bitcast.28), calls=%async_computation | async-start | bytes 5242880 | tf_op jit(solution)/shard_map/all_to_all | solution.py:615
  66.7 43.2 %collective-permute-start = (f32[32,4096]{1,0:T(8,128)S(1)}, f32[32,4096]{1,0:T(8,128)}, u32[]{:S(2)}, u32[]{:S(2)}) collective-permute-start(f32[32,4096]{1,0:T(8,128)S(1)} %copy-done.2), channel_id=1, source_target_pairs={{0,2},{1,3},{2,0},{3,1},{4,6},{5,7},{6,4},{7,5},{8,10},{9,11},{10,... | collective-permute-start | bytes 1572872 | tf_op jit(solution)/shard_map/ppermute | solution.py:547
  68.7 41.2 %collective-permute-start.1 = (f32[32,4096]{1,0:T(8,128)S(1)}, f32[32,4096]{1,0:T(8,128)}, u32[]{:S(2)}, u32[]{:S(2)}) collective-permute-start(f32[32,4096]{1,0:T(8,128)S(1)} %copy-done.2), channel_id=1, source_target_pairs={{0,4},{1,5},{2,6},{3,7},{4,0},{5,1},{6,2},{7,3},{8,12},{9,13},{10,... | collective-permute-start | bytes 1572872 | tf_op jit(solution)/shard_map/ppermute | solution.py:547
  70.1 51.4 %collective-permute-start.2 = (f32[32,4096]{1,0:T(8,128)S(1)}, f32[32,4096]{1,0:T(8,128)}, u32[]{:S(2)}, u32[]{:S(2)}) collective-permute-start(f32[32,4096]{1,0:T(8,128)S(1)} %copy-done.2), channel_id=1, source_target_pairs={{0,6},{1,7},{2,4},{3,5},{4,2},{5,3},{6,0},{7,1},{8,14},{9,15},{10,... | collective-permute-start | bytes 1572872 | tf_op jit(solution)/shard_map/ppermute | solution.py:547
  134.4 1.5 copy-start.1
  135.8 127.3 %all-to-all-start.1 = ((f32[8,640,128]{2,1,0:T(8,128)}), f32[8,640,128]{2,1,0:T(8,128)}, u32[]{:S(2)}, u32[]{:S(2)}) async-start(f32[8,640,128]{2,1,0:T(8,128)} %bitcast.27), calls=%async_computation.1 | async-start | bytes 5242880 | tf_op jit(solution)/shard_map/all_to_all | solution.py:615
  140.4 53.5 %collective-permute-start.10 = (f32[32,4096]{1,0:T(8,128)}, f32[32,4096]{1,0:T(8,128)S(1)}, u32[]{:S(2)}, u32[]{:S(2)}) collective-permute-start(f32[32,4096]{1,0:T(8,128)} %entry_product.3.refs_0_), channel_id=1, source_target_pairs={{0,4},{1,5},{2,6},{3,7},{4,0},{5,1},{6,2},{7,3},{8,12},{9,13},{10,... | collective-permute-start | bytes 1572872 | tf_op jit(solution)/shard_map/ppermute | solution.py:547
  142.1 51.8 %collective-permute-start.12 = (f32[32,4096]{1,0:T(8,128)}, f32[32,4096]{1,0:T(8,128)S(1)}, u32[]{:S(2)}, u32[]{:S(2)}) collective-permute-start(f32[32,4096]{1,0:T(8,128)} %entry_product.3.refs_0_), channel_id=1, source_target_pairs={{0,6},{1,7},{2,4},{3,5},{4,2},{5,3},{6,0},{7,1},{8,14},{9,15},{10,... | collective-permute-start | bytes 1572872 | tf_op jit(solution)/shard_map/ppermute | solution.py:547
  143.6 50.8 %collective-permute-start.8 = (f32[32,4096]{1,0:T(8,128)}, f32[32,4096]{1,0:T(8,128)S(1)}, u32[]{:S(2)}, u32[]{:S(2)}) collective-permute-start(f32[32,4096]{1,0:T(8,128)} %entry_product.3.refs_0_), channel_id=1, source_target_pairs={{0,2},{1,3},{2,0},{3,1},{4,6},{5,7},{6,4},{7,5},{8,10},{9,11},{10,... | collective-permute-start | bytes 1572872 | tf_op jit(solution)/shard_map/ppermute | solution.py:547
  144.0 51.0 %collective-permute-start.7 = (f32[32,4096]{1,0:T(8,128)}, f32[32,4096]{1,0:T(8,128)S(1)}, u32[]{:S(2)}, u32[]{:S(2)}) collective-permute-start(f32[32,4096]{1,0:T(8,128)} %entry_product.3.refs_0_), channel_id=1, source_target_pairs={{0,1},{1,0},{2,3},{3,2},{4,5},{5,4},{6,7},{7,6},{8,9},{9,8},{10,11... | collective-permute-start | bytes 1572872 | tf_op jit(solution)/shard_map/ppermute | solution.py:547
  193.9 6.6 %copy-start.3 = (f32[32,4096]{1,0:T(8,128)}, f32[32,4096]{1,0:T(8,128)S(1)}, u32[]{:S(2)}) copy-start(f32[32,4096]{1,0:T(8,128)S(1)} %collective-permute-done.10.refs_4_) | copy-start | bytes 1572868
  193.9 1.9 collective-permute-start.11
  193.9 6.5 %copy-start.4 = (f32[32,4096]{1,0:T(8,128)}, f32[32,4096]{1,0:T(8,128)S(1)}, u32[]{:S(2)}) copy-start(f32[32,4096]{1,0:T(8,128)S(1)} %collective-permute-done.12.refs_6_) | copy-start | bytes 1572868
  193.9 3.4 %collective-permute-start.13 = (f32[32,4096]{1,0:T(8,128)S(1)}, f32[32,4096]{1,0:T(8,128)S(1)}, u32[]{:S(2)}, u32[]{:S(2)}) collective-permute-start(f32[32,4096]{1,0:T(8,128)S(1)} %collective-permute-done.12.refs_6_), channel_id=1, source_target_pairs={{0,1},{1,0},{2,3},{3,2},{4,5},{5,4},{6,7},{7,6},{8,9},{9,8},{10,11... | collective-permute-start | bytes 1572872 | tf_op jit(solution)/shard_map/ppermute | solution.py:547
  194.4 6.0 %copy-start.5 = (f32[32,4096]{1,0:T(8,128)}, f32[32,4096]{1,0:T(8,128)S(1)}, u32[]{:S(2)}) copy-start(f32[32,4096]{1,0:T(8,128)S(1)} %collective-permute-done.8.refs_2_) | copy-start | bytes 1572868
  194.4 6.0 %collective-permute-start.9 = (f32[32,4096]{1,0:T(8,128)S(1)}, f32[32,4096]{1,0:T(8,128)}, u32[]{:S(2)}, u32[]{:S(2)}) collective-permute-start(f32[32,4096]{1,0:T(8,128)S(1)} %collective-permute-done.8.refs_2_), channel_id=1, source_target_pairs={{0,1},{1,0},{2,3},{3,2},{4,5},{5,4},{6,7},{7,6},{8,9},{9,8},{10,11... | collective-permute-start | bytes 1572872 | tf_op jit(solution)/shard_map/ppermute | solution.py:547
  194.5 25.4 %collective-permute-start.3 = (f32[32,4096]{1,0:T(8,128)S(1)}, f32[32,4096]{1,0:T(8,128)S(1)}, u32[]{:S(2)}, u32[]{:S(2)}) collective-permute-start(f32[32,4096]{1,0:T(8,128)S(1)} %copy-done.2), channel_id=1, source_target_pairs={{0,1},{1,0},{2,3},{3,2},{4,5},{5,4},{6,7},{7,6},{8,9},{9,8},{10,11... | collective-permute-start | bytes 1572872 | tf_op jit(solution)/shard_map/ppermute | solution.py:547
  195.0 5.5 %copy-start.7 = (f32[32,4096]{1,0:T(8,128)}, f32[32,4096]{1,0:T(8,128)S(1)}, u32[]{:S(2)}) copy-start(f32[32,4096]{1,0:T(8,128)S(1)} %collective-permute-done.7.refs_1_) | copy-start | bytes 1572868
  195.0 25.0 %collective-permute-start.4 = (f32[32,4096]{1,0:T(8,128)}, f32[32,4096]{1,0:T(8,128)}, u32[]{:S(2)}, u32[]{:S(2)}) collective-permute-start(f32[32,4096]{1,0:T(8,128)} %collective-permute-done.refs_0_.refs_2_), channel_id=1, source_target_pairs={{0,1},{1,0},{2,3},{3,2},{4,5},{5,4},{6,7},{7,6},{8,9},{9,8},{10,11... | collective-permute-start | bytes 1572872 | tf_op jit(solution)/shard_map/ppermute | solution.py:547
  195.8 1.5 copy-start.8
  195.8 24.1 %collective-permute-start.5 = (f32[32,4096]{1,0:T(8,128)}, f32[32,4096]{1,0:T(8,128)}, u32[]{:S(2)}, u32[]{:S(2)}) collective-permute-start(f32[32,4096]{1,0:T(8,128)} %collective-permute-done.1.refs_1_.refs_4_), channel_id=1, source_target_pairs={{0,1},{1,0},{2,3},{3,2},{4,5},{5,4},{6,7},{7,6},{8,9},{9,8},{10,11... | collective-permute-start | bytes 1572872 | tf_op jit(solution)/shard_map/ppermute | solution.py:547
  197.3 0.8 copy-start.9
  197.3 22.6 %collective-permute-start.6 = (f32[32,4096]{1,0:T(8,128)}, f32[32,4096]{1,0:T(8,128)}, u32[]{:S(2)}, u32[]{:S(2)}) collective-permute-start(f32[32,4096]{1,0:T(8,128)} %collective-permute-done.2.refs_2_.refs_6_), channel_id=1, source_target_pairs={{0,1},{1,0},{2,3},{3,2},{4,5},{5,4},{6,7},{7,6},{8,9},{9,8},{10,11... | collective-permute-start | bytes 1572872 | tf_op jit(solution)/shard_map/ppermute | solution.py:547
  219.9 0.8 copy-start.6
Sparse Core Ops, SparseCore 0:
  10.2 39.7 all-gather.4
  51.6 35.9 all-gather.6

commit v4 on v3

--- a/solution.py
+++ b/solution.py
@@ -111,18 +111,21 @@
 
 def dot3(left, right):
     (lh, ll), (rh, rl) = left, right
-    d = functools.partial(jnp.dot, preferred_element_type=F32)
-    return d(lh, rh) + (d(lh, rl) + d(ll, rh))
-
-
-def products(tmpl, strain_ref, where):
+    return jnp.dot(
+        jnp.concatenate([lh, lh, ll], axis=1),
+        jnp.concatenate([rh, rl, rh], axis=0),
+        preferred_element_type=F32,
+    )
+
+
+def products(tmpl, strain_ref, where, rows=slice(None)):
     per_piece = COARSE // strain_ref.shape[0]
     for u in range(COARSE):
         off = u % per_piece
         there = slice(off * LANES, (off + 1) * LANES)
         hr, hi = tmpl(0, u), tmpl(1, u)
-        sr = strain_ref[(u // per_piece,) + where + (0, slice(None), there)]
-        si = strain_ref[(u // per_piece,) + where + (1, slice(None), there)]
+        sr = strain_ref[(u // per_piece,) + where + (0, rows, there)]
+        si = strain_ref[(u // per_piece,) + where + (1, rows, there)]
         yield u, hr * sr + hi * si, hr * si - hi * sr
 
 
@@ -133,36 +136,40 @@
 def first_kernel(
     freq, info_ref, tmpl_ref, strain_ref, wh_ref, wl_ref, stage_ref, tw_ref, *refs
 ):
-    out_ref, gh, gl = refs[-3:]
+    out_ref, gh, gl, z = refs[-4:]
     rows = tmpl_ref.shape[2]
-    got = products(lambda p, u: tmpl_ref[0, p, :, tile(u)], strain_ref, (0,))
-    y = dft16([(re, im) for _, re, im in got])
-    for a in range(COARSE):
-        cos, sin = stage_ref[a : a + 1, :], stage_ref[COARSE + a : COARSE + a + 1, :]
-        yr, yi = y[a]
-        at = pl.ds(a * rows, rows)
-        gh[at, :LANES], gl[at, :LANES] = split(yr * cos - yi * sin)
-        gh[at, LANES:], gl[at, LANES:] = split(yr * sin + yi * cos)
-    z = dot3((gh[...], gl[...]), (wh_ref[...], wl_ref[...]))
+    for r in range(0, rows, ROWS):
+        at = slice(r, r + ROWS)
+        got = products(lambda p, u: tmpl_ref[0, p, at, tile(u)], strain_ref, (0,), at)
+        y = dft16([(re, im) for _, re, im in got])
+        for a in range(COARSE):
+            cos, sin = stage_ref[a : a + 1, :], stage_ref[COARSE + a : COARSE + a + 1, :]
+            yr, yi = y[a]
+            to = slice(a * rows + r, a * rows + r + ROWS)
+            gh[to, :LANES], gl[to, :LANES] = split(yr * cos - yi * sin)
+            gh[to, LANES:], gl[to, LANES:] = split(yr * sin + yi * cos)
+    z[...] = dot3((gh[...], gl[...]), (wh_ref[...], wl_ref[...]))
     width = LANES // freq
-    slot = lax.broadcasted_iota(jnp.int32, (rows, LANES), 1) // width
+    slot = lax.broadcasted_iota(jnp.int32, (ROWS, LANES), 1) // width
     for group in range(COARSE // freq):
-        turned = []
-        for i in range(freq):
-            a = group * freq + i
-            at = slice(a * rows, (a + 1) * rows)
-            zr, zi = z[at, :LANES], z[at, LANES:]
-            cos, sin = tw_ref[0, :, tile(a)], tw_ref[1, :, tile(a)]
-            pair = (zr * cos - zi * sin, zr * sin + zi * cos)
-            if i:
-                pair = tuple(pltpu.roll(v, i * width, 1) for v in pair)
-            turned.append(pair)
-        for q in range(freq):
-            for p in range(2):
-                value = turned[(0 - q) % freq][p]
-                for s in range(1, freq):
-                    value = jnp.where(slot == s, turned[(s - q) % freq][p], value)
-                out_ref[q, 0, p, group] = value
+        for r in range(0, rows, ROWS):
+            at = slice(r, r + ROWS)
+            turned = []
+            for i in range(freq):
+                a = group * freq + i
+                to = slice(a * rows + r, a * rows + r + ROWS)
+                zr, zi = z[to, :LANES], z[to, LANES:]
+                cos, sin = tw_ref[0, at, tile(a)], tw_ref[1, at, tile(a)]
+                pair = (zr * cos - zi * sin, zr * sin + zi * cos)
+                if i:
+                    pair = tuple(pltpu.roll(v, i * width, 1) for v in pair)
+                turned.append(pair)
+            for q in range(freq):
+                for p in range(2):
+                    value = turned[(0 - q) % freq][p]
+                    for s in range(1, freq):
+                        value = jnp.where(slot == s, turned[(s - q) % freq][p], value)
+                    out_ref[q, 0, p, group, at] = value
 
 
 ROWS = 16
@@ -173,7 +180,8 @@
     pieces, dets, _, cols, piece_len = strain.shape
     series = tmpls * dets - 1
     groups = COARSE // freq
-    steps = cols // ROWS
+    rows = 2 * ROWS if cols % (2 * ROWS) == 0 else ROWS
+    steps = cols // rows
     table = pl.BlockSpec((2 * LANES, 2 * LANES), lambda c, i, n: (0, 0))
     out = (freq, series, 2, groups, cols, LANES)
     return pl.pallas_call(
@@ -183,28 +191,31 @@
             grid=(steps, series),
             in_specs=[
                 pl.BlockSpec(
-                    (1, 2, ROWS, N1), lambda c, i, n: (n[1 + 2 * i], 0, half * steps + c, 0)
+                    (1, 2, rows, N1), lambda c, i, n: (n[1 + 2 * i], 0, half * steps + c, 0)
                 ),
                 pl.BlockSpec(
-                    (pieces, 1, 2, ROWS, piece_len), lambda c, i, n: (0, n[2 + 2 * i], 0, c, 0)
+                    (pieces, 1, 2, rows, piece_len), lambda c, i, n: (0, n[2 + 2 * i], 0, c, 0)
                 ),
                 table,
                 table,
                 pl.BlockSpec((2 * COARSE, LANES), lambda c, i, n: (0, 0)),
-                pl.BlockSpec((2, ROWS, N1), lambda c, i, n: (0, half * steps + c, 0)),
+                pl.BlockSpec((2, rows, N1), lambda c, i, n: (0, half * steps + c, 0)),
             ]
             + [ANY] * len(after),
             out_specs=pl.BlockSpec(
-                (freq, 1, 2, groups, ROWS, LANES), lambda c, i, n: (0, i, 0, 0, c, 0)
+                (freq, 1, 2, groups, rows, LANES), lambda c, i, n: (0, i, 0, 0, c, 0)
             ),
             scratch_shapes=[
-                pltpu.VMEM((COARSE * ROWS, 2 * LANES), BF16),
-                pltpu.VMEM((COARSE * ROWS, 2 * LANES), BF16),
+                pltpu.VMEM((COARSE * rows, 2 * LANES), BF16),
+                pltpu.VMEM((COARSE * rows, 2 * LANES), BF16),
+                pltpu.VMEM((COARSE * rows, 2 * LANES), F32),
             ],
         ),
         out_shape=jax.ShapeDtypeStruct(out, F32),
         compiler_params=pltpu.CompilerParams(vmem_limit_bytes=VMEM_LIMIT),
-        cost_estimate=COST,
+        cost_estimate=pl.CostEstimate(
+            flops=60 * series * cols * N1 * LANES, bytes_accessed=16 * MIB, transcendentals=0
+        ),
         name="first_section",
     )(info, templates, strain, first[0], first[1], stage, twist, *after)
 
@@ -319,50 +330,6 @@
     )(info, scale, *parts, *second, snr, *after)
 
 
-def sum_kernel(halves, which_ref, scale_ref, *refs):
-    total_refs, (w2h_ref, w2l_ref, out_ref, hold) = refs[:halves], refs[halves:]
-    times = out_ref.shape[3]
-    part_rows = LANES // halves
-    scale = scale_ref[which_ref[0]]
-
-    def rows_of(p, u):
-        at = slice(u * part_rows, (u + 1) * part_rows)
-        return jnp.concatenate([ref[p, at, :] for ref in total_refs], axis=0)
-
-    def keep(a, re, im):
-        for p, value in enumerate((re, im)):
-            for g in range(times // LANES):
-                hold[p, g, pl.ds(a, LANES, stride=FOUR), :] = value[:, tile(g)] * scale
-
-    x = [(rows_of(0, u), rows_of(1, u)) for u in range(FOUR)]
-    second_points(x, w2h_ref, w2l_ref, keep)
-    for p in range(2):
-        for g in range(times // LANES):
-            out_ref[0, 0, p, tile(g), :] = hold[p, g].T
-
-
-def entry_series(which, scale, totals, second, tmpls, dets):
-    _, rows, times = totals[0].shape
-    halves = len(totals)
-    smem = pl.BlockSpec(memory_space=pltpu.SMEM)
-    return pl.pallas_call(
-        functools.partial(sum_kernel, halves),
-        grid_spec=pltpu.PrefetchScalarGridSpec(
-            num_scalar_prefetch=1,
-            grid=(1,),
-            in_specs=[smem]
-            + [pl.BlockSpec((2, rows, times), lambda i, w: (0, 0, 0))] * halves
-            + [pl.BlockSpec((FOUR * 2 * LANES, 2 * LANES), lambda i, w: (0, 0))] * 2,
-            out_specs=pl.BlockSpec((1, 1, 2, times, N2), lambda i, w: (w[0], w[1], 0, 0, 0)),
-            scratch_shapes=[pltpu.VMEM((2, times // LANES, N2, LANES), F32)],
-        ),
-        out_shape=jax.ShapeDtypeStruct((tmpls, dets, 2, times, N2), F32),
-        compiler_params=pltpu.CompilerParams(vmem_limit_bytes=VMEM_LIMIT),
-        cost_estimate=COST,
-        name="entry_series",
-    )(which, scale, *totals, *second)
-
-
 BLOCKS = 4
 
 
@@ -423,22 +390,26 @@
             lax.fori_loop(0, 2 * N1 // (FOUR * LANES), cut, 0)
         total_ref[...] = jnp.zeros_like(total_ref)
 
-    def add(block, blocks):
+    def blocks_at(block, blocks):
         at = pl.ds(pl.multiple_of(block * LANES, LANES), blocks * LANES)
-        acc[...] += dot3((xh[:, at], xl[:, at]), (wh_ref[at, :], wl_ref[at, :]))
+        return dot3((xh[:, at], xl[:, at]), (wh_ref[at, :], wl_ref[at, :]))
 
     start, end = edge_ref[level], edge_ref[level + 1]
-    acc[...] = jnp.zeros_like(acc)
+    odd = (end - start) % 2
+
+    @pl.when(odd == 1)
+    def _():
+        acc[...] = blocks_at(end - 1, 1)
+
+    @pl.when(odd == 0)
+    def _():
+        acc[...] = blocks_at(end - 2, 2)
 
     def two(i, carry):
-        add(start + 2 * i, 2)
+        acc[...] += blocks_at(start + 2 * i, 2)
         return carry
 
-    lax.fori_loop(0, (end - start) // 2, two, 0)
-
-    @pl.when((end - start) % 2 == 1)
-    def _():
-        add(end - 1, 1)
+    lax.fori_loop(0, (end - start - 1) // 2, two, 0)
 
     for u in range(pieces * cols // LANES):
         at = tile(u)
@@ -483,9 +454,9 @@
     )(place, edges, *pieces, *table, twist, *after)
 
 
-def bins_second_kernel(halves, gain_ref, share_ref, *refs):
+def bins_second_kernel(halves, which_ref, scale_ref, gain_ref, share_ref, *refs):
     level_refs, total_refs = refs[:halves], refs[halves : 2 * halves]
-    w2h_ref, w2l_ref, out_ref, chi, hold = refs[2 * halves :]
+    w2h_ref, w2l_ref, out_ref, snr_ref, chi, hold = refs[2 * halves :]
     times = out_ref.shape[0]
     part_rows = LANES // halves
     level = pl.program_id(0)
@@ -495,65 +466,98 @@
     def _():
         chi[...] = jnp.zeros_like(chi)
 
-    def rows_of(p, u):
+    def rows_of(get, u):
         at = slice(u * part_rows, (u + 1) * part_rows)
-        return jnp.concatenate(
-            [
-                one[0, p, at, :] * gain - whole[p, at, :] * share
-                for one, whole in zip(level_refs, total_refs)
-            ],
-            axis=0,
-        )
+        return jnp.concatenate([get(h, at) for h in range(halves)], axis=0)
 
     def keep(a, re, im):
         chi[a] += re * re + im * im
 
-    x = [(rows_of(0, u), rows_of(1, u)) for u in range(FOUR)]
+    def deviation(p):
+        return lambda h, at: level_refs[h][0, p, at, :] * gain - total_refs[h][p, at, :] * share
+
+    x = [tuple(rows_of(deviation(p), u) for p in range(2)) for u in range(FOUR)]
     second_points(x, w2h_ref, w2l_ref, keep)
 
     @pl.when(level == BINS - 1)
     def _():
+        scale = scale_ref[which_ref[0]]
+
+        def whole(p):
+            return lambda h, at: total_refs[h][p, at, :] * scale
+
+        def put(a, re, im):
+            for p, value in enumerate((re, im)):
+                for g in range(times // LANES):
+                    hold[p, g, pl.ds(a, LANES, stride=FOUR), :] = value[:, tile(g)]
+
+        y = [tuple(rows_of(whole(p), u) for p in range(2)) for u in range(FOUR)]
+        second_points(y, w2h_ref, w2l_ref, put)
         for g in range(times // LANES):
             for a in range(FOUR):
-                hold[pl.ds(a, LANES, stride=FOUR), :] = chi[a, :, tile(g)]
-            out_ref[tile(g), :] = hold[...].T
-
-
-def bins_second(gain, share, levels, totals, second):
+                hold[2, g, pl.ds(a, LANES, stride=FOUR), :] = chi[a, :, tile(g)]
+            for p in range(2):
+                snr_ref[0, 0, p, tile(g), :] = hold[p, g].T
+            out_ref[tile(g), :] = hold[2, g].T
+
+
+def bins_second(which, scale, gain, share, levels, totals, second, tmpls, dets):
     _, _, rows, times = levels[0].shape
     halves = len(levels)
     smem = pl.BlockSpec(memory_space=pltpu.SMEM)
-    fixed = lambda shape: pl.BlockSpec(shape, lambda i: (0,) * len(shape))
+    fixed = lambda shape: pl.BlockSpec(shape, lambda i, w: (0,) * len(shape))
     return pl.pallas_call(
         functools.partial(bins_second_kernel, halves),
-        grid=(BINS,),
-        in_specs=[smem, smem]
-        + [pl.BlockSpec((1, 2, rows, times), lambda i: (i, 0, 0, 0))] * halves
-        + [fixed((2, rows, times))] * halves
-        + [fixed((FOUR * 2 * LANES, 2 * LANES))] * 2,
-        out_specs=fixed((times, N2)),
-        out_shape=jax.ShapeDtypeStruct((times, N2), F32),
-        scratch_shapes=[
-            pltpu.VMEM((FOUR, LANES, times), F32),
-            pltpu.VMEM((N2, LANES), F32),
+        grid_spec=pltpu.PrefetchScalarGridSpec(
+            num_scalar_prefetch=1,
+            grid=(BINS,),
+            in_specs=[smem, smem, smem]
+            + [pl.BlockSpec((1, 2, rows, times), lambda i, w: (i, 0, 0, 0))] * halves
+            + [fixed((2, rows, times))] * halves
+            + [fixed((FOUR * 2 * LANES, 2 * LANES))] * 2,
+            out_specs=[
+                fixed((times, N2)),
+                pl.BlockSpec((1, 1, 2, times, N2), lambda i, w: (w[0], w[1], 0, 0, 0)),
+            ],
+            scratch_shapes=[
+                pltpu.VMEM((FOUR, LANES, times), F32),
+                pltpu.VMEM((3, times // LANES, N2, LANES), F32),
+            ],
+        ),
+        out_shape=[
+            jax.ShapeDtypeStruct((times, N2), F32),
+            jax.ShapeDtypeStruct((tmpls, dets, 2, times, N2), F32),
         ],
         compiler_params=pltpu.CompilerParams(vmem_limit_bytes=VMEM_LIMIT),
         cost_estimate=COST,
         name="bins_second",
-    )(gain, share, *levels, *totals, *second)
+    )(which, scale, gain, share, *levels, *totals, *second)
+
+
+def handed_on(arrays, after):
+    count = len(arrays)
+    return pl.pallas_call(
+        lambda *refs: None,
+        in_specs=[ANY] * (count + len(after)),
+        out_specs=[ANY] * count,
+        out_shape=[jax.ShapeDtypeStruct(x.shape, x.dtype) for x in arrays],
+        input_output_aliases={i: i for i in range(count)},
+        compiler_params=pltpu.CompilerParams(vmem_limit_bytes=VMEM_LIMIT),
+        cost_estimate=COST,
+        name="handed_on",
+    )(*arrays, *after)
 
 
 def swap(x, freq, k):
     return lax.ppermute(x, "freq", [(i, i ^ k) for i in range(freq)])
 
 
-def spread_pieces(own, freq):
-    pieces = [own] + [None] * (freq - 1)
-    for k in range(2, freq, 2):
-        pieces[k] = swap(own, freq, k)
-    for k in range(1, freq, 2):
-        pieces[k] = swap(pieces[k - 1], freq, 1)
-    return pieces
+def far_pieces(own, freq):
+    return [own] + [swap(own, freq, k) for k in range(2, freq, 2)]
+
+
+def near_pieces(far, freq):
+    return [x for even in far for x in (even, swap(even, freq, 1))]
 
 
 HALVES = 2
@@ -610,28 +614,33 @@
     pieces, sent, parts, after = [], [], [], []
     for h in range(HALVES):
         half = [entry_product(w, h, templates, strains[h], after) for w in which]
-        early, pieces = pieces, [spread_pieces(x, freq) for x in half]
+        far = [far_pieces(x, freq) for x in half]
         sent = first_section(freq, h, info, templates, strains[h], first, stage, twist, half)
+        far = [x[:1] + list(handed_on(x[1:], [sent])) for x in far]
+        early, pieces = pieces, [near_pieces(x, freq) for x in far]
+        (ready,) = handed_on([sent], [x for entry in pieces for x in entry[1:]])
         got = lax.all_to_all(
-            sent.reshape(freq, -1, LANES), "freq", split_axis=0, concat_axis=0, tiled=True
+            ready.reshape(freq, -1, LANES), "freq", split_axis=0, concat_axis=0, tiled=True
         )
         parts.append(got.reshape(sent.shape))
-        after = [x for entry in pieces for x in entry[2::2]] + [sent]
-
-    chi, totals = [], []
+        after = [ready]
+
+    chi, snr = [], None
     for j in range(slots):
         t = coinc_tmpl[j]
         ends = jnp.zeros((1,), jnp.int32), jnp.full((1,), NBLK, jnp.int32)
         edges = jnp.concatenate([ends[0], bin_edges[t], ends[1]])
         halves = [
-            bins_first(here, edges, entry[j], table, own_twist[h], [sent, parts[0]])
-            for h, entry in enumerate((early, pieces))
+            bins_first(here, edges, early[j], table, own_twist[0], [sent]),
+            bins_first(here, edges, pieces[j], table, own_twist[1], [ready]),
         ]
-        levels, total = zip(*halves)
-        totals.append(total)
+        levels, totals = zip(*halves)
         gain = inv_sigma[t] * lax.rsqrt(weights[t])
-        chi.append(bins_second(gain, gain * weights[t], levels, total, second))
-    snr = entry_series(which[0], inv_sigma, totals[0], second, tmpls, dets)
+        one, series_of = bins_second(
+            which[j], inv_sigma, gain, gain * weights[t], levels, totals, second, tmpls, dets
+        )
+        chi.append(one)
+        snr = series_of if snr is None else snr
     snr = second_section(freq, info, inv_sigma, parts, second, snr, chi)
     return (snr, jnp.stack(chi))
 

time: 281 us -> 233 us (0.83)
  waiting for transfers between devices: 110 us -> 64.8 us
  Pallas kernels: 104 us -> 94.5 us
  local copies, waits for them, and re-layouts: 6.11 us -> 11.7 us
    ppermute x14, waiting for transfers between devices: 86.1 us -> 59.2 us  [swap(): return lax.ppermute(x, 'freq', [(i, i ^ k) for i in range(freq)])]
    all_gather x2, waiting for transfers between devices: 22.8 us -> 4.9 us  [per_device(): lax.all_gather(strain[:, :, h * part:(h + 1) * part], 'bank', axis=0, til...]
    unnamed x25 -> x40, local copies, waits for them, and re-layouts: 3.07 us -> 8.58 us
    pallas_call x2, Pallas kernels: 20.2 us -> 15.2 us  [first_section(): pl.pallas_call(functools.partial(first_kernel, freq), grid_spec=pltpu.Pre...]
    pallas_call x2 -> x5, Pallas kernels: 23.1 us -> 20.9 us  [the longest x1 20.9 us: bins_second(): pl.pallas_call(functools.partial(bins_second_kernel, halves), grid_spec=p...]
  transfers between devices with their start and end apart: 18 -> 18, of which waited for: 7 -> 13; matrix products, arithmetic and copies ran while one was open for 5% -> 7% of each run, Pallas kernels for 33% -> 36%
where the time goes in v4:
time: 233 us; the launch traced here: 231 us
  Pallas kernels  94.5 us (41%)
  waiting for transfers between devices  64.8 us (28%)
  starting transfers between devices  16.6 us (7%)
  blocking collectives  15.5 us (7%)
  between operations  15.5 us (7%)
  other arithmetic  12.7 us (5%)
  local copies, waits for them, and re-layouts  11.7 us (5%)
    ppermute x14, waiting for transfers between devices, swap(): return lax.ppermute(x, 'freq', [(i, i ^ k) for i in range(freq)])  59.2 us
    pallas_call x2, Pallas kernels, bins_first(): pl.pallas_call(functools.partial(bins_first_kernel, len(pieces)), grid=(B...  36.2 us
    pallas_call x1, Pallas kernels, bins_second(): pl.pallas_call(functools.partial(bins_second_kernel, halves), grid_spec=p...  20.9 us
    psum x1, blocking collectives, per_device(): block_power = lax.psum(local_power, 'freq')  15.5 us
    pallas_call x2, Pallas kernels, first_section(): pl.pallas_call(functools.partial(first_kernel, freq), grid_spec=pltpu.Pre...  15.2 us
    pallas_call x1, Pallas kernels, second_section(): pl.pallas_call(functools.partial(second_kernel, freq, halves), grid_spec=...  10.7 us
    unnamed x40, local copies, waits for them, and re-layouts  8.58 us
    all_to_all x2, starting transfers between devices, per_device(): lax.all_to_all(ready.reshape(freq, -1, LANES), 'freq', split_axis=0, conc...  8.35 us
  transfers between devices with their start and end apart: 18, of which 13 were waited for; matrix products, arithmetic and copies ran while one was open for 7% of the time, Pallas kernels for 36%

profile of v4, /device:TPU:0, one launch (start us, length us, event | category | flops | bytes accessed | tf_op | source)
XLA Modules:
  0.0 231.4 jit_solution(10099537151451785910)
XLA Ops:
  7.2 2.2 fusion.48
  9.5 0.7 all-gather.7.cloned.1.call-update
  10.3 0.3 fusion.24
  11.9 0.6 pad_add_fusion.1.which_ref
  12.5 0.1 copy.26
  12.6 0.1 reshape.720
  12.7 0.8 copy.24
  13.5 0.1 fusion.32
  13.6 0.2 add_reduce_fusion
  13.8 0.1 reshape.718
  13.8 0.1 reduce_sum.46
  13.9 15.5 %psum.7 = f32[2,32]{1,0:T(2,128)S(1)} all-reduce(f32[2,32]{1,0:T(2,128)S(1)} %reduce_sum.46), channel_id=1, replica_groups=mesh['bank'=4,'freq'=8] {'freq'}, use_global_device_ids=true, to_apply=%region_2.0 | all-reduce | flops 64 | bytes 512 | tf_op jit(solution)/shard_map/psum | solution.py:584
  29.4 0.1 reduce_sum.47
  29.6 0.1 select_reduce_fusion
  29.7 1.0 fusion.39
  30.7 0.7 pad_maximum_fusion.4.block_ref
  31.4 0.7 pad_maximum_fusion.3.inner_ref
  32.1 2.1 fusion.10
  34.2 1.1 pad_maximum_fusion.tw_ref
  35.3 2.1 fusion.12
  37.4 6.1 %bank_table.1 = (bf16[4096,512]{1,0:T(8,128)(2,1)}, bf16[4096,512]{1,0:T(8,128)(2,1)}) custom-call(f32[32,2,256]{2,1,0:T(2,128)} %pad_maximum_fusion.4.block_ref, f32[2,64,256]{2,1,0:T(8,128)} %pad_maximum_fusion.3.inner_ref), custom_call_target="tpu_custom_call" | custom-call | flops 1048576 | bytes 1048576 | tf_op jit(solution)/shard_map/bank_table/pallas_call | solution.py:357
  43.4 1.1 pad_maximum_fusion.1
  44.5 0.6 pad_add_fusion.2.info_ref
  45.1 4.9 %all-gather.5.cloned.1.call-done = f32[12,2,32,512]{3,2,1,0:T(8,128)} async-done(((f32[3,2,32,512]{3,2,1,0:T(8,128)}), f32[12,2,32,512]{3,2,1,0:T(8,128)}) %all-gather.5.cloned.1.call-update) | async-done | bytes 1572880 | tf_op jit(solution)/shard_map/all_gather | solution.py:575
  50.0 2.7 %entry_product.2.refs_0_ = f32[32,4096]{1,0:T(8,128)} custom-call(s32[2]{0:T(128)} %pad_add_fusion.1.which_ref, f32[2,2,64,2048]{3,2,1,0:T(8,128)} %tmpl_ref.7, f32[4,3,2,32,512]{4,3,2,1,0:T(8,128)} %bitcast.27), custom_call_target="tpu_custom_call" | custom-call | flops 1048576 | bytes 1048576 | tf_op jit(solution)/shard_map/entry_product/pallas_call | solution.py:235
  52.7 2.4 %collective-permute-start.3 = (f32[32,4096]{1,0:T(8,128)}, f32[32,4096]{1,0:T(8,128)S(1)}, u32[]{:S(2)}, u32[]{:S(2)}) collective-permute-start(f32[32,4096]{1,0:T(8,128)} %entry_product.2.refs_0_), channel_id=1, source_target_pairs={{0,6},{1,7},{2,4},{3,5},{4,2},{5,3},{6,0},{7,1},{8,14},{9,15},{10,... | collective-permute-start | bytes 1572872 | tf_op jit(solution)/shard_map/ppermute | solution.py:552
  55.1 0.5 collective-permute-start.2
  55.6 0.6 collective-permute-start.1
  56.2 7.7 %first_section.2.refs_3_.refs_0_ = f32[8,5,2,2,32,128]{5,4,3,2,1,0:T(8,128)} custom-call(s32[11]{0:T(128)} %pad_add_fusion.2.info_ref, f32[2,2,64,2048]{3,2,1,0:T(8,128)} %tmpl_ref.7, f32[4,3,2,32,512]{4,3,2,1,0:T(8,128)} %bitcast.28, bf16[256,256]{1,0:T(8,128)(2,1)} %constant.170.clone.wh_ref, bf16[256,256]{1,0:T(8,128)(2,1)} %constant.171.clone.wl_ref, ...), custom_call_target="tpu_custom_call" | custom-call | flops 2516582400 | bytes 16777216 | tf_op jit(solution)/shard_map/first_section/pallas_call | solution.py:187
  63.9 4.8 %collective-permute-done.3.refs_2_ = f32[32,4096]{1,0:T(8,128)S(1)} collective-permute-done((f32[32,4096]{1,0:T(8,128)}, f32[32,4096]{1,0:T(8,128)S(1)}, u32[]{:S(2)}, u32[]{:S(2)}) %collective-permute-start.3) | collective-permute-done | bytes 524320 | tf_op jit(solution)/shard_map/ppermute | solution.py:552
  68.7 9.9 %collective-permute-done.2.refs_1_ = f32[32,4096]{1,0:T(8,128)S(1)} collective-permute-done((f32[32,4096]{1,0:T(8,128)}, f32[32,4096]{1,0:T(8,128)S(1)}, u32[]{:S(2)}, u32[]{:S(2)}) %collective-permute-start.2) | collective-permute-done | bytes 524320 | tf_op jit(solution)/shard_map/ppermute | solution.py:552
  78.7 0.7 copy-done.7
  79.4 0.8 copy-done.8
  80.2 0.1 collective-permute-start.4
  80.3 0.4 collective-permute-start.5
  80.7 0.1 collective-permute-start.6
  80.8 1.5 collective-permute-done.4.refs_3_
  82.3 0.7 collective-permute-done.5.refs_5_
  83.1 0.7 collective-permute-done.6.refs_7_
  83.9 0.8 copy-done.12
  84.7 4.4 %all-to-all-start = ((f32[8,640,128]{2,1,0:T(8,128)}), f32[8,640,128]{2,1,0:T(8,128)}, u32[]{:S(2)}, u32[]{:S(2)}) async-start(f32[8,640,128]{2,1,0:T(8,128)} %bitcast.24), calls=%async_computation | async-start | bytes 5242880 | tf_op jit(solution)/shard_map/all_to_all | solution.py:622
  89.1 2.7 %entry_product.3.refs_0_ = f32[32,4096]{1,0:T(8,128)} custom-call(s32[2]{0:T(128)} %pad_add_fusion.1.which_ref, f32[2,2,64,2048]{3,2,1,0:T(8,128)} %tmpl_ref.7, f32[4,3,2,32,512]{4,3,2,1,0:T(8,128)} %bitcast.29, f32[8,5,2,2,32,128]{5,4,3,2,1,0:T(8,128)} %handed_on.5.refs_0_), custom_call_target="tpu_custom_call" | custom-call | flops 1048576 | bytes 1048576 | tf_op jit(solution)/shard_map/entry_product/pallas_call | solution.py:235
  91.8 2.8 %collective-permute-start.10 = (f32[32,4096]{1,0:T(8,128)}, f32[32,4096]{1,0:T(8,128)S(1)}, u32[]{:S(2)}, u32[]{:S(2)}) collective-permute-start(f32[32,4096]{1,0:T(8,128)} %entry_product.3.refs_0_), channel_id=1, source_target_pairs={{0,6},{1,7},{2,4},{3,5},{4,2},{5,3},{6,0},{7,1},{8,14},{9,15},{10,... | collective-permute-start | bytes 1572872 | tf_op jit(solution)/shard_map/ppermute | solution.py:552
  94.6 0.5 collective-permute-start.9
  95.2 0.2 collective-permute-start.8
  95.3 7.6 %first_section.3.refs_3_.refs_11_ = f32[8,5,2,2,32,128]{5,4,3,2,1,0:T(8,128)} custom-call(s32[11]{0:T(128)} %pad_add_fusion.2.info_ref, f32[2,2,64,2048]{3,2,1,0:T(8,128)} %tmpl_ref.7, f32[4,3,2,32,512]{4,3,2,1,0:T(8,128)} %bitcast.30, bf16[256,256]{1,0:T(8,128)(2,1)} %constant.170.clone.wh_ref, bf16[256,256]{1,0:T(8,128)(2,1)} %constant.171.clone.wl_ref, ...), custom_call_target="tpu_custom_call" | custom-call | flops 2516582400 | bytes 16777216 | tf_op jit(solution)/shard_map/first_section/pallas_call | solution.py:187
  102.9 30.1 %collective-permute-done.10.refs_2_ = f32[32,4096]{1,0:T(8,128)S(1)} collective-permute-done((f32[32,4096]{1,0:T(8,128)}, f32[32,4096]{1,0:T(8,128)S(1)}, u32[]{:S(2)}, u32[]{:S(2)}) %collective-permute-start.10) | collective-permute-done | bytes 524320 | tf_op jit(solution)/shard_map/ppermute | solution.py:552
  133.0 9.8 %collective-permute-done.9.refs_1_ = f32[32,4096]{1,0:T(8,128)S(1)} collective-permute-done((f32[32,4096]{1,0:T(8,128)}, f32[32,4096]{1,0:T(8,128)S(1)}, u32[]{:S(2)}, u32[]{:S(2)}) %collective-permute-start.9) | collective-permute-done | bytes 524320 | tf_op jit(solution)/shard_map/ppermute | solution.py:552
  142.8 0.7 copy-done.4
  143.6 0.8 copy-done.6
  144.4 0.5 collective-permute-start.12
  144.9 1.5 copy.39.refs_0_
  146.5 0.7 collective-permute-done.12.refs_5_
  147.2 0.7 collective-permute-done.13.refs_7_
  148.1 0.8 copy-done.16
  148.8 3.9 %all-to-all-start.1 = ((f32[8,640,128]{2,1,0:T(8,128)}), f32[8,640,128]{2,1,0:T(8,128)S(1)}, u32[]{:S(2)}, u32[]{:S(2)}) async-start(f32[8,640,128]{2,1,0:T(8,128)} %bitcast.25), calls=%async_computation.1 | async-start | bytes 5242880 | tf_op jit(solution)/shard_map/all_to_all | solution.py:622
  152.8 0.7 dynamic_slice.10
  153.5 0.6 pad_add_fusion.3.edge_ref
  154.1 1.2 bitcast_multiply_fusion
  155.3 18.0 %bins_first.2 = (f32[16,2,256,256]{3,2,1,0:T(8,128)}, f32[2,256,256]{2,1,0:T(8,128)}) custom-call(s32[1]{0:T(128)} %bitcast.place_ref, s32[17]{0:T(128)} %pad_add_fusion.3.edge_ref, f32[32,4096]{1,0:T(8,128)} %entry_product.2.refs_0_, f32[32,4096]{1,0:T(8,128)} %copy-done.9, f32[32,4096]{1,0:T(8,128)} %get-tuple-element.31.refs_2_, f32[32,4096]{1,0:T(8,128)} %copy-done.10, ...), custom_call_target="tpu_custom_call" | custom-call | flops 1048576 | bytes 1048576 | tf_op jit(solution)/shard_map/bins_first/pallas_call | solution.py:430
  173.3 18.1 %bins_first.3 = (f32[16,2,256,256]{3,2,1,0:T(8,128)}, f32[2,256,256]{2,1,0:T(8,128)}) custom-call(s32[1]{0:T(128)} %bitcast.place_ref, s32[17]{0:T(128)} %pad_add_fusion.3.edge_ref, f32[32,4096]{1,0:T(8,128)} %entry_product.3.refs_0_, f32[32,4096]{1,0:T(8,128)} %copy-done.13, f32[32,4096]{1,0:T(8,128)} %get-tuple-element.34.refs_2_, f32[32,4096]{1,0:T(8,128)} %copy-done.14, ...), custom_call_target="tpu_custom_call" | custom-call | flops 1048576 | bytes 1048576 | tf_op jit(solution)/shard_map/bins_first/pallas_call | solution.py:430
  191.5 20.9 %bins_second.1 = (f32[256,512]{1,0:T(8,128)}, f32[2,3,2,256,512]{4,3,2,1,0:T(8,128)}) custom-call(s32[2]{0:T(128)} %pad_add_fusion.1.which_ref, f32[2]{0:T(128)} %copy-done.17, f32[16]{0:T(128)} %get-tuple-element.49.gain_ref, f32[16]{0:T(128)} %get-tuple-element.48.share_ref, f32[16,2,256,256]{3,2,1,0:T(8,128)} %get-tuple-element.41.refs_0_, ...), custom_call_target="tpu_custom_call" | custom-call | flops 1048576 | bytes 1048576 | tf_op jit(solution)/shard_map/bins_second/pallas_call | solution.py:509
  212.4 1.5 copy-done.2
  213.8 10.7 %second_section.1 = f32[2,3,2,256,512]{4,3,2,1,0:T(8,128)} custom-call(s32[11]{0:T(128)} %pad_add_fusion.2.info_ref, f32[2]{0:T(128)} %copy-done.17, f32[8,5,2,2,32,128]{5,4,3,2,1,0:T(8,128)} %bitcast.5.refs_0_, f32[8,5,2,2,32,128]{5,4,3,2,1,0:T(8,128)} %bitcast.26, ...), custom_call_target="tpu_custom_call", output_to_operand_aliasing={{}: (6, {})} | custom-call | flops 1048576 | bytes 1048576 | tf_op jit(solution)/shard_map/second_section/pallas_call | solution.py:311
  (61 shorter events, 0.6 us)
Async XLA Ops:
  7.2 6.4 %copy-start.1 = (f32[2,2,64,2048]{3,2,1,0:T(8,128)S(1)}, f32[2,2,64,2048]{3,2,1,0:T(8,128)}, u32[]{:S(2)}) copy-start(f32[2,2,64,2048]{3,2,1,0:T(8,128)} %tmpl_ref.7) | copy-start | bytes 6291460
  7.2 42.8 %all-gather.5.cloned.1.call-start = ((), (), s32[]{:S(2)}) async-start(), calls=%async_computation.2 | async-start | bytes 1966080 | tf_op jit(solution)/shard_map/all_gather | solution.py:575
  9.4 79.7 %all-gather.7.cloned.1.call-start = ((), (), s32[]{:S(2)}) async-start(), calls=%async_computation.3 | async-start | bytes 1966080 | tf_op jit(solution)/shard_map/all_gather | solution.py:575
  29.7 123.2 %copy-start.17 = (f32[2]{0:T(128)}, f32[2]{0:T(128)S(1)}, u32[]{:S(2)}) copy-start(f32[2]{0:T(128)S(1)} %rsqrt.6.scale_ref) | copy-start | bytes 28
  52.7 16.0 %collective-permute-start.3 = (f32[32,4096]{1,0:T(8,128)}, f32[32,4096]{1,0:T(8,128)S(1)}, u32[]{:S(2)}, u32[]{:S(2)}) collective-permute-start(f32[32,4096]{1,0:T(8,128)} %entry_product.2.refs_0_), channel_id=1, source_target_pairs={{0,6},{1,7},{2,4},{3,5},{4,2},{5,3},{6,0},{7,1},{8,14},{9,15},{10,... | collective-permute-start | bytes 1572872 | tf_op jit(solution)/shard_map/ppermute | solution.py:552
  55.1 23.5 %collective-permute-start.2 = (f32[32,4096]{1,0:T(8,128)}, f32[32,4096]{1,0:T(8,128)S(1)}, u32[]{:S(2)}, u32[]{:S(2)}) collective-permute-start(f32[32,4096]{1,0:T(8,128)} %entry_product.2.refs_0_), channel_id=1, source_target_pairs={{0,4},{1,5},{2,6},{3,7},{4,0},{5,1},{6,2},{7,3},{8,12},{9,13},{10,... | collective-permute-start | bytes 1572872 | tf_op jit(solution)/shard_map/ppermute | solution.py:552
  55.6 23.0 %collective-permute-start.1 = (f32[32,4096]{1,0:T(8,128)}, f32[32,4096]{1,0:T(8,128)S(1)}, u32[]{:S(2)}, u32[]{:S(2)}) collective-permute-start(f32[32,4096]{1,0:T(8,128)} %entry_product.2.refs_0_), channel_id=1, source_target_pairs={{0,2},{1,3},{2,0},{3,1},{4,6},{5,7},{6,4},{7,5},{8,10},{9,11},{10,... | collective-permute-start | bytes 1572872 | tf_op jit(solution)/shard_map/ppermute | solution.py:552
  56.2 24.6 %collective-permute-start = (f32[32,4096]{1,0:T(8,128)}, f32[32,4096]{1,0:T(8,128)S(1)}, u32[]{:S(2)}, u32[]{:S(2)}) collective-permute-start(f32[32,4096]{1,0:T(8,128)} %entry_product.2.refs_0_), channel_id=1, source_target_pairs={{0,1},{1,0},{2,3},{3,2},{4,5},{5,4},{6,7},{7,6},{8,9},{9,8},{10,11... | collective-permute-start | bytes 1572872 | tf_op jit(solution)/shard_map/ppermute | solution.py:552
  68.7 10.0 %copy-start.5 = (f32[32,4096]{1,0:T(8,128)}, f32[32,4096]{1,0:T(8,128)S(1)}, u32[]{:S(2)}) copy-start(f32[32,4096]{1,0:T(8,128)S(1)} %collective-permute-done.3.refs_2_) | copy-start | bytes 1572868
  78.6 0.8 copy-start.7
  79.4 0.8 copy-start.8
  80.2 2.1 collective-permute-start.4
  80.3 2.7 %collective-permute-start.5 = (f32[32,4096]{1,0:T(8,128)}, f32[32,4096]{1,0:T(8,128)S(1)}, u32[]{:S(2)}, u32[]{:S(2)}) collective-permute-start(f32[32,4096]{1,0:T(8,128)} %get-tuple-element.32.refs_4_), channel_id=1, source_target_pairs={{0,1},{1,0},{2,3},{3,2},{4,5},{5,4},{6,7},{7,6},{8,9},{9,8},{10,11... | collective-permute-start | bytes 1572872 | tf_op jit(solution)/shard_map/ppermute | solution.py:552
  80.7 3.1 %collective-permute-start.6 = (f32[32,4096]{1,0:T(8,128)}, f32[32,4096]{1,0:T(8,128)S(1)}, u32[]{:S(2)}, u32[]{:S(2)}) collective-permute-start(f32[32,4096]{1,0:T(8,128)} %get-tuple-element.33.refs_6_), channel_id=1, source_target_pairs={{0,1},{1,0},{2,3},{3,2},{4,5},{5,4},{6,7},{7,6},{8,9},{9,8},{10,11... | collective-permute-start | bytes 1572872 | tf_op jit(solution)/shard_map/ppermute | solution.py:552
  80.8 3.0 %copy-start.9 = (f32[32,4096]{1,0:T(8,128)}, f32[32,4096]{1,0:T(8,128)S(1)}, u32[]{:S(2)}) copy-start(f32[32,4096]{1,0:T(8,128)S(1)} %collective-permute-done.refs_1_) | copy-start | bytes 1572868
  82.3 1.5 copy-start.10
  83.1 0.8 copy-start.11
  83.9 0.8 copy-start.12
  84.7 64.2 %all-to-all-start = ((f32[8,640,128]{2,1,0:T(8,128)}), f32[8,640,128]{2,1,0:T(8,128)}, u32[]{:S(2)}, u32[]{:S(2)}) async-start(f32[8,640,128]{2,1,0:T(8,128)} %bitcast.24), calls=%async_computation | async-start | bytes 5242880 | tf_op jit(solution)/shard_map/all_to_all | solution.py:622
  91.8 41.1 %collective-permute-start.10 = (f32[32,4096]{1,0:T(8,128)}, f32[32,4096]{1,0:T(8,128)S(1)}, u32[]{:S(2)}, u32[]{:S(2)}) collective-permute-start(f32[32,4096]{1,0:T(8,128)} %entry_product.3.refs_0_), channel_id=1, source_target_pairs={{0,6},{1,7},{2,4},{3,5},{4,2},{5,3},{6,0},{7,1},{8,14},{9,15},{10,... | collective-permute-start | bytes 1572872 | tf_op jit(solution)/shard_map/ppermute | solution.py:552
  94.6 48.1 %collective-permute-start.9 = (f32[32,4096]{1,0:T(8,128)}, f32[32,4096]{1,0:T(8,128)S(1)}, u32[]{:S(2)}, u32[]{:S(2)}) collective-permute-start(f32[32,4096]{1,0:T(8,128)} %entry_product.3.refs_0_), channel_id=1, source_target_pairs={{0,4},{1,5},{2,6},{3,7},{4,0},{5,1},{6,2},{7,3},{8,12},{9,13},{10,... | collective-permute-start | bytes 1572872 | tf_op jit(solution)/shard_map/ppermute | solution.py:552
  95.2 47.7 %collective-permute-start.8 = (f32[32,4096]{1,0:T(8,128)}, f32[32,4096]{1,0:T(8,128)S(1)}, u32[]{:S(2)}, u32[]{:S(2)}) collective-permute-start(f32[32,4096]{1,0:T(8,128)} %entry_product.3.refs_0_), channel_id=1, source_target_pairs={{0,2},{1,3},{2,0},{3,1},{4,6},{5,7},{6,4},{7,5},{8,10},{9,11},{10,... | collective-permute-start | bytes 1572872 | tf_op jit(solution)/shard_map/ppermute | solution.py:552
  95.3 51.1 %collective-permute-start.7 = (f32[32,4096]{1,0:T(8,128)}, f32[32,4096]{1,0:T(8,128)S(1)}, u32[]{:S(2)}, u32[]{:S(2)}) collective-permute-start(f32[32,4096]{1,0:T(8,128)} %entry_product.3.refs_0_), channel_id=1, source_target_pairs={{0,1},{1,0},{2,3},{3,2},{4,5},{5,4},{6,7},{7,6},{8,9},{9,8},{10,11... | collective-permute-start | bytes 1572872 | tf_op jit(solution)/shard_map/ppermute | solution.py:552
  102.9 42.0 %copy-start = (f32[8,5,2,2,32,128]{5,4,3,2,1,0:T(8,128)S(1)}, f32[8,5,2,2,32,128]{5,4,3,2,1,0:T(8,128)}, u32[]{:S(2)}) copy-start(f32[8,5,2,2,32,128]{5,4,3,2,1,0:T(8,128)} %first_section.3.refs_3_.refs_11_) | copy-start | bytes 7864324
  133.0 9.8 %copy-start.3 = (f32[32,4096]{1,0:T(8,128)}, f32[32,4096]{1,0:T(8,128)S(1)}, u32[]{:S(2)}) copy-start(f32[32,4096]{1,0:T(8,128)S(1)} %collective-permute-done.10.refs_2_) | copy-start | bytes 1572868
  142.8 0.8 copy-start.4
  143.6 0.8 copy-start.6
  144.4 2.1 collective-permute-start.11
  144.4 2.9 %collective-permute-start.12 = (f32[32,4096]{1,0:T(8,128)}, f32[32,4096]{1,0:T(8,128)S(1)}, u32[]{:S(2)}, u32[]{:S(2)}) collective-permute-start(f32[32,4096]{1,0:T(8,128)} %get-tuple-element.35.refs_4_), channel_id=1, source_target_pairs={{0,1},{1,0},{2,3},{3,2},{4,5},{5,4},{6,7},{7,6},{8,9},{9,8},{10,11... | collective-permute-start | bytes 1572872 | tf_op jit(solution)/shard_map/ppermute | solution.py:552
  144.9 3.1 %collective-permute-start.13 = (f32[32,4096]{1,0:T(8,128)}, f32[32,4096]{1,0:T(8,128)S(1)}, u32[]{:S(2)}, u32[]{:S(2)}) collective-permute-start(f32[32,4096]{1,0:T(8,128)} %get-tuple-element.36.refs_6_), channel_id=1, source_target_pairs={{0,1},{1,0},{2,3},{3,2},{4,5},{5,4},{6,7},{7,6},{8,9},{9,8},{10,11... | collective-permute-start | bytes 1572872 | tf_op jit(solution)/shard_map/ppermute | solution.py:552
  146.4 1.6 copy-start.13
  146.5 1.5 copy-start.14
  147.2 0.8 copy-start.15
  148.1 0.8 copy-start.16
  148.8 4.6 %copy-start.18 = (s32[2,15]{1,0:T(2,128)S(1)}, s32[2,15]{1,0:T(2,128)}, u32[]{:S(2)}) copy-start(s32[2,15]{1,0:T(2,128)} %param.14) | copy-start | bytes 364
  148.8 63.5 %all-to-all-start.1 = ((f32[8,640,128]{2,1,0:T(8,128)}), f32[8,640,128]{2,1,0:T(8,128)S(1)}, u32[]{:S(2)}, u32[]{:S(2)}) async-start(f32[8,640,128]{2,1,0:T(8,128)} %bitcast.25), calls=%async_computation.1 | async-start | bytes 5242880 | tf_op jit(solution)/shard_map/all_to_all | solution.py:622
  212.4 1.5 copy-start.2
Sparse Core Ops, SparseCore 0:
  10.2 39.7 all-gather.4
  51.5 35.9 all-gather.6

commit v5 on v4

--- a/solution.py
+++ b/solution.py
@@ -173,6 +173,7 @@
 
 
 ROWS = 16
+TOGETHER = 2
 
 
 def first_section(freq, half, info, templates, strain, first, stage, twist, after):
@@ -375,9 +376,9 @@
     level_ref, total_ref, xh, xl, acc = refs[-5:]
     times = total_ref.shape[-1]
     cols = piece_refs[0].shape[0]
-    level = pl.program_id(0)
-
-    @pl.when(level == 0)
+    step = pl.program_id(0)
+
+    @pl.when(step == 0)
     def _():
         for k, ref in enumerate(piece_refs):
             row = pl.multiple_of((place_ref[0] ^ k) * cols, cols)
@@ -394,32 +395,36 @@
         at = pl.ds(pl.multiple_of(block * LANES, LANES), blocks * LANES)
         return dot3((xh[:, at], xl[:, at]), (wh_ref[at, :], wl_ref[at, :]))
 
-    start, end = edge_ref[level], edge_ref[level + 1]
-    odd = (end - start) % 2
-
-    @pl.when(odd == 1)
-    def _():
-        acc[...] = blocks_at(end - 1, 1)
-
-    @pl.when(odd == 0)
-    def _():
-        acc[...] = blocks_at(end - 2, 2)
-
-    def two(i, carry):
-        acc[...] += blocks_at(start + 2 * i, 2)
-        return carry
-
-    lax.fori_loop(0, (end - start - 1) // 2, two, 0)
+    for i in range(TOGETHER):
+        start, end = edge_ref[step * TOGETHER + i], edge_ref[step * TOGETHER + i + 1]
+        odd = (end - start) % 2
+
+        @pl.when(odd == 1)
+        def _():
+            acc[i] = blocks_at(end - 1, 1)
+
+        @pl.when(odd == 0)
+        def _():
+            acc[i] = blocks_at(end - 2, 2)
+
+        def two(n, carry):
+            acc[i] += blocks_at(start + 2 * n, 2)
+            return carry
+
+        lax.fori_loop(0, (end - start - 1) // 2, two, 0)
 
     for u in range(pieces * cols // LANES):
         at = tile(u)
-        re, im = acc[at, :times], acc[at, times:]
         cos, sin = tw_ref[0, at, :], tw_ref[1, at, :]
-        vr, vi = re * cos - im * sin, re * sin + im * cos
-        level_ref[0, 0, at, :] = vr
-        level_ref[0, 1, at, :] = vi
-        total_ref[0, at, :] += vr
-        total_ref[1, at, :] += vi
+        sum_r, sum_i = total_ref[0, at, :], total_ref[1, at, :]
+        for i in range(TOGETHER):
+            re, im = acc[i, at, :times], acc[i, at, times:]
+            vr, vi = re * cos - im * sin, re * sin + im * cos
+            level_ref[i, 0, at, :] = vr
+            level_ref[i, 1, at, :] = vi
+            sum_r, sum_i = sum_r + vr, sum_i + vi
+        total_ref[0, at, :] = sum_r
+        total_ref[1, at, :] = sum_i
 
 
 def bins_first(place, edges, pieces, table, twist, after):
@@ -429,14 +434,14 @@
     fixed = lambda shape: pl.BlockSpec(shape, lambda i: (0,) * len(shape))
     return pl.pallas_call(
         functools.partial(bins_first_kernel, len(pieces)),
-        grid=(BINS,),
+        grid=(BINS // TOGETHER,),
         in_specs=[smem, smem]
         + [fixed((cols, 2 * N1))] * len(pieces)
         + [fixed((2 * N1, 2 * times))] * 2
         + [fixed((2, rows, times))]
         + [ANY] * len(after),
         out_specs=[
-            pl.BlockSpec((1, 2, rows, times), lambda i: (i, 0, 0, 0)),
+            pl.BlockSpec((TOGETHER, 2, rows, times), lambda i: (i, 0, 0, 0)),
             fixed((2, rows, times)),
         ],
         out_shape=[
@@ -446,7 +451,7 @@
         scratch_shapes=[
             pltpu.VMEM((rows, 2 * N1), BF16),
             pltpu.VMEM((rows, 2 * N1), BF16),
-            pltpu.VMEM((rows, 2 * times), F32),
+            pltpu.VMEM((TOGETHER, rows, 2 * times), F32),
         ],
         compiler_params=pltpu.CompilerParams(vmem_limit_bytes=VMEM_LIMIT),
         cost_estimate=COST,
@@ -459,10 +464,9 @@
     w2h_ref, w2l_ref, out_ref, snr_ref, chi, hold = refs[2 * halves :]
     times = out_ref.shape[0]
     part_rows = LANES // halves
-    level = pl.program_id(0)
-    gain, share = gain_ref[level], share_ref[level]
-
-    @pl.when(level == 0)
+    step = pl.program_id(0)
+
+    @pl.when(step == 0)
     def _():
         chi[...] = jnp.zeros_like(chi)
 
@@ -473,13 +477,18 @@
     def keep(a, re, im):
         chi[a] += re * re + im * im
 
-    def deviation(p):
-        return lambda h, at: level_refs[h][0, p, at, :] * gain - total_refs[h][p, at, :] * share
-
-    x = [tuple(rows_of(deviation(p), u) for p in range(2)) for u in range(FOUR)]
-    second_points(x, w2h_ref, w2l_ref, keep)
-
-    @pl.when(level == BINS - 1)
+    for i in range(TOGETHER):
+        gain, share = gain_ref[step * TOGETHER + i], share_ref[step * TOGETHER + i]
+
+        def deviation(p):
+            return lambda h, at: (
+                level_refs[h][i, p, at, :] * gain - total_refs[h][p, at, :] * share
+            )
+
+        x = [tuple(rows_of(deviation(p), u) for p in range(2)) for u in range(FOUR)]
+        second_points(x, w2h_ref, w2l_ref, keep)
+
+    @pl.when(step == BINS // TOGETHER - 1)
     def _():
         scale = scale_ref[which_ref[0]]
 
@@ -510,9 +519,9 @@
         functools.partial(bins_second_kernel, halves),
         grid_spec=pltpu.PrefetchScalarGridSpec(
             num_scalar_prefetch=1,
-            grid=(BINS,),
+            grid=(BINS // TOGETHER,),
             in_specs=[smem, smem, smem]
-            + [pl.BlockSpec((1, 2, rows, times), lambda i, w: (i, 0, 0, 0))] * halves
+            + [pl.BlockSpec((TOGETHER, 2, rows, times), lambda i, w: (i, 0, 0, 0))] * halves
             + [fixed((2, rows, times))] * halves
             + [fixed((FOUR * 2 * LANES, 2 * LANES))] * 2,
             out_specs=[
@@ -611,30 +620,32 @@
         (which, inv_sigma, weights, table, twist, own_twist, info)
     )
     here = place.reshape(1)
-    pieces, sent, parts, after = [], [], [], []
+    ends = jnp.zeros((1,), jnp.int32), jnp.full((1,), NBLK, jnp.int32)
+    edges = [
+        jnp.concatenate([ends[0], bin_edges[coinc_tmpl[j]], ends[1]]) for j in range(slots)
+    ]
+    parts, halves, after, bins = [], [], [], []
     for h in range(HALVES):
         half = [entry_product(w, h, templates, strains[h], after) for w in which]
         far = [far_pieces(x, freq) for x in half]
         sent = first_section(freq, h, info, templates, strains[h], first, stage, twist, half)
-        far = [x[:1] + list(handed_on(x[1:], [sent])) for x in far]
-        early, pieces = pieces, [near_pieces(x, freq) for x in far]
-        (ready,) = handed_on([sent], [x for entry in pieces for x in entry[1:]])
+        if bins:
+            halves.append([bins_first(here, *x, table, own_twist[h - 1], [sent]) for x in bins])
+        done = [sent] + [x[0] for x in halves[-1]] if halves else [sent]
+        far = [x[:1] + list(handed_on(x[1:], done)) for x in far]
+        bins = [(edges[j], near_pieces(x, freq)) for j, x in enumerate(far)]
+        (ready,) = handed_on([sent], [x for _, entry in bins for x in entry[1:]])
         got = lax.all_to_all(
             ready.reshape(freq, -1, LANES), "freq", split_axis=0, concat_axis=0, tiled=True
         )
         parts.append(got.reshape(sent.shape))
         after = [ready]
+    halves.append([bins_first(here, *x, table, own_twist[-1], after) for x in bins])
 
     chi, snr = [], None
     for j in range(slots):
         t = coinc_tmpl[j]
-        ends = jnp.zeros((1,), jnp.int32), jnp.full((1,), NBLK, jnp.int32)
-        edges = jnp.concatenate([ends[0], bin_edges[t], ends[1]])
-        halves = [
-            bins_first(here, edges, early[j], table, own_twist[0], [sent]),
-            bins_first(here, edges, pieces[j], table, own_twist[1], [ready]),
-        ]
-        levels, totals = zip(*halves)
+        levels, totals = zip(*[x[j] for x in halves])
         gain = inv_sigma[t] * lax.rsqrt(weights[t])
         one, series_of = bins_second(
             which[j], inv_sigma, gain, gain * weights[t], levels, totals, second, tmpls, dets

time: 233 us -> 207 us (0.89)
  waiting for transfers between devices: 64.8 us -> 48.8 us
  Pallas kernels: 94.5 us -> 88 us
  local copies, waits for them, and re-layouts: 11.7 us -> 8.71 us
    ppermute x14, waiting for transfers between devices: 59.2 us -> 43.2 us  [swap(): return lax.ppermute(x, 'freq', [(i, i ^ k) for i in range(freq)])]
    pallas_call x1, Pallas kernels: 20.9 us -> 16.7 us  [bins_second(): pl.pallas_call(functools.partial(bins_second_kernel, halves), grid_spec=p...]
    unnamed x40 -> x33, local copies, waits for them, and re-layouts: 8.58 us -> 5.64 us
    pallas_call x2, Pallas kernels: 36.2 us -> 33.7 us  [bins_first(): pl.pallas_call(functools.partial(bins_first_kernel, len(pieces)), grid=(B...]
  transfers between devices with their start and end apart: 18 -> 18, of which waited for: 13 -> 13; matrix products, arithmetic and copies ran while one was open for 7% -> 7% of each run, Pallas kernels for 36% -> 38%
where the time goes in v5:
time: 207 us; the launch traced here: 206 us
  Pallas kernels  88 us (43%)
  waiting for transfers between devices  48.8 us (24%)
  starting transfers between devices  16.5 us (8%)
  blocking collectives  15.5 us (7%)
  between operations  15.5 us (7%)
  other arithmetic  12.8 us (6%)
  local copies, waits for them, and re-layouts  8.71 us (4%)
    ppermute x14, waiting for transfers between devices, swap(): return lax.ppermute(x, 'freq', [(i, i ^ k) for i in range(freq)])  43.2 us
    pallas_call x2, Pallas kernels, bins_first(): pl.pallas_call(functools.partial(bins_first_kernel, len(pieces)), grid=(B...  33.7 us
    pallas_call x1, Pallas kernels, bins_second(): pl.pallas_call(functools.partial(bins_second_kernel, halves), grid_spec=p...  16.7 us
    psum x1, blocking collectives, per_device(): block_power = lax.psum(local_power, 'freq')  15.5 us
    pallas_call x2, Pallas kernels, first_section(): pl.pallas_call(functools.partial(first_kernel, freq), grid_spec=pltpu.Pre...  15.2 us
    pallas_call x1, Pallas kernels, second_section(): pl.pallas_call(functools.partial(second_kernel, freq, halves), grid_spec=...  10.7 us
    all_to_all x2, starting transfers between devices, per_device(): lax.all_to_all(ready.reshape(freq, -1, LANES), 'freq', split_axis=0, conc...  8.22 us
    ppermute x14, starting transfers between devices, swap(): return lax.ppermute(x, 'freq', [(i, i ^ k) for i in range(freq)])  8.18 us
  transfers between devices with their start and end apart: 18, of which 13 were waited for; matrix products, arithmetic and copies ran while one was open for 7% of the time, Pallas kernels for 38%

profile of v5, /device:TPU:0, one launch (start us, length us, event | category | flops | bytes accessed | tf_op | source)
XLA Modules:
  0.0 205.8 jit_solution(13059968065822378799)
XLA Ops:
  7.2 2.2 %fusion.48 = (f32[3,2,32,512]{3,2,1,0:T(8,128)}, f32[3,2,32,512]{3,2,1,0:T(8,128)}) fusion(f32[3,2,64,512]{3,2,1,0:T(8,128)} %param.10), kind=kLoop, calls=%fused_computation.102 | loop fusion | bytes 1572864 | tf_op jit(solution)/shard_map/slice | solution.py:584
  9.5 0.7 all-gather.7.cloned.1.call-update
  10.3 0.3 fusion.24
  11.9 0.6 pad_add_fusion.1.which_ref
  12.5 0.1 copy.26
  12.6 0.1 reshape.720
  12.7 0.8 copy.24
  13.4 0.1 fusion.32
  13.5 0.2 add_reduce_fusion
  13.7 0.1 reshape.718
  13.8 0.1 reduce_sum.46
  13.9 15.5 %psum.7 = f32[2,32]{1,0:T(2,128)S(1)} all-reduce(f32[2,32]{1,0:T(2,128)S(1)} %reduce_sum.46), channel_id=1, replica_groups=mesh['bank'=4,'freq'=8] {'freq'}, use_global_device_ids=true, to_apply=%region_2.0 | all-reduce | flops 64 | bytes 512 | tf_op jit(solution)/shard_map/psum | solution.py:593
  29.4 0.1 reduce_sum.47
  29.5 0.1 select_reduce_fusion
  29.6 0.1 broadcast_divide_fusion
  29.7 1.0 fusion.39
  30.7 0.7 pad_maximum_fusion.4.block_ref
  31.4 0.6 pad_maximum_fusion.3.inner_ref
  32.0 2.1 %fusion.10 = (f32[1,64,2048]{2,1,0:T(8,128)S(1)}, f32[1,64,2048]{2,1,0:T(8,128)S(1)}) fusion(s32[2048]{0:T(1024)S(1)} %fusion.35, s32[64]{0:T(128)S(1)} %iota_add_fusion.1), kind=kLoop, calls=%fused_computation.29 | loop fusion | flops 1835008 | bytes 1057024 | tf_op jit(solution)/shard_map/cos | solution.py:64
  34.1 1.1 pad_maximum_fusion.tw_ref
  35.3 2.1 %fusion.12 = (f32[1,256,256]{2,1,0:T(8,128)S(1)}, f32[1,256,256]{2,1,0:T(8,128)S(1)}, f32[1,256,256]{2,1,0:T(8,128)S(1)}, f32[1,256,256]{2,1,0:T(8,128)S(1)}) fusion(s32[256]{0:T(256)S(1)} %iota_add_fusion, s32[256]{0:T(256)S(1)} %add_add_fusion, s32[256]{0:T(256)S(1)} %fusion.45), kind=kLoop, calls=%fused_computation.32 | loop fusion | flops 1835008 | bytes 1051648 | tf_op jit(solution)/shard_map/cos | solution.py:64
  37.4 6.1 %bank_table.1 = (bf16[4096,512]{1,0:T(8,128)(2,1)}, bf16[4096,512]{1,0:T(8,128)(2,1)}) custom-call(f32[32,2,256]{2,1,0:T(2,128)} %pad_maximum_fusion.4.block_ref, f32[2,64,256]{2,1,0:T(8,128)} %pad_maximum_fusion.3.inner_ref), custom_call_target="tpu_custom_call" | custom-call | flops 1048576 | bytes 1048576 | tf_op jit(solution)/shard_map/bank_table/pallas_call | solution.py:358
  43.4 1.1 pad_maximum_fusion.1
  44.5 0.6 pad_add_fusion.2.info_ref
  45.1 4.9 %all-gather.5.cloned.1.call-done = f32[12,2,32,512]{3,2,1,0:T(8,128)} async-done(((f32[3,2,32,512]{3,2,1,0:T(8,128)}), f32[12,2,32,512]{3,2,1,0:T(8,128)}) %all-gather.5.cloned.1.call-update) | async-done | bytes 1572880 | tf_op jit(solution)/shard_map/all_gather | solution.py:584
  50.0 2.7 %entry_product.2.refs_0_ = f32[32,4096]{1,0:T(8,128)} custom-call(s32[2]{0:T(128)} %pad_add_fusion.1.which_ref, f32[2,2,64,2048]{3,2,1,0:T(8,128)} %tmpl_ref.7, f32[4,3,2,32,512]{4,3,2,1,0:T(8,128)} %bitcast.27), custom_call_target="tpu_custom_call" | custom-call | flops 1048576 | bytes 1048576 | tf_op jit(solution)/shard_map/entry_product/pallas_call | solution.py:236
  52.7 2.4 %collective-permute-start.3 = (f32[32,4096]{1,0:T(8,128)}, f32[32,4096]{1,0:T(8,128)S(1)}, u32[]{:S(2)}, u32[]{:S(2)}) collective-permute-start(f32[32,4096]{1,0:T(8,128)} %entry_product.2.refs_0_), channel_id=1, source_target_pairs={{0,6},{1,7},{2,4},{3,5},{4,2},{5,3},{6,0},{7,1},{8,14},{9,15},{10,... | collective-permute-start | bytes 1572872 | tf_op jit(solution)/shard_map/ppermute | solution.py:561
  55.1 0.5 collective-permute-start.2
  55.6 0.6 collective-permute-start.1
  56.2 7.7 %first_section.2.refs_3_.refs_0_ = f32[8,5,2,2,32,128]{5,4,3,2,1,0:T(8,128)} custom-call(s32[11]{0:T(128)} %pad_add_fusion.2.info_ref, f32[2,2,64,2048]{3,2,1,0:T(8,128)} %tmpl_ref.7, f32[4,3,2,32,512]{4,3,2,1,0:T(8,128)} %bitcast.28, bf16[256,256]{1,0:T(8,128)(2,1)} %constant.170.clone.wh_ref, bf16[256,256]{1,0:T(8,128)(2,1)} %constant.171.clone.wl_ref, ...), custom_call_target="tpu_custom_call" | custom-call | flops 2516582400 | bytes 16777216 | tf_op jit(solution)/shard_map/first_section/pallas_call | solution.py:188
  63.9 4.8 %collective-permute-done.3.refs_2_ = f32[32,4096]{1,0:T(8,128)S(1)} collective-permute-done((f32[32,4096]{1,0:T(8,128)}, f32[32,4096]{1,0:T(8,128)S(1)}, u32[]{:S(2)}, u32[]{:S(2)}) %collective-permute-start.3) | collective-permute-done | bytes 524320 | tf_op jit(solution)/shard_map/ppermute | solution.py:561
  68.7 9.9 %collective-permute-done.2.refs_1_ = f32[32,4096]{1,0:T(8,128)S(1)} collective-permute-done((f32[32,4096]{1,0:T(8,128)}, f32[32,4096]{1,0:T(8,128)S(1)}, u32[]{:S(2)}, u32[]{:S(2)}) %collective-permute-start.2) | collective-permute-done | bytes 524320 | tf_op jit(solution)/shard_map/ppermute | solution.py:561
  78.7 0.8 copy-done.4
  79.4 0.8 copy-done.5
  80.2 0.1 collective-permute-start.4
  80.3 0.4 collective-permute-start.5
  80.7 0.1 collective-permute-start.6
  80.8 1.5 collective-permute-done.4.refs_3_
  82.3 0.7 collective-permute-done.5.refs_5_
  83.1 0.7 collective-permute-done.6.refs_7_
  83.9 0.8 copy-done.10
  84.7 3.6 %all-to-all-start = ((f32[8,640,128]{2,1,0:T(8,128)}), f32[8,640,128]{2,1,0:T(8,128)S(1)}, u32[]{:S(2)}, u32[]{:S(2)}) async-start(f32[8,640,128]{2,1,0:T(8,128)} %bitcast.25), calls=%async_computation | async-start | bytes 5242880 | tf_op jit(solution)/shard_map/all_to_all | solution.py:638
  88.4 2.9 %entry_product.3.refs_0_ = f32[32,4096]{1,0:T(8,128)} custom-call(s32[2]{0:T(128)} %pad_add_fusion.1.which_ref, f32[2,2,64,2048]{3,2,1,0:T(8,128)} %tmpl_ref.7, f32[4,3,2,32,512]{4,3,2,1,0:T(8,128)} %bitcast.29, f32[8,5,2,2,32,128]{5,4,3,2,1,0:T(8,128)} %handed_on.5.refs_0_), custom_call_target="tpu_custom_call" | custom-call | flops 1048576 | bytes 1048576 | tf_op jit(solution)/shard_map/entry_product/pallas_call | solution.py:236
  91.2 2.8 %collective-permute-start.10 = (f32[32,4096]{1,0:T(8,128)}, f32[32,4096]{1,0:T(8,128)S(1)}, u32[]{:S(2)}, u32[]{:S(2)}) collective-permute-start(f32[32,4096]{1,0:T(8,128)} %entry_product.3.refs_0_), channel_id=1, source_target_pairs={{0,6},{1,7},{2,4},{3,5},{4,2},{5,3},{6,0},{7,1},{8,14},{9,15},{10,... | collective-permute-start | bytes 1572872 | tf_op jit(solution)/shard_map/ppermute | solution.py:561
  94.0 0.5 collective-permute-start.9
  94.6 0.2 collective-permute-start.8
  94.7 0.6 pad_add_fusion.3.edge_ref
  95.3 7.6 %first_section.3.refs_11_.refs_3_.refs_0_ = f32[8,5,2,2,32,128]{5,4,3,2,1,0:T(8,128)} custom-call(s32[11]{0:T(128)} %pad_add_fusion.2.info_ref, f32[2,2,64,2048]{3,2,1,0:T(8,128)} %tmpl_ref.7, f32[4,3,2,32,512]{4,3,2,1,0:T(8,128)} %bitcast.30, bf16[256,256]{1,0:T(8,128)(2,1)} %constant.170.clone.wh_ref, bf16[256,256]{1,0:T(8,128)(2,1)} %constant.171.clone.wl_ref, ...), custom_call_target="tpu_custom_call" | custom-call | flops 2516582400 | bytes 16777216 | tf_op jit(solution)/shard_map/first_section/pallas_call | solution.py:188
  102.9 16.9 %bins_first.2 = (f32[16,2,256,256]{3,2,1,0:T(8,128)}, f32[2,256,256]{2,1,0:T(8,128)}) custom-call(s32[1]{0:T(128)} %bitcast.place_ref, s32[17]{0:T(128)} %pad_add_fusion.3.edge_ref, f32[32,4096]{1,0:T(8,128)} %entry_product.2.refs_0_, f32[32,4096]{1,0:T(8,128)} %copy-done.6, f32[32,4096]{1,0:T(8,128)} %get-tuple-element.31.refs_2_, f32[32,4096]{1,0:T(8,128)} %copy-done.8, ...), custom_call_target="tpu_custom_call" | custom-call | flops 1048576 | bytes 1048576 | tf_op jit(solution)/shard_map/bins_first/pallas_call | solution.py:435
  119.8 12.4 %collective-permute-done.10.refs_2_ = f32[32,4096]{1,0:T(8,128)S(1)} collective-permute-done((f32[32,4096]{1,0:T(8,128)}, f32[32,4096]{1,0:T(8,128)S(1)}, u32[]{:S(2)}, u32[]{:S(2)}) %collective-permute-start.10) | collective-permute-done | bytes 524320 | tf_op jit(solution)/shard_map/ppermute | solution.py:561
  132.3 9.9 %collective-permute-done.9.refs_1_ = f32[32,4096]{1,0:T(8,128)} collective-permute-done((f32[32,4096]{1,0:T(8,128)}, f32[32,4096]{1,0:T(8,128)}, u32[]{:S(2)}, u32[]{:S(2)}) %collective-permute-start.9) | collective-permute-done | bytes 524320 | tf_op jit(solution)/shard_map/ppermute | solution.py:561
  142.1 0.1 collective-permute-done.8.refs_0_
  142.2 0.5 collective-permute-start.12
  142.8 1.6 collective-permute-done.11.refs_3_
  144.3 0.7 collective-permute-done.12.refs_5_
  145.1 0.7 collective-permute-done.13.refs_7_
  145.9 0.8 copy-done.13
  146.7 1.6 copy-done.1
  148.3 4.6 %all-to-all-start.1 = ((f32[8,640,128]{2,1,0:T(8,128)}), f32[8,640,128]{2,1,0:T(8,128)}, u32[]{:S(2)}, u32[]{:S(2)}) async-start(f32[8,640,128]{2,1,0:T(8,128)} %bitcast.24), calls=%async_computation.1 | async-start | bytes 5242880 | tf_op jit(solution)/shard_map/all_to_all | solution.py:638
  152.9 0.6 dynamic_slice.11
  153.5 1.2 bitcast_multiply_fusion
  154.7 16.8 %bins_first.3 = (f32[16,2,256,256]{3,2,1,0:T(8,128)}, f32[2,256,256]{2,1,0:T(8,128)}) custom-call(s32[1]{0:T(128)} %bitcast.place_ref, s32[17]{0:T(128)} %pad_add_fusion.3.edge_ref, f32[32,4096]{1,0:T(8,128)} %entry_product.3.refs_0_, f32[32,4096]{1,0:T(8,128)} %copy-done.7, f32[32,4096]{1,0:T(8,128)} %get-tuple-element.38.refs_2_, f32[32,4096]{1,0:T(8,128)} %copy-done.11, ...), custom_call_target="tpu_custom_call" | custom-call | flops 1048576 | bytes 1048576 | tf_op jit(solution)/shard_map/bins_first/pallas_call | solution.py:435
  171.5 16.7 %bins_second.1 = (f32[256,512]{1,0:T(8,128)}, f32[2,3,2,256,512]{4,3,2,1,0:T(8,128)}) custom-call(s32[2]{0:T(128)} %pad_add_fusion.1.which_ref, f32[2]{0:T(128)} %copy-done.14, f32[16]{0:T(128)} %get-tuple-element.49.gain_ref, f32[16]{0:T(128)} %get-tuple-element.48.share_ref, f32[16,2,256,256]{3,2,1,0:T(8,128)} %get-tuple-element.37.refs_4_.refs_0_, ...), custom_call_target="tpu_custom_call" | custom-call | flops 1048576 | bytes 1048576 | tf_op jit(solution)/shard_map/bins_second/pallas_call | solution.py:518
  188.2 10.7 %second_section.1 = f32[2,3,2,256,512]{4,3,2,1,0:T(8,128)} custom-call(s32[11]{0:T(128)} %pad_add_fusion.2.info_ref, f32[2]{0:T(128)} %copy-done.14, f32[8,5,2,2,32,128]{5,4,3,2,1,0:T(8,128)} %bitcast.26, f32[8,5,2,2,32,128]{5,4,3,2,1,0:T(8,128)} %bitcast.9.refs_1_, ...), custom_call_target="tpu_custom_call", output_to_operand_aliasing={{}: (6, {})} | custom-call | flops 1048576 | bytes 1048576 | tf_op jit(solution)/shard_map/second_section/pallas_call | solution.py:312
  (54 shorter events, 0.5 us)
Async XLA Ops:
  7.2 6.4 %copy-start = (f32[2,2,64,2048]{3,2,1,0:T(8,128)S(1)}, f32[2,2,64,2048]{3,2,1,0:T(8,128)}, u32[]{:S(2)}) copy-start(f32[2,2,64,2048]{3,2,1,0:T(8,128)} %tmpl_ref.7) | copy-start | bytes 6291460
  7.2 42.8 %all-gather.5.cloned.1.call-start = ((), (), s32[]{:S(2)}) async-start(), calls=%async_computation.2 | async-start | bytes 1966080 | tf_op jit(solution)/shard_map/all_gather | solution.py:584
  9.4 78.9 %all-gather.7.cloned.1.call-start = ((), (), s32[]{:S(2)}) async-start(), calls=%async_computation.3 | async-start | bytes 1966080 | tf_op jit(solution)/shard_map/all_gather | solution.py:584
  29.6 123.3 %copy-start.14 = (f32[2]{0:T(128)}, f32[2]{0:T(128)S(1)}, u32[]{:S(2)}) copy-start(f32[2]{0:T(128)S(1)} %rsqrt.6.scale_ref) | copy-start | bytes 28
  52.7 16.0 %collective-permute-start.3 = (f32[32,4096]{1,0:T(8,128)}, f32[32,4096]{1,0:T(8,128)S(1)}, u32[]{:S(2)}, u32[]{:S(2)}) collective-permute-start(f32[32,4096]{1,0:T(8,128)} %entry_product.2.refs_0_), channel_id=1, source_target_pairs={{0,6},{1,7},{2,4},{3,5},{4,2},{5,3},{6,0},{7,1},{8,14},{9,15},{10,... | collective-permute-start | bytes 1572872 | tf_op jit(solution)/shard_map/ppermute | solution.py:561
  55.1 23.5 %collective-permute-start.2 = (f32[32,4096]{1,0:T(8,128)}, f32[32,4096]{1,0:T(8,128)S(1)}, u32[]{:S(2)}, u32[]{:S(2)}) collective-permute-start(f32[32,4096]{1,0:T(8,128)} %entry_product.2.refs_0_), channel_id=1, source_target_pairs={{0,4},{1,5},{2,6},{3,7},{4,0},{5,1},{6,2},{7,3},{8,12},{9,13},{10,... | collective-permute-start | bytes 1572872 | tf_op jit(solution)/shard_map/ppermute | solution.py:561
  55.6 23.0 %collective-permute-start.1 = (f32[32,4096]{1,0:T(8,128)}, f32[32,4096]{1,0:T(8,128)S(1)}, u32[]{:S(2)}, u32[]{:S(2)}) collective-permute-start(f32[32,4096]{1,0:T(8,128)} %entry_product.2.refs_0_), channel_id=1, source_target_pairs={{0,2},{1,3},{2,0},{3,1},{4,6},{5,7},{6,4},{7,5},{8,10},{9,11},{10,... | collective-permute-start | bytes 1572872 | tf_op jit(solution)/shard_map/ppermute | solution.py:561
  56.2 24.6 %collective-permute-start = (f32[32,4096]{1,0:T(8,128)}, f32[32,4096]{1,0:T(8,128)S(1)}, u32[]{:S(2)}, u32[]{:S(2)}) collective-permute-start(f32[32,4096]{1,0:T(8,128)} %entry_product.2.refs_0_), channel_id=1, source_target_pairs={{0,1},{1,0},{2,3},{3,2},{4,5},{5,4},{6,7},{7,6},{8,9},{9,8},{10,11... | collective-permute-start | bytes 1572872 | tf_op jit(solution)/shard_map/ppermute | solution.py:561
  68.7 10.0 %copy-start.3 = (f32[32,4096]{1,0:T(8,128)}, f32[32,4096]{1,0:T(8,128)S(1)}, u32[]{:S(2)}) copy-start(f32[32,4096]{1,0:T(8,128)S(1)} %collective-permute-done.3.refs_2_) | copy-start | bytes 1572868
  78.6 0.8 copy-start.4
  79.4 0.8 copy-start.5
  80.2 2.1 %collective-permute-start.4 = (f32[32,4096]{1,0:T(8,128)}, f32[32,4096]{1,0:T(8,128)S(1)}, u32[]{:S(2)}, u32[]{:S(2)}) collective-permute-start(f32[32,4096]{1,0:T(8,128)} %get-tuple-element.31.refs_2_), channel_id=1, source_target_pairs={{0,1},{1,0},{2,3},{3,2},{4,5},{5,4},{6,7},{7,6},{8,9},{9,8},{10,11... | collective-permute-start | bytes 1572872 | tf_op jit(solution)/shard_map/ppermute | solution.py:561
  80.3 2.7 %collective-permute-start.5 = (f32[32,4096]{1,0:T(8,128)}, f32[32,4096]{1,0:T(8,128)S(1)}, u32[]{:S(2)}, u32[]{:S(2)}) collective-permute-start(f32[32,4096]{1,0:T(8,128)} %get-tuple-element.32.refs_4_), channel_id=1, source_target_pairs={{0,1},{1,0},{2,3},{3,2},{4,5},{5,4},{6,7},{7,6},{8,9},{9,8},{10,11... | collective-permute-start | bytes 1572872 | tf_op jit(solution)/shard_map/ppermute | solution.py:561
  80.7 3.1 %collective-permute-start.6 = (f32[32,4096]{1,0:T(8,128)}, f32[32,4096]{1,0:T(8,128)S(1)}, u32[]{:S(2)}, u32[]{:S(2)}) collective-permute-start(f32[32,4096]{1,0:T(8,128)} %get-tuple-element.33.refs_6_), channel_id=1, source_target_pairs={{0,1},{1,0},{2,3},{3,2},{4,5},{5,4},{6,7},{7,6},{8,9},{9,8},{10,11... | collective-permute-start | bytes 1572872 | tf_op jit(solution)/shard_map/ppermute | solution.py:561
  80.8 3.0 %copy-start.6 = (f32[32,4096]{1,0:T(8,128)}, f32[32,4096]{1,0:T(8,128)S(1)}, u32[]{:S(2)}) copy-start(f32[32,4096]{1,0:T(8,128)S(1)} %collective-permute-done.refs_1_) | copy-start | bytes 1572868
  82.3 1.5 copy-start.8
  83.1 0.8 copy-start.9
  83.9 0.8 copy-start.10
  84.7 62.0 %all-to-all-start = ((f32[8,640,128]{2,1,0:T(8,128)}), f32[8,640,128]{2,1,0:T(8,128)S(1)}, u32[]{:S(2)}, u32[]{:S(2)}) async-start(f32[8,640,128]{2,1,0:T(8,128)} %bitcast.25), calls=%async_computation | async-start | bytes 5242880 | tf_op jit(solution)/shard_map/all_to_all | solution.py:638
  88.3 6.4 %copy-start.15 = (s32[2,15]{1,0:T(2,128)S(1)}, s32[2,15]{1,0:T(2,128)}, u32[]{:S(2)}) copy-start(s32[2,15]{1,0:T(2,128)} %param.14) | copy-start | bytes 364
  91.2 41.0 %collective-permute-start.10 = (f32[32,4096]{1,0:T(8,128)}, f32[32,4096]{1,0:T(8,128)S(1)}, u32[]{:S(2)}, u32[]{:S(2)}) collective-permute-start(f32[32,4096]{1,0:T(8,128)} %entry_product.3.refs_0_), channel_id=1, source_target_pairs={{0,6},{1,7},{2,4},{3,5},{4,2},{5,3},{6,0},{7,1},{8,14},{9,15},{10,... | collective-permute-start | bytes 1572872 | tf_op jit(solution)/shard_map/ppermute | solution.py:561
  94.0 48.1 %collective-permute-start.9 = (f32[32,4096]{1,0:T(8,128)}, f32[32,4096]{1,0:T(8,128)}, u32[]{:S(2)}, u32[]{:S(2)}) collective-permute-start(f32[32,4096]{1,0:T(8,128)} %entry_product.3.refs_0_), channel_id=1, source_target_pairs={{0,4},{1,5},{2,6},{3,7},{4,0},{5,1},{6,2},{7,3},{8,12},{9,13},{10,... | collective-permute-start | bytes 1572872 | tf_op jit(solution)/shard_map/ppermute | solution.py:561
  94.6 47.6 %collective-permute-start.8 = (f32[32,4096]{1,0:T(8,128)}, f32[32,4096]{1,0:T(8,128)}, u32[]{:S(2)}, u32[]{:S(2)}) collective-permute-start(f32[32,4096]{1,0:T(8,128)} %entry_product.3.refs_0_), channel_id=1, source_target_pairs={{0,2},{1,3},{2,0},{3,1},{4,6},{5,7},{6,4},{7,5},{8,10},{9,11},{10,... | collective-permute-start | bytes 1572872 | tf_op jit(solution)/shard_map/ppermute | solution.py:561
  95.3 47.4 %collective-permute-start.7 = (f32[32,4096]{1,0:T(8,128)}, f32[32,4096]{1,0:T(8,128)S(1)}, u32[]{:S(2)}, u32[]{:S(2)}) collective-permute-start(f32[32,4096]{1,0:T(8,128)} %entry_product.3.refs_0_), channel_id=1, source_target_pairs={{0,1},{1,0},{2,3},{3,2},{4,5},{5,4},{6,7},{7,6},{8,9},{9,8},{10,11... | collective-permute-start | bytes 1572872 | tf_op jit(solution)/shard_map/ppermute | solution.py:561
  132.3 9.9 %copy-start.2 = (f32[32,4096]{1,0:T(8,128)}, f32[32,4096]{1,0:T(8,128)S(1)}, u32[]{:S(2)}) copy-start(f32[32,4096]{1,0:T(8,128)S(1)} %collective-permute-done.10.refs_2_) | copy-start | bytes 1572868
  142.2 2.1 %collective-permute-start.11 = (f32[32,4096]{1,0:T(8,128)}, f32[32,4096]{1,0:T(8,128)S(1)}, u32[]{:S(2)}, u32[]{:S(2)}) collective-permute-start(f32[32,4096]{1,0:T(8,128)} %get-tuple-element.38.refs_2_), channel_id=1, source_target_pairs={{0,1},{1,0},{2,3},{3,2},{4,5},{5,4},{6,7},{7,6},{8,9},{9,8},{10,11... | collective-permute-start | bytes 1572872 | tf_op jit(solution)/shard_map/ppermute | solution.py:561
  142.2 2.9 %collective-permute-start.12 = (f32[32,4096]{1,0:T(8,128)}, f32[32,4096]{1,0:T(8,128)S(1)}, u32[]{:S(2)}, u32[]{:S(2)}) collective-permute-start(f32[32,4096]{1,0:T(8,128)} %get-tuple-element.39.refs_4_), channel_id=1, source_target_pairs={{0,1},{1,0},{2,3},{3,2},{4,5},{5,4},{6,7},{7,6},{8,9},{9,8},{10,11... | collective-permute-start | bytes 1572872 | tf_op jit(solution)/shard_map/ppermute | solution.py:561
  142.7 3.1 %collective-permute-start.13 = (f32[32,4096]{1,0:T(8,128)}, f32[32,4096]{1,0:T(8,128)S(1)}, u32[]{:S(2)}, u32[]{:S(2)}) collective-permute-start(f32[32,4096]{1,0:T(8,128)} %get-tuple-element.40.refs_6_), channel_id=1, source_target_pairs={{0,1},{1,0},{2,3},{3,2},{4,5},{5,4},{6,7},{7,6},{8,9},{9,8},{10,11... | collective-permute-start | bytes 1572872 | tf_op jit(solution)/shard_map/ppermute | solution.py:561
  142.8 3.1 %copy-start.7 = (f32[32,4096]{1,0:T(8,128)}, f32[32,4096]{1,0:T(8,128)S(1)}, u32[]{:S(2)}) copy-start(f32[32,4096]{1,0:T(8,128)S(1)} %collective-permute-done.7.refs_1_) | copy-start | bytes 1572868
  144.3 1.5 copy-start.11
  145.1 0.8 copy-start.12
  145.9 0.8 copy-start.13
  146.7 1.6 copy-start.1
  148.3 39.9 %all-to-all-start.1 = ((f32[8,640,128]{2,1,0:T(8,128)}), f32[8,640,128]{2,1,0:T(8,128)}, u32[]{:S(2)}, u32[]{:S(2)}) async-start(f32[8,640,128]{2,1,0:T(8,128)} %bitcast.24), calls=%async_computation.1 | async-start | bytes 5242880 | tf_op jit(solution)/shard_map/all_to_all | solution.py:638
Sparse Core Ops, SparseCore 0:
  10.2 39.7 all-gather.4
  51.5 35.9 all-gather.6

commit v6 on v5

--- a/solution.py
+++ b/solution.py
@@ -136,7 +136,8 @@
 def first_kernel(
     freq, info_ref, tmpl_ref, strain_ref, wh_ref, wl_ref, stage_ref, tw_ref, *refs
 ):
-    out_ref, gh, gl, z = refs[-4:]
+    out_ref, token_ref, gh, gl, z = refs[-5:]
+    token_ref[...] = jnp.zeros_like(token_ref)
     rows = tmpl_ref.shape[2]
     for r in range(0, rows, ROWS):
         at = slice(r, r + ROWS)
@@ -173,83 +174,95 @@
 
 
 ROWS = 16
+HALVES = 2
 TOGETHER = 2
 
 
-def first_section(freq, half, info, templates, strain, first, stage, twist, after):
+def first_section(freq, half, info, templates, strain, first, stage, twist, earlier):
     tmpls = templates.shape[0]
     pieces, dets, _, cols, piece_len = strain.shape
     series = tmpls * dets - 1
     groups = COARSE // freq
-    rows = 2 * ROWS if cols % (2 * ROWS) == 0 else ROWS
-    steps = cols // rows
-    table = pl.BlockSpec((2 * LANES, 2 * LANES), lambda c, i, n: (0, 0))
+    rows = cols // HALVES
+    table = pl.BlockSpec((2 * LANES, 2 * LANES), lambda i, n: (0, 0))
     out = (freq, series, 2, groups, cols, LANES)
     return pl.pallas_call(
         functools.partial(first_kernel, freq),
         grid_spec=pltpu.PrefetchScalarGridSpec(
             num_scalar_prefetch=1,
-            grid=(steps, series),
+            grid=(series,),
             in_specs=[
                 pl.BlockSpec(
-                    (1, 2, rows, N1), lambda c, i, n: (n[1 + 2 * i], 0, half * steps + c, 0)
+                    (1, 2, rows, N1), lambda i, n: (n[1 + 2 * i], 0, half, 0)
                 ),
                 pl.BlockSpec(
-                    (pieces, 1, 2, rows, piece_len), lambda c, i, n: (0, n[2 + 2 * i], 0, c, 0)
+                    (pieces, 1, 2, rows, piece_len), lambda i, n: (0, n[2 + 2 * i], 0, half, 0)
                 ),
                 table,
                 table,
-                pl.BlockSpec((2 * COARSE, LANES), lambda c, i, n: (0, 0)),
-                pl.BlockSpec((2, rows, N1), lambda c, i, n: (0, half * steps + c, 0)),
+                pl.BlockSpec((2 * COARSE, LANES), lambda i, n: (0, 0)),
+                pl.BlockSpec((2, rows, N1), lambda i, n: (0, half, 0)),
             ]
-            + [ANY] * len(after),
-            out_specs=pl.BlockSpec(
-                (freq, 1, 2, groups, rows, LANES), lambda c, i, n: (0, i, 0, 0, c, 0)
-            ),
+            + [ANY] * len(earlier),
+            out_specs=[
+                pl.BlockSpec(
+                    (freq, 1, 2, groups, rows, LANES), lambda i, n: (0, i, 0, 0, half, 0)
+                ),
+                pl.BlockSpec((8, LANES), lambda i, n: (0, 0)),
+            ],
             scratch_shapes=[
                 pltpu.VMEM((COARSE * rows, 2 * LANES), BF16),
                 pltpu.VMEM((COARSE * rows, 2 * LANES), BF16),
                 pltpu.VMEM((COARSE * rows, 2 * LANES), F32),
             ],
         ),
-        out_shape=jax.ShapeDtypeStruct(out, F32),
+        out_shape=[
+            jax.ShapeDtypeStruct(out, F32),
+            jax.ShapeDtypeStruct((8, LANES), F32),
+        ],
+        input_output_aliases={7: 0} if earlier else {},
         compiler_params=pltpu.CompilerParams(vmem_limit_bytes=VMEM_LIMIT),
         cost_estimate=pl.CostEstimate(
             flops=60 * series * cols * N1 * LANES, bytes_accessed=16 * MIB, transcendentals=0
         ),
         name="first_section",
-    )(info, templates, strain, first[0], first[1], stage, twist, *after)
-
-
-def entry_kernel(which_ref, tmpl_ref, strain_ref, *refs):
-    out_ref = refs[-1]
+    )(info, templates, strain, first[0], first[1], stage, twist, *earlier)
+
+
+def entry_kernel(which_ref, tmpl_ref, *refs):
+    quarter_refs, out_ref = refs[:-1], refs[-1]
+    banks = len(quarter_refs)
+    length = N1 // banks
     first_half = lax.broadcasted_iota(jnp.int32, (ROWS, LANES), 1) < BLOCK
-    got = products(lambda p, u: tmpl_ref[0, p, :, tile(u)], strain_ref, (0,))
-    for u, re, im in got:
-        out_ref[:, tile(2 * u)] = jnp.where(first_half, re, pltpu.roll(im, BLOCK, 1))
-        out_ref[:, tile(2 * u + 1)] = jnp.where(first_half, pltpu.roll(re, BLOCK, 1), im)
-
-
-def entry_product(which, half, templates, strain, after):
-    pieces, _, _, cols, piece_len = strain.shape
-    steps = cols // ROWS
+    for k, ref in enumerate(quarter_refs):
+        start = lax.rem(which_ref[1] - k + banks, banks) * length
+        for u in range(length // LANES):
+            lane = pl.ds(pl.multiple_of(start + u * LANES, LANES), LANES)
+            hr, hi = tmpl_ref[0, 0, :, lane], tmpl_ref[0, 1, :, lane]
+            sr, si = ref[0, :, tile(u)], ref[1, :, tile(u)]
+            re, im = hr * sr + hi * si, hr * si - hi * sr
+            to = pl.multiple_of(2 * start + 2 * u * LANES, 2 * LANES)
+            out_ref[:, pl.ds(to, LANES)] = jnp.where(first_half, re, pltpu.roll(im, BLOCK, 1))
+            to = pl.multiple_of(to + LANES, LANES)
+            out_ref[:, pl.ds(to, LANES)] = jnp.where(first_half, pltpu.roll(re, BLOCK, 1), im)
+
+
+def entry_product(which, templates, quarters):
+    _, cols, length = quarters[0].shape
     return pl.pallas_call(
         entry_kernel,
         grid_spec=pltpu.PrefetchScalarGridSpec(
             num_scalar_prefetch=1,
-            grid=(steps,),
-            in_specs=[
-                pl.BlockSpec((1, 2, ROWS, N1), lambda c, w: (w[0], 0, half * steps + c, 0)),
-                pl.BlockSpec((pieces, 1, 2, ROWS, piece_len), lambda c, w: (0, w[1], 0, c, 0)),
-            ]
-            + [ANY] * len(after),
+            grid=(cols // ROWS,),
+            in_specs=[pl.BlockSpec((1, 2, ROWS, N1), lambda c, w: (w[0], 0, c, 0))]
+            + [pl.BlockSpec((2, ROWS, length), lambda c, w: (0, c, 0))] * len(quarters),
             out_specs=pl.BlockSpec((ROWS, 2 * N1), lambda c, w: (c, 0)),
         ),
         out_shape=jax.ShapeDtypeStruct((cols, 2 * N1), F32),
         compiler_params=pltpu.CompilerParams(vmem_limit_bytes=VMEM_LIMIT),
         cost_estimate=COST,
         name="entry_product",
-    )(which, templates, strain, *after)
+    )(which, templates, *quarters)
 
 
 def second_points(x, w2h_ref, w2l_ref, use):
@@ -427,8 +440,8 @@
         total_ref[1, at, :] = sum_i
 
 
-def bins_first(place, edges, pieces, table, twist, after):
-    cols = pieces[0].shape[0]
+def bins_first(half, place, edges, pieces, table, twist, after):
+    cols = pieces[0].shape[0] // HALVES
     rows, times = twist.shape[1:]
     smem = pl.BlockSpec(memory_space=pltpu.SMEM)
     fixed = lambda shape: pl.BlockSpec(shape, lambda i: (0,) * len(shape))
@@ -436,7 +449,7 @@
         functools.partial(bins_first_kernel, len(pieces)),
         grid=(BINS // TOGETHER,),
         in_specs=[smem, smem]
-        + [fixed((cols, 2 * N1))] * len(pieces)
+        + [pl.BlockSpec((cols, 2 * N1), lambda i: (half, 0))] * len(pieces)
         + [fixed((2 * N1, 2 * times))] * 2
         + [fixed((2, rows, times))]
         + [ANY] * len(after),
@@ -569,28 +582,37 @@
     return [x for even in far for x in (even, swap(even, freq, 1))]
 
 
-HALVES = 2
-
-
 def per_device(strain, templates, coinc_tmpl, coinc_det, bin_edges):
-    freq = lax.axis_size("freq")
+    freq, banks = lax.axis_size("freq"), lax.axis_size("bank")
     place = lax.axis_index("freq").astype(jnp.int32)
+    bank = lax.axis_index("bank").astype(jnp.int32)
     tmpls, _, cols, _ = templates.shape
     slots, dets = coinc_tmpl.shape[0], strain.shape[0]
     times = N1 // freq
     part = cols // HALVES
 
-    strains = [
-        lax.all_gather(strain[:, :, h * part : (h + 1) * part], "bank", axis=0, tiled=False)
-        for h in range(HALVES)
-    ]
+    def to_bank(x, k):
+        return lax.ppermute(x, "bank", [(i, (i + k) % banks) for i in range(banks)])
+
+    asked = [coinc_det] + [to_bank(coinc_det, -k) for k in range(1, banks)]
+    quarters = []
+    for j in range(slots):
+        own = lax.dynamic_index_in_dim(strain, coinc_det[j], 0, keepdims=False)
+        one = [own]
+        for k in range(1, banks):
+            picked = lax.dynamic_index_in_dim(strain, asked[k][j], 0, keepdims=False)
+            one.append(to_bank(picked, k))
+        quarters.append(one)
+    strains = lax.all_gather(strain, "bank", axis=0, tiled=False)
+
     first = tuple(jnp.asarray(t) for t in first_table())
-    second = tuple(jnp.asarray(t) for t in second_table(cols, HALVES))
+    second = tuple(jnp.asarray(t) for t in second_table(cols, 1))
+    second_halves = tuple(jnp.asarray(t) for t in second_table(cols, HALVES))
     stage = jnp.asarray(stage_table())
 
     power = (templates[:, 0] ** 2 + templates[:, 1] ** 2).sum(axis=1)
     local_power = power.reshape(tmpls, NBLK, BLOCK).sum(axis=2)
-    block_power = lax.psum(local_power, "freq")
+    block_power = lax.all_gather(local_power, "freq", axis=0, tiled=False).sum(axis=0)
     sigma_sq = block_power.sum(axis=1)
     inv_sigma = lax.rsqrt(sigma_sq)
     bin_of = jnp.sum(
@@ -616,43 +638,46 @@
     series = series + (series >= which[0][0] * dets + which[0][1])
     info = jnp.stack([series // dets, series % dets], axis=1).reshape(-1)
     info = jnp.concatenate([place.reshape(1), info])
-    which, inv_sigma, weights, table, twist, own_twist, info = lax.optimization_barrier(
-        (which, inv_sigma, weights, table, twist, own_twist, info)
-    )
-    here = place.reshape(1)
     ends = jnp.zeros((1,), jnp.int32), jnp.full((1,), NBLK, jnp.int32)
     edges = [
         jnp.concatenate([ends[0], bin_edges[coinc_tmpl[j]], ends[1]]) for j in range(slots)
     ]
-    parts, halves, after, bins = [], [], [], []
-    for h in range(HALVES):
-        half = [entry_product(w, h, templates, strains[h], after) for w in which]
-        far = [far_pieces(x, freq) for x in half]
-        sent = first_section(freq, h, info, templates, strains[h], first, stage, twist, half)
-        if bins:
-            halves.append([bins_first(here, *x, table, own_twist[h - 1], [sent]) for x in bins])
-        done = [sent] + [x[0] for x in halves[-1]] if halves else [sent]
-        far = [x[:1] + list(handed_on(x[1:], done)) for x in far]
-        bins = [(edges[j], near_pieces(x, freq)) for j, x in enumerate(far)]
-        (ready,) = handed_on([sent], [x for _, entry in bins for x in entry[1:]])
-        got = lax.all_to_all(
-            ready.reshape(freq, -1, LANES), "freq", split_axis=0, concat_axis=0, tiled=True
-        )
-        parts.append(got.reshape(sent.shape))
-        after = [ready]
-    halves.append([bins_first(here, *x, table, own_twist[-1], after) for x in bins])
+    info, edges, table, twist, own_twist = lax.optimization_barrier(
+        (info, edges, table, twist, own_twist)
+    )
+
+    here = place.reshape(1)
+    own = [
+        entry_product(jnp.stack([coinc_tmpl[j], bank]), templates, quarters[j])
+        for j in range(slots)
+    ]
+    far = [far_pieces(x, freq) for x in own]
+    sent, token = first_section(freq, 0, info, templates, strains, first, stage, twist, [])
+    far = [x[:1] + list(handed_on(x[1:], [token])) for x in far]
+    pieces = [near_pieces(x, freq) for x in far]
+    sent, _ = first_section(freq, 1, info, templates, strains, first, stage, twist, [sent])
+    (ready,) = handed_on([sent], [x for entry in pieces for x in entry[1:]])
+    got = lax.all_to_all(
+        ready.reshape(freq, -1, LANES), "freq", split_axis=0, concat_axis=0, tiled=True
+    )
+    got = got.reshape(sent.shape)
 
     chi, snr = [], None
     for j in range(slots):
         t = coinc_tmpl[j]
-        levels, totals = zip(*[x[j] for x in halves])
+        halves = [
+            bins_first(h, here, edges[j], pieces[j], table, own_twist[h], [ready])
+            for h in range(HALVES)
+        ]
+        levels, totals = zip(*halves)
         gain = inv_sigma[t] * lax.rsqrt(weights[t])
+        share = gain * weights[t]
         one, series_of = bins_second(
-            which[j], inv_sigma, gain, gain * weights[t], levels, totals, second, tmpls, dets
+            which[j], inv_sigma, gain, share, levels, totals, second_halves, tmpls, dets
         )
         chi.append(one)
         snr = series_of if snr is None else snr
-    snr = second_section(freq, info, inv_sigma, parts, second, snr, chi)
+    snr = second_section(freq, info, inv_sigma, [got], second, snr, chi)
     return (snr, jnp.stack(chi))
 
 

time: 207 us -> 287 us (1.39)
  the two profiles are of different devices: /device:TPU:0 before, /device:TPU:9 now
where the time goes in v6:
time: 287 us; the launch traced here: 286 us
  Pallas kernels  86.4 us (30%)
  waiting for transfers between devices  75.8 us (26%)
  blocking collectives  62.7 us (22%)
  between operations  21.2 us (7%)
  starting transfers between devices  18.5 us (6%)
  other arithmetic  14.1 us (5%)
  local copies, waits for them, and re-layouts  6.99 us (2%)
    all_gather x1, blocking collectives, per_device(): lax.all_gather(local_power, 'freq', axis=0, tiled=False).sum(axis=0)  62.7 us
    ppermute x6, waiting for transfers between devices, to_bank(): return lax.ppermute(x, 'bank', [(i, (i + k) % banks) for i in range(banks)])  42.3 us
    pallas_call x2, Pallas kernels, bins_first(): pl.pallas_call(functools.partial(bins_first_kernel, len(pieces)), grid=(B...  33.2 us
    ppermute x7, waiting for transfers between devices, swap(): return lax.ppermute(x, 'freq', [(i, i ^ k) for i in range(freq)])  32.9 us
    pallas_call x1, Pallas kernels, bins_second(): pl.pallas_call(functools.partial(bins_second_kernel, halves), grid_spec=p...  16.7 us
    pallas_call x2, Pallas kernels, first_section(): pl.pallas_call(functools.partial(first_kernel, freq), grid_spec=pltpu.Pre...  15.3 us
    pallas_call x1, Pallas kernels, second_section(): pl.pallas_call(functools.partial(second_kernel, freq, halves), grid_spec=...  10.8 us
    ppermute x6, starting transfers between devices, to_bank(): return lax.ppermute(x, 'bank', [(i, (i + k) % banks) for i in range(banks)])  7.09 us
  transfers between devices with their start and end apart: 15, of which 6 were waited for; matrix products, arithmetic and copies ran while one was open for 6% of the time, Pallas kernels for 26%

profile of v6, /device:TPU:9, one launch (start us, length us, event | category | flops | bytes accessed | tf_op | source)
XLA Modules:
  0.0 285.7 jit_solution(12286391096732145116)
XLA Ops:
  7.2 0.0 all-gather.5.cloned.1.call-start
  7.2 0.7 all-gather.5.cloned.1.call-update
  7.9 0.1 collective-permute-start
  8.0 2.5 collective-permute-start.2
  10.4 2.2 collective-permute-start.4
  14.0 0.1 copy.23
  14.1 0.1 reshape.713
  14.2 0.6 pad_add_fusion.3.which_ref
  14.8 0.6 pad_add_fusion.1.info_ref
  15.4 0.7 fusion.43
  16.1 1.0 fusion.39
  17.1 0.7 pad_maximum_fusion.4.block_ref
  17.8 0.3 fusion.24
  18.1 0.7 pad_maximum_fusion.3.inner_ref
  18.7 2.1 fusion.12
  22.0 0.0 collective-permute-done.2
  23.4 0.0 collective-permute-done.4
  26.5 2.1 dynamic-slice_bitcast_fusion
  28.6 0.0 collective-permute-start.1
  28.6 1.3 collective-permute-start.3
  29.9 1.0 collective-permute-start.5
  30.9 0.7 pad_add_fusion.2.edge_ref
  31.6 6.1 %bank_table.1 = (bf16[4096,512]{1,0:T(8,128)(2,1)}, bf16[4096,512]{1,0:T(8,128)(2,1)}) custom-call(f32[32,2,256]{2,1,0:T(2,128)} %pad_maximum_fusion.4.block_ref, f32[2,64,256]{2,1,0:T(8,128)} %pad_maximum_fusion.3.inner_ref), custom_call_target="tpu_custom_call" | custom-call | flops 1048576 | bytes 1048576 | tf_op jit(solution)/shard_map/bank_table/pallas_call | solution.py:371
  37.7 0.8 pad_maximum_fusion.1.refs_10_
  38.5 0.9 pad_maximum_fusion.2.refs_10_
  39.4 8.1 %collective-permute-done.1.refs_1_ = f32[2,64,512]{2,1,0:T(8,128)S(1)} collective-permute-done((f32[2,64,512]{2,1,0:T(8,128)S(1)}, f32[2,64,512]{2,1,0:T(8,128)S(1)}, u32[]{:S(2)}, u32[]{:S(2)}) %collective-permute-start.1) | collective-permute-done | bytes 262176 | tf_op jit(solution)/shard_map/ppermute | solution.py:595
  47.5 31.0 %collective-permute-done.3.refs_2_ = f32[2,64,512]{2,1,0:T(8,128)S(1)} collective-permute-done((f32[2,64,512]{2,1,0:T(8,128)S(1)}, f32[2,64,512]{2,1,0:T(8,128)S(1)}, u32[]{:S(2)}, u32[]{:S(2)}) %collective-permute-start.3) | collective-permute-done | bytes 262176 | tf_op jit(solution)/shard_map/ppermute | solution.py:595
  78.5 3.2 %collective-permute-done.5.refs_3_ = f32[2,64,512]{2,1,0:T(8,128)S(1)} collective-permute-done((f32[2,64,512]{2,1,0:T(8,128)S(1)}, f32[2,64,512]{2,1,0:T(8,128)S(1)}, u32[]{:S(2)}, u32[]{:S(2)}) %collective-permute-start.5) | collective-permute-done | bytes 262176 | tf_op jit(solution)/shard_map/ppermute | solution.py:595
  81.7 0.7 copy-done.9
  82.4 4.4 %entry_product.1.refs_0_ = f32[64,4096]{1,0:T(8,128)} custom-call(s32[2]{0:T(128)} %pad_add_fusion.3.which_ref, f32[2,2,64,2048]{3,2,1,0:T(8,128)} %tmpl_ref.5, f32[2,64,512]{2,1,0:T(8,128)} %get-tuple-element.50.refs_0_, f32[2,64,512]{2,1,0:T(8,128)} %copy-done.7, f32[2,64,512]{2,1,0:T(8,128)} %copy-done.8, f32[2,64,512]{2,1,0:T(8,128)} %copy-done.9), custom_call_target="tpu_custom_call" | custom-call | flops 1048576 | bytes 1048576 | tf_op jit(solution)/shard_map/entry_product/pallas_call | solution.py:252
  86.8 1.2 collective-permute-start.7
  88.0 1.2 collective-permute-start.8
  89.2 0.2 collective-permute-start.9
  89.5 2.1 fusion.10
  91.6 1.1 pad_maximum_fusion.tw_ref
  92.6 1.4 collective-permute-start.6
  94.1 7.7 %first_section.2 = (f32[8,5,2,2,64,128]{5,4,3,2,1,0:T(8,128)}, f32[8,128]{1,0:T(8,128)}) custom-call(s32[11]{0:T(128)} %pad_add_fusion.1.info_ref, f32[2,2,64,2048]{3,2,1,0:T(8,128)} %tmpl_ref.5, f32[4,3,2,64,512]{4,3,2,1,0:T(8,128)} %bitcast.41, bf16[256,256]{1,0:T(8,128)(2,1)} %constant.188.clone.wh_ref, bf16[256,256]{1,0:T(8,128)(2,1)} %constant.189.clone.wl_ref, ...), custom_call_target="tpu_custom_call" | custom-call | flops 5033164800 | bytes 16777216 | tf_op jit(solution)/shard_map/first_section/pallas_call | solution.py:189
  101.7 9.5 %collective-permute-done.7.refs_0_ = f32[64,4096]{1,0:T(8,128)S(1)} collective-permute-done((f32[64,4096]{1,0:T(8,128)}, f32[64,4096]{1,0:T(8,128)S(1)}, u32[]{:S(2)}, u32[]{:S(2)}) %collective-permute-start.7) | collective-permute-done | bytes 1048608 | tf_op jit(solution)/shard_map/ppermute | solution.py:574
  111.2 0.9 collective-permute-done.8.refs_1_
  112.1 22.5 %collective-permute-done.9.refs_2_ = f32[64,4096]{1,0:T(8,128)S(1)} collective-permute-done((f32[64,4096]{1,0:T(8,128)}, f32[64,4096]{1,0:T(8,128)S(1)}, u32[]{:S(2)}, u32[]{:S(2)}) %collective-permute-start.9) | collective-permute-done | bytes 1048608 | tf_op jit(solution)/shard_map/ppermute | solution.py:574
  134.6 1.0 copy-done.2
  135.5 2.0 collective-permute-start.10
  137.6 0.5 collective-permute-start.12
  138.1 7.7 %first_section.3 = (f32[8,5,2,2,64,128]{5,4,3,2,1,0:T(8,128)}, f32[8,128]{1,0:T(8,128)}) custom-call(s32[11]{0:T(128)} %pad_add_fusion.1.info_ref, f32[2,2,64,2048]{3,2,1,0:T(8,128)} %tmpl_ref.5, f32[4,3,2,64,512]{4,3,2,1,0:T(8,128)} %bitcast.42, bf16[256,256]{1,0:T(8,128)(2,1)} %constant.188.clone.wh_ref, ...), custom_call_target="tpu_custom_call", output_to_operand_aliasing={{0}: (7, {})} | custom-call | flops 5033164800 | bytes 16777216 | tf_op jit(solution)/shard_map/first_section/pallas_call | solution.py:189
  145.8 0.9 copy-done.3
  146.7 0.3 copy-done.4
  147.0 0.3 copy-done.5
  147.4 4.8 %all-to-all-start = ((f32[8,1280,128]{2,1,0:T(8,128)}), f32[8,1280,128]{2,1,0:T(8,128)}, u32[]{:S(2)}, u32[]{:S(2)}) async-start(f32[8,1280,128]{2,1,0:T(8,128)} %bitcast.38), calls=%async_computation | async-start | bytes 10485760 | tf_op jit(solution)/shard_map/all_to_all | solution.py:660
  152.2 0.1 copy.25
  152.2 0.2 add_reduce_fusion
  152.4 0.1 reshape.714
  152.5 0.1 reduce_sum.55
  152.6 62.7 %all-gather.2 = f32[8,2,32]{2,1,0:T(2,128)S(1)} all-gather(f32[1,2,32]{2,1,0:T(2,128)S(1)} %bitcast.40), channel_id=2, replica_groups=mesh['bank'=4,'freq'=8] {'freq'}, dimensions={0}, use_global_device_ids=true | all-gather | bytes 2304 | tf_op jit(solution)/shard_map/all_gather | solution.py:615
  215.3 0.1 fusion.49
  215.4 0.6 dynamic_slice.28
  216.0 0.7 pad_add_fusion.4.which_ref
  216.7 0.1 fusion.32
  216.8 0.1 select_reduce_fusion
  216.9 0.1 broadcast_divide_fusion
  216.9 1.3 fusion.48
  218.2 16.6 %bins_first.3 = (f32[16,2,256,256]{3,2,1,0:T(8,128)}, f32[2,256,256]{2,1,0:T(8,128)}) custom-call(s32[1]{0:T(128)} %bitcast.place_ref, s32[17]{0:T(128)} %pad_add_fusion.2.edge_ref, f32[64,4096]{1,0:T(8,128)} %entry_product.1.refs_0_, f32[64,4096]{1,0:T(8,128)} %collective-permute-done.6.refs_1_, f32[64,4096]{1,0:T(8,128)} %get-tuple-element.30.refs_2_, ...), custom_call_target="tpu_custom_call" | custom-call | flops 1048576 | bytes 1048576 | tf_op jit(solution)/shard_map/bins_first/pallas_call | solution.py:448
  234.8 16.6 %bins_first.2 = (f32[16,2,256,256]{3,2,1,0:T(8,128)}, f32[2,256,256]{2,1,0:T(8,128)}) custom-call(s32[1]{0:T(128)} %bitcast.place_ref, s32[17]{0:T(128)} %pad_add_fusion.2.edge_ref, f32[64,4096]{1,0:T(8,128)} %entry_product.1.refs_0_, f32[64,4096]{1,0:T(8,128)} %collective-permute-done.6.refs_1_, f32[64,4096]{1,0:T(8,128)} %get-tuple-element.30.refs_2_, ...), custom_call_target="tpu_custom_call" | custom-call | flops 1048576 | bytes 1048576 | tf_op jit(solution)/shard_map/bins_first/pallas_call | solution.py:448
  251.4 16.7 %bins_second.1 = (f32[256,512]{1,0:T(8,128)}, f32[2,3,2,256,512]{4,3,2,1,0:T(8,128)}) custom-call(s32[2]{0:T(128)} %pad_add_fusion.4.which_ref, f32[2]{0:T(128)} %copy-done.10, f32[16]{0:T(128)} %get-tuple-element.47.gain_ref, f32[16]{0:T(128)} %get-tuple-element.46.share_ref, f32[16,2,256,256]{3,2,1,0:T(8,128)} %get-tuple-element.37.refs_0_, ...), custom_call_target="tpu_custom_call" | custom-call | flops 1048576 | bytes 1048576 | tf_op jit(solution)/shard_map/bins_second/pallas_call | solution.py:531
  268.1 10.8 %second_section.1 = f32[2,3,2,256,512]{4,3,2,1,0:T(8,128)} custom-call(s32[11]{0:T(128)} %pad_add_fusion.1.info_ref, f32[2]{0:T(128)} %copy-done.10, f32[8,5,2,2,64,128]{5,4,3,2,1,0:T(8,128)} %bitcast.15.refs_0_, bf16[1024,256]{1,0:T(8,128)(2,1)} %constant.190.clone.refs_1_, ...), custom_call_target="tpu_custom_call", output_to_operand_aliasing={{}: (5, {})} | custom-call | flops 1048576 | bytes 1048576 | tf_op jit(solution)/shard_map/second_section/pallas_call | solution.py:325
  (37 shorter events, 0.1 us)
Async XLA Ops:
  7.2 86.9 %all-gather.5.cloned.1.call-start = ((), (), s32[]{:S(2)}) async-start(), calls=%async_computation.1 | async-start | bytes 3932160 | tf_op jit(solution)/shard_map/all_gather | solution.py:606
  7.9 13.0 %collective-permute-start = (s32[1]{0:T(128)}, s32[1]{0:T(128)}, u32[]{:S(2)}, u32[]{:S(2)}) collective-permute-start(s32[1]{0:T(128)} %param.15), channel_id=1, source_target_pairs={{0,24},{8,0},{16,8},{24,16},{1,25},{9,1},{17,9},{25,17},{2,26},{10... | collective-permute-start | bytes 20 | tf_op jit(solution)/shard_map/ppermute | solution.py:595
  8.0 14.0 %collective-permute-start.2 = (s32[1]{0:T(128)}, s32[1]{0:T(128)}, u32[]{:S(2)}, u32[]{:S(2)}) collective-permute-start(s32[1]{0:T(128)} %param.15), channel_id=1, source_target_pairs={{0,16},{8,24},{16,0},{24,8},{1,17},{9,25},{17,1},{25,9},{2,18},{10... | collective-permute-start | bytes 20 | tf_op jit(solution)/shard_map/ppermute | solution.py:595
  10.4 13.0 %collective-permute-start.4 = (s32[1]{0:T(128)}, s32[1]{0:T(128)}, u32[]{:S(2)}, u32[]{:S(2)}) collective-permute-start(s32[1]{0:T(128)} %param.15), channel_id=1, source_target_pairs={{0,8},{8,16},{16,24},{24,0},{1,9},{9,17},{17,25},{25,1},{2,10},{10... | collective-permute-start | bytes 20 | tf_op jit(solution)/shard_map/ppermute | solution.py:595
  28.6 19.0 %collective-permute-start.1 = (f32[2,64,512]{2,1,0:T(8,128)S(1)}, f32[2,64,512]{2,1,0:T(8,128)S(1)}, u32[]{:S(2)}, u32[]{:S(2)}) collective-permute-start(f32[2,64,512]{2,1,0:T(8,128)S(1)} %get-tuple-element.49), channel_id=1, source_target_pairs={{0,8},{8,16},{16,24},{24,0},{1,9},{9,17},{17,25},{25,1},{2,10},{10... | collective-permute-start | bytes 786440 | tf_op jit(solution)/shard_map/ppermute | solution.py:595
  28.6 49.9 %collective-permute-start.3 = (f32[2,64,512]{2,1,0:T(8,128)S(1)}, f32[2,64,512]{2,1,0:T(8,128)S(1)}, u32[]{:S(2)}, u32[]{:S(2)}) collective-permute-start(f32[2,64,512]{2,1,0:T(8,128)S(1)} %get-tuple-element.51), channel_id=1, source_target_pairs={{0,16},{8,24},{16,0},{24,8},{1,17},{9,25},{17,1},{25,9},{2,18},{10... | collective-permute-start | bytes 786440 | tf_op jit(solution)/shard_map/ppermute | solution.py:595
  29.9 51.8 %collective-permute-start.5 = (f32[2,64,512]{2,1,0:T(8,128)S(1)}, f32[2,64,512]{2,1,0:T(8,128)S(1)}, u32[]{:S(2)}, u32[]{:S(2)}) collective-permute-start(f32[2,64,512]{2,1,0:T(8,128)S(1)} %get-tuple-element.48), channel_id=1, source_target_pairs={{0,24},{8,0},{16,8},{24,16},{1,25},{9,1},{17,9},{25,17},{2,26},{10... | collective-permute-start | bytes 786440 | tf_op jit(solution)/shard_map/ppermute | solution.py:595
  47.5 34.2 %copy-start.7 = (f32[2,64,512]{2,1,0:T(8,128)}, f32[2,64,512]{2,1,0:T(8,128)S(1)}, u32[]{:S(2)}) copy-start(f32[2,64,512]{2,1,0:T(8,128)S(1)} %collective-permute-done.1.refs_1_) | copy-start | bytes 786436
  78.5 3.2 %copy-start.8 = (f32[2,64,512]{2,1,0:T(8,128)}, f32[2,64,512]{2,1,0:T(8,128)S(1)}, u32[]{:S(2)}) copy-start(f32[2,64,512]{2,1,0:T(8,128)S(1)} %collective-permute-done.3.refs_2_) | copy-start | bytes 786436
  81.7 0.7 copy-start.9
  86.8 24.4 %collective-permute-start.7 = (f32[64,4096]{1,0:T(8,128)}, f32[64,4096]{1,0:T(8,128)S(1)}, u32[]{:S(2)}, u32[]{:S(2)}) collective-permute-start(f32[64,4096]{1,0:T(8,128)} %entry_product.1.refs_0_), channel_id=1, source_target_pairs={{0,2},{1,3},{2,0},{3,1},{4,6},{5,7},{6,4},{7,5},{8,10},{9,11},{10,... | collective-permute-start | bytes 3145736 | tf_op jit(solution)/shard_map/ppermute | solution.py:574
  88.0 24.0 %collective-permute-start.8 = (f32[64,4096]{1,0:T(8,128)}, f32[64,4096]{1,0:T(8,128)S(1)}, u32[]{:S(2)}, u32[]{:S(2)}) collective-permute-start(f32[64,4096]{1,0:T(8,128)} %entry_product.1.refs_0_), channel_id=1, source_target_pairs={{0,4},{1,5},{2,6},{3,7},{4,0},{5,1},{6,2},{7,3},{8,12},{9,13},{10,... | collective-permute-start | bytes 3145736 | tf_op jit(solution)/shard_map/ppermute | solution.py:574
  89.2 45.3 %collective-permute-start.9 = (f32[64,4096]{1,0:T(8,128)}, f32[64,4096]{1,0:T(8,128)S(1)}, u32[]{:S(2)}, u32[]{:S(2)}) collective-permute-start(f32[64,4096]{1,0:T(8,128)} %entry_product.1.refs_0_), channel_id=1, source_target_pairs={{0,6},{1,7},{2,4},{3,5},{4,2},{5,3},{6,0},{7,1},{8,14},{9,15},{10,... | collective-permute-start | bytes 3145736 | tf_op jit(solution)/shard_map/ppermute | solution.py:574
  92.6 53.1 %collective-permute-start.6 = (f32[64,4096]{1,0:T(8,128)}, f32[64,4096]{1,0:T(8,128)}, u32[]{:S(2)}, u32[]{:S(2)}) collective-permute-start(f32[64,4096]{1,0:T(8,128)} %entry_product.1.refs_0_), channel_id=1, source_target_pairs={{0,1},{1,0},{2,3},{3,2},{4,5},{5,4},{6,7},{7,6},{8,9},{9,8},{10,11... | collective-permute-start | bytes 3145736 | tf_op jit(solution)/shard_map/ppermute | solution.py:574
  111.2 23.4 %copy-start = (f32[64,4096]{1,0:T(8,128)}, f32[64,4096]{1,0:T(8,128)S(1)}, u32[]{:S(2)}) copy-start(f32[64,4096]{1,0:T(8,128)S(1)} %collective-permute-done.7.refs_0_) | copy-start | bytes 3145732
  112.0 22.5 %copy-start.1 = (f32[64,4096]{1,0:T(8,128)}, f32[64,4096]{1,0:T(8,128)S(1)}, u32[]{:S(2)}) copy-start(f32[64,4096]{1,0:T(8,128)S(1)} %collective-permute-done.8.refs_1_) | copy-start | bytes 3145732
  134.6 1.0 copy-start.2
  135.5 10.2 %collective-permute-start.10 = (f32[64,4096]{1,0:T(8,128)}, f32[64,4096]{1,0:T(8,128)S(1)}, u32[]{:S(2)}, u32[]{:S(2)}) collective-permute-start(f32[64,4096]{1,0:T(8,128)} %get-tuple-element.30.refs_2_), channel_id=1, source_target_pairs={{0,1},{1,0},{2,3},{3,2},{4,5},{5,4},{6,7},{7,6},{8,9},{9,8},{10,11... | collective-permute-start | bytes 3145736 | tf_op jit(solution)/shard_map/ppermute | solution.py:574
  137.6 8.2 %collective-permute-start.11 = (f32[64,4096]{1,0:T(8,128)}, f32[64,4096]{1,0:T(8,128)S(1)}, u32[]{:S(2)}, u32[]{:S(2)}) collective-permute-start(f32[64,4096]{1,0:T(8,128)} %get-tuple-element.31.refs_4_), channel_id=1, source_target_pairs={{0,1},{1,0},{2,3},{3,2},{4,5},{5,4},{6,7},{7,6},{8,9},{9,8},{10,11... | collective-permute-start | bytes 3145736 | tf_op jit(solution)/shard_map/ppermute | solution.py:574
  137.6 8.2 %collective-permute-start.12 = (f32[64,4096]{1,0:T(8,128)}, f32[64,4096]{1,0:T(8,128)S(1)}, u32[]{:S(2)}, u32[]{:S(2)}) collective-permute-start(f32[64,4096]{1,0:T(8,128)} %get-tuple-element.32.refs_6_), channel_id=1, source_target_pairs={{0,1},{1,0},{2,3},{3,2},{4,5},{5,4},{6,7},{7,6},{8,9},{9,8},{10,11... | collective-permute-start | bytes 3145736 | tf_op jit(solution)/shard_map/ppermute | solution.py:574
  145.7 1.0 copy-start.3
  145.8 1.3 copy-start.4
  145.8 1.6 copy-start.5
  147.4 4.8 %copy-start.11 = (s32[2,15]{1,0:T(2,128)S(1)}, s32[2,15]{1,0:T(2,128)}, u32[]{:S(2)}) copy-start(s32[2,15]{1,0:T(2,128)} %param.16) | copy-start | bytes 364
  147.4 4.9 %copy-start.6 = (f32[2,2,64,2048]{3,2,1,0:T(8,128)S(1)}, f32[2,2,64,2048]{3,2,1,0:T(8,128)}, u32[]{:S(2)}) copy-start(f32[2,2,64,2048]{3,2,1,0:T(8,128)} %tmpl_ref.5) | copy-start | bytes 6291460
  147.4 120.7 %all-to-all-start = ((f32[8,1280,128]{2,1,0:T(8,128)}), f32[8,1280,128]{2,1,0:T(8,128)}, u32[]{:S(2)}, u32[]{:S(2)}) async-start(f32[8,1280,128]{2,1,0:T(8,128)} %bitcast.38), calls=%async_computation | async-start | bytes 10485760 | tf_op jit(solution)/shard_map/all_to_all | solution.py:660
  215.4 19.4 %copy-start.10 = (f32[2]{0:T(128)}, f32[2]{0:T(128)S(1)}, u32[]{:S(2)}) copy-start(f32[2]{0:T(128)S(1)} %rsqrt.6.scale_ref) | copy-start | bytes 28
Sparse Core Ops, SparseCore 0:
  9.6 83.2 all-gather.4

commit v7 on v6

--- a/solution.py
+++ b/solution.py
@@ -180,10 +180,10 @@
 
 def first_section(freq, half, info, templates, strain, first, stage, twist, earlier):
     tmpls = templates.shape[0]
-    pieces, dets, _, cols, piece_len = strain.shape
+    pieces, dets, _, rows, piece_len = strain.shape
+    cols = templates.shape[2]
     series = tmpls * dets - 1
     groups = COARSE // freq
-    rows = cols // HALVES
     table = pl.BlockSpec((2 * LANES, 2 * LANES), lambda i, n: (0, 0))
     out = (freq, series, 2, groups, cols, LANES)
     return pl.pallas_call(
@@ -196,7 +196,7 @@
                     (1, 2, rows, N1), lambda i, n: (n[1 + 2 * i], 0, half, 0)
                 ),
                 pl.BlockSpec(
-                    (pieces, 1, 2, rows, piece_len), lambda i, n: (0, n[2 + 2 * i], 0, half, 0)
+                    (pieces, 1, 2, rows, piece_len), lambda i, n: (0, n[2 + 2 * i], 0, 0, 0)
                 ),
                 table,
                 table,
@@ -229,40 +229,43 @@
     )(info, templates, strain, first[0], first[1], stage, twist, *earlier)
 
 
-def entry_kernel(which_ref, tmpl_ref, *refs):
-    quarter_refs, out_ref = refs[:-1], refs[-1]
-    banks = len(quarter_refs)
+def entry_kernel(steps, banks, which_ref, tmpl_ref, strain_ref, *refs):
+    out_ref = refs[-1]
     length = N1 // banks
     first_half = lax.broadcasted_iota(jnp.int32, (ROWS, LANES), 1) < BLOCK
-    for k, ref in enumerate(quarter_refs):
-        start = lax.rem(which_ref[1] - k + banks, banks) * length
+    for n, k in enumerate(steps):
+        part = lax.rem(which_ref[2] + k, banks)
         for u in range(length // LANES):
-            lane = pl.ds(pl.multiple_of(start + u * LANES, LANES), LANES)
+            lane = pl.ds(pl.multiple_of(part * length + u * LANES, LANES), LANES)
             hr, hi = tmpl_ref[0, 0, :, lane], tmpl_ref[0, 1, :, lane]
-            sr, si = ref[0, :, tile(u)], ref[1, :, tile(u)]
+            piece = 0 if strain_ref.shape[0] == 1 else part
+            sr, si = strain_ref[piece, 0, 0, :, tile(u)], strain_ref[piece, 0, 1, :, tile(u)]
             re, im = hr * sr + hi * si, hr * si - hi * sr
-            to = pl.multiple_of(2 * start + 2 * u * LANES, 2 * LANES)
-            out_ref[:, pl.ds(to, LANES)] = jnp.where(first_half, re, pltpu.roll(im, BLOCK, 1))
-            to = pl.multiple_of(to + LANES, LANES)
-            out_ref[:, pl.ds(to, LANES)] = jnp.where(first_half, pltpu.roll(re, BLOCK, 1), im)
-
-
-def entry_product(which, templates, quarters):
-    _, cols, length = quarters[0].shape
+            to = 2 * (n * length // LANES + u)
+            out_ref[:, tile(to)] = jnp.where(first_half, re, pltpu.roll(im, BLOCK, 1))
+            out_ref[:, tile(to + 1)] = jnp.where(first_half, pltpu.roll(re, BLOCK, 1), im)
+
+
+def entry_product(steps, banks, half, which, templates, strain, after):
+    pieces, _, _, cols, length = strain.shape
+    first = half * cols // ROWS
     return pl.pallas_call(
-        entry_kernel,
+        functools.partial(entry_kernel, steps, banks),
         grid_spec=pltpu.PrefetchScalarGridSpec(
             num_scalar_prefetch=1,
             grid=(cols // ROWS,),
-            in_specs=[pl.BlockSpec((1, 2, ROWS, N1), lambda c, w: (w[0], 0, c, 0))]
-            + [pl.BlockSpec((2, ROWS, length), lambda c, w: (0, c, 0))] * len(quarters),
-            out_specs=pl.BlockSpec((ROWS, 2 * N1), lambda c, w: (c, 0)),
+            in_specs=[
+                pl.BlockSpec((1, 2, ROWS, N1), lambda c, w: (w[0], 0, first + c, 0)),
+                pl.BlockSpec((pieces, 1, 2, ROWS, length), lambda c, w: (0, w[1], 0, c, 0)),
+            ]
+            + [ANY] * len(after),
+            out_specs=pl.BlockSpec((ROWS, 2 * length * len(steps)), lambda c, w: (c, 0)),
         ),
-        out_shape=jax.ShapeDtypeStruct((cols, 2 * N1), F32),
+        out_shape=jax.ShapeDtypeStruct((cols, 2 * length * len(steps)), F32),
         compiler_params=pltpu.CompilerParams(vmem_limit_bytes=VMEM_LIMIT),
         cost_estimate=COST,
         name="entry_product",
-    )(which, templates, *quarters)
+    )(which, templates, strain, *after)
 
 
 def second_points(x, w2h_ref, w2l_ref, use):
@@ -383,25 +386,32 @@
     )(block, inner)
 
 
-def bins_first_kernel(pieces, place_ref, edge_ref, *refs):
-    piece_refs = refs[:pieces]
-    wh_ref, wl_ref, tw_ref = refs[pieces : pieces + 3]
+def bins_first_kernel(pieces, banks, place_ref, edge_ref, *refs):
+    own_refs, rest_refs = refs[:pieces], refs[pieces : 2 * pieces]
+    wh_ref, wl_ref, tw_ref = refs[2 * pieces : 2 * pieces + 3]
     level_ref, total_ref, xh, xl, acc = refs[-5:]
     times = total_ref.shape[-1]
-    cols = piece_refs[0].shape[0]
+    cols = own_refs[0].shape[0]
+    length = 2 * N1 // banks
+    chunk = FOUR * LANES
     step = pl.program_id(0)
 
     @pl.when(step == 0)
     def _():
-        for k, ref in enumerate(piece_refs):
-            row = pl.multiple_of((place_ref[0] ^ k) * cols, cols)
-
-            def cut(i, carry):
-                at = pl.ds(pl.multiple_of(i * FOUR * LANES, FOUR * LANES), FOUR * LANES)
-                xh[pl.ds(row, cols), at], xl[pl.ds(row, cols), at] = split(ref[:, at])
-                return carry
-
-            lax.fori_loop(0, 2 * N1 // (FOUR * LANES), cut, 0)
+        for k in range(pieces):
+            row = pl.ds(pl.multiple_of((place_ref[0] ^ k) * cols, cols), cols)
+            for n in range(banks):
+                ref = rest_refs[k] if n else own_refs[k]
+                start = lax.rem(place_ref[1] + n, banks) * length
+
+                def cut(i, carry):
+                    lane = max(n - 1, 0) * length + i * chunk
+                    x = ref[:, pl.ds(pl.multiple_of(lane, chunk), chunk)]
+                    to = pl.ds(pl.multiple_of(start + i * chunk, chunk), chunk)
+                    xh[row, to], xl[row, to] = split(x)
+                    return carry
+
+                lax.fori_loop(0, length // chunk, cut, 0)
         total_ref[...] = jnp.zeros_like(total_ref)
 
     def blocks_at(block, blocks):
@@ -440,16 +450,17 @@
         total_ref[1, at, :] = sum_i
 
 
-def bins_first(half, place, edges, pieces, table, twist, after):
-    cols = pieces[0].shape[0] // HALVES
+def bins_first(half, banks, place, edges, own, rest, table, twist, after):
+    cols, length = rest[0].shape
     rows, times = twist.shape[1:]
     smem = pl.BlockSpec(memory_space=pltpu.SMEM)
     fixed = lambda shape: pl.BlockSpec(shape, lambda i: (0,) * len(shape))
     return pl.pallas_call(
-        functools.partial(bins_first_kernel, len(pieces)),
+        functools.partial(bins_first_kernel, len(own), banks),
         grid=(BINS // TOGETHER,),
         in_specs=[smem, smem]
-        + [pl.BlockSpec((cols, 2 * N1), lambda i: (half, 0))] * len(pieces)
+        + [pl.BlockSpec((cols, 2 * N1 - length), lambda i: (half, 0))] * len(own)
+        + [fixed((cols, length))] * len(rest)
         + [fixed((2 * N1, 2 * times))] * 2
         + [fixed((2, rows, times))]
         + [ANY] * len(after),
@@ -469,7 +480,7 @@
         compiler_params=pltpu.CompilerParams(vmem_limit_bytes=VMEM_LIMIT),
         cost_estimate=COST,
         name="bins_first",
-    )(place, edges, *pieces, *table, twist, *after)
+    )(place, edges, *own, *rest, *table, twist, *after)
 
 
 def bins_second_kernel(halves, which_ref, scale_ref, gain_ref, share_ref, *refs):
@@ -591,20 +602,10 @@
     times = N1 // freq
     part = cols // HALVES
 
-    def to_bank(x, k):
-        return lax.ppermute(x, "bank", [(i, (i + k) % banks) for i in range(banks)])
-
-    asked = [coinc_det] + [to_bank(coinc_det, -k) for k in range(1, banks)]
-    quarters = []
-    for j in range(slots):
-        own = lax.dynamic_index_in_dim(strain, coinc_det[j], 0, keepdims=False)
-        one = [own]
-        for k in range(1, banks):
-            picked = lax.dynamic_index_in_dim(strain, asked[k][j], 0, keepdims=False)
-            one.append(to_bank(picked, k))
-        quarters.append(one)
-    strains = lax.all_gather(strain, "bank", axis=0, tiled=False)
-
+    strains = [
+        lax.all_gather(strain[:, :, h * part : (h + 1) * part], "bank", axis=0, tiled=False)
+        for h in range(HALVES)
+    ]
     first = tuple(jnp.asarray(t) for t in first_table())
     second = tuple(jnp.asarray(t) for t in second_table(cols, 1))
     second_halves = tuple(jnp.asarray(t) for t in second_table(cols, HALVES))
@@ -612,7 +613,7 @@
 
     power = (templates[:, 0] ** 2 + templates[:, 1] ** 2).sum(axis=1)
     local_power = power.reshape(tmpls, NBLK, BLOCK).sum(axis=2)
-    block_power = lax.all_gather(local_power, "freq", axis=0, tiled=False).sum(axis=0)
+    block_power = lax.psum(local_power, "freq")
     sigma_sq = block_power.sum(axis=1)
     inv_sigma = lax.rsqrt(sigma_sq)
     bin_of = jnp.sum(
@@ -633,7 +634,7 @@
         rows = rows // part * cols + h * part + rows % part
         own_twist.append(jnp.stack(phase(rows[:, None] * own_time[None, :], N1 * N2)))
 
-    which = [jnp.stack([coinc_tmpl[j], coinc_det[j]]) for j in range(slots)]
+    which = [jnp.stack([coinc_tmpl[j], coinc_det[j], bank]) for j in range(slots)]
     series = jnp.arange(tmpls * dets - 1, dtype=jnp.int32)
     series = series + (series >= which[0][0] * dets + which[0][1])
     info = jnp.stack([series // dets, series % dets], axis=1).reshape(-1)
@@ -642,31 +643,40 @@
     edges = [
         jnp.concatenate([ends[0], bin_edges[coinc_tmpl[j]], ends[1]]) for j in range(slots)
     ]
-    info, edges, table, twist, own_twist = lax.optimization_barrier(
-        (info, edges, table, twist, own_twist)
+    here = jnp.stack([place, bank])
+
+    own = [entry_product((0,), banks, 0, w, templates, strain[None], []) for w in which]
+    own = [near_pieces(far_pieces(x, freq), freq) for x in own]
+    gathered = [x for entry in own for x in entry[1:]]
+    which, inv_sigma, weights, twist, info = lax.optimization_barrier(
+        (which, inv_sigma, weights, twist, info)
     )
 
-    here = place.reshape(1)
-    own = [
-        entry_product(jnp.stack([coinc_tmpl[j], bank]), templates, quarters[j])
-        for j in range(slots)
-    ]
-    far = [far_pieces(x, freq) for x in own]
-    sent, token = first_section(freq, 0, info, templates, strains, first, stage, twist, [])
-    far = [x[:1] + list(handed_on(x[1:], [token])) for x in far]
-    pieces = [near_pieces(x, freq) for x in far]
-    sent, _ = first_section(freq, 1, info, templates, strains, first, stage, twist, [sent])
-    (ready,) = handed_on([sent], [x for entry in pieces for x in entry[1:]])
+    rest, sent = [], []
+    later = tuple(range(1, banks))
+    for h in range(HALVES):
+        after = gathered if h == 0 else gathered + [table[0], *own_twist]
+        half = [entry_product(later, banks, h, w, templates, strains[h], after) for w in which]
+        far = [far_pieces(x, freq) for x in half]
+        *sent, token = first_section(
+            freq, h, info, templates, strains[h], first, stage, twist, sent
+        )
+        far = [x[:1] + list(handed_on(x[1:], [token])) for x in far]
+        rest.append([near_pieces(x, freq) for x in far])
+        gathered = [x for entry in rest[-1] for x in entry[1:]]
+    (ready,) = handed_on(sent, gathered)
     got = lax.all_to_all(
         ready.reshape(freq, -1, LANES), "freq", split_axis=0, concat_axis=0, tiled=True
     )
-    got = got.reshape(sent.shape)
+    got = got.reshape(ready.shape)
 
     chi, snr = [], None
     for j in range(slots):
         t = coinc_tmpl[j]
         halves = [
-            bins_first(h, here, edges[j], pieces[j], table, own_twist[h], [ready])
+            bins_first(
+                h, banks, here, edges[j], own[j], rest[h][j], table, own_twist[h], [ready]
+            )
             for h in range(HALVES)
         ]
         levels, totals = zip(*halves)

time: 287 us -> 200 us (0.70)
  the two profiles are of different devices: /device:TPU:9 before, /device:TPU:0 now
where the time goes in v7:
time: 200 us; the launch traced here: 199 us
  Pallas kernels  91.9 us (46%)
  waiting for transfers between devices  34.1 us (17%)
  blocking collectives  19.4 us (10%)
  starting transfers between devices  18 us (9%)
  between operations  15.7 us (8%)
  other arithmetic  13.3 us (7%)
  local copies, waits for them, and re-layouts  6.84 us (3%)
    pallas_call x2, Pallas kernels, bins_first(): pl.pallas_call(functools.partial(bins_first_kernel, len(own), banks), gri...  33.4 us
    ppermute x21, waiting for transfers between devices, swap(): return lax.ppermute(x, 'freq', [(i, i ^ k) for i in range(freq)])  20.8 us
    psum x1, blocking collectives, per_device(): block_power = lax.psum(local_power, 'freq')  19.4 us
    pallas_call x1, Pallas kernels, bins_second(): pl.pallas_call(functools.partial(bins_second_kernel, halves), grid_spec=p...  16.7 us
    pallas_call x2, Pallas kernels, first_section(): pl.pallas_call(functools.partial(first_kernel, freq), grid_spec=pltpu.Pre...  15.6 us
    ppermute x21, starting transfers between devices, swap(): return lax.ppermute(x, 'freq', [(i, i ^ k) for i in range(freq)])  13.1 us
    pallas_call x1, Pallas kernels, second_section(): pl.pallas_call(functools.partial(second_kernel, freq, halves), grid_spec=...  10.8 us
    pallas_call x3, Pallas kernels, entry_product(): pl.pallas_call(functools.partial(entry_kernel, steps, banks), grid_spec=p...  9.43 us
  transfers between devices with their start and end apart: 24, of which 10 were waited for; matrix products, arithmetic and copies ran while one was open for 7% of the time, Pallas kernels for 39%

profile of v7, /device:TPU:0, one launch (start us, length us, event | category | flops | bytes accessed | tf_op | source)
XLA Modules:
  0.0 199.3 jit_solution(11880338503105642484)
XLA Ops:
  7.2 2.2 %fusion.48 = (f32[3,2,32,512]{3,2,1,0:T(8,128)}, f32[3,2,32,512]{3,2,1,0:T(8,128)}) fusion(f32[3,2,64,512]{3,2,1,0:T(8,128)} %param.12), kind=kLoop, calls=%fused_computation.103 | loop fusion | bytes 1572864 | tf_op jit(solution)/shard_map/slice | solution.py:606
  10.8 0.7 pad_add_fusion.1.which_ref
  11.5 4.0 %entry_product.3.refs_0_ = f32[64,1024]{1,0:T(8,128)} custom-call(s32[3]{0:T(128)} %pad_add_fusion.1.which_ref, f32[2,2,64,2048]{3,2,1,0:T(8,128)} %tmpl_ref.9, f32[1,3,2,64,512]{4,3,2,1,0:T(8,128)} %bitcast.25), custom_call_target="tpu_custom_call" | custom-call | flops 1048576 | bytes 1048576 | tf_op jit(solution)/shard_map/entry_product/pallas_call | solution.py:252
  15.5 2.9 %collective-permute-start.1 = (f32[64,1024]{1,0:T(8,128)}, f32[64,1024]{1,0:T(8,128)S(1)}, u32[]{:S(2)}, u32[]{:S(2)}) collective-permute-start(f32[64,1024]{1,0:T(8,128)} %entry_product.3.refs_0_), channel_id=1, source_target_pairs={{0,2},{1,3},{2,0},{3,1},{4,6},{5,7},{6,4},{7,5},{8,10},{9,11},{10,... | collective-permute-start | bytes 786440 | tf_op jit(solution)/shard_map/ppermute | solution.py:585
  18.5 1.5 collective-permute-start.3
  20.0 0.2 add_reduce_fusion
  20.3 0.3 fusion.24
  20.6 0.1 reshape.711
  20.8 19.4 %psum.7 = f32[2,32]{1,0:T(2,128)S(1)} all-reduce(f32[2,32]{1,0:T(2,128)S(1)} %reduce_sum.46), channel_id=1, replica_groups=mesh['bank'=4,'freq'=8] {'freq'}, use_global_device_ids=true, to_apply=%region_2.0 | all-reduce | flops 64 | bytes 512 | tf_op jit(solution)/shard_map/psum | solution.py:616
  40.2 0.1 reduce_sum.47
  40.3 0.1 copy.26
  40.4 0.1 fusion.32
  40.6 1.0 fusion.39
  41.6 2.1 %fusion.10 = (f32[1,64,2048]{2,1,0:T(8,128)S(1)}, f32[1,64,2048]{2,1,0:T(8,128)S(1)}) fusion(s32[2048]{0:T(1024)S(1)} %fusion.35, s32[64]{0:T(128)S(1)} %iota_add_fusion.1), kind=kLoop, calls=%fused_computation.29 | loop fusion | flops 1835008 | bytes 1057024 | tf_op jit(solution)/shard_map/cos | solution.py:64
  43.8 0.1 copy.27
  43.9 1.0 pad_maximum_fusion.tw_ref
  45.0 0.5 collective-permute-start.4
  45.6 0.6 pad_add_fusion.2.info_ref
  46.2 0.7 pad_maximum_fusion.4.block_ref
  46.9 0.7 pad_maximum_fusion.3.inner_ref
  47.6 2.4 %all-gather.7.cloned.1.call-done = f32[12,2,32,512]{3,2,1,0:T(8,128)} async-done(((f32[3,2,32,512]{3,2,1,0:T(8,128)}), f32[12,2,32,512]{3,2,1,0:T(8,128)}) %all-gather.7.cloned.1.call-update) | async-done | bytes 1572880 | tf_op jit(solution)/shard_map/all_gather | solution.py:606
  50.0 2.7 %entry_product.4.refs_8_ = f32[32,3072]{1,0:T(8,128)} custom-call(s32[3]{0:T(128)} %pad_add_fusion.1.which_ref, f32[2,2,64,2048]{3,2,1,0:T(8,128)} %tmpl_ref.9, f32[4,3,2,32,512]{4,3,2,1,0:T(8,128)} %bitcast.28, f32[64,1024]{1,0:T(8,128)} %copy-done.10, f32[64,1024]{1,0:T(8,128)} %copy-done.7, f32[64,1024]{1,0:T(8,128)} %copy-done.11, f32[64,1024]{1,0:T(8,128)} %copy-done.8, ...), custom_call_target="tpu_custom_call" | custom-call | flops 1048576 | bytes 1048576 | tf_op jit(solution)/shard_map/entry_product/pallas_call | solution.py:252
  52.7 2.4 %collective-permute-start.10 = (f32[32,3072]{1,0:T(8,128)}, f32[32,3072]{1,0:T(8,128)S(1)}, u32[]{:S(2)}, u32[]{:S(2)}) collective-permute-start(f32[32,3072]{1,0:T(8,128)} %entry_product.4.refs_8_), channel_id=1, source_target_pairs={{0,6},{1,7},{2,4},{3,5},{4,2},{5,3},{6,0},{7,1},{8,14},{9,15},{10,... | collective-permute-start | bytes 1179656 | tf_op jit(solution)/shard_map/ppermute | solution.py:585
  55.1 0.5 collective-permute-start.8
  55.7 0.6 collective-permute-start.9
  56.2 7.8 %first_section.2 = (f32[8,5,2,2,64,128]{5,4,3,2,1,0:T(8,128)}, f32[8,128]{1,0:T(8,128)}) custom-call(s32[11]{0:T(128)} %pad_add_fusion.2.info_ref, f32[2,2,64,2048]{3,2,1,0:T(8,128)} %tmpl_ref.9, f32[4,3,2,32,512]{4,3,2,1,0:T(8,128)} %bitcast.29, bf16[256,256]{1,0:T(8,128)(2,1)} %constant.178.clone.wh_ref, bf16[256,256]{1,0:T(8,128)(2,1)} %constant.179.clone.wl_ref, ...), custom_call_target="tpu_custom_call" | custom-call | flops 5033164800 | bytes 16777216 | tf_op jit(solution)/shard_map/first_section/pallas_call | solution.py:189
  64.0 1.9 collective-permute-done.10.refs_2_
  65.9 7.2 %collective-permute-done.8.refs_0_ = f32[32,3072]{1,0:T(8,128)S(1)} collective-permute-done((f32[32,3072]{1,0:T(8,128)}, f32[32,3072]{1,0:T(8,128)S(1)}, u32[]{:S(2)}, u32[]{:S(2)}) %collective-permute-start.8) | collective-permute-done | bytes 393248 | tf_op jit(solution)/shard_map/ppermute | solution.py:585
  73.1 0.7 copy-done.5
  73.8 0.2 copy-done.6
  74.0 0.5 collective-permute-start.12
  74.5 6.0 %bank_table.1 = (bf16[4096,512]{1,0:T(8,128)(2,1)}, bf16[4096,512]{1,0:T(8,128)(2,1)}) custom-call(f32[32,2,256]{2,1,0:T(2,128)} %pad_maximum_fusion.4.block_ref, f32[2,64,256]{2,1,0:T(8,128)} %pad_maximum_fusion.3.inner_ref), custom_call_target="tpu_custom_call" | custom-call | flops 1048576 | bytes 1048576 | tf_op jit(solution)/shard_map/bank_table/pallas_call | solution.py:374
  80.5 2.1 %fusion.12 = (f32[1,256,256]{2,1,0:T(8,128)S(1)}, f32[1,256,256]{2,1,0:T(8,128)S(1)}, f32[1,256,256]{2,1,0:T(8,128)S(1)}, f32[1,256,256]{2,1,0:T(8,128)S(1)}) fusion(s32[256]{0:T(256)S(1)} %iota_add_fusion, s32[256]{0:T(256)S(1)} %add_add_fusion, s32[256]{0:T(256)S(1)} %fusion.45), kind=kLoop, calls=%fused_computation.32 | loop fusion | flops 1835008 | bytes 1051648 | tf_op jit(solution)/shard_map/cos | solution.py:64
  82.6 1.1 pad_maximum_fusion.1
  83.7 3.8 %all-gather.5.cloned.1.call-done = f32[12,2,32,512]{3,2,1,0:T(8,128)} async-done(((f32[3,2,32,512]{3,2,1,0:T(8,128)}), f32[12,2,32,512]{3,2,1,0:T(8,128)}) %all-gather.5.cloned.1.call-update) | async-done | bytes 1572880 | tf_op jit(solution)/shard_map/all_gather | solution.py:606
  87.6 0.7 copy-done.14
  88.3 0.1 copy-done.15
  88.4 0.2 copy-done.16
  88.6 0.1 copy-done.17
  88.7 2.7 %entry_product.5.refs_8_ = f32[32,3072]{1,0:T(8,128)} custom-call(s32[3]{0:T(128)} %pad_add_fusion.1.which_ref, f32[2,2,64,2048]{3,2,1,0:T(8,128)} %tmpl_ref.9, f32[4,3,2,32,512]{4,3,2,1,0:T(8,128)} %bitcast.26, f32[32,3072]{1,0:T(8,128)} %copy-done.14, f32[32,3072]{1,0:T(8,128)} %get-tuple-element.32.refs_1_.refs_10_, f32[32,3072]{1,0:T(8,128)} %copy-done.15, ...), custom_call_target="tpu_custom_call" | custom-call | flops 1048576 | bytes 1048576 | tf_op jit(solution)/shard_map/entry_product/pallas_call | solution.py:252
  91.4 1.5 collective-permute-start.15
  92.9 1.5 collective-permute-start.16
  94.3 0.5 collective-permute-start.17
  94.9 7.8 %first_section.3 = (f32[8,5,2,2,64,128]{5,4,3,2,1,0:T(8,128)}, f32[8,128]{1,0:T(8,128)}) custom-call(s32[11]{0:T(128)} %pad_add_fusion.2.info_ref, f32[2,2,64,2048]{3,2,1,0:T(8,128)} %tmpl_ref.9, f32[4,3,2,32,512]{4,3,2,1,0:T(8,128)} %bitcast.27, bf16[256,256]{1,0:T(8,128)(2,1)} %constant.178.clone.wh_ref, ...), custom_call_target="tpu_custom_call", output_to_operand_aliasing={{0}: (7, {})} | custom-call | flops 5033164800 | bytes 16777216 | tf_op jit(solution)/shard_map/first_section/pallas_call | solution.py:189
  102.8 0.8 collective-permute-done.15.refs_0_
  103.6 8.3 %collective-permute-done.16.refs_1_ = f32[32,3072]{1,0:T(8,128)S(1)} collective-permute-done((f32[32,3072]{1,0:T(8,128)}, f32[32,3072]{1,0:T(8,128)S(1)}, u32[]{:S(2)}, u32[]{:S(2)}) %collective-permute-start.16) | collective-permute-done | bytes 393248 | tf_op jit(solution)/shard_map/ppermute | solution.py:585
  112.0 0.7 copy-done.2
  112.7 0.1 copy-done.4
  112.9 0.5 collective-permute-start.19
  113.4 1.4 collective-permute-done.18.refs_3_.refs_11_
  114.8 0.6 collective-permute-done.19.refs_5_.refs_13_
  115.4 0.6 collective-permute-done.20.refs_7_.refs_15_
  115.9 0.2 copy-done.21
  116.1 0.5 copy-done.22
  116.7 4.8 %all-to-all-start = ((f32[8,1280,128]{2,1,0:T(8,128)}), f32[8,1280,128]{2,1,0:T(8,128)}, u32[]{:S(2)}, u32[]{:S(2)}) async-start(f32[8,1280,128]{2,1,0:T(8,128)} %bitcast.24), calls=%async_computation | async-start | bytes 10485760 | tf_op jit(solution)/shard_map/all_to_all | solution.py:668
  121.5 0.6 dynamic_slice.10
  122.1 0.6 pad_add_fusion.3.place_ref
  122.7 0.7 pad_add_fusion.4.edge_ref
  123.4 1.2 bitcast_multiply_fusion
  124.6 16.7 %bins_first.3 = (f32[16,2,256,256]{3,2,1,0:T(8,128)}, f32[2,256,256]{2,1,0:T(8,128)}) custom-call(s32[2]{0:T(128)} %pad_add_fusion.3.place_ref, s32[17]{0:T(128)} %pad_add_fusion.4.edge_ref, f32[64,1024]{1,0:T(8,128)} %entry_product.3.refs_0_, f32[64,1024]{1,0:T(8,128)} %copy-done.10, f32[64,1024]{1,0:T(8,128)} %copy-done.7, f32[64,1024]{1,0:T(8,128)} %copy-done.11, ...), custom_call_target="tpu_custom_call" | custom-call | flops 1048576 | bytes 1048576 | tf_op jit(solution)/shard_map/bins_first/pallas_call | solution.py:458
  141.3 16.6 %bins_first.2 = (f32[16,2,256,256]{3,2,1,0:T(8,128)}, f32[2,256,256]{2,1,0:T(8,128)}) custom-call(s32[2]{0:T(128)} %pad_add_fusion.3.place_ref, s32[17]{0:T(128)} %pad_add_fusion.4.edge_ref, f32[64,1024]{1,0:T(8,128)} %entry_product.3.refs_0_, f32[64,1024]{1,0:T(8,128)} %copy-done.10, f32[64,1024]{1,0:T(8,128)} %copy-done.7, f32[64,1024]{1,0:T(8,128)} %copy-done.11, ...), custom_call_target="tpu_custom_call" | custom-call | flops 1048576 | bytes 1048576 | tf_op jit(solution)/shard_map/bins_first/pallas_call | solution.py:458
  157.9 16.7 %bins_second.1 = (f32[256,512]{1,0:T(8,128)}, f32[2,3,2,256,512]{4,3,2,1,0:T(8,128)}) custom-call(s32[3]{0:T(128)} %pad_add_fusion.1.which_ref, f32[2]{0:T(128)} %copy-done.23, f32[16]{0:T(128)} %get-tuple-element.49.gain_ref, f32[16]{0:T(128)} %get-tuple-element.48.share_ref, f32[16,2,256,256]{3,2,1,0:T(8,128)} %get-tuple-element.42.refs_0_, ...), custom_call_target="tpu_custom_call" | custom-call | flops 1048576 | bytes 1048576 | tf_op jit(solution)/shard_map/bins_second/pallas_call | solution.py:542
  174.6 7.1 %all-to-all-done = f32[8,1280,128]{2,1,0:T(8,128)} async-done(((f32[8,1280,128]{2,1,0:T(8,128)}), f32[8,1280,128]{2,1,0:T(8,128)}, u32[]{:S(2)}, u32[]{:S(2)}) %all-to-all-start) | async-done | bytes 5242912 | tf_op jit(solution)/shard_map/all_to_all | solution.py:668
  181.7 10.8 %second_section.1 = f32[2,3,2,256,512]{4,3,2,1,0:T(8,128)} custom-call(s32[11]{0:T(128)} %pad_add_fusion.2.info_ref, f32[2]{0:T(128)} %copy-done.23, f32[8,5,2,2,64,128]{5,4,3,2,1,0:T(8,128)} %bitcast.8.refs_0_, bf16[1024,256]{1,0:T(8,128)(2,1)} %constant.180.clone.refs_1_, ...), custom_call_target="tpu_custom_call", output_to_operand_aliasing={{}: (5, {})} | custom-call | flops 1048576 | bytes 1048576 | tf_op jit(solution)/shard_map/second_section/pallas_call | solution.py:328
  (85 shorter events, 0.8 us)
Async XLA Ops:
  7.2 12.9 %copy-start = (f32[2,2,64,2048]{3,2,1,0:T(8,128)S(1)}, f32[2,2,64,2048]{3,2,1,0:T(8,128)}, u32[]{:S(2)}) copy-start(f32[2,2,64,2048]{3,2,1,0:T(8,128)} %tmpl_ref.9) | copy-start | bytes 6291460
  7.2 33.1 %copy-start.24 = (s32[2,15]{1,0:T(2,128)S(1)}, s32[2,15]{1,0:T(2,128)}, u32[]{:S(2)}) copy-start(s32[2,15]{1,0:T(2,128)} %param.16) | copy-start | bytes 364
  7.2 42.8 %all-gather.7.cloned.1.call-start = ((), (), s32[]{:S(2)}) async-start(), calls=%async_computation.2 | async-start | bytes 1966080 | tf_op jit(solution)/shard_map/all_gather | solution.py:606
  9.5 78.1 %all-gather.5.cloned.1.call-start = ((), (), s32[]{:S(2)}) async-start(), calls=%async_computation.1 | async-start | bytes 1966080 | tf_op jit(solution)/shard_map/all_gather | solution.py:606
  15.5 29.4 %collective-permute-start.1 = (f32[64,1024]{1,0:T(8,128)}, f32[64,1024]{1,0:T(8,128)S(1)}, u32[]{:S(2)}, u32[]{:S(2)}) collective-permute-start(f32[64,1024]{1,0:T(8,128)} %entry_product.3.refs_0_), channel_id=1, source_target_pairs={{0,2},{1,3},{2,0},{3,1},{4,6},{5,7},{6,4},{7,5},{8,10},{9,11},{10,... | collective-permute-start | bytes 786440 | tf_op jit(solution)/shard_map/ppermute | solution.py:585
  18.5 26.5 %collective-permute-start.3 = (f32[64,1024]{1,0:T(8,128)}, f32[64,1024]{1,0:T(8,128)S(1)}, u32[]{:S(2)}, u32[]{:S(2)}) collective-permute-start(f32[64,1024]{1,0:T(8,128)} %entry_product.3.refs_0_), channel_id=1, source_target_pairs={{0,4},{1,5},{2,6},{3,7},{4,0},{5,1},{6,2},{7,3},{8,12},{9,13},{10,... | collective-permute-start | bytes 786440 | tf_op jit(solution)/shard_map/ppermute | solution.py:585
  20.0 25.5 %collective-permute-start.5 = (f32[64,1024]{1,0:T(8,128)}, f32[64,1024]{1,0:T(8,128)S(1)}, u32[]{:S(2)}, u32[]{:S(2)}) collective-permute-start(f32[64,1024]{1,0:T(8,128)} %entry_product.3.refs_0_), channel_id=1, source_target_pairs={{0,6},{1,7},{2,4},{3,5},{4,2},{5,3},{6,0},{7,1},{8,14},{9,15},{10,... | collective-permute-start | bytes 786440 | tf_op jit(solution)/shard_map/ppermute | solution.py:585
  20.0 27.5 %collective-permute-start = (f32[64,1024]{1,0:T(8,128)}, f32[64,1024]{1,0:T(8,128)S(1)}, u32[]{:S(2)}, u32[]{:S(2)}) collective-permute-start(f32[64,1024]{1,0:T(8,128)} %entry_product.3.refs_0_), channel_id=1, source_target_pairs={{0,1},{1,0},{2,3},{3,2},{4,5},{5,4},{6,7},{7,6},{8,9},{9,8},{10,11... | collective-permute-start | bytes 786440 | tf_op jit(solution)/shard_map/ppermute | solution.py:585
  45.0 5.0 %copy-start.7 = (f32[64,1024]{1,0:T(8,128)}, f32[64,1024]{1,0:T(8,128)S(1)}, u32[]{:S(2)}) copy-start(f32[64,1024]{1,0:T(8,128)S(1)} %collective-permute-done.1.refs_1_.refs_2_) | copy-start | bytes 786436
  45.0 2.6 %collective-permute-start.2 = (f32[64,1024]{1,0:T(8,128)S(1)}, f32[64,1024]{1,0:T(8,128)S(1)}, u32[]{:S(2)}, u32[]{:S(2)}) collective-permute-start(f32[64,1024]{1,0:T(8,128)S(1)} %collective-permute-done.1.refs_1_.refs_2_), channel_id=1, source_target_pairs={{0,1},{1,0},{2,3},{3,2},{4,5},{5,4},{6,7},{7,6},{8,9},{9,8},{10,11... | collective-permute-start | bytes 786440 | tf_op jit(solution)/shard_map/ppermute | solution.py:585
  45.0 5.0 %copy-start.8 = (f32[64,1024]{1,0:T(8,128)}, f32[64,1024]{1,0:T(8,128)S(1)}, u32[]{:S(2)}) copy-start(f32[64,1024]{1,0:T(8,128)S(1)} %collective-permute-done.3.refs_3_.refs_4_) | copy-start | bytes 786436
  45.0 2.5 %collective-permute-start.4 = (f32[64,1024]{1,0:T(8,128)S(1)}, f32[64,1024]{1,0:T(8,128)S(1)}, u32[]{:S(2)}, u32[]{:S(2)}) collective-permute-start(f32[64,1024]{1,0:T(8,128)S(1)} %collective-permute-done.3.refs_3_.refs_4_), channel_id=1, source_target_pairs={{0,1},{1,0},{2,3},{3,2},{4,5},{5,4},{6,7},{7,6},{8,9},{9,8},{10,11... | collective-permute-start | bytes 786440 | tf_op jit(solution)/shard_map/ppermute | solution.py:585
  45.5 4.5 %copy-start.9 = (f32[64,1024]{1,0:T(8,128)}, f32[64,1024]{1,0:T(8,128)S(1)}, u32[]{:S(2)}) copy-start(f32[64,1024]{1,0:T(8,128)S(1)} %collective-permute-done.5.refs_5_.refs_6_) | copy-start | bytes 786436
  45.5 2.1 %collective-permute-start.6 = (f32[64,1024]{1,0:T(8,128)S(1)}, f32[64,1024]{1,0:T(8,128)S(1)}, u32[]{:S(2)}, u32[]{:S(2)}) collective-permute-start(f32[64,1024]{1,0:T(8,128)S(1)} %collective-permute-done.5.refs_5_.refs_6_), channel_id=1, source_target_pairs={{0,1},{1,0},{2,3},{3,2},{4,5},{5,4},{6,7},{7,6},{8,9},{9,8},{10,11... | collective-permute-start | bytes 786440 | tf_op jit(solution)/shard_map/ppermute | solution.py:585
  46.2 75.4 %copy-start.23 = (f32[2]{0:T(128)}, f32[2]{0:T(128)S(1)}, u32[]{:S(2)}) copy-start(f32[2]{0:T(128)S(1)} %rsqrt.6.scale_ref) | copy-start | bytes 28
  47.5 2.5 %copy-start.10 = (f32[64,1024]{1,0:T(8,128)}, f32[64,1024]{1,0:T(8,128)S(1)}, u32[]{:S(2)}) copy-start(f32[64,1024]{1,0:T(8,128)S(1)} %collective-permute-done.refs_0_.refs_1_) | copy-start | bytes 786436
  47.5 2.5 %copy-start.11 = (f32[64,1024]{1,0:T(8,128)}, f32[64,1024]{1,0:T(8,128)S(1)}, u32[]{:S(2)}) copy-start(f32[64,1024]{1,0:T(8,128)S(1)} %collective-permute-done.2.refs_2_.refs_3_) | copy-start | bytes 786436
  47.6 2.5 %copy-start.12 = (f32[64,1024]{1,0:T(8,128)}, f32[64,1024]{1,0:T(8,128)S(1)}, u32[]{:S(2)}) copy-start(f32[64,1024]{1,0:T(8,128)S(1)} %collective-permute-done.4.refs_4_.refs_5_) | copy-start | bytes 786436
  47.6 2.4 %copy-start.13 = (f32[64,1024]{1,0:T(8,128)}, f32[64,1024]{1,0:T(8,128)S(1)}, u32[]{:S(2)}) copy-start(f32[64,1024]{1,0:T(8,128)S(1)} %collective-permute-done.6.refs_6_.refs_7_) | copy-start | bytes 786436
  52.7 13.2 %collective-permute-start.10 = (f32[32,3072]{1,0:T(8,128)}, f32[32,3072]{1,0:T(8,128)S(1)}, u32[]{:S(2)}, u32[]{:S(2)}) collective-permute-start(f32[32,3072]{1,0:T(8,128)} %entry_product.4.refs_8_), channel_id=1, source_target_pairs={{0,6},{1,7},{2,4},{3,5},{4,2},{5,3},{6,0},{7,1},{8,14},{9,15},{10,... | collective-permute-start | bytes 1179656 | tf_op jit(solution)/shard_map/ppermute | solution.py:585
  55.1 17.9 %collective-permute-start.8 = (f32[32,3072]{1,0:T(8,128)}, f32[32,3072]{1,0:T(8,128)S(1)}, u32[]{:S(2)}, u32[]{:S(2)}) collective-permute-start(f32[32,3072]{1,0:T(8,128)} %entry_product.4.refs_8_), channel_id=1, source_target_pairs={{0,2},{1,3},{2,0},{3,1},{4,6},{5,7},{6,4},{7,5},{8,10},{9,11},{10,... | collective-permute-start | bytes 1179656 | tf_op jit(solution)/shard_map/ppermute | solution.py:585
  55.7 17.4 %collective-permute-start.9 = (f32[32,3072]{1,0:T(8,128)}, f32[32,3072]{1,0:T(8,128)S(1)}, u32[]{:S(2)}, u32[]{:S(2)}) collective-permute-start(f32[32,3072]{1,0:T(8,128)} %entry_product.4.refs_8_), channel_id=1, source_target_pairs={{0,4},{1,5},{2,6},{3,7},{4,0},{5,1},{6,2},{7,3},{8,12},{9,13},{10,... | collective-permute-start | bytes 1179656 | tf_op jit(solution)/shard_map/ppermute | solution.py:585
  56.2 31.3 %collective-permute-start.7 = (f32[32,3072]{1,0:T(8,128)}, f32[32,3072]{1,0:T(8,128)S(1)}, u32[]{:S(2)}, u32[]{:S(2)}) collective-permute-start(f32[32,3072]{1,0:T(8,128)} %entry_product.4.refs_8_), channel_id=1, source_target_pairs={{0,1},{1,0},{2,3},{3,2},{4,5},{5,4},{6,7},{7,6},{8,9},{9,8},{10,11... | collective-permute-start | bytes 1179656 | tf_op jit(solution)/shard_map/ppermute | solution.py:585
  65.9 7.2 %copy-start.3 = (f32[32,3072]{1,0:T(8,128)}, f32[32,3072]{1,0:T(8,128)S(1)}, u32[]{:S(2)}) copy-start(f32[32,3072]{1,0:T(8,128)S(1)} %collective-permute-done.10.refs_2_) | copy-start | bytes 1179652
  73.0 0.7 copy-start.5
  73.1 0.9 copy-start.6
  74.0 13.6 %collective-permute-start.11 = (f32[32,3072]{1,0:T(8,128)}, f32[32,3072]{1,0:T(8,128)S(1)}, u32[]{:S(2)}, u32[]{:S(2)}) collective-permute-start(f32[32,3072]{1,0:T(8,128)} %get-tuple-element.32.refs_1_.refs_10_), channel_id=1, source_target_pairs={{0,1},{1,0},{2,3},{3,2},{4,5},{5,4},{6,7},{7,6},{8,9},{9,8},{10,11... | collective-permute-start | bytes 1179656 | tf_op jit(solution)/shard_map/ppermute | solution.py:585
  74.0 13.6 %collective-permute-start.12 = (f32[32,3072]{1,0:T(8,128)}, f32[32,3072]{1,0:T(8,128)S(1)}, u32[]{:S(2)}, u32[]{:S(2)}) collective-permute-start(f32[32,3072]{1,0:T(8,128)} %get-tuple-element.33.refs_3_.refs_12_), channel_id=1, source_target_pairs={{0,1},{1,0},{2,3},{3,2},{4,5},{5,4},{6,7},{7,6},{8,9},{9,8},{10,11... | collective-permute-start | bytes 1179656 | tf_op jit(solution)/shard_map/ppermute | solution.py:585
  74.5 13.1 %collective-permute-start.13 = (f32[32,3072]{1,0:T(8,128)}, f32[32,3072]{1,0:T(8,128)S(1)}, u32[]{:S(2)}, u32[]{:S(2)}) collective-permute-start(f32[32,3072]{1,0:T(8,128)} %get-tuple-element.34.refs_5_.refs_14_), channel_id=1, source_target_pairs={{0,1},{1,0},{2,3},{3,2},{4,5},{5,4},{6,7},{7,6},{8,9},{9,8},{10,11... | collective-permute-start | bytes 1179656 | tf_op jit(solution)/shard_map/ppermute | solution.py:585
  87.5 0.8 copy-start.14
  87.6 0.9 copy-start.15
  87.6 1.0 copy-start.16
  87.6 1.1 copy-start.17
  91.4 12.2 %collective-permute-start.15 = (f32[32,3072]{1,0:T(8,128)}, f32[32,3072]{1,0:T(8,128)S(1)}, u32[]{:S(2)}, u32[]{:S(2)}) collective-permute-start(f32[32,3072]{1,0:T(8,128)} %entry_product.5.refs_8_), channel_id=1, source_target_pairs={{0,2},{1,3},{2,0},{3,1},{4,6},{5,7},{6,4},{7,5},{8,10},{9,11},{10,... | collective-permute-start | bytes 1179656 | tf_op jit(solution)/shard_map/ppermute | solution.py:585
  92.9 19.1 %collective-permute-start.16 = (f32[32,3072]{1,0:T(8,128)}, f32[32,3072]{1,0:T(8,128)S(1)}, u32[]{:S(2)}, u32[]{:S(2)}) collective-permute-start(f32[32,3072]{1,0:T(8,128)} %entry_product.5.refs_8_), channel_id=1, source_target_pairs={{0,4},{1,5},{2,6},{3,7},{4,0},{5,1},{6,2},{7,3},{8,12},{9,13},{10,... | collective-permute-start | bytes 1179656 | tf_op jit(solution)/shard_map/ppermute | solution.py:585
  94.3 17.6 %collective-permute-start.17 = (f32[32,3072]{1,0:T(8,128)}, f32[32,3072]{1,0:T(8,128)S(1)}, u32[]{:S(2)}, u32[]{:S(2)}) collective-permute-start(f32[32,3072]{1,0:T(8,128)} %entry_product.5.refs_8_), channel_id=1, source_target_pairs={{0,6},{1,7},{2,4},{3,5},{4,2},{5,3},{6,0},{7,1},{8,14},{9,15},{10,... | collective-permute-start | bytes 1179656 | tf_op jit(solution)/shard_map/ppermute | solution.py:585
  94.9 7.9 %copy-start.18 = (f32[32,3072]{1,0:T(8,128)S(1)}, f32[32,3072]{1,0:T(8,128)}, u32[]{:S(2)}) copy-start(f32[32,3072]{1,0:T(8,128)} %entry_product.5.refs_8_) | copy-start | bytes 1179652
  102.7 10.6 %collective-permute-start.14 = (f32[32,3072]{1,0:T(8,128)S(1)}, f32[32,3072]{1,0:T(8,128)S(1)}, u32[]{:S(2)}, u32[]{:S(2)}) collective-permute-start(f32[32,3072]{1,0:T(8,128)S(1)} %copy-done.18), channel_id=1, source_target_pairs={{0,1},{1,0},{2,3},{3,2},{4,5},{5,4},{6,7},{7,6},{8,9},{9,8},{10,11... | collective-permute-start | bytes 1179656 | tf_op jit(solution)/shard_map/ppermute | solution.py:585
  103.6 8.3 %copy-start.1 = (f32[32,3072]{1,0:T(8,128)}, f32[32,3072]{1,0:T(8,128)S(1)}, u32[]{:S(2)}) copy-start(f32[32,3072]{1,0:T(8,128)S(1)} %collective-permute-done.15.refs_0_) | copy-start | bytes 1179652
  112.0 0.7 copy-start.2
  112.0 0.9 copy-start.4
  112.9 1.9 collective-permute-start.18
  112.9 2.5 %collective-permute-start.19 = (f32[32,3072]{1,0:T(8,128)}, f32[32,3072]{1,0:T(8,128)S(1)}, u32[]{:S(2)}, u32[]{:S(2)}) collective-permute-start(f32[32,3072]{1,0:T(8,128)} %get-tuple-element.38.refs_4_.refs_12_), channel_id=1, source_target_pairs={{0,1},{1,0},{2,3},{3,2},{4,5},{5,4},{6,7},{7,6},{8,9},{9,8},{10,11... | collective-permute-start | bytes 1179656 | tf_op jit(solution)/shard_map/ppermute | solution.py:585
  113.4 2.5 %collective-permute-start.20 = (f32[32,3072]{1,0:T(8,128)}, f32[32,3072]{1,0:T(8,128)S(1)}, u32[]{:S(2)}, u32[]{:S(2)}) collective-permute-start(f32[32,3072]{1,0:T(8,128)} %get-tuple-element.39.refs_6_.refs_14_), channel_id=1, source_target_pairs={{0,1},{1,0},{2,3},{3,2},{4,5},{5,4},{6,7},{7,6},{8,9},{9,8},{10,11... | collective-permute-start | bytes 1179656 | tf_op jit(solution)/shard_map/ppermute | solution.py:585
  113.4 2.5 %copy-start.19 = (f32[32,3072]{1,0:T(8,128)}, f32[32,3072]{1,0:T(8,128)S(1)}, u32[]{:S(2)}) copy-start(f32[32,3072]{1,0:T(8,128)S(1)} %collective-permute-done.14.refs_1_.refs_9_) | copy-start | bytes 1179652
  114.8 1.1 copy-start.20
  115.4 0.8 copy-start.21
  115.9 0.8 copy-start.22
  116.7 65.0 %all-to-all-start = ((f32[8,1280,128]{2,1,0:T(8,128)}), f32[8,1280,128]{2,1,0:T(8,128)}, u32[]{:S(2)}, u32[]{:S(2)}) async-start(f32[8,1280,128]{2,1,0:T(8,128)} %bitcast.24), calls=%async_computation | async-start | bytes 10485760 | tf_op jit(solution)/shard_map/all_to_all | solution.py:668
Sparse Core Ops, SparseCore 0:
  10.2 39.7 all-gather.6
  51.6 35.9 all-gather.4

commit v8 on v7

--- a/solution.py
+++ b/solution.py
@@ -175,17 +175,16 @@
 
 ROWS = 16
 HALVES = 2
-TOGETHER = 2
-
-
-def first_section(freq, half, info, templates, strain, first, stage, twist, earlier):
+TOGETHER = 4
+
+
+def first_section(freq, half, info, templates, strain, first, stage, twist):
     tmpls = templates.shape[0]
     pieces, dets, _, rows, piece_len = strain.shape
-    cols = templates.shape[2]
     series = tmpls * dets - 1
     groups = COARSE // freq
     table = pl.BlockSpec((2 * LANES, 2 * LANES), lambda i, n: (0, 0))
-    out = (freq, series, 2, groups, cols, LANES)
+    out = (freq, series, 2, groups, rows, LANES)
     return pl.pallas_call(
         functools.partial(first_kernel, freq),
         grid_spec=pltpu.PrefetchScalarGridSpec(
@@ -202,11 +201,10 @@
                 table,
                 pl.BlockSpec((2 * COARSE, LANES), lambda i, n: (0, 0)),
                 pl.BlockSpec((2, rows, N1), lambda i, n: (0, half, 0)),
-            ]
-            + [ANY] * len(earlier),
+            ],
             out_specs=[
                 pl.BlockSpec(
-                    (freq, 1, 2, groups, rows, LANES), lambda i, n: (0, i, 0, 0, half, 0)
+                    (freq, 1, 2, groups, rows, LANES), lambda i, n: (0, i, 0, 0, 0, 0)
                 ),
                 pl.BlockSpec((8, LANES), lambda i, n: (0, 0)),
             ],
@@ -220,13 +218,12 @@
             jax.ShapeDtypeStruct(out, F32),
             jax.ShapeDtypeStruct((8, LANES), F32),
         ],
-        input_output_aliases={7: 0} if earlier else {},
         compiler_params=pltpu.CompilerParams(vmem_limit_bytes=VMEM_LIMIT),
         cost_estimate=pl.CostEstimate(
-            flops=60 * series * cols * N1 * LANES, bytes_accessed=16 * MIB, transcendentals=0
+            flops=60 * series * rows * N1 * LANES, bytes_accessed=16 * MIB, transcendentals=0
         ),
         name="first_section",
-    )(info, templates, strain, first[0], first[1], stage, twist, *earlier)
+    )(info, templates, strain, first[0], first[1], stage, twist)
 
 
 def entry_kernel(steps, banks, which_ref, tmpl_ref, strain_ref, *refs):
@@ -607,20 +604,8 @@
         for h in range(HALVES)
     ]
     first = tuple(jnp.asarray(t) for t in first_table())
-    second = tuple(jnp.asarray(t) for t in second_table(cols, 1))
-    second_halves = tuple(jnp.asarray(t) for t in second_table(cols, HALVES))
+    second = tuple(jnp.asarray(t) for t in second_table(cols, HALVES))
     stage = jnp.asarray(stage_table())
-
-    power = (templates[:, 0] ** 2 + templates[:, 1] ** 2).sum(axis=1)
-    local_power = power.reshape(tmpls, NBLK, BLOCK).sum(axis=2)
-    block_power = lax.psum(local_power, "freq")
-    sigma_sq = block_power.sum(axis=1)
-    inv_sigma = lax.rsqrt(sigma_sq)
-    bin_of = jnp.sum(
-        jnp.arange(NBLK, dtype=jnp.int32)[None, :, None] >= bin_edges[:, None, :], axis=2
-    )
-    inside = bin_of[:, None, :] == jnp.arange(BINS, dtype=jnp.int32)[None, :, None]
-    weights = jnp.where(inside, block_power[:, None, :], 0.0).sum(axis=2) / sigma_sq[:, None]
 
     column = place * cols + jnp.arange(cols, dtype=jnp.int32)
     lane = jnp.arange(N1, dtype=jnp.int32)
@@ -645,49 +630,63 @@
     ]
     here = jnp.stack([place, bank])
 
+    power = (templates[:, 0] ** 2 + templates[:, 1] ** 2).sum(axis=1)
+    power = power.reshape(tmpls, NBLK, BLOCK).sum(axis=2)
     own = [entry_product((0,), banks, 0, w, templates, strain[None], []) for w in which]
+    wide = own[0].shape[1]
+    power = jnp.pad(power.reshape(1, -1), ((0, 7), (0, wide - tmpls * NBLK)))
+    own[0] = jnp.concatenate([own[0], power], axis=0)
     own = [near_pieces(far_pieces(x, freq), freq) for x in own]
     gathered = [x for entry in own for x in entry[1:]]
-    which, inv_sigma, weights, twist, info = lax.optimization_barrier(
-        (which, inv_sigma, weights, twist, info)
+
+    block_power = sum(x[cols, : tmpls * NBLK] for x in own[0]).reshape(tmpls, NBLK)
+    sigma_sq = block_power.sum(axis=1)
+    inv_sigma = lax.rsqrt(sigma_sq)
+    bin_of = jnp.sum(
+        jnp.arange(NBLK, dtype=jnp.int32)[None, :, None] >= bin_edges[:, None, :], axis=2
     )
-
-    rest, sent = [], []
+    inside = bin_of[:, None, :] == jnp.arange(BINS, dtype=jnp.int32)[None, :, None]
+    weights = jnp.where(inside, block_power[:, None, :], 0.0).sum(axis=2) / sigma_sq[:, None]
+    gains = [inv_sigma[coinc_tmpl[j]] * lax.rsqrt(weights[coinc_tmpl[j]]) for j in range(slots)]
+    shares = [gains[j] * weights[coinc_tmpl[j]] for j in range(slots)]
+    which, inv_sigma, gains, shares, twist, info, edges, here, table, own_twist = (
+        lax.optimization_barrier(
+            (which, inv_sigma, gains, shares, twist, info, edges, here, table, own_twist)
+        )
+    )
+
+    parts, halves = [], []
     later = tuple(range(1, banks))
     for h in range(HALVES):
-        after = gathered if h == 0 else gathered + [table[0], *own_twist]
+        after = [x[0] for x in halves[-1]] if halves else gathered
         half = [entry_product(later, banks, h, w, templates, strains[h], after) for w in which]
         far = [far_pieces(x, freq) for x in half]
-        *sent, token = first_section(
-            freq, h, info, templates, strains[h], first, stage, twist, sent
+        sent, token = first_section(freq, h, info, templates, strains[h], first, stage, twist)
+        far = [x[:1] + list(handed_on(x[1:], [token] + parts)) for x in far]
+        rest = [near_pieces(x, freq) for x in far]
+        (ready,) = handed_on([sent], [x for entry in rest for x in entry[1:]])
+        got = lax.all_to_all(
+            ready.reshape(freq, -1, LANES), "freq", split_axis=0, concat_axis=0, tiled=True
         )
-        far = [x[:1] + list(handed_on(x[1:], [token])) for x in far]
-        rest.append([near_pieces(x, freq) for x in far])
-        gathered = [x for entry in rest[-1] for x in entry[1:]]
-    (ready,) = handed_on(sent, gathered)
-    got = lax.all_to_all(
-        ready.reshape(freq, -1, LANES), "freq", split_axis=0, concat_axis=0, tiled=True
-    )
-    got = got.reshape(ready.shape)
+        parts.append(got.reshape(ready.shape))
+        halves.append(
+            [
+                bins_first(
+                    h, banks, here, edges[j], own[j], rest[j], table, own_twist[h], [ready]
+                )
+                for j in range(slots)
+            ]
+        )
 
     chi, snr = [], None
     for j in range(slots):
-        t = coinc_tmpl[j]
-        halves = [
-            bins_first(
-                h, banks, here, edges[j], own[j], rest[h][j], table, own_twist[h], [ready]
-            )
-            for h in range(HALVES)
-        ]
-        levels, totals = zip(*halves)
-        gain = inv_sigma[t] * lax.rsqrt(weights[t])
-        share = gain * weights[t]
+        levels, totals = zip(*[x[j] for x in halves])
         one, series_of = bins_second(
-            which[j], inv_sigma, gain, share, levels, totals, second_halves, tmpls, dets
+            which[j], inv_sigma, gains[j], shares[j], levels, totals, second, tmpls, dets
         )
         chi.append(one)
         snr = series_of if snr is None else snr
-    snr = second_section(freq, info, inv_sigma, [got], second, snr, chi)
+    snr = second_section(freq, info, inv_sigma, parts, second, snr, chi)
     return (snr, jnp.stack(chi))
 
 

time: 200 us -> 203 us (1.015)
  blocking collectives: 19.4 us -> 0 us
  waiting for transfers between devices: 34.1 us -> 50 us
  starting transfers between devices: 18 us -> 21.3 us
  other arithmetic: 13.3 us -> 15.8 us
    psum x1 -> x0, blocking collectives: 19.4 us -> none  [per_device(): block_power = lax.psum(local_power, 'freq')]
    ppermute x21, waiting for transfers between devices: 20.8 us -> 33.1 us  [swap(): return lax.ppermute(x, 'freq', [(i, i ^ k) for i in range(freq)])]
    all_gather x2, waiting for transfers between devices: 6.25 us -> 16.9 us  [per_device(): lax.all_gather(strain[:, :, h * part:(h + 1) * part], 'bank', axis=0, til...]
    all_to_all x1 -> x2, waiting for transfers between devices: 7.06 us -> 0.01 us  [per_device(): lax.all_to_all(ready.reshape(freq, -1, LANES), 'freq', split_axis=0, conc...]
    all_to_all x1 -> x2, starting transfers between devices: 4.85 us -> 7.43 us  [per_device(): lax.all_to_all(ready.reshape(freq, -1, LANES), 'freq', split_axis=0, conc...]
  transfers between devices with their start and end apart: 24 -> 25, of which waited for: 10 -> 15; matrix products, arithmetic and copies ran while one was open for 7% -> 7% of each run, Pallas kernels for 39% -> 36%
where the time goes in v8:
time: 203 us; the launch traced here: 202 us
  Pallas kernels  91.3 us (45%)
  waiting for transfers between devices  50 us (25%)
  starting transfers between devices  21.3 us (10%)
  other arithmetic  15.8 us (8%)
  between operations  15.6 us (8%)
  local copies, waits for them, and re-layouts  8.27 us (4%)
    pallas_call x2, Pallas kernels, bins_first(): pl.pallas_call(functools.partial(bins_first_kernel, len(own), banks), gri...  33.7 us
    ppermute x21, waiting for transfers between devices, swap(): return lax.ppermute(x, 'freq', [(i, i ^ k) for i in range(freq)])  33.1 us
    all_gather x2, waiting for transfers between devices, per_device(): lax.all_gather(strain[:, :, h * part:(h + 1) * part], 'bank', axis=0, til...  16.9 us
    pallas_call x1, Pallas kernels, bins_second(): pl.pallas_call(functools.partial(bins_second_kernel, halves), grid_spec=p...  16.1 us
    pallas_call x2, Pallas kernels, first_section(): pl.pallas_call(functools.partial(first_kernel, freq), grid_spec=pltpu.Pre...  15.2 us
    ppermute x21, starting transfers between devices, swap(): return lax.ppermute(x, 'freq', [(i, i ^ k) for i in range(freq)])  13.8 us
    pallas_call x1, Pallas kernels, second_section(): pl.pallas_call(functools.partial(second_kernel, freq, halves), grid_spec=...  10.7 us
    pallas_call x3, Pallas kernels, entry_product(): pl.pallas_call(functools.partial(entry_kernel, steps, banks), grid_spec=p...  9.55 us
  transfers between devices with their start and end apart: 25, of which 15 were waited for; matrix products, arithmetic and copies ran while one was open for 7% of the time, Pallas kernels for 36%

profile of v8, /device:TPU:0, one launch (start us, length us, event | category | flops | bytes accessed | tf_op | source)
XLA Modules:
  0.0 202.3 jit_solution(4763590469989608289)
XLA Ops:
  8.5 1.8 add_reduce_fusion
  10.6 0.6 pad_add_fusion.1.which_ref
  11.2 4.2 %entry_product.3 = f32[64,1024]{1,0:T(8,128)} custom-call(s32[3]{0:T(128)} %pad_add_fusion.1.which_ref, f32[2,2,64,2048]{3,2,1,0:T(8,128)} %tmpl_ref.9, f32[1,3,2,64,512]{4,3,2,1,0:T(8,128)} %bitcast.31), custom_call_target="tpu_custom_call" | custom-call | flops 1048576 | bytes 1048576 | tf_op jit(solution)/shard_map/entry_product/pallas_call | solution.py:249
  15.4 1.0 select_maximum_fusion.refs_0_
  16.3 4.0 %collective-permute-start.5 = (f32[72,1024]{1,0:T(8,128)S(1)}, f32[72,1024]{1,0:T(8,128)S(1)}, u32[]{:S(2)}, u32[]{:S(2)}) collective-permute-start(f32[72,1024]{1,0:T(8,128)S(1)} %select_maximum_fusion.refs_0_), channel_id=1, source_target_pairs={{0,6},{1,7},{2,4},{3,5},{4,2},{5,3},{6,0},{7,1},{8,14},{9,15},{10,... | collective-permute-start | bytes 884744 | tf_op jit(solution)/shard_map/ppermute | solution.py:582
  20.3 0.5 collective-permute-start.3
  21.0 1.0 fusion.49
  22.1 0.3 fusion.24
  22.4 0.6 pad_add_fusion.4.place_ref
  23.4 1.0 fusion.39
  24.4 0.7 pad_maximum_fusion.4.block_ref
  25.1 0.7 pad_maximum_fusion.3.inner_ref
  25.8 2.1 %fusion.12 = (f32[1,256,256]{2,1,0:T(8,128)S(1)}, f32[1,256,256]{2,1,0:T(8,128)S(1)}, f32[1,256,256]{2,1,0:T(8,128)S(1)}, f32[1,256,256]{2,1,0:T(8,128)S(1)}) fusion(s32[256]{0:T(256)S(1)} %iota_add_fusion, s32[256]{0:T(256)S(1)} %add_add_fusion, s32[256]{0:T(256)S(1)} %fusion.45), kind=kLoop, calls=%fused_computation.34 | loop fusion | flops 1835008 | bytes 1051648 | tf_op jit(solution)/shard_map/cos | solution.py:64
  27.9 6.0 %bank_table.1 = (bf16[4096,512]{1,0:T(8,128)(2,1)}, bf16[4096,512]{1,0:T(8,128)(2,1)}) custom-call(f32[32,2,256]{2,1,0:T(2,128)} %pad_maximum_fusion.4.block_ref, f32[2,64,256]{2,1,0:T(8,128)} %pad_maximum_fusion.3.inner_ref), custom_call_target="tpu_custom_call" | custom-call | flops 1048576 | bytes 1048576 | tf_op jit(solution)/shard_map/bank_table/pallas_call | solution.py:371
  33.9 1.0 pad_maximum_fusion.1
  34.9 2.1 %fusion.10 = (f32[1,64,2048]{2,1,0:T(8,128)S(1)}, f32[1,64,2048]{2,1,0:T(8,128)S(1)}) fusion(s32[2048]{0:T(1024)S(1)} %fusion.35, s32[64]{0:T(128)S(1)} %iota_add_fusion.1), kind=kLoop, calls=%fused_computation.31 | loop fusion | flops 1835008 | bytes 1057024 | tf_op jit(solution)/shard_map/cos | solution.py:64
  37.1 1.1 pad_maximum_fusion.tw_ref
  38.2 0.6 pad_add_fusion.2.info_ref
  38.8 0.6 pad_add_fusion.3.edge_ref
  39.5 0.5 collective-permute-start.6
  40.2 0.5 collective-permute-start.2
  40.8 0.4 collective-permute-done.6.refs_6_.refs_7_
  41.3 0.4 collective-permute-done.4.refs_4_.refs_5_
  41.8 0.3 collective-permute-done.2.refs_2_.refs_3_
  42.3 0.6 dynamic_slice.10
  43.0 1.2 bitcast_multiply_fusion
  44.2 16.8 %all-gather.5.cloned.1.call-done = f32[12,2,32,512]{3,2,1,0:T(8,128)} async-done(((f32[3,2,32,512]{3,2,1,0:T(8,128)}), f32[12,2,32,512]{3,2,1,0:T(8,128)}) %all-gather.5.cloned.1.call-update) | async-done | bytes 1572880 | tf_op jit(solution)/shard_map/all_gather | solution.py:603
  61.1 2.7 %entry_product.4.refs_8_ = f32[32,3072]{1,0:T(8,128)} custom-call(s32[3]{0:T(128)} %pad_add_fusion.1.which_ref, f32[2,2,64,2048]{3,2,1,0:T(8,128)} %tmpl_ref.9, f32[4,3,2,32,512]{4,3,2,1,0:T(8,128)} %bitcast.34, f32[72,1024]{1,0:T(8,128)} %copy-done.11, f32[72,1024]{1,0:T(8,128)} %copy-done.10, f32[72,1024]{1,0:T(8,128)} %copy-done.14, ...), custom_call_target="tpu_custom_call" | custom-call | flops 1048576 | bytes 1048576 | tf_op jit(solution)/shard_map/entry_product/pallas_call | solution.py:249
  63.8 2.4 %collective-permute-start.10 = (f32[32,3072]{1,0:T(8,128)}, f32[32,3072]{1,0:T(8,128)S(1)}, u32[]{:S(2)}, u32[]{:S(2)}) collective-permute-start(f32[32,3072]{1,0:T(8,128)} %entry_product.4.refs_8_), channel_id=1, source_target_pairs={{0,6},{1,7},{2,4},{3,5},{4,2},{5,3},{6,0},{7,1},{8,14},{9,15},{10,... | collective-permute-start | bytes 1179656 | tf_op jit(solution)/shard_map/ppermute | solution.py:582
  66.1 0.6 collective-permute-start.9
  66.7 0.6 collective-permute-start.8
  67.4 7.6 %first_section.2 = (f32[8,5,2,2,32,128]{5,4,3,2,1,0:T(8,128)}, f32[8,128]{1,0:T(8,128)}) custom-call(s32[11]{0:T(128)} %pad_add_fusion.2.info_ref, f32[2,2,64,2048]{3,2,1,0:T(8,128)} %tmpl_ref.9, f32[4,3,2,32,512]{4,3,2,1,0:T(8,128)} %bitcast.35, bf16[256,256]{1,0:T(8,128)(2,1)} %constant.175.clone.wh_ref, bf16[256,256]{1,0:T(8,128)(2,1)} %constant.176.clone.wl_ref, ...), custom_call_target="tpu_custom_call" | custom-call | flops 2516582400 | bytes 16777216 | tf_op jit(solution)/shard_map/first_section/pallas_call | solution.py:188
  74.9 2.0 collective-permute-done.10.refs_2_
  76.9 7.1 %collective-permute-done.9.refs_1_ = f32[32,3072]{1,0:T(8,128)S(1)} collective-permute-done((f32[32,3072]{1,0:T(8,128)}, f32[32,3072]{1,0:T(8,128)S(1)}, u32[]{:S(2)}, u32[]{:S(2)}) %collective-permute-start.9) | collective-permute-done | bytes 393248 | tf_op jit(solution)/shard_map/ppermute | solution.py:582
  84.1 0.7 copy-done.5
  84.8 0.2 copy-done.6
  85.1 0.4 collective-permute-start.12
  85.6 1.3 collective-permute-done.11.refs_3_.refs_11_
  86.9 0.6 collective-permute-done.12.refs_5_.refs_13_
  87.5 0.6 collective-permute-done.13.refs_7_.refs_15_
  88.0 0.2 copy-done.21
  88.2 0.6 copy-done.22
  88.8 3.8 %all-to-all-start = ((f32[8,640,128]{2,1,0:T(8,128)}), f32[8,640,128]{2,1,0:T(8,128)S(1)}, u32[]{:S(2)}, u32[]{:S(2)}) async-start(f32[8,640,128]{2,1,0:T(8,128)} %bitcast.29), calls=%async_computation | async-start | bytes 5242880 | tf_op jit(solution)/shard_map/all_to_all | solution.py:668
  92.6 16.9 %bins_first.2 = (f32[16,2,256,256]{3,2,1,0:T(8,128)}, f32[2,256,256]{2,1,0:T(8,128)}) custom-call(s32[2]{0:T(128)} %pad_add_fusion.4.place_ref, s32[17]{0:T(128)} %pad_add_fusion.3.edge_ref, f32[72,1024]{1,0:T(8,128)} %copy-done.15, f32[72,1024]{1,0:T(8,128)} %copy-done.11, f32[72,1024]{1,0:T(8,128)} %copy-done.10, f32[72,1024]{1,0:T(8,128)} %copy-done.14, ...), custom_call_target="tpu_custom_call" | custom-call | flops 1048576 | bytes 1048576 | tf_op jit(solution)/shard_map/bins_first/pallas_call | solution.py:455
  109.5 2.7 %entry_product.5.refs_8_ = f32[32,3072]{1,0:T(8,128)} custom-call(s32[3]{0:T(128)} %pad_add_fusion.1.which_ref, f32[2,2,64,2048]{3,2,1,0:T(8,128)} %tmpl_ref.9, f32[4,3,2,32,512]{4,3,2,1,0:T(8,128)} %bitcast.32, f32[16,2,256,256]{3,2,1,0:T(8,128)} %get-tuple-element.49.refs_0_), custom_call_target="tpu_custom_call" | custom-call | flops 1048576 | bytes 1048576 | tf_op jit(solution)/shard_map/entry_product/pallas_call | solution.py:249
  112.2 2.7 %collective-permute-start.17 = (f32[32,3072]{1,0:T(8,128)}, f32[32,3072]{1,0:T(8,128)S(1)}, u32[]{:S(2)}, u32[]{:S(2)}) collective-permute-start(f32[32,3072]{1,0:T(8,128)} %entry_product.5.refs_8_), channel_id=1, source_target_pairs={{0,6},{1,7},{2,4},{3,5},{4,2},{5,3},{6,0},{7,1},{8,14},{9,15},{10,... | collective-permute-start | bytes 1179656 | tf_op jit(solution)/shard_map/ppermute | solution.py:582
  114.9 0.5 collective-permute-start.16
  115.4 0.3 collective-permute-start.15
  115.7 7.6 %first_section.3 = (f32[8,5,2,2,32,128]{5,4,3,2,1,0:T(8,128)}, f32[8,128]{1,0:T(8,128)}) custom-call(s32[11]{0:T(128)} %pad_add_fusion.2.info_ref, f32[2,2,64,2048]{3,2,1,0:T(8,128)} %tmpl_ref.9, f32[4,3,2,32,512]{4,3,2,1,0:T(8,128)} %bitcast.33, bf16[256,256]{1,0:T(8,128)(2,1)} %constant.175.clone.wh_ref, bf16[256,256]{1,0:T(8,128)(2,1)} %constant.176.clone.wl_ref, ...), custom_call_target="tpu_custom_call" | custom-call | flops 2516582400 | bytes 16777216 | tf_op jit(solution)/shard_map/first_section/pallas_call | solution.py:188
  123.3 10.3 %collective-permute-done.17.refs_2_ = f32[32,3072]{1,0:T(8,128)S(1)} collective-permute-done((f32[32,3072]{1,0:T(8,128)}, f32[32,3072]{1,0:T(8,128)S(1)}, u32[]{:S(2)}, u32[]{:S(2)}) %collective-permute-start.17) | collective-permute-done | bytes 393248 | tf_op jit(solution)/shard_map/ppermute | solution.py:582
  133.6 7.6 %collective-permute-done.16.refs_1_ = f32[32,3072]{1,0:T(8,128)S(1)} collective-permute-done((f32[32,3072]{1,0:T(8,128)}, f32[32,3072]{1,0:T(8,128)S(1)}, u32[]{:S(2)}, u32[]{:S(2)}) %collective-permute-start.16) | collective-permute-done | bytes 393248 | tf_op jit(solution)/shard_map/ppermute | solution.py:582
  141.2 0.7 copy-done.3
  141.9 0.9 copy-done
  142.8 0.5 collective-permute-start.19
  143.3 1.4 collective-permute-done.18.refs_3_.refs_11_
  144.8 0.6 collective-permute-done.19.refs_5_.refs_13_
  145.3 0.6 collective-permute-done.20.refs_7_.refs_15_
  145.9 0.2 copy-done.18
  146.1 0.6 copy-done.19
  146.7 3.6 %all-to-all-start.1 = ((f32[8,640,128]{2,1,0:T(8,128)}), f32[8,640,128]{2,1,0:T(8,128)S(1)}, u32[]{:S(2)}, u32[]{:S(2)}) async-start(f32[8,640,128]{2,1,0:T(8,128)} %bitcast.28), calls=%async_computation.1 | async-start | bytes 5242880 | tf_op jit(solution)/shard_map/all_to_all | solution.py:668
  150.3 16.8 %bins_first.3 = (f32[16,2,256,256]{3,2,1,0:T(8,128)}, f32[2,256,256]{2,1,0:T(8,128)}) custom-call(s32[2]{0:T(128)} %pad_add_fusion.4.place_ref, s32[17]{0:T(128)} %pad_add_fusion.3.edge_ref, f32[72,1024]{1,0:T(8,128)} %copy-done.15, f32[72,1024]{1,0:T(8,128)} %copy-done.11, f32[72,1024]{1,0:T(8,128)} %copy-done.10, f32[72,1024]{1,0:T(8,128)} %copy-done.14, ...), custom_call_target="tpu_custom_call" | custom-call | flops 1048576 | bytes 1048576 | tf_op jit(solution)/shard_map/bins_first/pallas_call | solution.py:455
  167.1 16.1 %bins_second.1 = (f32[256,512]{1,0:T(8,128)}, f32[2,3,2,256,512]{4,3,2,1,0:T(8,128)}) custom-call(s32[3]{0:T(128)} %pad_add_fusion.1.which_ref, f32[2]{0:T(128)} %copy-done.23, f32[16]{0:T(128)} %get-tuple-element.54.gain_ref, f32[16]{0:T(128)} %get-tuple-element.55.share_ref, f32[16,2,256,256]{3,2,1,0:T(8,128)} %get-tuple-element.49.refs_0_, ...), custom_call_target="tpu_custom_call" | custom-call | flops 1048576 | bytes 1048576 | tf_op jit(solution)/shard_map/bins_second/pallas_call | solution.py:539
  183.2 1.5 copy-done.1
  184.7 10.7 %second_section.1 = f32[2,3,2,256,512]{4,3,2,1,0:T(8,128)} custom-call(s32[11]{0:T(128)} %pad_add_fusion.2.info_ref, f32[2]{0:T(128)} %copy-done.23, f32[8,5,2,2,32,128]{5,4,3,2,1,0:T(8,128)} %bitcast.27, f32[8,5,2,2,32,128]{5,4,3,2,1,0:T(8,128)} %bitcast.30, bf16[1024,256]{1,0:T(8,128)(2,1)} %constant.177.clone.refs_4_.refs_2_, ...), custom_call_target="tpu_custom_call", output_to_operand_aliasing={{}: (6, {})} | custom-call | flops 1048576 | bytes 1048576 | tf_op jit(solution)/shard_map/second_section/pallas_call | solution.py:325
  (103 shorter events, 2.5 us)
Async XLA Ops:
  7.2 53.9 %all-gather.5.cloned.1.call-start = ((), (), s32[]{:S(2)}) async-start(), calls=%async_computation.2 | async-start | bytes 1966080 | tf_op jit(solution)/shard_map/all_gather | solution.py:603
  8.5 12.4 %copy-start.7 = (f32[3,2,64,512]{3,2,1,0:T(8,128)S(1)}, f32[3,2,64,512]{3,2,1,0:T(8,128)}, u32[]{:S(2)}) copy-start(f32[3,2,64,512]{3,2,1,0:T(8,128)} %param.10) | copy-start | bytes 2359300
  11.2 12.0 %copy-start.24 = (s32[2,15]{1,0:T(2,128)S(1)}, s32[2,15]{1,0:T(2,128)}, u32[]{:S(2)}) copy-start(s32[2,15]{1,0:T(2,128)} %param.14) | copy-start | bytes 364
  16.3 18.6 %copy-start.15 = (f32[72,1024]{1,0:T(8,128)}, f32[72,1024]{1,0:T(8,128)S(1)}, u32[]{:S(2)}) copy-start(f32[72,1024]{1,0:T(8,128)S(1)} %select_maximum_fusion.refs_0_) | copy-start | bytes 884740
  16.3 23.0 %collective-permute-start.5 = (f32[72,1024]{1,0:T(8,128)S(1)}, f32[72,1024]{1,0:T(8,128)S(1)}, u32[]{:S(2)}, u32[]{:S(2)}) collective-permute-start(f32[72,1024]{1,0:T(8,128)S(1)} %select_maximum_fusion.refs_0_), channel_id=1, source_target_pairs={{0,6},{1,7},{2,4},{3,5},{4,2},{5,3},{6,0},{7,1},{8,14},{9,15},{10,... | collective-permute-start | bytes 884744 | tf_op jit(solution)/shard_map/ppermute | solution.py:582
  20.3 19.6 %collective-permute-start.3 = (f32[72,1024]{1,0:T(8,128)S(1)}, f32[72,1024]{1,0:T(8,128)S(1)}, u32[]{:S(2)}, u32[]{:S(2)}) collective-permute-start(f32[72,1024]{1,0:T(8,128)S(1)} %select_maximum_fusion.refs_0_), channel_id=1, source_target_pairs={{0,4},{1,5},{2,6},{3,7},{4,0},{5,1},{6,2},{7,3},{8,12},{9,13},{10,... | collective-permute-start | bytes 884744 | tf_op jit(solution)/shard_map/ppermute | solution.py:582
  20.8 19.3 %collective-permute-start.1 = (f32[72,1024]{1,0:T(8,128)S(1)}, f32[72,1024]{1,0:T(8,128)S(1)}, u32[]{:S(2)}, u32[]{:S(2)}) collective-permute-start(f32[72,1024]{1,0:T(8,128)S(1)} %select_maximum_fusion.refs_0_), channel_id=1, source_target_pairs={{0,2},{1,3},{2,0},{3,1},{4,6},{5,7},{6,4},{7,5},{8,10},{9,11},{10,... | collective-permute-start | bytes 884744 | tf_op jit(solution)/shard_map/ppermute | solution.py:582
  20.9 19.7 %collective-permute-start = (f32[72,1024]{1,0:T(8,128)S(1)}, f32[72,1024]{1,0:T(8,128)S(1)}, u32[]{:S(2)}, u32[]{:S(2)}) collective-permute-start(f32[72,1024]{1,0:T(8,128)S(1)} %select_maximum_fusion.refs_0_), channel_id=1, source_target_pairs={{0,1},{1,0},{2,3},{3,2},{4,5},{5,4},{6,7},{7,6},{8,9},{9,8},{10,11... | collective-permute-start | bytes 884744 | tf_op jit(solution)/shard_map/ppermute | solution.py:582
  22.0 87.5 %all-gather.7.cloned.1.call-start = ((), (), s32[]{:S(2)}) async-start(), calls=%async_computation.3 | async-start | bytes 1966080 | tf_op jit(solution)/shard_map/all_gather | solution.py:603
  39.4 21.7 %copy-start.8 = (f32[72,1024]{1,0:T(8,128)}, f32[72,1024]{1,0:T(8,128)S(1)}, u32[]{:S(2)}) copy-start(f32[72,1024]{1,0:T(8,128)S(1)} %collective-permute-done.5.refs_5_.refs_6_) | copy-start | bytes 884740
  39.5 1.7 collective-permute-start.6
  40.0 21.1 %copy-start.9 = (f32[72,1024]{1,0:T(8,128)}, f32[72,1024]{1,0:T(8,128)S(1)}, u32[]{:S(2)}) copy-start(f32[72,1024]{1,0:T(8,128)S(1)} %collective-permute-done.3.refs_3_.refs_4_) | copy-start | bytes 884740
  40.1 1.6 collective-permute-start.4
  40.1 20.9 %copy-start.10 = (f32[72,1024]{1,0:T(8,128)}, f32[72,1024]{1,0:T(8,128)S(1)}, u32[]{:S(2)}) copy-start(f32[72,1024]{1,0:T(8,128)S(1)} %collective-permute-done.1.refs_1_.refs_2_) | copy-start | bytes 884740
  40.2 1.9 collective-permute-start.2
  40.7 20.4 %copy-start.11 = (f32[72,1024]{1,0:T(8,128)}, f32[72,1024]{1,0:T(8,128)S(1)}, u32[]{:S(2)}) copy-start(f32[72,1024]{1,0:T(8,128)S(1)} %collective-permute-done.refs_0_.refs_1_) | copy-start | bytes 884740
  41.2 19.9 %copy-start.12 = (f32[72,1024]{1,0:T(8,128)}, f32[72,1024]{1,0:T(8,128)S(1)}, u32[]{:S(2)}) copy-start(f32[72,1024]{1,0:T(8,128)S(1)} %collective-permute-done.6.refs_6_.refs_7_) | copy-start | bytes 884740
  41.6 19.4 %copy-start.13 = (f32[72,1024]{1,0:T(8,128)}, f32[72,1024]{1,0:T(8,128)S(1)}, u32[]{:S(2)}) copy-start(f32[72,1024]{1,0:T(8,128)S(1)} %collective-permute-done.4.refs_4_.refs_5_) | copy-start | bytes 884740
  42.1 19.0 %copy-start.14 = (f32[72,1024]{1,0:T(8,128)}, f32[72,1024]{1,0:T(8,128)S(1)}, u32[]{:S(2)}) copy-start(f32[72,1024]{1,0:T(8,128)S(1)} %collective-permute-done.2.refs_2_.refs_3_) | copy-start | bytes 884740
  42.3 21.5 %copy-start.23 = (f32[2]{0:T(128)}, f32[2]{0:T(128)S(1)}, u32[]{:S(2)}) copy-start(f32[2]{0:T(128)S(1)} %rsqrt.6.scale_ref) | copy-start | bytes 28
  63.8 13.2 %collective-permute-start.10 = (f32[32,3072]{1,0:T(8,128)}, f32[32,3072]{1,0:T(8,128)S(1)}, u32[]{:S(2)}, u32[]{:S(2)}) collective-permute-start(f32[32,3072]{1,0:T(8,128)} %entry_product.4.refs_8_), channel_id=1, source_target_pairs={{0,6},{1,7},{2,4},{3,5},{4,2},{5,3},{6,0},{7,1},{8,14},{9,15},{10,... | collective-permute-start | bytes 1179656 | tf_op jit(solution)/shard_map/ppermute | solution.py:582
  66.1 17.9 %collective-permute-start.9 = (f32[32,3072]{1,0:T(8,128)}, f32[32,3072]{1,0:T(8,128)S(1)}, u32[]{:S(2)}, u32[]{:S(2)}) collective-permute-start(f32[32,3072]{1,0:T(8,128)} %entry_product.4.refs_8_), channel_id=1, source_target_pairs={{0,4},{1,5},{2,6},{3,7},{4,0},{5,1},{6,2},{7,3},{8,12},{9,13},{10,... | collective-permute-start | bytes 1179656 | tf_op jit(solution)/shard_map/ppermute | solution.py:582
  66.7 17.4 %collective-permute-start.8 = (f32[32,3072]{1,0:T(8,128)}, f32[32,3072]{1,0:T(8,128)S(1)}, u32[]{:S(2)}, u32[]{:S(2)}) collective-permute-start(f32[32,3072]{1,0:T(8,128)} %entry_product.4.refs_8_), channel_id=1, source_target_pairs={{0,2},{1,3},{2,0},{3,1},{4,6},{5,7},{6,4},{7,5},{8,10},{9,11},{10,... | collective-permute-start | bytes 1179656 | tf_op jit(solution)/shard_map/ppermute | solution.py:582
  67.3 18.3 %collective-permute-start.7 = (f32[32,3072]{1,0:T(8,128)}, f32[32,3072]{1,0:T(8,128)S(1)}, u32[]{:S(2)}, u32[]{:S(2)}) collective-permute-start(f32[32,3072]{1,0:T(8,128)} %entry_product.4.refs_8_), channel_id=1, source_target_pairs={{0,1},{1,0},{2,3},{3,2},{4,5},{5,4},{6,7},{7,6},{8,9},{9,8},{10,11... | collective-permute-start | bytes 1179656 | tf_op jit(solution)/shard_map/ppermute | solution.py:582
  76.9 7.2 %copy-start.4 = (f32[32,3072]{1,0:T(8,128)}, f32[32,3072]{1,0:T(8,128)S(1)}, u32[]{:S(2)}) copy-start(f32[32,3072]{1,0:T(8,128)S(1)} %collective-permute-done.10.refs_2_) | copy-start | bytes 1179652
  84.0 0.8 copy-start.5
  84.1 0.9 copy-start.6
  85.0 1.9 collective-permute-start.11
  85.1 2.4 %collective-permute-start.12 = (f32[32,3072]{1,0:T(8,128)}, f32[32,3072]{1,0:T(8,128)S(1)}, u32[]{:S(2)}, u32[]{:S(2)}) collective-permute-start(f32[32,3072]{1,0:T(8,128)} %get-tuple-element.41.refs_4_.refs_12_), channel_id=1, source_target_pairs={{0,1},{1,0},{2,3},{3,2},{4,5},{5,4},{6,7},{7,6},{8,9},{9,8},{10,11... | collective-permute-start | bytes 1179656 | tf_op jit(solution)/shard_map/ppermute | solution.py:582
  85.5 2.5 %collective-permute-start.13 = (f32[32,3072]{1,0:T(8,128)}, f32[32,3072]{1,0:T(8,128)S(1)}, u32[]{:S(2)}, u32[]{:S(2)}) collective-permute-start(f32[32,3072]{1,0:T(8,128)} %get-tuple-element.42.refs_6_.refs_14_), channel_id=1, source_target_pairs={{0,1},{1,0},{2,3},{3,2},{4,5},{5,4},{6,7},{7,6},{8,9},{9,8},{10,11... | collective-permute-start | bytes 1179656 | tf_op jit(solution)/shard_map/ppermute | solution.py:582
  85.6 2.4 %copy-start.16 = (f32[32,3072]{1,0:T(8,128)}, f32[32,3072]{1,0:T(8,128)S(1)}, u32[]{:S(2)}) copy-start(f32[32,3072]{1,0:T(8,128)S(1)} %collective-permute-done.7.refs_1_.refs_9_) | copy-start | bytes 1179652
  86.9 1.1 copy-start.20
  87.5 0.7 copy-start.21
  88.0 0.7 copy-start.22
  88.8 52.4 %all-to-all-start = ((f32[8,640,128]{2,1,0:T(8,128)}), f32[8,640,128]{2,1,0:T(8,128)S(1)}, u32[]{:S(2)}, u32[]{:S(2)}) async-start(f32[8,640,128]{2,1,0:T(8,128)} %bitcast.29), calls=%async_computation | async-start | bytes 5242880 | tf_op jit(solution)/shard_map/all_to_all | solution.py:668
  112.2 21.4 %collective-permute-start.17 = (f32[32,3072]{1,0:T(8,128)}, f32[32,3072]{1,0:T(8,128)S(1)}, u32[]{:S(2)}, u32[]{:S(2)}) collective-permute-start(f32[32,3072]{1,0:T(8,128)} %entry_product.5.refs_8_), channel_id=1, source_target_pairs={{0,6},{1,7},{2,4},{3,5},{4,2},{5,3},{6,0},{7,1},{8,14},{9,15},{10,... | collective-permute-start | bytes 1179656 | tf_op jit(solution)/shard_map/ppermute | solution.py:582
  114.9 26.3 %collective-permute-start.16 = (f32[32,3072]{1,0:T(8,128)}, f32[32,3072]{1,0:T(8,128)S(1)}, u32[]{:S(2)}, u32[]{:S(2)}) collective-permute-start(f32[32,3072]{1,0:T(8,128)} %entry_product.5.refs_8_), channel_id=1, source_target_pairs={{0,4},{1,5},{2,6},{3,7},{4,0},{5,1},{6,2},{7,3},{8,12},{9,13},{10,... | collective-permute-start | bytes 1179656 | tf_op jit(solution)/shard_map/ppermute | solution.py:582
  115.4 25.8 %collective-permute-start.15 = (f32[32,3072]{1,0:T(8,128)}, f32[32,3072]{1,0:T(8,128)}, u32[]{:S(2)}, u32[]{:S(2)}) collective-permute-start(f32[32,3072]{1,0:T(8,128)} %entry_product.5.refs_8_), channel_id=1, source_target_pairs={{0,2},{1,3},{2,0},{3,1},{4,6},{5,7},{6,4},{7,5},{8,10},{9,11},{10,... | collective-permute-start | bytes 1179656 | tf_op jit(solution)/shard_map/ppermute | solution.py:582
  123.3 20.1 %collective-permute-start.14 = (f32[32,3072]{1,0:T(8,128)}, f32[32,3072]{1,0:T(8,128)}, u32[]{:S(2)}, u32[]{:S(2)}) collective-permute-start(f32[32,3072]{1,0:T(8,128)} %entry_product.5.refs_8_), channel_id=1, source_target_pairs={{0,1},{1,0},{2,3},{3,2},{4,5},{5,4},{6,7},{7,6},{8,9},{9,8},{10,11... | collective-permute-start | bytes 1179656 | tf_op jit(solution)/shard_map/ppermute | solution.py:582
  133.6 7.6 %copy-start.2 = (f32[32,3072]{1,0:T(8,128)}, f32[32,3072]{1,0:T(8,128)S(1)}, u32[]{:S(2)}) copy-start(f32[32,3072]{1,0:T(8,128)S(1)} %collective-permute-done.17.refs_2_) | copy-start | bytes 1179652
  141.2 0.7 copy-start.3
  141.2 1.6 copy-start
  142.8 1.9 collective-permute-start.18
  142.8 2.5 %collective-permute-start.19 = (f32[32,3072]{1,0:T(8,128)}, f32[32,3072]{1,0:T(8,128)S(1)}, u32[]{:S(2)}, u32[]{:S(2)}) collective-permute-start(f32[32,3072]{1,0:T(8,128)} %get-tuple-element.52.refs_4_.refs_12_), channel_id=1, source_target_pairs={{0,1},{1,0},{2,3},{3,2},{4,5},{5,4},{6,7},{7,6},{8,9},{9,8},{10,11... | collective-permute-start | bytes 1179656 | tf_op jit(solution)/shard_map/ppermute | solution.py:582
  143.3 2.5 %collective-permute-start.20 = (f32[32,3072]{1,0:T(8,128)}, f32[32,3072]{1,0:T(8,128)S(1)}, u32[]{:S(2)}, u32[]{:S(2)}) collective-permute-start(f32[32,3072]{1,0:T(8,128)} %get-tuple-element.53.refs_6_.refs_14_), channel_id=1, source_target_pairs={{0,1},{1,0},{2,3},{3,2},{4,5},{5,4},{6,7},{7,6},{8,9},{9,8},{10,11... | collective-permute-start | bytes 1179656 | tf_op jit(solution)/shard_map/ppermute | solution.py:582
  144.8 1.1 copy-start.17
  145.3 0.8 copy-start.18
  145.9 0.8 copy-start.19
  146.7 36.6 %all-to-all-start.1 = ((f32[8,640,128]{2,1,0:T(8,128)}), f32[8,640,128]{2,1,0:T(8,128)S(1)}, u32[]{:S(2)}, u32[]{:S(2)}) async-start(f32[8,640,128]{2,1,0:T(8,128)} %bitcast.28), calls=%async_computation.1 | async-start | bytes 5242880 | tf_op jit(solution)/shard_map/all_to_all | solution.py:668
  183.2 1.5 copy-start.1
Sparse Core Ops, SparseCore 0:
  22.1 38.9 all-gather.4
  67.4 35.9 all-gather.6

commit v9 on v8

--- a/solution.py
+++ b/solution.py
@@ -175,16 +175,15 @@
 
 ROWS = 16
 HALVES = 2
-TOGETHER = 4
-
-
-def first_section(freq, half, info, templates, strain, first, stage, twist):
-    tmpls = templates.shape[0]
-    pieces, dets, _, rows, piece_len = strain.shape
-    series = tmpls * dets - 1
+TOGETHER = 2
+
+
+def first_section(freq, half, lot, slot, slots, info, templates, strain, first, stage, twist, earlier, after):
+    pieces, _, _, rows, piece_len = strain.shape
+    base, series = lot[0], len(lot)
     groups = COARSE // freq
     table = pl.BlockSpec((2 * LANES, 2 * LANES), lambda i, n: (0, 0))
-    out = (freq, series, 2, groups, rows, LANES)
+    out = (freq, slots, 2, groups, rows, LANES)
     return pl.pallas_call(
         functools.partial(first_kernel, freq),
         grid_spec=pltpu.PrefetchScalarGridSpec(
@@ -192,19 +191,20 @@
             grid=(series,),
             in_specs=[
                 pl.BlockSpec(
-                    (1, 2, rows, N1), lambda i, n: (n[1 + 2 * i], 0, half, 0)
+                    (1, 2, rows, N1), lambda i, n: (n[1 + 2 * (base + i)], 0, half, 0)
                 ),
                 pl.BlockSpec(
-                    (pieces, 1, 2, rows, piece_len), lambda i, n: (0, n[2 + 2 * i], 0, 0, 0)
+                    (pieces, 1, 2, rows, piece_len), lambda i, n: (0, n[2 + 2 * (base + i)], 0, 0, 0)
                 ),
                 table,
                 table,
                 pl.BlockSpec((2 * COARSE, LANES), lambda i, n: (0, 0)),
                 pl.BlockSpec((2, rows, N1), lambda i, n: (0, half, 0)),
-            ],
+            ]
+            + [ANY] * (len(earlier) + len(after)),
             out_specs=[
                 pl.BlockSpec(
-                    (freq, 1, 2, groups, rows, LANES), lambda i, n: (0, i, 0, 0, 0, 0)
+                    (freq, 1, 2, groups, rows, LANES), lambda i, n: (0, slot + i, 0, 0, 0, 0)
                 ),
                 pl.BlockSpec((8, LANES), lambda i, n: (0, 0)),
             ],
@@ -218,12 +218,13 @@
             jax.ShapeDtypeStruct(out, F32),
             jax.ShapeDtypeStruct((8, LANES), F32),
         ],
+        input_output_aliases={7: 0} if earlier else {},
         compiler_params=pltpu.CompilerParams(vmem_limit_bytes=VMEM_LIMIT),
         cost_estimate=pl.CostEstimate(
             flops=60 * series * rows * N1 * LANES, bytes_accessed=16 * MIB, transcendentals=0
         ),
         name="first_section",
-    )(info, templates, strain, first[0], first[1], stage, twist)
+    )(info, templates, strain, first[0], first[1], stage, twist, *earlier, *after)
 
 
 def entry_kernel(steps, banks, which_ref, tmpl_ref, strain_ref, *refs):
@@ -273,14 +274,14 @@
         use(a, z[:LANES], z[LANES:])
 
 
-def second_kernel(freq, halves, info_ref, scale_ref, *refs):
+def second_kernel(freq, base, halves, info_ref, scale_ref, *refs):
     part_refs, (w2h_ref, w2l_ref) = refs[:halves], refs[halves : halves + 2]
     out_ref, hold, order = refs[-3:]
     place = info_ref[0]
     groups, cols = part_refs[0].shape[3:5]
     per = LANES // (halves * cols)
     width = LANES // freq
-    scale = scale_ref[info_ref[1 + 2 * pl.program_id(0)]]
+    scale = scale_ref[info_ref[1 + 2 * (base + pl.program_id(0))]]
 
     def rows_of(p, u):
         tiles = [
@@ -313,23 +314,29 @@
             out_ref[0, 0, p, :, tile(j)] = order[p, j]
 
 
-def second_section(freq, info, scale, parts, second, snr, after):
-    _, series, _, groups, cols, _ = parts[0].shape
+def second_section(freq, lot, info, scale, parts, second, snr, after):
+    parts, firsts = zip(*parts)
+    base, series = lot[0], len(lot)
+    _, _, _, groups, cols, _ = parts[0].shape
     halves = len(parts)
     times = groups * LANES
     smem = pl.BlockSpec(memory_space=pltpu.SMEM)
     table = pl.BlockSpec((FOUR * 2 * LANES, 2 * LANES), lambda i, n: (0, 0))
-    part = pl.BlockSpec(
-        (freq, 1, 2, groups, cols, LANES), lambda i, n: (0, i, 0, 0, 0, 0)
-    )
+
+
+    def part(slot):
+        return pl.BlockSpec(
+            (freq, 1, 2, groups, cols, LANES), lambda i, n: (0, slot + i, 0, 0, 0, 0)
+        )
+
     return pl.pallas_call(
-        functools.partial(second_kernel, freq, halves),
+        functools.partial(second_kernel, freq, base, halves),
         grid_spec=pltpu.PrefetchScalarGridSpec(
             num_scalar_prefetch=1,
             grid=(series,),
-            in_specs=[smem] + [part] * halves + [table, table, ANY] + [ANY] * len(after),
+            in_specs=[smem] + [part(x) for x in firsts] + [table, table, ANY] + [ANY] * len(after),
             out_specs=pl.BlockSpec(
-                (1, 1, 2, times, N2), lambda i, n: (n[1 + 2 * i], n[2 + 2 * i], 0, 0, 0)
+                (1, 1, 2, times, N2), lambda i, n: (n[1 + 2 * (base + i)], n[2 + 2 * (base + i)], 0, 0, 0)
             ),
             scratch_shapes=[
                 pltpu.VMEM((2, groups, N2, LANES), F32),
@@ -599,10 +606,8 @@
     times = N1 // freq
     part = cols // HALVES
 
-    strains = [
-        lax.all_gather(strain[:, :, h * part : (h + 1) * part], "bank", axis=0, tiled=False)
-        for h in range(HALVES)
-    ]
+    slices = [strain[:, :, h * part : (h + 1) * part] for h in range(HALVES)]
+    strains = [lax.all_gather(x, "bank", axis=0, tiled=False) for x in slices]
     first = tuple(jnp.asarray(t) for t in first_table())
     second = tuple(jnp.asarray(t) for t in second_table(cols, HALVES))
     stage = jnp.asarray(stage_table())
@@ -632,7 +637,7 @@
 
     power = (templates[:, 0] ** 2 + templates[:, 1] ** 2).sum(axis=1)
     power = power.reshape(tmpls, NBLK, BLOCK).sum(axis=2)
-    own = [entry_product((0,), banks, 0, w, templates, strain[None], []) for w in which]
+    own = [entry_product((0,), banks, 0, w, templates, strain[None], slices) for w in which]
     wide = own[0].shape[1]
     power = jnp.pad(power.reshape(1, -1), ((0, 7), (0, wide - tmpls * NBLK)))
     own[0] = jnp.concatenate([own[0], power], axis=0)
@@ -655,20 +660,29 @@
         )
     )
 
-    parts, halves = [], []
+    def exchange(x):
+        got = lax.all_to_all(
+            x.reshape(freq, -1, LANES), "freq", split_axis=0, concat_axis=0, tiled=True
+        )
+        return got.reshape(x.shape)
+
+    early = range((tmpls * dets + 1) // 2)
+    late = range(len(early), tmpls * dets - 1)
+    parts, halves, last = [], [], []
     later = tuple(range(1, banks))
     for h in range(HALVES):
         after = [x[0] for x in halves[-1]] if halves else gathered
         half = [entry_product(later, banks, h, w, templates, strains[h], after) for w in which]
         far = [far_pieces(x, freq) for x in half]
-        sent, token = first_section(freq, h, info, templates, strains[h], first, stage, twist)
-        far = [x[:1] + list(handed_on(x[1:], [token] + parts)) for x in far]
+        fixed = info, templates, strains[h], first, stage, twist
+        sent, token = first_section(freq, h, early, 0, len(early), *fixed, [], half)
+        *last, token2 = first_section(
+            freq, h, late, h * len(late), HALVES * len(late), *fixed, last, half
+        )
+        far = [x[:1] + list(handed_on(x[1:], [token, token2] + parts)) for x in far]
         rest = [near_pieces(x, freq) for x in far]
         (ready,) = handed_on([sent], [x for entry in rest for x in entry[1:]])
-        got = lax.all_to_all(
-            ready.reshape(freq, -1, LANES), "freq", split_axis=0, concat_axis=0, tiled=True
-        )
-        parts.append(got.reshape(ready.shape))
+        parts.append(exchange(ready))
         halves.append(
             [
                 bins_first(
@@ -677,6 +691,7 @@
                 for j in range(slots)
             ]
         )
+    last = exchange(handed_on(last, [parts[-1]] + [x[1] for x in halves[-1]])[0])
 
     chi, snr = [], None
     for j in range(slots):
@@ -686,7 +701,10 @@
         )
         chi.append(one)
         snr = series_of if snr is None else snr
-    snr = second_section(freq, info, inv_sigma, parts, second, snr, chi)
+    parts = [(x, 0) for x in parts]
+    snr = second_section(freq, early, info, inv_sigma, parts, second, snr, chi)
+    parts = [(last, h * len(late)) for h in range(HALVES)]
+    snr = second_section(freq, late, info, inv_sigma, parts, second, snr, [])
     return (snr, jnp.stack(chi))
 
 

time: 203 us -> 198 us (0.975)
  waiting for transfers between devices: 50 us -> 30.7 us
  Pallas kernels: 91.3 us -> 99.6 us
  starting transfers between devices: 21.3 us -> 24.8 us
    all_gather x2, waiting for transfers between devices: 16.9 us -> 3.98 us  [per_device(): strains = [lax.all_gather(x, 'bank', axis=0, tiled=False) for x in slices]]
    ppermute x21, waiting for transfers between devices: 33.1 us -> 20.2 us  [swap(): return lax.ppermute(x, 'freq', [(i, i ^ k) for i in range(freq)])]
    all_to_all x2 -> x3, waiting for transfers between devices: 0.01 us -> 6.45 us  [exchange(): lax.all_to_all(x.reshape(freq, -1, LANES), 'freq', split_axis=0, concat_a...]
    pallas_call x2 -> x4, Pallas kernels: 15.2 us -> 20.1 us  [first_section(): pl.pallas_call(functools.partial(first_kernel, freq), grid_spec=pltpu.Pre...]
    all_to_all x2 -> x3, starting transfers between devices: 7.43 us -> 10.9 us  [exchange(): lax.all_to_all(x.reshape(freq, -1, LANES), 'freq', split_axis=0, concat_a...]
    pallas_call x1 -> x2, Pallas kernels: 10.7 us -> 13.8 us  [second_section(): pl.pallas_call(functools.partial(second_kernel, freq, base, halves), grid...]
    unnamed x51 -> x55, local copies, waits for them, and re-layouts: 5.65 us -> 6.32 us
  transfers between devices with their start and end apart: 25 -> 26, of which waited for: 15 -> 16; matrix products, arithmetic and copies ran while one was open for 7% -> 9% of each run, Pallas kernels for 36% -> 48%
where the time goes in v9:
time: 198 us; the launch traced here: 197 us
  Pallas kernels  99.6 us (50%)
  waiting for transfers between devices  30.7 us (16%)
  starting transfers between devices  24.8 us (13%)
  other arithmetic  15.8 us (8%)
  between operations  15.6 us (8%)
  local copies, waits for them, and re-layouts  10.2 us (5%)
    pallas_call x2, Pallas kernels, bins_first(): pl.pallas_call(functools.partial(bins_first_kernel, len(own), banks), gri...  33.4 us
    ppermute x21, waiting for transfers between devices, swap(): return lax.ppermute(x, 'freq', [(i, i ^ k) for i in range(freq)])  20.2 us
    pallas_call x4, Pallas kernels, first_section(): pl.pallas_call(functools.partial(first_kernel, freq), grid_spec=pltpu.Pre...  20.1 us
    pallas_call x1, Pallas kernels, bins_second(): pl.pallas_call(functools.partial(bins_second_kernel, halves), grid_spec=p...  16.7 us
    pallas_call x2, Pallas kernels, second_section(): pl.pallas_call(functools.partial(second_kernel, freq, base, halves), grid...  13.8 us
    ppermute x21, starting transfers between devices, swap(): return lax.ppermute(x, 'freq', [(i, i ^ k) for i in range(freq)])  13.8 us
    all_to_all x3, starting transfers between devices, exchange(): lax.all_to_all(x.reshape(freq, -1, LANES), 'freq', split_axis=0, concat_a...  10.9 us
    pallas_call x3, Pallas kernels, entry_product(): pl.pallas_call(functools.partial(entry_kernel, steps, banks), grid_spec=p...  9.57 us
  transfers between devices with their start and end apart: 26, of which 16 were waited for; matrix products, arithmetic and copies ran while one was open for 9% of the time, Pallas kernels for 48%

profile of v9, /device:TPU:0, one launch (start us, length us, event | category | flops | bytes accessed | tf_op | source)
XLA Modules:
  0.0 196.7 jit_solution(17699486632174494294)
XLA Ops:
  7.2 2.1 %fusion.49 = (f32[3,2,32,512]{3,2,1,0:T(8,128)}, f32[3,2,32,512]{3,2,1,0:T(8,128)}) fusion(f32[3,2,64,512]{3,2,1,0:T(8,128)} %param.10), kind=kLoop, calls=%fused_computation.114 | loop fusion | bytes 1572864 | tf_op jit(solution)/shard_map/slice | solution.py:609
  10.7 1.7 add_reduce_fusion
  12.7 0.6 pad_add_fusion.1.which_ref
  13.3 4.2 %entry_product.3 = f32[64,1024]{1,0:T(8,128)} custom-call(s32[3]{0:T(128)} %pad_add_fusion.1.which_ref, f32[2,2,64,2048]{3,2,1,0:T(8,128)} %tmpl_ref.13, f32[1,3,2,64,512]{4,3,2,1,0:T(8,128)} %bitcast.43, f32[3,2,32,512]{3,2,1,0:T(8,128)} %get-tuple-element.75.refs_0_, f32[3,2,32,512]{3,2,1,0:T(8,128)} %get-tuple-element.74.refs_1_), custom_call_target="tpu_custom_call" | custom-call | flops 1048576 | bytes 1048576 | tf_op jit(solution)/shard_map/entry_product/pallas_call | solution.py:250
  17.5 1.0 select_maximum_fusion.refs_0_
  18.5 4.0 %collective-permute-start.5 = (f32[72,1024]{1,0:T(8,128)S(1)}, f32[72,1024]{1,0:T(8,128)S(1)}, u32[]{:S(2)}, u32[]{:S(2)}) collective-permute-start(f32[72,1024]{1,0:T(8,128)S(1)} %select_maximum_fusion.refs_0_), channel_id=1, source_target_pairs={{0,6},{1,7},{2,4},{3,5},{4,2},{5,3},{6,0},{7,1},{8,14},{9,15},{10,... | collective-permute-start | bytes 884744 | tf_op jit(solution)/shard_map/ppermute | solution.py:589
  22.5 0.5 collective-permute-start.3
  23.5 0.6 pad_add_fusion.4.place_ref
  24.5 1.0 fusion.39
  25.5 0.7 pad_maximum_fusion.4.block_ref
  26.2 0.7 pad_maximum_fusion.3.inner_ref
  26.9 2.1 %fusion.10 = (f32[1,64,2048]{2,1,0:T(8,128)S(1)}, f32[1,64,2048]{2,1,0:T(8,128)S(1)}) fusion(s32[2048]{0:T(1024)S(1)} %fusion.35, s32[64]{0:T(128)S(1)} %iota_add_fusion.1), kind=kLoop, calls=%fused_computation.31 | loop fusion | flops 1835008 | bytes 1057024 | tf_op jit(solution)/shard_map/cos | solution.py:64
  29.0 1.1 pad_maximum_fusion.tw_ref
  30.0 2.1 %fusion.12 = (f32[1,256,256]{2,1,0:T(8,128)S(1)}, f32[1,256,256]{2,1,0:T(8,128)S(1)}, f32[1,256,256]{2,1,0:T(8,128)S(1)}, f32[1,256,256]{2,1,0:T(8,128)S(1)}) fusion(s32[256]{0:T(256)S(1)} %iota_add_fusion, s32[256]{0:T(256)S(1)} %add_add_fusion, s32[256]{0:T(256)S(1)} %fusion.45), kind=kLoop, calls=%fused_computation.34 | loop fusion | flops 1835008 | bytes 1051648 | tf_op jit(solution)/shard_map/cos | solution.py:64
  32.2 6.0 %bank_table.1 = (bf16[4096,512]{1,0:T(8,128)(2,1)}, bf16[4096,512]{1,0:T(8,128)(2,1)}) custom-call(f32[32,2,256]{2,1,0:T(2,128)} %pad_maximum_fusion.4.block_ref, f32[2,64,256]{2,1,0:T(8,128)} %pad_maximum_fusion.3.inner_ref), custom_call_target="tpu_custom_call" | custom-call | flops 1048576 | bytes 1048576 | tf_op jit(solution)/shard_map/bank_table/pallas_call | solution.py:378
  38.2 1.0 pad_maximum_fusion.1
  39.3 0.6 pad_add_fusion.2.info_ref
  39.9 0.6 pad_add_fusion.3.edge_ref
  40.5 0.5 collective-permute-start.6
  41.3 0.5 collective-permute-start.2
  41.9 0.4 collective-permute-done.6.refs_6_.refs_7_
  42.4 0.4 collective-permute-done.4.refs_4_.refs_5_
  42.8 0.3 collective-permute-done.2.refs_2_.refs_3_
  43.4 0.7 dynamic_slice.10
  44.2 1.2 bitcast_multiply_fusion
  45.4 4.0 %all-gather.7.cloned.1.call-done = f32[12,2,32,512]{3,2,1,0:T(8,128)} async-done(((f32[3,2,32,512]{3,2,1,0:T(8,128)}), f32[12,2,32,512]{3,2,1,0:T(8,128)}) %all-gather.7.cloned.1.call-update) | async-done | bytes 1572880 | tf_op jit(solution)/shard_map/all_gather | solution.py:610
  49.4 2.7 %entry_product.4.refs_0_.refs_8_ = f32[32,3072]{1,0:T(8,128)} custom-call(s32[3]{0:T(128)} %pad_add_fusion.1.which_ref, f32[2,2,64,2048]{3,2,1,0:T(8,128)} %tmpl_ref.13, f32[4,3,2,32,512]{4,3,2,1,0:T(8,128)} %bitcast.40, f32[72,1024]{1,0:T(8,128)} %copy-done.12, f32[72,1024]{1,0:T(8,128)} %copy-done.11, f32[72,1024]{1,0:T(8,128)} %copy-done.15, ...), custom_call_target="tpu_custom_call" | custom-call | flops 1048576 | bytes 1048576 | tf_op jit(solution)/shard_map/entry_product/pallas_call | solution.py:250
  52.1 2.4 %collective-permute-start.10 = (f32[32,3072]{1,0:T(8,128)}, f32[32,3072]{1,0:T(8,128)S(1)}, u32[]{:S(2)}, u32[]{:S(2)}) collective-permute-start(f32[32,3072]{1,0:T(8,128)} %entry_product.4.refs_0_.refs_8_), channel_id=1, source_target_pairs={{0,6},{1,7},{2,4},{3,5},{4,2},{5,3},{6,0},{7,1},{8,14},{9,15},{10,... | collective-permute-start | bytes 1179656 | tf_op jit(solution)/shard_map/ppermute | solution.py:589
  54.5 0.5 collective-permute-start.9
  55.1 0.6 collective-permute-start.8
  55.6 4.5 %first_section.4 = (f32[8,4,2,2,32,128]{5,4,3,2,1,0:T(8,128)}, f32[8,128]{1,0:T(8,128)}) custom-call(s32[11]{0:T(128)} %pad_add_fusion.2.info_ref, f32[2,2,64,2048]{3,2,1,0:T(8,128)} %tmpl_ref.13, f32[4,3,2,32,512]{4,3,2,1,0:T(8,128)} %bitcast.41, bf16[256,256]{1,0:T(8,128)(2,1)} %constant.175.clone.wh_ref, bf16[256,256]{1,0:T(8,128)(2,1)} %constant.176.clone.wl_ref, ...), custom_call_target="tpu_custom_call" | custom-call | flops 1006632960 | bytes 16777216 | tf_op jit(solution)/shard_map/first_section/pallas_call | solution.py:187
  60.1 5.6 %first_section.5 = (f32[8,3,2,2,32,128]{5,4,3,2,1,0:T(8,128)}, f32[8,128]{1,0:T(8,128)}) custom-call(s32[11]{0:T(128)} %pad_add_fusion.2.info_ref, f32[2,2,64,2048]{3,2,1,0:T(8,128)} %tmpl_ref.13, f32[4,3,2,32,512]{4,3,2,1,0:T(8,128)} %bitcast.42, bf16[256,256]{1,0:T(8,128)(2,1)} %constant.175.clone.wh_ref, bf16[256,256]{1,0:T(8,128)(2,1)} %constant.176.clone.wl_ref, ...), custom_call_target="tpu_custom_call" | custom-call | flops 1509949440 | bytes 16777216 | tf_op jit(solution)/shard_map/first_section/pallas_call | solution.py:187
  65.8 6.7 %collective-permute-done.9.refs_1_ = f32[32,3072]{1,0:T(8,128)S(1)} collective-permute-done((f32[32,3072]{1,0:T(8,128)}, f32[32,3072]{1,0:T(8,128)S(1)}, u32[]{:S(2)}, u32[]{:S(2)}) %collective-permute-start.9) | collective-permute-done | bytes 393248 | tf_op jit(solution)/shard_map/ppermute | solution.py:589
  72.5 0.7 copy-done.4
  73.4 0.4 collective-permute-start.12
  73.9 1.3 collective-permute-done.11.refs_3_.refs_11_
  75.2 0.6 collective-permute-done.12.refs_5_.refs_13_
  75.8 0.6 collective-permute-done.13.refs_7_.refs_15_
  76.6 0.6 copy-done.24
  77.1 3.8 %all-to-all-start = ((f32[8,384,128]{2,1,0:T(8,128)}), f32[8,384,128]{2,1,0:T(8,128)S(1)}, u32[]{:S(2)}, u32[]{:S(2)}) async-start(f32[8,384,128]{2,1,0:T(8,128)} %bitcast.36), calls=%async_computation | async-start | bytes 3145728 | tf_op jit(solution)/shard_map/all_to_all | solution.py:664
  80.9 16.7 %bins_first.2 = (f32[16,2,256,256]{3,2,1,0:T(8,128)}, f32[2,256,256]{2,1,0:T(8,128)}) custom-call(s32[2]{0:T(128)} %pad_add_fusion.4.place_ref, s32[17]{0:T(128)} %pad_add_fusion.3.edge_ref, f32[72,1024]{1,0:T(8,128)} %copy-done.16, f32[72,1024]{1,0:T(8,128)} %copy-done.12, f32[72,1024]{1,0:T(8,128)} %copy-done.11, f32[72,1024]{1,0:T(8,128)} %copy-done.15, ...), custom_call_target="tpu_custom_call" | custom-call | flops 1048576 | bytes 1048576 | tf_op jit(solution)/shard_map/bins_first/pallas_call | solution.py:462
  97.6 2.7 %entry_product.5.refs_1_.refs_0_.refs_8_ = f32[32,3072]{1,0:T(8,128)} custom-call(s32[3]{0:T(128)} %pad_add_fusion.1.which_ref, f32[2,2,64,2048]{3,2,1,0:T(8,128)} %tmpl_ref.13, f32[4,3,2,32,512]{4,3,2,1,0:T(8,128)} %bitcast.37, f32[16,2,256,256]{3,2,1,0:T(8,128)} %get-tuple-element.54.refs_0_), custom_call_target="tpu_custom_call" | custom-call | flops 1048576 | bytes 1048576 | tf_op jit(solution)/shard_map/entry_product/pallas_call | solution.py:250
  100.3 2.7 %collective-permute-start.17 = (f32[32,3072]{1,0:T(8,128)}, f32[32,3072]{1,0:T(8,128)S(1)}, u32[]{:S(2)}, u32[]{:S(2)}) collective-permute-start(f32[32,3072]{1,0:T(8,128)} %entry_product.5.refs_1_.refs_0_.refs_8_), channel_id=1, source_target_pairs={{0,6},{1,7},{2,4},{3,5},{4,2},{5,3},{6,0},{7,1},{8,14},{9,15},{10,... | collective-permute-start | bytes 1179656 | tf_op jit(solution)/shard_map/ppermute | solution.py:589
  103.0 0.5 collective-permute-start.16
  103.8 4.4 %first_section.6 = (f32[8,4,2,2,32,128]{5,4,3,2,1,0:T(8,128)}, f32[8,128]{1,0:T(8,128)}) custom-call(s32[11]{0:T(128)} %pad_add_fusion.2.info_ref, f32[2,2,64,2048]{3,2,1,0:T(8,128)} %tmpl_ref.13, f32[4,3,2,32,512]{4,3,2,1,0:T(8,128)} %bitcast.38, bf16[256,256]{1,0:T(8,128)(2,1)} %constant.175.clone.wh_ref, ...), custom_call_target="tpu_custom_call", output_to_operand_aliasing={{0}: (7, {})} | custom-call | flops 1006632960 | bytes 16777216 | tf_op jit(solution)/shard_map/first_section/pallas_call | solution.py:187
  108.2 5.6 %first_section.7 = (f32[8,3,2,2,32,128]{5,4,3,2,1,0:T(8,128)}, f32[8,128]{1,0:T(8,128)}) custom-call(s32[11]{0:T(128)} %pad_add_fusion.2.info_ref, f32[2,2,64,2048]{3,2,1,0:T(8,128)} %tmpl_ref.13, f32[4,3,2,32,512]{4,3,2,1,0:T(8,128)} %bitcast.39, bf16[256,256]{1,0:T(8,128)(2,1)} %constant.175.clone.wh_ref, bf16[256,256]{1,0:T(8,128)(2,1)} %constant.176.clone.wl_ref, ...), custom_call_target="tpu_custom_call" | custom-call | flops 1509949440 | bytes 16777216 | tf_op jit(solution)/shard_map/first_section/pallas_call | solution.py:187
  113.8 7.2 %collective-permute-done.16.refs_1_ = f32[32,3072]{1,0:T(8,128)S(1)} collective-permute-done((f32[32,3072]{1,0:T(8,128)}, f32[32,3072]{1,0:T(8,128)S(1)}, u32[]{:S(2)}, u32[]{:S(2)}) %collective-permute-start.16) | collective-permute-done | bytes 393248 | tf_op jit(solution)/shard_map/ppermute | solution.py:589
  121.3 0.5 copy-done.7
  122.1 0.5 copy-done.1
  122.6 0.5 collective-permute-start.19
  123.1 1.4 collective-permute-done.18.refs_3_.refs_11_
  124.6 0.6 collective-permute-done.19.refs_5_.refs_13_
  125.1 0.6 collective-permute-done.20.refs_7_.refs_15_
  125.9 0.6 copy-done.21
  126.5 3.6 %all-to-all-start.1 = ((f32[8,384,128]{2,1,0:T(8,128)}), f32[8,384,128]{2,1,0:T(8,128)S(1)}, u32[]{:S(2)}, u32[]{:S(2)}) async-start(f32[8,384,128]{2,1,0:T(8,128)} %bitcast.35), calls=%async_computation.1 | async-start | bytes 3145728 | tf_op jit(solution)/shard_map/all_to_all | solution.py:664
  130.0 16.7 %bins_first.3 = (f32[16,2,256,256]{3,2,1,0:T(8,128)}, f32[2,256,256]{2,1,0:T(8,128)}) custom-call(s32[2]{0:T(128)} %pad_add_fusion.4.place_ref, s32[17]{0:T(128)} %pad_add_fusion.3.edge_ref, f32[72,1024]{1,0:T(8,128)} %copy-done.16, f32[72,1024]{1,0:T(8,128)} %copy-done.12, f32[72,1024]{1,0:T(8,128)} %copy-done.11, f32[72,1024]{1,0:T(8,128)} %copy-done.15, ...), custom_call_target="tpu_custom_call" | custom-call | flops 1048576 | bytes 1048576 | tf_op jit(solution)/shard_map/bins_first/pallas_call | solution.py:462
  146.8 4.2 %all-to-all-done.1 = f32[8,384,128]{2,1,0:T(8,128)S(1)} async-done(((f32[8,384,128]{2,1,0:T(8,128)}), f32[8,384,128]{2,1,0:T(8,128)S(1)}, u32[]{:S(2)}, u32[]{:S(2)}) %all-to-all-start.1) | async-done | bytes 1572896 | tf_op jit(solution)/shard_map/all_to_all | solution.py:664
  151.0 1.2 copy-done.2
  152.2 3.6 %all-to-all-start.2 = ((f32[8,512,128]{2,1,0:T(8,128)}), f32[8,512,128]{2,1,0:T(8,128)S(1)}, u32[]{:S(2)}, u32[]{:S(2)}) async-start(f32[8,512,128]{2,1,0:T(8,128)} %bitcast.30), calls=%async_computation.2 | async-start | bytes 4194304 | tf_op jit(solution)/shard_map/all_to_all | solution.py:664
  155.8 16.7 %bins_second.1 = (f32[256,512]{1,0:T(8,128)}, f32[2,3,2,256,512]{4,3,2,1,0:T(8,128)}) custom-call(s32[3]{0:T(128)} %pad_add_fusion.1.which_ref, f32[2]{0:T(128)} %copy-done.25, f32[16]{0:T(128)} %get-tuple-element.64.gain_ref, f32[16]{0:T(128)} %get-tuple-element.65.share_ref, f32[16,2,256,256]{3,2,1,0:T(8,128)} %get-tuple-element.54.refs_0_, ...), custom_call_target="tpu_custom_call" | custom-call | flops 1048576 | bytes 1048576 | tf_op jit(solution)/shard_map/bins_second/pallas_call | solution.py:546
  172.5 7.7 %second_section.2.refs_4_ = f32[2,3,2,256,512]{4,3,2,1,0:T(8,128)} custom-call(s32[11]{0:T(128)} %pad_add_fusion.2.info_ref, f32[2]{0:T(128)} %copy-done.25, f32[8,3,2,2,32,128]{5,4,3,2,1,0:T(8,128)} %bitcast.32, f32[8,3,2,2,32,128]{5,4,3,2,1,0:T(8,128)} %bitcast.34, ...), custom_call_target="tpu_custom_call", output_to_operand_aliasing={{}: (6, {})} | custom-call | flops 1048576 | bytes 1048576 | tf_op jit(solution)/shard_map/second_section/pallas_call | solution.py:332
  180.2 2.2 %all-to-all-done.2 = f32[8,512,128]{2,1,0:T(8,128)S(1)} async-done(((f32[8,512,128]{2,1,0:T(8,128)}), f32[8,512,128]{2,1,0:T(8,128)S(1)}, u32[]{:S(2)}, u32[]{:S(2)}) %all-to-all-start.2) | async-done | bytes 2097184 | tf_op jit(solution)/shard_map/all_to_all | solution.py:664
  182.4 1.4 copy-done
  183.7 6.1 %second_section.3 = f32[2,3,2,256,512]{4,3,2,1,0:T(8,128)} custom-call(s32[11]{0:T(128)} %pad_add_fusion.2.info_ref, f32[2]{0:T(128)} %copy-done.25, f32[8,4,2,2,32,128]{5,4,3,2,1,0:T(8,128)} %bitcast.28, f32[8,4,2,2,32,128]{5,4,3,2,1,0:T(8,128)} %bitcast.29, bf16[1024,256]{1,0:T(8,128)(2,1)} %constant.177.clone.refs_4_.refs_2_, ...), custom_call_target="tpu_custom_call", output_to_operand_aliasing={{}: (6, {})} | custom-call | flops 1048576 | bytes 1048576 | tf_op jit(solution)/shard_map/second_section/pallas_call | solution.py:332
  (113 shorter events, 4.1 us)
Async XLA Ops:
  7.2 42.2 %all-gather.7.cloned.1.call-start = ((), (), s32[]{:S(2)}) async-start(), calls=%async_computation.4 | async-start | bytes 1966080 | tf_op jit(solution)/shard_map/all_gather | solution.py:610
  9.4 88.2 %all-gather.5.cloned.1.call-start = ((), (), s32[]{:S(2)}) async-start(), calls=%async_computation.3 | async-start | bytes 1966080 | tf_op jit(solution)/shard_map/all_gather | solution.py:610
  13.3 11.0 %copy-start.26 = (s32[2,15]{1,0:T(2,128)S(1)}, s32[2,15]{1,0:T(2,128)}, u32[]{:S(2)}) copy-start(s32[2,15]{1,0:T(2,128)} %param.14) | copy-start | bytes 364
  18.5 11.6 %copy-start.16 = (f32[72,1024]{1,0:T(8,128)}, f32[72,1024]{1,0:T(8,128)S(1)}, u32[]{:S(2)}) copy-start(f32[72,1024]{1,0:T(8,128)S(1)} %select_maximum_fusion.refs_0_) | copy-start | bytes 884740
  18.5 21.9 %collective-permute-start.5 = (f32[72,1024]{1,0:T(8,128)S(1)}, f32[72,1024]{1,0:T(8,128)S(1)}, u32[]{:S(2)}, u32[]{:S(2)}) collective-permute-start(f32[72,1024]{1,0:T(8,128)S(1)} %select_maximum_fusion.refs_0_), channel_id=1, source_target_pairs={{0,6},{1,7},{2,4},{3,5},{4,2},{5,3},{6,0},{7,1},{8,14},{9,15},{10,... | collective-permute-start | bytes 884744 | tf_op jit(solution)/shard_map/ppermute | solution.py:589
  22.5 18.6 %collective-permute-start.3 = (f32[72,1024]{1,0:T(8,128)S(1)}, f32[72,1024]{1,0:T(8,128)S(1)}, u32[]{:S(2)}, u32[]{:S(2)}) collective-permute-start(f32[72,1024]{1,0:T(8,128)S(1)} %select_maximum_fusion.refs_0_), channel_id=1, source_target_pairs={{0,4},{1,5},{2,6},{3,7},{4,0},{5,1},{6,2},{7,3},{8,12},{9,13},{10,... | collective-permute-start | bytes 884744 | tf_op jit(solution)/shard_map/ppermute | solution.py:589
  23.0 18.2 %collective-permute-start.1 = (f32[72,1024]{1,0:T(8,128)S(1)}, f32[72,1024]{1,0:T(8,128)S(1)}, u32[]{:S(2)}, u32[]{:S(2)}) collective-permute-start(f32[72,1024]{1,0:T(8,128)S(1)} %select_maximum_fusion.refs_0_), channel_id=1, source_target_pairs={{0,2},{1,3},{2,0},{3,1},{4,6},{5,7},{6,4},{7,5},{8,10},{9,11},{10,... | collective-permute-start | bytes 884744 | tf_op jit(solution)/shard_map/ppermute | solution.py:589
  23.1 18.7 %collective-permute-start = (f32[72,1024]{1,0:T(8,128)S(1)}, f32[72,1024]{1,0:T(8,128)S(1)}, u32[]{:S(2)}, u32[]{:S(2)}) collective-permute-start(f32[72,1024]{1,0:T(8,128)S(1)} %select_maximum_fusion.refs_0_), channel_id=1, source_target_pairs={{0,1},{1,0},{2,3},{3,2},{4,5},{5,4},{6,7},{7,6},{8,9},{9,8},{10,11... | collective-permute-start | bytes 884744 | tf_op jit(solution)/shard_map/ppermute | solution.py:589
  40.4 9.0 %copy-start.9 = (f32[72,1024]{1,0:T(8,128)}, f32[72,1024]{1,0:T(8,128)S(1)}, u32[]{:S(2)}) copy-start(f32[72,1024]{1,0:T(8,128)S(1)} %collective-permute-done.5.refs_5_.refs_6_) | copy-start | bytes 884740
  40.5 1.7 collective-permute-start.6
  41.0 8.4 %copy-start.10 = (f32[72,1024]{1,0:T(8,128)}, f32[72,1024]{1,0:T(8,128)S(1)}, u32[]{:S(2)}) copy-start(f32[72,1024]{1,0:T(8,128)S(1)} %collective-permute-done.3.refs_3_.refs_4_) | copy-start | bytes 884740
  41.1 1.6 collective-permute-start.4
  41.2 8.2 %copy-start.11 = (f32[72,1024]{1,0:T(8,128)}, f32[72,1024]{1,0:T(8,128)S(1)}, u32[]{:S(2)}) copy-start(f32[72,1024]{1,0:T(8,128)S(1)} %collective-permute-done.1.refs_1_.refs_2_) | copy-start | bytes 884740
  41.3 1.9 collective-permute-start.2
  41.8 7.6 %copy-start.12 = (f32[72,1024]{1,0:T(8,128)}, f32[72,1024]{1,0:T(8,128)S(1)}, u32[]{:S(2)}) copy-start(f32[72,1024]{1,0:T(8,128)S(1)} %collective-permute-done.refs_0_.refs_1_) | copy-start | bytes 884740
  42.2 7.2 %copy-start.13 = (f32[72,1024]{1,0:T(8,128)}, f32[72,1024]{1,0:T(8,128)S(1)}, u32[]{:S(2)}) copy-start(f32[72,1024]{1,0:T(8,128)S(1)} %collective-permute-done.6.refs_6_.refs_7_) | copy-start | bytes 884740
  42.7 6.7 %copy-start.14 = (f32[72,1024]{1,0:T(8,128)}, f32[72,1024]{1,0:T(8,128)S(1)}, u32[]{:S(2)}) copy-start(f32[72,1024]{1,0:T(8,128)S(1)} %collective-permute-done.4.refs_4_.refs_5_) | copy-start | bytes 884740
  43.2 6.3 %copy-start.15 = (f32[72,1024]{1,0:T(8,128)}, f32[72,1024]{1,0:T(8,128)S(1)}, u32[]{:S(2)}) copy-start(f32[72,1024]{1,0:T(8,128)S(1)} %collective-permute-done.2.refs_2_.refs_3_) | copy-start | bytes 884740
  43.4 8.7 %copy-start.25 = (f32[2]{0:T(128)}, f32[2]{0:T(128)S(1)}, u32[]{:S(2)}) copy-start(f32[2]{0:T(128)S(1)} %rsqrt.6.scale_ref) | copy-start | bytes 28
  52.1 13.6 %collective-permute-start.10 = (f32[32,3072]{1,0:T(8,128)}, f32[32,3072]{1,0:T(8,128)S(1)}, u32[]{:S(2)}, u32[]{:S(2)}) collective-permute-start(f32[32,3072]{1,0:T(8,128)} %entry_product.4.refs_0_.refs_8_), channel_id=1, source_target_pairs={{0,6},{1,7},{2,4},{3,5},{4,2},{5,3},{6,0},{7,1},{8,14},{9,15},{10,... | collective-permute-start | bytes 1179656 | tf_op jit(solution)/shard_map/ppermute | solution.py:589
  54.5 17.9 %collective-permute-start.9 = (f32[32,3072]{1,0:T(8,128)}, f32[32,3072]{1,0:T(8,128)S(1)}, u32[]{:S(2)}, u32[]{:S(2)}) collective-permute-start(f32[32,3072]{1,0:T(8,128)} %entry_product.4.refs_0_.refs_8_), channel_id=1, source_target_pairs={{0,4},{1,5},{2,6},{3,7},{4,0},{5,1},{6,2},{7,3},{8,12},{9,13},{10,... | collective-permute-start | bytes 1179656 | tf_op jit(solution)/shard_map/ppermute | solution.py:589
  55.1 17.4 %collective-permute-start.8 = (f32[32,3072]{1,0:T(8,128)}, f32[32,3072]{1,0:T(8,128)S(1)}, u32[]{:S(2)}, u32[]{:S(2)}) collective-permute-start(f32[32,3072]{1,0:T(8,128)} %entry_product.4.refs_0_.refs_8_), channel_id=1, source_target_pairs={{0,2},{1,3},{2,0},{3,1},{4,6},{5,7},{6,4},{7,5},{8,10},{9,11},{10,... | collective-permute-start | bytes 1179656 | tf_op jit(solution)/shard_map/ppermute | solution.py:589
  55.6 18.3 %collective-permute-start.7 = (f32[32,3072]{1,0:T(8,128)}, f32[32,3072]{1,0:T(8,128)S(1)}, u32[]{:S(2)}, u32[]{:S(2)}) collective-permute-start(f32[32,3072]{1,0:T(8,128)} %entry_product.4.refs_0_.refs_8_), channel_id=1, source_target_pairs={{0,1},{1,0},{2,3},{3,2},{4,5},{5,4},{6,7},{7,6},{8,9},{9,8},{10,11... | collective-permute-start | bytes 1179656 | tf_op jit(solution)/shard_map/ppermute | solution.py:589
  65.7 6.7 %copy-start.3 = (f32[32,3072]{1,0:T(8,128)}, f32[32,3072]{1,0:T(8,128)S(1)}, u32[]{:S(2)}) copy-start(f32[32,3072]{1,0:T(8,128)S(1)} %collective-permute-done.10.refs_2_) | copy-start | bytes 1179652
  72.4 0.8 copy-start.4
  72.5 0.8 copy-start.5
  73.3 1.9 collective-permute-start.11
  73.4 2.4 %collective-permute-start.12 = (f32[32,3072]{1,0:T(8,128)}, f32[32,3072]{1,0:T(8,128)S(1)}, u32[]{:S(2)}, u32[]{:S(2)}) collective-permute-start(f32[32,3072]{1,0:T(8,128)} %get-tuple-element.48.refs_4_.refs_12_), channel_id=1, source_target_pairs={{0,1},{1,0},{2,3},{3,2},{4,5},{5,4},{6,7},{7,6},{8,9},{9,8},{10,11... | collective-permute-start | bytes 1179656 | tf_op jit(solution)/shard_map/ppermute | solution.py:589
  73.8 2.5 %collective-permute-start.13 = (f32[32,3072]{1,0:T(8,128)}, f32[32,3072]{1,0:T(8,128)S(1)}, u32[]{:S(2)}, u32[]{:S(2)}) collective-permute-start(f32[32,3072]{1,0:T(8,128)} %get-tuple-element.49.refs_6_.refs_14_), channel_id=1, source_target_pairs={{0,1},{1,0},{2,3},{3,2},{4,5},{5,4},{6,7},{7,6},{8,9},{9,8},{10,11... | collective-permute-start | bytes 1179656 | tf_op jit(solution)/shard_map/ppermute | solution.py:589
  73.9 2.4 %copy-start.18 = (f32[32,3072]{1,0:T(8,128)}, f32[32,3072]{1,0:T(8,128)S(1)}, u32[]{:S(2)}) copy-start(f32[32,3072]{1,0:T(8,128)S(1)} %collective-permute-done.7.refs_1_.refs_9_) | copy-start | bytes 1179652
  75.2 1.1 copy-start.22
  75.8 0.8 copy-start.23
  76.3 0.8 copy-start.24
  77.1 44.2 %all-to-all-start = ((f32[8,384,128]{2,1,0:T(8,128)}), f32[8,384,128]{2,1,0:T(8,128)S(1)}, u32[]{:S(2)}, u32[]{:S(2)}) async-start(f32[8,384,128]{2,1,0:T(8,128)} %bitcast.36), calls=%async_computation | async-start | bytes 3145728 | tf_op jit(solution)/shard_map/all_to_all | solution.py:664
  100.3 13.5 %collective-permute-start.17 = (f32[32,3072]{1,0:T(8,128)}, f32[32,3072]{1,0:T(8,128)S(1)}, u32[]{:S(2)}, u32[]{:S(2)}) collective-permute-start(f32[32,3072]{1,0:T(8,128)} %entry_product.5.refs_1_.refs_0_.refs_8_), channel_id=1, source_target_pairs={{0,6},{1,7},{2,4},{3,5},{4,2},{5,3},{6,0},{7,1},{8,14},{9,15},{10,... | collective-permute-start | bytes 1179656 | tf_op jit(solution)/shard_map/ppermute | solution.py:589
  103.0 18.1 %collective-permute-start.16 = (f32[32,3072]{1,0:T(8,128)}, f32[32,3072]{1,0:T(8,128)S(1)}, u32[]{:S(2)}, u32[]{:S(2)}) collective-permute-start(f32[32,3072]{1,0:T(8,128)} %entry_product.5.refs_1_.refs_0_.refs_8_), channel_id=1, source_target_pairs={{0,4},{1,5},{2,6},{3,7},{4,0},{5,1},{6,2},{7,3},{8,12},{9,13},{10,... | collective-permute-start | bytes 1179656 | tf_op jit(solution)/shard_map/ppermute | solution.py:589
  103.5 17.8 %collective-permute-start.15 = (f32[32,3072]{1,0:T(8,128)}, f32[32,3072]{1,0:T(8,128)S(1)}, u32[]{:S(2)}, u32[]{:S(2)}) collective-permute-start(f32[32,3072]{1,0:T(8,128)} %entry_product.5.refs_1_.refs_0_.refs_8_), channel_id=1, source_target_pairs={{0,2},{1,3},{2,0},{3,1},{4,6},{5,7},{6,4},{7,5},{8,10},{9,11},{10,... | collective-permute-start | bytes 1179656 | tf_op jit(solution)/shard_map/ppermute | solution.py:589
  103.8 19.3 %collective-permute-start.14 = (f32[32,3072]{1,0:T(8,128)}, f32[32,3072]{1,0:T(8,128)S(1)}, u32[]{:S(2)}, u32[]{:S(2)}) collective-permute-start(f32[32,3072]{1,0:T(8,128)} %entry_product.5.refs_1_.refs_0_.refs_8_), channel_id=1, source_target_pairs={{0,1},{1,0},{2,3},{3,2},{4,5},{5,4},{6,7},{7,6},{8,9},{9,8},{10,11... | collective-permute-start | bytes 1179656 | tf_op jit(solution)/shard_map/ppermute | solution.py:589
  113.8 7.5 %copy-start.6 = (f32[32,3072]{1,0:T(8,128)}, f32[32,3072]{1,0:T(8,128)S(1)}, u32[]{:S(2)}) copy-start(f32[32,3072]{1,0:T(8,128)S(1)} %collective-permute-done.17.refs_2_) | copy-start | bytes 1179652
  121.1 0.7 copy-start.7
  121.3 0.8 copy-start.8
  121.3 1.3 copy-start.1
  122.6 1.9 collective-permute-start.18
  122.6 2.5 %collective-permute-start.19 = (f32[32,3072]{1,0:T(8,128)}, f32[32,3072]{1,0:T(8,128)S(1)}, u32[]{:S(2)}, u32[]{:S(2)}) collective-permute-start(f32[32,3072]{1,0:T(8,128)} %get-tuple-element.60.refs_4_.refs_12_), channel_id=1, source_target_pairs={{0,1},{1,0},{2,3},{3,2},{4,5},{5,4},{6,7},{7,6},{8,9},{9,8},{10,11... | collective-permute-start | bytes 1179656 | tf_op jit(solution)/shard_map/ppermute | solution.py:589
  123.1 2.5 %collective-permute-start.20 = (f32[32,3072]{1,0:T(8,128)}, f32[32,3072]{1,0:T(8,128)S(1)}, u32[]{:S(2)}, u32[]{:S(2)}) collective-permute-start(f32[32,3072]{1,0:T(8,128)} %get-tuple-element.61.refs_6_.refs_14_), channel_id=1, source_target_pairs={{0,1},{1,0},{2,3},{3,2},{4,5},{5,4},{6,7},{7,6},{8,9},{9,8},{10,11... | collective-permute-start | bytes 1179656 | tf_op jit(solution)/shard_map/ppermute | solution.py:589
  123.1 2.5 %copy-start.17 = (f32[32,3072]{1,0:T(8,128)}, f32[32,3072]{1,0:T(8,128)S(1)}, u32[]{:S(2)}) copy-start(f32[32,3072]{1,0:T(8,128)S(1)} %collective-permute-done.14.refs_1_.refs_9_) | copy-start | bytes 1179652
  124.6 1.1 copy-start.19
  125.1 0.8 copy-start.20
  125.7 0.8 copy-start.21
  126.5 24.5 %all-to-all-start.1 = ((f32[8,384,128]{2,1,0:T(8,128)}), f32[8,384,128]{2,1,0:T(8,128)S(1)}, u32[]{:S(2)}, u32[]{:S(2)}) async-start(f32[8,384,128]{2,1,0:T(8,128)} %bitcast.35), calls=%async_computation.1 | async-start | bytes 3145728 | tf_op jit(solution)/shard_map/all_to_all | solution.py:664
  151.0 1.2 copy-start.2
  152.2 30.2 %all-to-all-start.2 = ((f32[8,512,128]{2,1,0:T(8,128)}), f32[8,512,128]{2,1,0:T(8,128)S(1)}, u32[]{:S(2)}, u32[]{:S(2)}) async-start(f32[8,512,128]{2,1,0:T(8,128)} %bitcast.30), calls=%async_computation.2 | async-start | bytes 4194304 | tf_op jit(solution)/shard_map/all_to_all | solution.py:664
  182.4 1.4 copy-start
Sparse Core Ops, SparseCore 0:
  9.6 39.7 all-gather.6
  51.0 35.9 all-gather.4

commit v10 on v8

--- a/solution.py
+++ b/solution.py
@@ -174,17 +174,17 @@
 
 
 ROWS = 16
-HALVES = 2
-TOGETHER = 4
-
-
-def first_section(freq, half, info, templates, strain, first, stage, twist):
-    tmpls = templates.shape[0]
+LOTS = 2
+TOGETHER = 2
+
+
+def first_section(freq, start, info, templates, strain, first, stage, twist, earlier, after):
+    tmpls, _, cols, _ = templates.shape
     pieces, dets, _, rows, piece_len = strain.shape
-    series = tmpls * dets - 1
+    block, series = start // rows, tmpls * dets - 1
     groups = COARSE // freq
     table = pl.BlockSpec((2 * LANES, 2 * LANES), lambda i, n: (0, 0))
-    out = (freq, series, 2, groups, rows, LANES)
+    out = (freq, series, 2, groups, cols, LANES)
     return pl.pallas_call(
         functools.partial(first_kernel, freq),
         grid_spec=pltpu.PrefetchScalarGridSpec(
@@ -192,19 +192,20 @@
             grid=(series,),
             in_specs=[
                 pl.BlockSpec(
-                    (1, 2, rows, N1), lambda i, n: (n[1 + 2 * i], 0, half, 0)
+                    (1, 2, rows, N1), lambda i, n: (n[1 + 2 * (i)], 0, block, 0)
                 ),
                 pl.BlockSpec(
-                    (pieces, 1, 2, rows, piece_len), lambda i, n: (0, n[2 + 2 * i], 0, 0, 0)
+                    (pieces, 1, 2, rows, piece_len), lambda i, n: (0, n[2 + 2 * (i)], 0, 0, 0)
                 ),
                 table,
                 table,
                 pl.BlockSpec((2 * COARSE, LANES), lambda i, n: (0, 0)),
-                pl.BlockSpec((2, rows, N1), lambda i, n: (0, half, 0)),
-            ],
+                pl.BlockSpec((2, rows, N1), lambda i, n: (0, block, 0)),
+            ]
+            + [ANY] * (len(earlier) + len(after)),
             out_specs=[
                 pl.BlockSpec(
-                    (freq, 1, 2, groups, rows, LANES), lambda i, n: (0, i, 0, 0, 0, 0)
+                    (freq, 1, 2, groups, rows, LANES), lambda i, n: (0, i, 0, 0, block, 0)
                 ),
                 pl.BlockSpec((8, LANES), lambda i, n: (0, 0)),
             ],
@@ -218,12 +219,13 @@
             jax.ShapeDtypeStruct(out, F32),
             jax.ShapeDtypeStruct((8, LANES), F32),
         ],
+        input_output_aliases={7: 0} if earlier else {},
         compiler_params=pltpu.CompilerParams(vmem_limit_bytes=VMEM_LIMIT),
         cost_estimate=pl.CostEstimate(
             flops=60 * series * rows * N1 * LANES, bytes_accessed=16 * MIB, transcendentals=0
         ),
         name="first_section",
-    )(info, templates, strain, first[0], first[1], stage, twist)
+    )(info, templates, strain, first[0], first[1], stage, twist, *earlier, *after)
 
 
 def entry_kernel(steps, banks, which_ref, tmpl_ref, strain_ref, *refs):
@@ -243,9 +245,9 @@
             out_ref[:, tile(to + 1)] = jnp.where(first_half, pltpu.roll(re, BLOCK, 1), im)
 
 
-def entry_product(steps, banks, half, which, templates, strain, after):
+def entry_product(steps, banks, start, which, templates, strain, after):
     pieces, _, _, cols, length = strain.shape
-    first = half * cols // ROWS
+    first = start // ROWS
     return pl.pallas_call(
         functools.partial(entry_kernel, steps, banks),
         grid_spec=pltpu.PrefetchScalarGridSpec(
@@ -319,6 +321,8 @@
     times = groups * LANES
     smem = pl.BlockSpec(memory_space=pltpu.SMEM)
     table = pl.BlockSpec((FOUR * 2 * LANES, 2 * LANES), lambda i, n: (0, 0))
+
+
     part = pl.BlockSpec(
         (freq, 1, 2, groups, cols, LANES), lambda i, n: (0, i, 0, 0, 0, 0)
     )
@@ -384,31 +388,39 @@
 
 
 def bins_first_kernel(pieces, banks, place_ref, edge_ref, *refs):
-    own_refs, rest_refs = refs[:pieces], refs[pieces : 2 * pieces]
-    wh_ref, wl_ref, tw_ref = refs[2 * pieces : 2 * pieces + 3]
+    lots = LOTS
+    own_refs, rest_refs = refs[:pieces], refs[pieces : (1 + lots) * pieces]
+    wh_ref, wl_ref, tw_ref = refs[(1 + lots) * pieces :][:3]
     level_ref, total_ref, xh, xl, acc = refs[-5:]
     times = total_ref.shape[-1]
-    cols = own_refs[0].shape[0]
+    cols = total_ref.shape[1] // pieces
     length = 2 * N1 // banks
     chunk = FOUR * LANES
     step = pl.program_id(0)
 
+    def put(ref, row, lane, to):
+        def cut(i, carry):
+            at = pl.ds(pl.multiple_of(lane + i * chunk, chunk), chunk)
+            there = pl.ds(pl.multiple_of(to + i * chunk, chunk), chunk)
+            xh[row, there], xl[row, there] = split(ref[:, at])
+            return carry
+
+        lax.fori_loop(0, length // chunk, cut, 0)
+
     @pl.when(step == 0)
     def _():
         for k in range(pieces):
-            row = pl.ds(pl.multiple_of((place_ref[0] ^ k) * cols, cols), cols)
-            for n in range(banks):
-                ref = rest_refs[k] if n else own_refs[k]
-                start = lax.rem(place_ref[1] + n, banks) * length
-
-                def cut(i, carry):
-                    lane = max(n - 1, 0) * length + i * chunk
-                    x = ref[:, pl.ds(pl.multiple_of(lane, chunk), chunk)]
-                    to = pl.ds(pl.multiple_of(start + i * chunk, chunk), chunk)
-                    xh[row, to], xl[row, to] = split(x)
-                    return carry
-
-                lax.fori_loop(0, length // chunk, cut, 0)
+            base = (place_ref[0] ^ k) * cols
+            row = pl.ds(pl.multiple_of(base, ROWS), cols)
+            put(own_refs[k], row, 0, place_ref[1] * length)
+            for n in range(1, banks):
+                start = 0
+                for lot in range(lots):
+                    ref = rest_refs[lot * pieces + k]
+                    rows = ref.shape[0]
+                    row = pl.ds(pl.multiple_of(base + start, ROWS), rows)
+                    put(ref, row, (n - 1) * length, lax.rem(place_ref[1] + n, banks) * length)
+                    start += rows
         total_ref[...] = jnp.zeros_like(total_ref)
 
     def blocks_at(block, blocks):
@@ -433,7 +445,7 @@
 
         lax.fori_loop(0, (end - start - 1) // 2, two, 0)
 
-    for u in range(pieces * cols // LANES):
+    for u in range(FOUR):
         at = tile(u)
         cos, sin = tw_ref[0, at, :], tw_ref[1, at, :]
         sum_r, sum_i = total_ref[0, at, :], total_ref[1, at, :]
@@ -447,23 +459,28 @@
         total_ref[1, at, :] = sum_i
 
 
-def bins_first(half, banks, place, edges, own, rest, table, twist, after):
-    cols, length = rest[0].shape
+def bins_first(banks, place, edges, own, rest, table, twist, after):
     rows, times = twist.shape[1:]
     smem = pl.BlockSpec(memory_space=pltpu.SMEM)
-    fixed = lambda shape: pl.BlockSpec(shape, lambda i: (0,) * len(shape))
+    once = pl.Buffered(1)
+
+    def fixed(shape):
+        return pl.BlockSpec(shape, lambda i: (0,) * len(shape), pipeline_mode=once)
+
+    rest = [x for lot in rest for x in lot]
+    cols = rows // len(own)
     return pl.pallas_call(
         functools.partial(bins_first_kernel, len(own), banks),
         grid=(BINS // TOGETHER,),
         in_specs=[smem, smem]
-        + [pl.BlockSpec((cols, 2 * N1 - length), lambda i: (half, 0))] * len(own)
-        + [fixed((cols, length))] * len(rest)
+        + [fixed((cols, x.shape[1])) for x in own]
+        + [fixed(x.shape) for x in rest]
         + [fixed((2 * N1, 2 * times))] * 2
         + [fixed((2, rows, times))]
         + [ANY] * len(after),
         out_specs=[
             pl.BlockSpec((TOGETHER, 2, rows, times), lambda i: (i, 0, 0, 0)),
-            fixed((2, rows, times)),
+            pl.BlockSpec((2, rows, times), lambda i: (0, 0, 0)),
         ],
         out_shape=[
             jax.ShapeDtypeStruct((BINS, 2, rows, times), F32),
@@ -597,14 +614,12 @@
     tmpls, _, cols, _ = templates.shape
     slots, dets = coinc_tmpl.shape[0], strain.shape[0]
     times = N1 // freq
-    part = cols // HALVES
-
-    strains = [
-        lax.all_gather(strain[:, :, h * part : (h + 1) * part], "bank", axis=0, tiled=False)
-        for h in range(HALVES)
-    ]
+
+    starts = (0, cols - ROWS, cols)
+    slices = [strain[:, :, starts[h] : starts[h + 1]] for h in range(LOTS)]
+    strains = [lax.all_gather(x, "bank", axis=0, tiled=False) for x in slices]
     first = tuple(jnp.asarray(t) for t in first_table())
-    second = tuple(jnp.asarray(t) for t in second_table(cols, HALVES))
+    second = tuple(jnp.asarray(t) for t in second_table(cols, 1))
     stage = jnp.asarray(stage_table())
 
     column = place * cols + jnp.arange(cols, dtype=jnp.int32)
@@ -613,11 +628,8 @@
     twist = jnp.stack(phase(column[:, None] * time_of_lane[None, :], N1 * N2))
     own_time = place * times + jnp.arange(times, dtype=jnp.int32)
     table = bank_table(own_time)
-    own_twist = []
-    for h in range(HALVES):
-        rows = jnp.arange(freq * part, dtype=jnp.int32)
-        rows = rows // part * cols + h * part + rows % part
-        own_twist.append(jnp.stack(phase(rows[:, None] * own_time[None, :], N1 * N2)))
+    all_columns = jnp.arange(N2, dtype=jnp.int32)
+    own_twist = jnp.stack(phase(all_columns[:, None] * own_time[None, :], N1 * N2))
 
     which = [jnp.stack([coinc_tmpl[j], coinc_det[j], bank]) for j in range(slots)]
     series = jnp.arange(tmpls * dets - 1, dtype=jnp.int32)
@@ -632,7 +644,7 @@
 
     power = (templates[:, 0] ** 2 + templates[:, 1] ** 2).sum(axis=1)
     power = power.reshape(tmpls, NBLK, BLOCK).sum(axis=2)
-    own = [entry_product((0,), banks, 0, w, templates, strain[None], []) for w in which]
+    own = [entry_product((0,), banks, 0, w, templates, strain[None], slices) for w in which]
     wide = own[0].shape[1]
     power = jnp.pad(power.reshape(1, -1), ((0, 7), (0, wide - tmpls * NBLK)))
     own[0] = jnp.concatenate([own[0], power], axis=0)
@@ -655,38 +667,38 @@
         )
     )
 
-    parts, halves = [], []
+    rest, sent = [], []
     later = tuple(range(1, banks))
-    for h in range(HALVES):
-        after = [x[0] for x in halves[-1]] if halves else gathered
-        half = [entry_product(later, banks, h, w, templates, strains[h], after) for w in which]
-        far = [far_pieces(x, freq) for x in half]
-        sent, token = first_section(freq, h, info, templates, strains[h], first, stage, twist)
-        far = [x[:1] + list(handed_on(x[1:], [token] + parts)) for x in far]
-        rest = [near_pieces(x, freq) for x in far]
-        (ready,) = handed_on([sent], [x for entry in rest for x in entry[1:]])
-        got = lax.all_to_all(
-            ready.reshape(freq, -1, LANES), "freq", split_axis=0, concat_axis=0, tiled=True
+    for h in range(LOTS):
+        lot = [
+            entry_product(later, banks, starts[h], w, templates, strains[h], gathered)
+            for w in which
+        ]
+        far = [far_pieces(x, freq) for x in lot]
+        *sent, token = first_section(
+            freq, starts[h], info, templates, strains[h], first, stage, twist, sent, lot
         )
-        parts.append(got.reshape(ready.shape))
-        halves.append(
-            [
-                bins_first(
-                    h, banks, here, edges[j], own[j], rest[j], table, own_twist[h], [ready]
-                )
-                for j in range(slots)
-            ]
-        )
+        far = [x[:1] + list(handed_on(x[1:], [token])) for x in far]
+        rest.append([near_pieces(x, freq) for x in far])
+        gathered = [x for entry in rest[-1] for x in entry[1:]]
+    (ready,) = handed_on(sent, gathered)
+    got = lax.all_to_all(
+        ready.reshape(freq, -1, LANES), "freq", split_axis=0, concat_axis=0, tiled=True
+    )
+    got = got.reshape(ready.shape)
 
     chi, snr = [], None
     for j in range(slots):
-        levels, totals = zip(*[x[j] for x in halves])
+        entry = [x[j] for x in rest]
+        levels, total = bins_first(
+            banks, here, edges[j], own[j], entry, table, own_twist, [ready]
+        )
         one, series_of = bins_second(
-            which[j], inv_sigma, gains[j], shares[j], levels, totals, second, tmpls, dets
+            which[j], inv_sigma, gains[j], shares[j], [levels], [total], second, tmpls, dets
         )
         chi.append(one)
         snr = series_of if snr is None else snr
-    snr = second_section(freq, info, inv_sigma, parts, second, snr, chi)
+    snr = second_section(freq, info, inv_sigma, [got], second, snr, chi)
     return (snr, jnp.stack(chi))
 
 

time: 203 us -> 217 us (1.069)
  blocking collectives: 0 us -> 18.2 us
  Pallas kernels: 91.3 us -> 84.6 us
  waiting for transfers between devices: 50 us -> 54.2 us
  starting transfers between devices: 21.3 us -> 18.5 us
    all_to_all x2 -> x1, waiting for transfers between devices: 0.01 us -> 18.3 us  [per_device(): lax.all_to_all(ready.reshape(freq, -1, LANES), 'freq', split_axis=0, conc...]
    all_gather x0 -> x1, blocking collectives: none -> 18.2 us  [per_device(): strains = [lax.all_gather(x, 'bank', axis=0, tiled=False) for x in slices]]
    ppermute x21, waiting for transfers between devices: 33.1 us -> 19.8 us  [swap(): return lax.ppermute(x, 'freq', [(i, i ^ k) for i in range(freq)])]
    pallas_call x2 -> x1, Pallas kernels: 33.7 us -> 25 us  [bins_first(): pl.pallas_call(functools.partial(bins_first_kernel, len(own), banks), gri...]
    all_to_all x2 -> x1, starting transfers between devices: 7.43 us -> 4.83 us  [per_device(): lax.all_to_all(ready.reshape(freq, -1, LANES), 'freq', split_axis=0, conc...]
    slice x1 -> x2, local copies, waits for them, and re-layouts: 0.97 us -> 3.58 us  [per_device(): slices = [strain[:, :, starts[h]:starts[h + 1]] for h in range(LOTS)]]
    all_gather x2 -> x1, waiting for transfers between devices: 16.9 us -> 16.1 us  [per_device(): strains = [lax.all_gather(x, 'bank', axis=0, tiled=False) for x in slices]]
  transfers between devices with their start and end apart: 25 -> 23, of which waited for: 15 -> 13; matrix products, arithmetic and copies ran while one was open for 7% -> 9% of each run, Pallas kernels for 36% -> 31%
where the time goes in v10:
time: 217 us; the launch traced here: 216 us
  Pallas kernels  84.6 us (39%)
  waiting for transfers between devices  54.2 us (25%)
  starting transfers between devices  18.5 us (9%)
  blocking collectives  18.2 us (8%)
  other arithmetic  15.8 us (7%)
  between operations  15.6 us (7%)
  local copies, waits for them, and re-layouts  9.11 us (4%)
    pallas_call x1, Pallas kernels, bins_first(): pl.pallas_call(functools.partial(bins_first_kernel, len(own), banks), gri...  25 us
    ppermute x21, waiting for transfers between devices, swap(): return lax.ppermute(x, 'freq', [(i, i ^ k) for i in range(freq)])  19.8 us
    all_to_all x1, waiting for transfers between devices, per_device(): lax.all_to_all(ready.reshape(freq, -1, LANES), 'freq', split_axis=0, conc...  18.3 us
    all_gather x1, blocking collectives, per_device(): strains = [lax.all_gather(x, 'bank', axis=0, tiled=False) for x in slices]  18.2 us
    pallas_call x1, Pallas kernels, bins_second(): pl.pallas_call(functools.partial(bins_second_kernel, halves), grid_spec=p...  16.9 us
    all_gather x1, waiting for transfers between devices, per_device(): strains = [lax.all_gather(x, 'bank', axis=0, tiled=False) for x in slices]  16.1 us
    pallas_call x2, Pallas kernels, first_section(): pl.pallas_call(functools.partial(first_kernel, freq), grid_spec=pltpu.Pre...  15.6 us
    ppermute x21, starting transfers between devices, swap(): return lax.ppermute(x, 'freq', [(i, i ^ k) for i in range(freq)])  13.7 us
  transfers between devices with their start and end apart: 23, of which 13 were waited for; matrix products, arithmetic and copies ran while one was open for 9% of the time, Pallas kernels for 31%

profile of v10, /device:TPU:0, one launch (start us, length us, event | category | flops | bytes accessed | tf_op | source)
XLA Modules:
  0.0 216.0 jit_solution(2002176752210171111)
XLA Ops:
  7.2 2.0 slice.36.refs_0_
  9.2 1.6 slice.37.refs_1_
  12.1 1.7 add_reduce_fusion
  14.1 0.6 pad_add_fusion.1.which_ref
  14.7 4.0 %entry_product.3 = f32[64,1024]{1,0:T(8,128)} custom-call(s32[3]{0:T(128)} %pad_add_fusion.1.which_ref, f32[2,2,64,2048]{3,2,1,0:T(8,128)} %tmpl_ref.9, f32[1,3,2,64,512]{4,3,2,1,0:T(8,128)} %bitcast.27, f32[3,2,48,512]{3,2,1,0:T(8,128)} %slice.36.refs_0_, f32[3,2,16,512]{3,2,1,0:T(8,128)} %slice.37.refs_1_), custom_call_target="tpu_custom_call" | custom-call | flops 1048576 | bytes 1048576 | tf_op jit(solution)/shard_map/entry_product/pallas_call | solution.py:251
  18.8 1.0 select_maximum_fusion.refs_0_
  19.8 4.0 %collective-permute-start.5 = (f32[72,1024]{1,0:T(8,128)S(1)}, f32[72,1024]{1,0:T(8,128)S(1)}, u32[]{:S(2)}, u32[]{:S(2)}) collective-permute-start(f32[72,1024]{1,0:T(8,128)S(1)} %select_maximum_fusion.refs_0_), channel_id=1, source_target_pairs={{0,6},{1,7},{2,4},{3,5},{4,2},{5,3},{6,0},{7,1},{8,14},{9,15},{10,... | collective-permute-start | bytes 884744 | tf_op jit(solution)/shard_map/ppermute | solution.py:599
  23.7 0.5 collective-permute-start.3
  24.3 0.1 collective-permute-start.1
  24.4 0.3 fusion.22
  25.0 1.0 fusion.37
  26.0 0.7 pad_maximum_fusion.3.block_ref
  26.7 0.7 pad_maximum_fusion.2.inner_ref
  27.4 6.1 %bank_table.1 = (bf16[4096,512]{1,0:T(8,128)(2,1)}, bf16[4096,512]{1,0:T(8,128)(2,1)}) custom-call(f32[32,2,256]{2,1,0:T(2,128)} %pad_maximum_fusion.3.block_ref, f32[2,64,256]{2,1,0:T(8,128)} %pad_maximum_fusion.2.inner_ref), custom_call_target="tpu_custom_call" | custom-call | flops 1048576 | bytes 1048576 | tf_op jit(solution)/shard_map/bank_table/pallas_call | solution.py:375
  33.5 0.7 pad_add_fusion.4.place_ref
  34.2 2.1 fusion.10
  36.3 1.1 pad_maximum_fusion.1.refs_26_
  37.3 2.1 fusion.12
  39.4 1.1 pad_maximum_fusion.tw_ref
  40.5 0.6 pad_add_fusion.2.info_ref
  41.1 0.6 pad_add_fusion.3.edge_ref
  41.9 0.5 collective-permute-start.6
  42.6 0.5 collective-permute-start.2
  43.2 0.4 collective-permute-done.6.refs_6_.refs_7_
  43.7 0.4 collective-permute-done.4.refs_4_.refs_5_
  44.2 0.3 collective-permute-done.2.refs_2_.refs_3_
  44.6 0.1 fusion.42
  44.7 0.7 dynamic_slice.10
  45.6 1.2 bitcast_multiply_fusion
  46.7 16.1 %all-gather.4.cloned.1.call-done = f32[12,2,48,512]{3,2,1,0:T(8,128)} async-done(((f32[3,2,48,512]{3,2,1,0:T(8,128)}), f32[12,2,48,512]{3,2,1,0:T(8,128)}) %all-gather.4.cloned.1.call-update) | async-done | bytes 2359312 | tf_op jit(solution)/shard_map/all_gather | solution.py:620
  62.8 3.8 %entry_product.4.refs_0_.refs_8_ = f32[48,3072]{1,0:T(8,128)} custom-call(s32[3]{0:T(128)} %pad_add_fusion.1.which_ref, f32[2,2,64,2048]{3,2,1,0:T(8,128)} %tmpl_ref.9, f32[4,3,2,48,512]{4,3,2,1,0:T(8,128)} %bitcast.28, f32[72,1024]{1,0:T(8,128)} %copy-done.14, f32[72,1024]{1,0:T(8,128)} %copy-done.13, f32[72,1024]{1,0:T(8,128)} %copy-done.17, ...), custom_call_target="tpu_custom_call" | custom-call | flops 1048576 | bytes 1048576 | tf_op jit(solution)/shard_map/entry_product/pallas_call | solution.py:251
  66.7 2.4 %collective-permute-start.10 = (f32[48,3072]{1,0:T(8,128)}, f32[48,3072]{1,0:T(8,128)S(1)}, u32[]{:S(2)}, u32[]{:S(2)}) collective-permute-start(f32[48,3072]{1,0:T(8,128)} %entry_product.4.refs_0_.refs_8_), channel_id=1, source_target_pairs={{0,6},{1,7},{2,4},{3,5},{4,2},{5,3},{6,0},{7,1},{8,14},{9,15},{10,... | collective-permute-start | bytes 1769480 | tf_op jit(solution)/shard_map/ppermute | solution.py:599
  69.1 0.6 collective-permute-start.9
  69.6 0.6 collective-permute-start.8
  70.2 9.4 %first_section.2 = (f32[8,5,2,2,64,128]{5,4,3,2,1,0:T(8,128)}, f32[8,128]{1,0:T(8,128)}) custom-call(s32[11]{0:T(128)} %pad_add_fusion.2.info_ref, f32[2,2,64,2048]{3,2,1,0:T(8,128)} %tmpl_ref.9, f32[4,3,2,48,512]{4,3,2,1,0:T(8,128)} %bitcast.29, bf16[256,256]{1,0:T(8,128)(2,1)} %constant.139.clone.wh_ref, bf16[256,256]{1,0:T(8,128)(2,1)} %constant.140.clone.wl_ref, ...), custom_call_target="tpu_custom_call" | custom-call | flops 3774873600 | bytes 16777216 | tf_op jit(solution)/shard_map/first_section/pallas_call | solution.py:188
  79.5 4.5 %collective-permute-done.10.refs_2_ = f32[48,3072]{1,0:T(8,128)S(1)} collective-permute-done((f32[48,3072]{1,0:T(8,128)}, f32[48,3072]{1,0:T(8,128)S(1)}, u32[]{:S(2)}, u32[]{:S(2)}) %collective-permute-start.10) | collective-permute-done | bytes 589856 | tf_op jit(solution)/shard_map/ppermute | solution.py:599
  84.1 11.3 %collective-permute-done.9.refs_1_ = f32[48,3072]{1,0:T(8,128)S(1)} collective-permute-done((f32[48,3072]{1,0:T(8,128)}, f32[48,3072]{1,0:T(8,128)S(1)}, u32[]{:S(2)}, u32[]{:S(2)}) %collective-permute-start.9) | collective-permute-done | bytes 589856 | tf_op jit(solution)/shard_map/ppermute | solution.py:599
  95.5 0.7 copy-done.1
  96.2 0.3 copy-done.2
  96.5 0.5 collective-permute-start.12
  97.0 18.2 %all-gather = f32[12,2,16,512]{3,2,1,0:T(8,128)} all-gather(f32[3,2,16,512]{3,2,1,0:T(8,128)S(1)} %copy-done.10), channel_id=2, replica_groups=mesh['bank'=4,'freq'=8] {'bank'}, dimensions={0}, use_global_device_ids=true | all-gather | bytes 983040 | tf_op jit(solution)/shard_map/all_gather | solution.py:620
  115.3 0.8 copy-done.3
  116.1 0.2 copy-done.4
  116.3 0.2 copy-done.5
  116.5 0.1 copy-done.6
  116.6 2.5 %entry_product.5.refs_1_.refs_16_ = f32[16,3072]{1,0:T(8,128)} custom-call(s32[3]{0:T(128)} %pad_add_fusion.1.which_ref, f32[2,2,64,2048]{3,2,1,0:T(8,128)} %tmpl_ref.9, f32[4,3,2,16,512]{4,3,2,1,0:T(8,128)} %bitcast.25, f32[48,3072]{1,0:T(8,128)} %copy-done.3, f32[48,3072]{1,0:T(8,128)} %get-tuple-element.37.refs_1_.refs_10_, f32[48,3072]{1,0:T(8,128)} %copy-done.4, ...), custom_call_target="tpu_custom_call" | custom-call | flops 1048576 | bytes 1048576 | tf_op jit(solution)/shard_map/entry_product/pallas_call | solution.py:251
  119.1 1.7 collective-permute-start.17
  120.8 1.1 collective-permute-start.16
  122.0 0.6 collective-permute-start.15
  122.6 6.2 %first_section.3 = (f32[8,5,2,2,64,128]{5,4,3,2,1,0:T(8,128)}, f32[8,128]{1,0:T(8,128)}) custom-call(s32[11]{0:T(128)} %pad_add_fusion.2.info_ref, f32[2,2,64,2048]{3,2,1,0:T(8,128)} %tmpl_ref.9, f32[4,3,2,16,512]{4,3,2,1,0:T(8,128)} %bitcast.26, bf16[256,256]{1,0:T(8,128)(2,1)} %constant.139.clone.wh_ref, ...), custom_call_target="tpu_custom_call", output_to_operand_aliasing={{0}: (7, {})} | custom-call | flops 1258291200 | bytes 16777216 | tf_op jit(solution)/shard_map/first_section/pallas_call | solution.py:188
  128.8 0.9 collective-permute-done.16.refs_1_
  129.9 0.6 copy-done.8
  130.5 0.5 collective-permute-start.19
  131.1 1.1 collective-permute-done.18.refs_3_.refs_19_
  132.2 0.3 collective-permute-done.19.refs_5_.refs_21_
  132.5 0.3 collective-permute-done.20.refs_7_.refs_23_
  132.8 0.1 copy-done.20
  132.9 0.3 copy-done.21
  133.1 0.3 copy-done.22
  133.4 4.8 %all-to-all-start = ((f32[8,1280,128]{2,1,0:T(8,128)}), f32[8,1280,128]{2,1,0:T(8,128)}, u32[]{:S(2)}, u32[]{:S(2)}) async-start(f32[8,1280,128]{2,1,0:T(8,128)} %bitcast.24), calls=%async_computation | async-start | bytes 10485760 | tf_op jit(solution)/shard_map/all_to_all | solution.py:685
  138.2 25.0 %bins_first.1 = (f32[16,2,512,256]{3,2,1,0:T(8,128)}, f32[2,512,256]{2,1,0:T(8,128)}) custom-call(s32[2]{0:T(128)} %pad_add_fusion.4.place_ref, s32[17]{0:T(128)} %pad_add_fusion.3.edge_ref, f32[72,1024]{1,0:T(8,128)} %copy-done.18, f32[72,1024]{1,0:T(8,128)} %copy-done.14, f32[72,1024]{1,0:T(8,128)} %copy-done.13, f32[72,1024]{1,0:T(8,128)} %copy-done.17, ...), custom_call_target="tpu_custom_call" | custom-call | flops 1048576 | bytes 1048576 | tf_op jit(solution)/shard_map/bins_first/pallas_call | solution.py:472
  163.2 16.9 %bins_second.1 = (f32[256,512]{1,0:T(8,128)}, f32[2,3,2,256,512]{4,3,2,1,0:T(8,128)}) custom-call(s32[3]{0:T(128)} %pad_add_fusion.1.which_ref, f32[2]{0:T(128)} %copy-done.23, f32[16]{0:T(128)} %get-tuple-element.45.gain_ref, f32[16]{0:T(128)} %get-tuple-element.46.share_ref, f32[16,2,512,256]{3,2,1,0:T(8,128)} %get-tuple-element.52.refs_0_, ...), custom_call_target="tpu_custom_call" | custom-call | flops 1048576 | bytes 1048576 | tf_op jit(solution)/shard_map/bins_second/pallas_call | solution.py:556
  180.1 18.3 %all-to-all-done = f32[8,1280,128]{2,1,0:T(8,128)} async-done(((f32[8,1280,128]{2,1,0:T(8,128)}), f32[8,1280,128]{2,1,0:T(8,128)}, u32[]{:S(2)}, u32[]{:S(2)}) %all-to-all-start) | async-done | bytes 5242912 | tf_op jit(solution)/shard_map/all_to_all | solution.py:685
  198.4 10.7 %second_section.1 = f32[2,3,2,256,512]{4,3,2,1,0:T(8,128)} custom-call(s32[11]{0:T(128)} %pad_add_fusion.2.info_ref, f32[2]{0:T(128)} %copy-done.23, f32[8,5,2,2,64,128]{5,4,3,2,1,0:T(8,128)} %bitcast.11.refs_0_, bf16[1024,256]{1,0:T(8,128)(2,1)} %constant.141.clone.refs_2_.refs_1_, ...), custom_call_target="tpu_custom_call", output_to_operand_aliasing={{}: (5, {})} | custom-call | flops 1048576 | bytes 1048576 | tf_op jit(solution)/shard_map/second_section/pallas_call | solution.py:329
  (96 shorter events, 2.1 us)
Async XLA Ops:
  7.2 17.8 %copy-start.24 = (s32[2,15]{1,0:T(2,128)S(1)}, s32[2,15]{1,0:T(2,128)}, u32[]{:S(2)}) copy-start(s32[2,15]{1,0:T(2,128)} %param.14) | copy-start | bytes 364
  7.2 55.6 %all-gather.4.cloned.1.call-start = ((), (), s32[]{:S(2)}) async-start(), calls=%async_computation.1 | async-start | bytes 2949120 | tf_op jit(solution)/shard_map/all_gather | solution.py:620
  19.8 46.9 %copy-start.18 = (f32[72,1024]{1,0:T(8,128)}, f32[72,1024]{1,0:T(8,128)S(1)}, u32[]{:S(2)}) copy-start(f32[72,1024]{1,0:T(8,128)S(1)} %select_maximum_fusion.refs_0_) | copy-start | bytes 884740
  19.8 22.0 %collective-permute-start.5 = (f32[72,1024]{1,0:T(8,128)S(1)}, f32[72,1024]{1,0:T(8,128)S(1)}, u32[]{:S(2)}, u32[]{:S(2)}) collective-permute-start(f32[72,1024]{1,0:T(8,128)S(1)} %select_maximum_fusion.refs_0_), channel_id=1, source_target_pairs={{0,6},{1,7},{2,4},{3,5},{4,2},{5,3},{6,0},{7,1},{8,14},{9,15},{10,... | collective-permute-start | bytes 884744 | tf_op jit(solution)/shard_map/ppermute | solution.py:599
  23.7 18.6 %collective-permute-start.3 = (f32[72,1024]{1,0:T(8,128)S(1)}, f32[72,1024]{1,0:T(8,128)S(1)}, u32[]{:S(2)}, u32[]{:S(2)}) collective-permute-start(f32[72,1024]{1,0:T(8,128)S(1)} %select_maximum_fusion.refs_0_), channel_id=1, source_target_pairs={{0,4},{1,5},{2,6},{3,7},{4,0},{5,1},{6,2},{7,3},{8,12},{9,13},{10,... | collective-permute-start | bytes 884744 | tf_op jit(solution)/shard_map/ppermute | solution.py:599
  24.3 18.2 %collective-permute-start.1 = (f32[72,1024]{1,0:T(8,128)S(1)}, f32[72,1024]{1,0:T(8,128)S(1)}, u32[]{:S(2)}, u32[]{:S(2)}) collective-permute-start(f32[72,1024]{1,0:T(8,128)S(1)} %select_maximum_fusion.refs_0_), channel_id=1, source_target_pairs={{0,2},{1,3},{2,0},{3,1},{4,6},{5,7},{6,4},{7,5},{8,10},{9,11},{10,... | collective-permute-start | bytes 884744 | tf_op jit(solution)/shard_map/ppermute | solution.py:599
  24.4 18.7 %collective-permute-start = (f32[72,1024]{1,0:T(8,128)S(1)}, f32[72,1024]{1,0:T(8,128)S(1)}, u32[]{:S(2)}, u32[]{:S(2)}) collective-permute-start(f32[72,1024]{1,0:T(8,128)S(1)} %select_maximum_fusion.refs_0_), channel_id=1, source_target_pairs={{0,1},{1,0},{2,3},{3,2},{4,5},{5,4},{6,7},{7,6},{8,9},{9,8},{10,11... | collective-permute-start | bytes 884744 | tf_op jit(solution)/shard_map/ppermute | solution.py:599
  41.7 21.1 %copy-start.11 = (f32[72,1024]{1,0:T(8,128)}, f32[72,1024]{1,0:T(8,128)S(1)}, u32[]{:S(2)}) copy-start(f32[72,1024]{1,0:T(8,128)S(1)} %collective-permute-done.5.refs_5_.refs_6_) | copy-start | bytes 884740
  41.9 1.7 collective-permute-start.6
  42.4 20.4 %copy-start.12 = (f32[72,1024]{1,0:T(8,128)}, f32[72,1024]{1,0:T(8,128)S(1)}, u32[]{:S(2)}) copy-start(f32[72,1024]{1,0:T(8,128)S(1)} %collective-permute-done.3.refs_3_.refs_4_) | copy-start | bytes 884740
  42.5 1.6 collective-permute-start.4
  42.5 20.3 %copy-start.13 = (f32[72,1024]{1,0:T(8,128)}, f32[72,1024]{1,0:T(8,128)S(1)}, u32[]{:S(2)}) copy-start(f32[72,1024]{1,0:T(8,128)S(1)} %collective-permute-done.1.refs_1_.refs_2_) | copy-start | bytes 884740
  42.6 1.9 collective-permute-start.2
  43.1 19.7 %copy-start.14 = (f32[72,1024]{1,0:T(8,128)}, f32[72,1024]{1,0:T(8,128)S(1)}, u32[]{:S(2)}) copy-start(f32[72,1024]{1,0:T(8,128)S(1)} %collective-permute-done.refs_0_.refs_1_) | copy-start | bytes 884740
  43.6 19.2 %copy-start.15 = (f32[72,1024]{1,0:T(8,128)}, f32[72,1024]{1,0:T(8,128)S(1)}, u32[]{:S(2)}) copy-start(f32[72,1024]{1,0:T(8,128)S(1)} %collective-permute-done.6.refs_6_.refs_7_) | copy-start | bytes 884740
  44.1 18.8 %copy-start.16 = (f32[72,1024]{1,0:T(8,128)}, f32[72,1024]{1,0:T(8,128)S(1)}, u32[]{:S(2)}) copy-start(f32[72,1024]{1,0:T(8,128)S(1)} %collective-permute-done.4.refs_4_.refs_5_) | copy-start | bytes 884740
  44.5 18.3 %copy-start.17 = (f32[72,1024]{1,0:T(8,128)}, f32[72,1024]{1,0:T(8,128)S(1)}, u32[]{:S(2)}) copy-start(f32[72,1024]{1,0:T(8,128)S(1)} %collective-permute-done.2.refs_2_.refs_3_) | copy-start | bytes 884740
  44.7 34.8 %copy-start.23 = (f32[2]{0:T(128)}, f32[2]{0:T(128)S(1)}, u32[]{:S(2)}) copy-start(f32[2]{0:T(128)S(1)} %rsqrt.6.scale_ref) | copy-start | bytes 28
  66.7 30.4 %copy-start.10 = (f32[3,2,16,512]{3,2,1,0:T(8,128)S(1)}, f32[3,2,16,512]{3,2,1,0:T(8,128)}, u32[]{:S(2)}) copy-start(f32[3,2,16,512]{3,2,1,0:T(8,128)} %slice.37.refs_1_) | copy-start | bytes 589828
  66.7 17.4 %collective-permute-start.10 = (f32[48,3072]{1,0:T(8,128)}, f32[48,3072]{1,0:T(8,128)S(1)}, u32[]{:S(2)}, u32[]{:S(2)}) collective-permute-start(f32[48,3072]{1,0:T(8,128)} %entry_product.4.refs_0_.refs_8_), channel_id=1, source_target_pairs={{0,6},{1,7},{2,4},{3,5},{4,2},{5,3},{6,0},{7,1},{8,14},{9,15},{10,... | collective-permute-start | bytes 1769480 | tf_op jit(solution)/shard_map/ppermute | solution.py:599
  69.1 26.4 %collective-permute-start.9 = (f32[48,3072]{1,0:T(8,128)}, f32[48,3072]{1,0:T(8,128)S(1)}, u32[]{:S(2)}, u32[]{:S(2)}) collective-permute-start(f32[48,3072]{1,0:T(8,128)} %entry_product.4.refs_0_.refs_8_), channel_id=1, source_target_pairs={{0,4},{1,5},{2,6},{3,7},{4,0},{5,1},{6,2},{7,3},{8,12},{9,13},{10,... | collective-permute-start | bytes 1769480 | tf_op jit(solution)/shard_map/ppermute | solution.py:599
  69.6 25.9 %collective-permute-start.8 = (f32[48,3072]{1,0:T(8,128)}, f32[48,3072]{1,0:T(8,128)S(1)}, u32[]{:S(2)}, u32[]{:S(2)}) collective-permute-start(f32[48,3072]{1,0:T(8,128)} %entry_product.4.refs_0_.refs_8_), channel_id=1, source_target_pairs={{0,2},{1,3},{2,0},{3,1},{4,6},{5,7},{6,4},{7,5},{8,10},{9,11},{10,... | collective-permute-start | bytes 1769480 | tf_op jit(solution)/shard_map/ppermute | solution.py:599
  70.2 45.1 %collective-permute-start.7 = (f32[48,3072]{1,0:T(8,128)}, f32[48,3072]{1,0:T(8,128)S(1)}, u32[]{:S(2)}, u32[]{:S(2)}) collective-permute-start(f32[48,3072]{1,0:T(8,128)} %entry_product.4.refs_0_.refs_8_), channel_id=1, source_target_pairs={{0,1},{1,0},{2,3},{3,2},{4,5},{5,4},{6,7},{7,6},{8,9},{9,8},{10,11... | collective-permute-start | bytes 1769480 | tf_op jit(solution)/shard_map/ppermute | solution.py:599
  84.1 11.5 %copy-start = (f32[48,3072]{1,0:T(8,128)}, f32[48,3072]{1,0:T(8,128)S(1)}, u32[]{:S(2)}) copy-start(f32[48,3072]{1,0:T(8,128)S(1)} %collective-permute-done.10.refs_2_) | copy-start | bytes 1769476
  95.4 0.8 copy-start.1
  95.5 1.0 copy-start.2
  96.5 18.8 %collective-permute-start.11 = (f32[48,3072]{1,0:T(8,128)}, f32[48,3072]{1,0:T(8,128)S(1)}, u32[]{:S(2)}, u32[]{:S(2)}) collective-permute-start(f32[48,3072]{1,0:T(8,128)} %get-tuple-element.37.refs_1_.refs_10_), channel_id=1, source_target_pairs={{0,1},{1,0},{2,3},{3,2},{4,5},{5,4},{6,7},{7,6},{8,9},{9,8},{10,11... | collective-permute-start | bytes 1769480 | tf_op jit(solution)/shard_map/ppermute | solution.py:599
  96.5 18.8 %collective-permute-start.12 = (f32[48,3072]{1,0:T(8,128)}, f32[48,3072]{1,0:T(8,128)S(1)}, u32[]{:S(2)}, u32[]{:S(2)}) collective-permute-start(f32[48,3072]{1,0:T(8,128)} %get-tuple-element.38.refs_3_.refs_12_), channel_id=1, source_target_pairs={{0,1},{1,0},{2,3},{3,2},{4,5},{5,4},{6,7},{7,6},{8,9},{9,8},{10,11... | collective-permute-start | bytes 1769480 | tf_op jit(solution)/shard_map/ppermute | solution.py:599
  97.0 18.3 %collective-permute-start.13 = (f32[48,3072]{1,0:T(8,128)}, f32[48,3072]{1,0:T(8,128)S(1)}, u32[]{:S(2)}, u32[]{:S(2)}) collective-permute-start(f32[48,3072]{1,0:T(8,128)} %get-tuple-element.39.refs_5_.refs_14_), channel_id=1, source_target_pairs={{0,1},{1,0},{2,3},{3,2},{4,5},{5,4},{6,7},{7,6},{8,9},{9,8},{10,11... | collective-permute-start | bytes 1769480 | tf_op jit(solution)/shard_map/ppermute | solution.py:599
  115.3 0.8 copy-start.3
  115.3 1.1 copy-start.4
  115.3 1.2 copy-start.5
  115.3 1.3 copy-start.6
  119.1 9.7 %collective-permute-start.17 = (f32[16,3072]{1,0:T(8,128)}, f32[16,3072]{1,0:T(8,128)S(1)}, u32[]{:S(2)}, u32[]{:S(2)}) collective-permute-start(f32[16,3072]{1,0:T(8,128)} %entry_product.5.refs_1_.refs_16_), channel_id=1, source_target_pairs={{0,6},{1,7},{2,4},{3,5},{4,2},{5,3},{6,0},{7,1},{8,14},{9,15},{10,... | collective-permute-start | bytes 589832 | tf_op jit(solution)/shard_map/ppermute | solution.py:599
  120.8 8.9 %collective-permute-start.16 = (f32[16,3072]{1,0:T(8,128)}, f32[16,3072]{1,0:T(8,128)S(1)}, u32[]{:S(2)}, u32[]{:S(2)}) collective-permute-start(f32[16,3072]{1,0:T(8,128)} %entry_product.5.refs_1_.refs_16_), channel_id=1, source_target_pairs={{0,4},{1,5},{2,6},{3,7},{4,0},{5,1},{6,2},{7,3},{8,12},{9,13},{10,... | collective-permute-start | bytes 589832 | tf_op jit(solution)/shard_map/ppermute | solution.py:599
  122.0 7.9 %collective-permute-start.15 = (f32[16,3072]{1,0:T(8,128)}, f32[16,3072]{1,0:T(8,128)S(1)}, u32[]{:S(2)}, u32[]{:S(2)}) collective-permute-start(f32[16,3072]{1,0:T(8,128)} %entry_product.5.refs_1_.refs_16_), channel_id=1, source_target_pairs={{0,2},{1,3},{2,0},{3,1},{4,6},{5,7},{6,4},{7,5},{8,10},{9,11},{10,... | collective-permute-start | bytes 589832 | tf_op jit(solution)/shard_map/ppermute | solution.py:599
  122.6 8.4 %collective-permute-start.14 = (f32[16,3072]{1,0:T(8,128)}, f32[16,3072]{1,0:T(8,128)S(1)}, u32[]{:S(2)}, u32[]{:S(2)}) collective-permute-start(f32[16,3072]{1,0:T(8,128)} %entry_product.5.refs_1_.refs_16_), channel_id=1, source_target_pairs={{0,1},{1,0},{2,3},{3,2},{4,5},{5,4},{6,7},{7,6},{8,9},{9,8},{10,11... | collective-permute-start | bytes 589832 | tf_op jit(solution)/shard_map/ppermute | solution.py:599
  128.8 1.0 copy-start.7
  129.8 0.7 copy-start.8
  129.9 0.7 copy-start.9
  130.5 1.7 collective-permute-start.18
  130.5 1.9 collective-permute-start.19
  131.0 1.7 collective-permute-start.20
  131.0 1.7 copy-start.19
  132.2 0.7 copy-start.20
  132.5 0.7 copy-start.21
  132.7 0.7 copy-start.22
  133.4 65.0 %all-to-all-start = ((f32[8,1280,128]{2,1,0:T(8,128)}), f32[8,1280,128]{2,1,0:T(8,128)}, u32[]{:S(2)}, u32[]{:S(2)}) async-start(f32[8,1280,128]{2,1,0:T(8,128)} %bitcast.24), calls=%async_computation | async-start | bytes 10485760 | tf_op jit(solution)/shard_map/all_to_all | solution.py:685
Sparse Core Ops, SparseCore 0:
  9.6 53.1 all-gather.3

commit v11 on v8

--- a/solution.py
+++ b/solution.py
@@ -175,10 +175,10 @@
 
 ROWS = 16
 HALVES = 2
-TOGETHER = 4
-
-
-def first_section(freq, half, info, templates, strain, first, stage, twist):
+TOGETHER = 2
+
+
+def first_section(freq, half, info, templates, strain, first, stage, twist, after):
     tmpls = templates.shape[0]
     pieces, dets, _, rows, piece_len = strain.shape
     series = tmpls * dets - 1
@@ -201,7 +201,8 @@
                 table,
                 pl.BlockSpec((2 * COARSE, LANES), lambda i, n: (0, 0)),
                 pl.BlockSpec((2, rows, N1), lambda i, n: (0, half, 0)),
-            ],
+            ]
+            + [ANY] * len(after),
             out_specs=[
                 pl.BlockSpec(
                     (freq, 1, 2, groups, rows, LANES), lambda i, n: (0, i, 0, 0, 0, 0)
@@ -223,7 +224,7 @@
             flops=60 * series * rows * N1 * LANES, bytes_accessed=16 * MIB, transcendentals=0
         ),
         name="first_section",
-    )(info, templates, strain, first[0], first[1], stage, twist)
+    )(info, templates, strain, first[0], first[1], stage, twist, *after)
 
 
 def entry_kernel(steps, banks, which_ref, tmpl_ref, strain_ref, *refs):
@@ -385,8 +386,8 @@
 
 def bins_first_kernel(pieces, banks, place_ref, edge_ref, *refs):
     own_refs, rest_refs = refs[:pieces], refs[pieces : 2 * pieces]
-    wh_ref, wl_ref, tw_ref = refs[2 * pieces : 2 * pieces + 3]
-    level_ref, total_ref, xh, xl, acc = refs[-5:]
+    table_refs, tw_ref = refs[2 * pieces : 2 * pieces + 2], refs[2 * pieces + 2]
+    level_ref, total_ref, xh, xl, acc, wh_ref, wl_ref, sems = refs[-8:]
     times = total_ref.shape[-1]
     cols = own_refs[0].shape[0]
     length = 2 * N1 // banks
@@ -395,6 +396,12 @@
 
     @pl.when(step == 0)
     def _():
+        copies = [
+            pltpu.make_async_copy(source, target, sems.at[i])
+            for i, (source, target) in enumerate(zip(table_refs, (wh_ref, wl_ref)))
+        ]
+        for copy in copies:
+            copy.start()
         for k in range(pieces):
             row = pl.ds(pl.multiple_of((place_ref[0] ^ k) * cols, cols), cols)
             for n in range(banks):
@@ -410,6 +417,8 @@
 
                 lax.fori_loop(0, length // chunk, cut, 0)
         total_ref[...] = jnp.zeros_like(total_ref)
+        for copy in copies:
+            copy.wait()
 
     def blocks_at(block, blocks):
         at = pl.ds(pl.multiple_of(block * LANES, LANES), blocks * LANES)
@@ -458,7 +467,7 @@
         in_specs=[smem, smem]
         + [pl.BlockSpec((cols, 2 * N1 - length), lambda i: (half, 0))] * len(own)
         + [fixed((cols, length))] * len(rest)
-        + [fixed((2 * N1, 2 * times))] * 2
+        + [ANY] * 2
         + [fixed((2, rows, times))]
         + [ANY] * len(after),
         out_specs=[
@@ -473,6 +482,9 @@
             pltpu.VMEM((rows, 2 * N1), BF16),
             pltpu.VMEM((rows, 2 * N1), BF16),
             pltpu.VMEM((TOGETHER, rows, 2 * times), F32),
+            pltpu.VMEM((2 * N1, 2 * times), BF16),
+            pltpu.VMEM((2 * N1, 2 * times), BF16),
+            pltpu.SemaphoreType.DMA((2,)),
         ],
         compiler_params=pltpu.CompilerParams(vmem_limit_bytes=VMEM_LIMIT),
         cost_estimate=COST,
@@ -599,10 +611,8 @@
     times = N1 // freq
     part = cols // HALVES
 
-    strains = [
-        lax.all_gather(strain[:, :, h * part : (h + 1) * part], "bank", axis=0, tiled=False)
-        for h in range(HALVES)
-    ]
+    slices = [strain[:, :, h * part : (h + 1) * part] for h in range(HALVES)]
+    strains = [lax.all_gather(x, "bank", axis=0, tiled=False) for x in slices]
     first = tuple(jnp.asarray(t) for t in first_table())
     second = tuple(jnp.asarray(t) for t in second_table(cols, HALVES))
     stage = jnp.asarray(stage_table())
@@ -632,7 +642,7 @@
 
     power = (templates[:, 0] ** 2 + templates[:, 1] ** 2).sum(axis=1)
     power = power.reshape(tmpls, NBLK, BLOCK).sum(axis=2)
-    own = [entry_product((0,), banks, 0, w, templates, strain[None], []) for w in which]
+    own = [entry_product((0,), banks, 0, w, templates, strain[None], slices) for w in which]
     wide = own[0].shape[1]
     power = jnp.pad(power.reshape(1, -1), ((0, 7), (0, wide - tmpls * NBLK)))
     own[0] = jnp.concatenate([own[0], power], axis=0)
@@ -661,7 +671,9 @@
         after = [x[0] for x in halves[-1]] if halves else gathered
         half = [entry_product(later, banks, h, w, templates, strains[h], after) for w in which]
         far = [far_pieces(x, freq) for x in half]
-        sent, token = first_section(freq, h, info, templates, strains[h], first, stage, twist)
+        sent, token = first_section(
+            freq, h, info, templates, strains[h], first, stage, twist, half
+        )
         far = [x[:1] + list(handed_on(x[1:], [token] + parts)) for x in far]
         rest = [near_pieces(x, freq) for x in far]
         (ready,) = handed_on([sent], [x for entry in rest for x in entry[1:]])

time: 203 us -> 193 us (0.951)
  waiting for transfers between devices: 50 us -> 37 us
    all_gather x2, waiting for transfers between devices: 16.9 us -> 4.03 us  [per_device(): strains = [lax.all_gather(x, 'bank', axis=0, tiled=False) for x in slices]]
    unnamed x51 -> x49, local copies, waits for them, and re-layouts: 5.65 us -> 5.55 us
  transfers between devices with their start and end apart: 25 -> 25, of which waited for: 15 -> 15; matrix products, arithmetic and copies ran while one was open for 7% -> 9% of each run, Pallas kernels for 36% -> 41%
where the time goes in v11:
time: 193 us; the launch traced here: 192 us
  Pallas kernels  92.6 us (48%)
  waiting for transfers between devices  37 us (19%)
  starting transfers between devices  21.3 us (11%)
  other arithmetic  16 us (8%)
  between operations  15.6 us (8%)
  local copies, waits for them, and re-layouts  9.3 us (5%)
    pallas_call x2, Pallas kernels, bins_first(): pl.pallas_call(functools.partial(bins_first_kernel, len(own), banks), gri...  34.3 us
    ppermute x21, waiting for transfers between devices, swap(): return lax.ppermute(x, 'freq', [(i, i ^ k) for i in range(freq)])  32.9 us
    pallas_call x1, Pallas kernels, bins_second(): pl.pallas_call(functools.partial(bins_second_kernel, halves), grid_spec=p...  16.7 us
    pallas_call x2, Pallas kernels, first_section(): pl.pallas_call(functools.partial(first_kernel, freq), grid_spec=pltpu.Pre...  15.4 us
    ppermute x21, starting transfers between devices, swap(): return lax.ppermute(x, 'freq', [(i, i ^ k) for i in range(freq)])  13.8 us
    pallas_call x1, Pallas kernels, second_section(): pl.pallas_call(functools.partial(second_kernel, freq, halves), grid_spec=...  10.7 us
    pallas_call x3, Pallas kernels, entry_product(): pl.pallas_call(functools.partial(entry_kernel, steps, banks), grid_spec=p...  9.43 us
    all_to_all x2, starting transfers between devices, per_device(): lax.all_to_all(ready.reshape(freq, -1, LANES), 'freq', split_axis=0, conc...  7.43 us
  transfers between devices with their start and end apart: 25, of which 15 were waited for; matrix products, arithmetic and copies ran while one was open for 9% of the time, Pallas kernels for 41%

profile of v11, /device:TPU:0, one launch (start us, length us, event | category | flops | bytes accessed | tf_op | source)
XLA Modules:
  0.0 191.7 jit_solution(16729824105504593604)
XLA Ops:
  7.2 2.1 %fusion.49 = (f32[3,2,32,512]{3,2,1,0:T(8,128)}, f32[3,2,32,512]{3,2,1,0:T(8,128)}) fusion(f32[3,2,64,512]{3,2,1,0:T(8,128)} %param.10), kind=kLoop, calls=%fused_computation.114 | loop fusion | bytes 1572864 | tf_op jit(solution)/shard_map/slice | solution.py:614
  10.7 1.7 add_reduce_fusion
  12.7 0.7 pad_add_fusion.1.which_ref
  13.3 4.0 %entry_product.3 = f32[64,1024]{1,0:T(8,128)} custom-call(s32[3]{0:T(128)} %pad_add_fusion.1.which_ref, f32[2,2,64,2048]{3,2,1,0:T(8,128)} %tmpl_ref.9, f32[1,3,2,64,512]{4,3,2,1,0:T(8,128)} %bitcast.31, f32[3,2,32,512]{3,2,1,0:T(8,128)} %get-tuple-element.67.refs_0_, f32[3,2,32,512]{3,2,1,0:T(8,128)} %get-tuple-element.66.refs_1_), custom_call_target="tpu_custom_call" | custom-call | flops 1048576 | bytes 1048576 | tf_op jit(solution)/shard_map/entry_product/pallas_call | solution.py:250
  17.4 1.0 select_maximum_fusion.refs_0_
  18.4 4.0 %collective-permute-start.5 = (f32[72,1024]{1,0:T(8,128)S(1)}, f32[72,1024]{1,0:T(8,128)S(1)}, u32[]{:S(2)}, u32[]{:S(2)}) collective-permute-start(f32[72,1024]{1,0:T(8,128)S(1)} %select_maximum_fusion.refs_0_), channel_id=1, source_target_pairs={{0,6},{1,7},{2,4},{3,5},{4,2},{5,3},{6,0},{7,1},{8,14},{9,15},{10,... | collective-permute-start | bytes 884744 | tf_op jit(solution)/shard_map/ppermute | solution.py:594
  22.3 0.5 collective-permute-start.3
  23.0 0.3 fusion.24
  23.3 0.7 pad_add_fusion.4.place_ref
  24.4 1.0 fusion.39
  25.4 0.7 pad_maximum_fusion.4.block_ref
  26.1 0.7 pad_maximum_fusion.3.inner_ref
  26.8 2.1 %fusion.12 = (f32[1,256,256]{2,1,0:T(8,128)S(1)}, f32[1,256,256]{2,1,0:T(8,128)S(1)}, f32[1,256,256]{2,1,0:T(8,128)S(1)}, f32[1,256,256]{2,1,0:T(8,128)S(1)}) fusion(s32[256]{0:T(256)S(1)} %iota_add_fusion, s32[256]{0:T(256)S(1)} %add_add_fusion, s32[256]{0:T(256)S(1)} %fusion.45), kind=kLoop, calls=%fused_computation.34 | loop fusion | flops 1835008 | bytes 1051648 | tf_op jit(solution)/shard_map/cos | solution.py:64
  28.9 6.1 %bank_table.1 = (bf16[4096,512]{1,0:T(8,128)(2,1)}, bf16[4096,512]{1,0:T(8,128)(2,1)}) custom-call(f32[32,2,256]{2,1,0:T(2,128)} %pad_maximum_fusion.4.block_ref, f32[2,64,256]{2,1,0:T(8,128)} %pad_maximum_fusion.3.inner_ref), custom_call_target="tpu_custom_call" | custom-call | flops 1048576 | bytes 1048576 | tf_op jit(solution)/shard_map/bank_table/pallas_call | solution.py:372
  34.9 1.0 pad_maximum_fusion.1
  36.0 2.1 %fusion.10 = (f32[1,64,2048]{2,1,0:T(8,128)S(1)}, f32[1,64,2048]{2,1,0:T(8,128)S(1)}) fusion(s32[2048]{0:T(1024)S(1)} %fusion.35, s32[64]{0:T(128)S(1)} %iota_add_fusion.1), kind=kLoop, calls=%fused_computation.31 | loop fusion | flops 1835008 | bytes 1057024 | tf_op jit(solution)/shard_map/cos | solution.py:64
  38.1 1.1 pad_maximum_fusion.tw_ref
  39.2 0.6 pad_add_fusion.2.info_ref
  39.8 0.6 pad_add_fusion.3.edge_ref
  40.5 0.5 collective-permute-start.6
  41.3 0.5 collective-permute-start.2
  41.9 0.4 collective-permute-done.6.refs_6_.refs_7_
  42.3 0.4 collective-permute-done.4.refs_4_.refs_5_
  42.8 0.3 collective-permute-done.2.refs_2_.refs_3_
  43.4 0.6 dynamic_slice.10
  44.1 1.2 bitcast_multiply_fusion
  45.4 4.0 %all-gather.5.cloned.1.call-done = f32[12,2,32,512]{3,2,1,0:T(8,128)} async-done(((f32[3,2,32,512]{3,2,1,0:T(8,128)}), f32[12,2,32,512]{3,2,1,0:T(8,128)}) %all-gather.5.cloned.1.call-update) | async-done | bytes 1572880 | tf_op jit(solution)/shard_map/all_gather | solution.py:615
  49.4 2.7 %entry_product.4.refs_0_.refs_8_ = f32[32,3072]{1,0:T(8,128)} custom-call(s32[3]{0:T(128)} %pad_add_fusion.1.which_ref, f32[2,2,64,2048]{3,2,1,0:T(8,128)} %tmpl_ref.9, f32[4,3,2,32,512]{4,3,2,1,0:T(8,128)} %bitcast.34, f32[72,1024]{1,0:T(8,128)} %copy-done.10, f32[72,1024]{1,0:T(8,128)} %copy-done.9, f32[72,1024]{1,0:T(8,128)} %copy-done.13, ...), custom_call_target="tpu_custom_call" | custom-call | flops 1048576 | bytes 1048576 | tf_op jit(solution)/shard_map/entry_product/pallas_call | solution.py:250
  52.1 2.4 %collective-permute-start.10 = (f32[32,3072]{1,0:T(8,128)}, f32[32,3072]{1,0:T(8,128)S(1)}, u32[]{:S(2)}, u32[]{:S(2)}) collective-permute-start(f32[32,3072]{1,0:T(8,128)} %entry_product.4.refs_0_.refs_8_), channel_id=1, source_target_pairs={{0,6},{1,7},{2,4},{3,5},{4,2},{5,3},{6,0},{7,1},{8,14},{9,15},{10,... | collective-permute-start | bytes 1179656 | tf_op jit(solution)/shard_map/ppermute | solution.py:594
  54.6 0.5 collective-permute-start.9
  55.1 0.5 collective-permute-start.8
  55.7 7.7 %first_section.2 = (f32[8,5,2,2,32,128]{5,4,3,2,1,0:T(8,128)}, f32[8,128]{1,0:T(8,128)}) custom-call(s32[11]{0:T(128)} %pad_add_fusion.2.info_ref, f32[2,2,64,2048]{3,2,1,0:T(8,128)} %tmpl_ref.9, f32[4,3,2,32,512]{4,3,2,1,0:T(8,128)} %bitcast.35, bf16[256,256]{1,0:T(8,128)(2,1)} %constant.175.clone.wh_ref, bf16[256,256]{1,0:T(8,128)(2,1)} %constant.176.clone.wl_ref, ...), custom_call_target="tpu_custom_call" | custom-call | flops 2516582400 | bytes 16777216 | tf_op jit(solution)/shard_map/first_section/pallas_call | solution.py:188
  63.4 1.9 collective-permute-done.10.refs_2_
  65.3 7.1 %collective-permute-done.9.refs_1_ = f32[32,3072]{1,0:T(8,128)S(1)} collective-permute-done((f32[32,3072]{1,0:T(8,128)}, f32[32,3072]{1,0:T(8,128)S(1)}, u32[]{:S(2)}, u32[]{:S(2)}) %collective-permute-start.9) | collective-permute-done | bytes 393248 | tf_op jit(solution)/shard_map/ppermute | solution.py:594
  72.4 0.2 collective-permute-done.8.refs_0_
  72.6 0.6 copy-done.5
  73.2 0.2 copy-done.6
  73.5 0.4 collective-permute-start.12
  74.0 1.3 collective-permute-done.11.refs_3_.refs_11_
  75.3 0.6 collective-permute-done.12.refs_5_.refs_13_
  75.9 0.6 collective-permute-done.13.refs_7_.refs_15_
  76.6 0.6 copy-done.21
  77.2 3.8 %all-to-all-start = ((f32[8,640,128]{2,1,0:T(8,128)}), f32[8,640,128]{2,1,0:T(8,128)S(1)}, u32[]{:S(2)}, u32[]{:S(2)}) async-start(f32[8,640,128]{2,1,0:T(8,128)} %bitcast.29), calls=%async_computation | async-start | bytes 5242880 | tf_op jit(solution)/shard_map/all_to_all | solution.py:680
  81.0 17.2 %bins_first.2 = (f32[16,2,256,256]{3,2,1,0:T(8,128)}, f32[2,256,256]{2,1,0:T(8,128)}) custom-call(s32[2]{0:T(128)} %pad_add_fusion.4.place_ref, s32[17]{0:T(128)} %pad_add_fusion.3.edge_ref, f32[72,1024]{1,0:T(8,128)} %copy-done.14, f32[72,1024]{1,0:T(8,128)} %copy-done.10, f32[72,1024]{1,0:T(8,128)} %copy-done.9, f32[72,1024]{1,0:T(8,128)} %copy-done.13, ...), custom_call_target="tpu_custom_call" | custom-call | flops 1048576 | bytes 1048576 | tf_op jit(solution)/shard_map/bins_first/pallas_call | solution.py:464
  98.2 2.7 %entry_product.5.refs_0_.refs_8_ = f32[32,3072]{1,0:T(8,128)} custom-call(s32[3]{0:T(128)} %pad_add_fusion.1.which_ref, f32[2,2,64,2048]{3,2,1,0:T(8,128)} %tmpl_ref.9, f32[4,3,2,32,512]{4,3,2,1,0:T(8,128)} %bitcast.32, f32[16,2,256,256]{3,2,1,0:T(8,128)} %get-tuple-element.48.refs_0_), custom_call_target="tpu_custom_call" | custom-call | flops 1048576 | bytes 1048576 | tf_op jit(solution)/shard_map/entry_product/pallas_call | solution.py:250
  100.9 2.7 %collective-permute-start.17 = (f32[32,3072]{1,0:T(8,128)}, f32[32,3072]{1,0:T(8,128)S(1)}, u32[]{:S(2)}, u32[]{:S(2)}) collective-permute-start(f32[32,3072]{1,0:T(8,128)} %entry_product.5.refs_0_.refs_8_), channel_id=1, source_target_pairs={{0,6},{1,7},{2,4},{3,5},{4,2},{5,3},{6,0},{7,1},{8,14},{9,15},{10,... | collective-permute-start | bytes 1179656 | tf_op jit(solution)/shard_map/ppermute | solution.py:594
  103.6 0.5 collective-permute-start.16
  104.1 0.3 collective-permute-start.15
  104.4 7.7 %first_section.3 = (f32[8,5,2,2,32,128]{5,4,3,2,1,0:T(8,128)}, f32[8,128]{1,0:T(8,128)}) custom-call(s32[11]{0:T(128)} %pad_add_fusion.2.info_ref, f32[2,2,64,2048]{3,2,1,0:T(8,128)} %tmpl_ref.9, f32[4,3,2,32,512]{4,3,2,1,0:T(8,128)} %bitcast.33, bf16[256,256]{1,0:T(8,128)(2,1)} %constant.175.clone.wh_ref, bf16[256,256]{1,0:T(8,128)(2,1)} %constant.176.clone.wl_ref, ...), custom_call_target="tpu_custom_call" | custom-call | flops 2516582400 | bytes 16777216 | tf_op jit(solution)/shard_map/first_section/pallas_call | solution.py:188
  112.1 9.9 %collective-permute-done.17.refs_2_ = f32[32,3072]{1,0:T(8,128)S(1)} collective-permute-done((f32[32,3072]{1,0:T(8,128)}, f32[32,3072]{1,0:T(8,128)S(1)}, u32[]{:S(2)}, u32[]{:S(2)}) %collective-permute-start.17) | collective-permute-done | bytes 393248 | tf_op jit(solution)/shard_map/ppermute | solution.py:594
  122.0 7.8 %collective-permute-done.16.refs_1_ = f32[32,3072]{1,0:T(8,128)S(1)} collective-permute-done((f32[32,3072]{1,0:T(8,128)}, f32[32,3072]{1,0:T(8,128)S(1)}, u32[]{:S(2)}, u32[]{:S(2)}) %collective-permute-start.16) | collective-permute-done | bytes 393248 | tf_op jit(solution)/shard_map/ppermute | solution.py:594
  129.8 0.7 copy-done.3
  130.5 0.9 copy-done
  131.4 0.5 collective-permute-start.19
  131.9 1.4 collective-permute-done.18.refs_3_.refs_11_
  133.3 0.6 collective-permute-done.19.refs_5_.refs_13_
  133.9 0.6 collective-permute-done.20.refs_7_.refs_15_
  134.4 0.2 copy-done.17
  134.6 0.6 copy-done.18
  135.2 3.6 %all-to-all-start.1 = ((f32[8,640,128]{2,1,0:T(8,128)}), f32[8,640,128]{2,1,0:T(8,128)S(1)}, u32[]{:S(2)}, u32[]{:S(2)}) async-start(f32[8,640,128]{2,1,0:T(8,128)} %bitcast.28), calls=%async_computation.1 | async-start | bytes 5242880 | tf_op jit(solution)/shard_map/all_to_all | solution.py:680
  138.8 17.1 %bins_first.3 = (f32[16,2,256,256]{3,2,1,0:T(8,128)}, f32[2,256,256]{2,1,0:T(8,128)}) custom-call(s32[2]{0:T(128)} %pad_add_fusion.4.place_ref, s32[17]{0:T(128)} %pad_add_fusion.3.edge_ref, f32[72,1024]{1,0:T(8,128)} %copy-done.14, f32[72,1024]{1,0:T(8,128)} %copy-done.10, f32[72,1024]{1,0:T(8,128)} %copy-done.9, f32[72,1024]{1,0:T(8,128)} %copy-done.13, ...), custom_call_target="tpu_custom_call" | custom-call | flops 1048576 | bytes 1048576 | tf_op jit(solution)/shard_map/bins_first/pallas_call | solution.py:464
  156.0 16.7 %bins_second.1 = (f32[256,512]{1,0:T(8,128)}, f32[2,3,2,256,512]{4,3,2,1,0:T(8,128)}) custom-call(s32[3]{0:T(128)} %pad_add_fusion.1.which_ref, f32[2]{0:T(128)} %copy-done.22, f32[16]{0:T(128)} %get-tuple-element.54.gain_ref, f32[16]{0:T(128)} %get-tuple-element.55.share_ref, f32[16,2,256,256]{3,2,1,0:T(8,128)} %get-tuple-element.48.refs_0_, ...), custom_call_target="tpu_custom_call" | custom-call | flops 1048576 | bytes 1048576 | tf_op jit(solution)/shard_map/bins_second/pallas_call | solution.py:551
  172.7 1.5 copy-done.1
  174.2 10.7 %second_section.1 = f32[2,3,2,256,512]{4,3,2,1,0:T(8,128)} custom-call(s32[11]{0:T(128)} %pad_add_fusion.2.info_ref, f32[2]{0:T(128)} %copy-done.22, f32[8,5,2,2,32,128]{5,4,3,2,1,0:T(8,128)} %bitcast.27, f32[8,5,2,2,32,128]{5,4,3,2,1,0:T(8,128)} %bitcast.30, bf16[1024,256]{1,0:T(8,128)(2,1)} %constant.177.clone.refs_4_.refs_2_, ...), custom_call_target="tpu_custom_call", output_to_operand_aliasing={{}: (6, {})} | custom-call | flops 1048576 | bytes 1048576 | tf_op jit(solution)/shard_map/second_section/pallas_call | solution.py:326
  (101 shorter events, 2.5 us)
Async XLA Ops:
  7.2 42.2 %all-gather.5.cloned.1.call-start = ((), (), s32[]{:S(2)}) async-start(), calls=%async_computation.2 | async-start | bytes 1966080 | tf_op jit(solution)/shard_map/all_gather | solution.py:615
  9.3 88.9 %all-gather.7.cloned.1.call-start = ((), (), s32[]{:S(2)}) async-start(), calls=%async_computation.3 | async-start | bytes 1966080 | tf_op jit(solution)/shard_map/all_gather | solution.py:615
  12.4 11.8 %copy-start.23 = (s32[2,15]{1,0:T(2,128)S(1)}, s32[2,15]{1,0:T(2,128)}, u32[]{:S(2)}) copy-start(s32[2,15]{1,0:T(2,128)} %param.14) | copy-start | bytes 364
  18.4 20.8 %copy-start.14 = (f32[72,1024]{1,0:T(8,128)}, f32[72,1024]{1,0:T(8,128)S(1)}, u32[]{:S(2)}) copy-start(f32[72,1024]{1,0:T(8,128)S(1)} %select_maximum_fusion.refs_0_) | copy-start | bytes 884740
  18.4 22.1 %collective-permute-start.5 = (f32[72,1024]{1,0:T(8,128)S(1)}, f32[72,1024]{1,0:T(8,128)S(1)}, u32[]{:S(2)}, u32[]{:S(2)}) collective-permute-start(f32[72,1024]{1,0:T(8,128)S(1)} %select_maximum_fusion.refs_0_), channel_id=1, source_target_pairs={{0,6},{1,7},{2,4},{3,5},{4,2},{5,3},{6,0},{7,1},{8,14},{9,15},{10,... | collective-permute-start | bytes 884744 | tf_op jit(solution)/shard_map/ppermute | solution.py:594
  22.3 18.7 %collective-permute-start.3 = (f32[72,1024]{1,0:T(8,128)S(1)}, f32[72,1024]{1,0:T(8,128)S(1)}, u32[]{:S(2)}, u32[]{:S(2)}) collective-permute-start(f32[72,1024]{1,0:T(8,128)S(1)} %select_maximum_fusion.refs_0_), channel_id=1, source_target_pairs={{0,4},{1,5},{2,6},{3,7},{4,0},{5,1},{6,2},{7,3},{8,12},{9,13},{10,... | collective-permute-start | bytes 884744 | tf_op jit(solution)/shard_map/ppermute | solution.py:594
  22.8 18.3 %collective-permute-start.1 = (f32[72,1024]{1,0:T(8,128)S(1)}, f32[72,1024]{1,0:T(8,128)S(1)}, u32[]{:S(2)}, u32[]{:S(2)}) collective-permute-start(f32[72,1024]{1,0:T(8,128)S(1)} %select_maximum_fusion.refs_0_), channel_id=1, source_target_pairs={{0,2},{1,3},{2,0},{3,1},{4,6},{5,7},{6,4},{7,5},{8,10},{9,11},{10,... | collective-permute-start | bytes 884744 | tf_op jit(solution)/shard_map/ppermute | solution.py:594
  23.0 18.8 %collective-permute-start = (f32[72,1024]{1,0:T(8,128)S(1)}, f32[72,1024]{1,0:T(8,128)S(1)}, u32[]{:S(2)}, u32[]{:S(2)}) collective-permute-start(f32[72,1024]{1,0:T(8,128)S(1)} %select_maximum_fusion.refs_0_), channel_id=1, source_target_pairs={{0,1},{1,0},{2,3},{3,2},{4,5},{5,4},{6,7},{7,6},{8,9},{9,8},{10,11... | collective-permute-start | bytes 884744 | tf_op jit(solution)/shard_map/ppermute | solution.py:594
  40.4 9.0 %copy-start.7 = (f32[72,1024]{1,0:T(8,128)}, f32[72,1024]{1,0:T(8,128)S(1)}, u32[]{:S(2)}) copy-start(f32[72,1024]{1,0:T(8,128)S(1)} %collective-permute-done.5.refs_5_.refs_6_) | copy-start | bytes 884740
  40.5 1.7 collective-permute-start.6
  41.0 8.4 %copy-start.8 = (f32[72,1024]{1,0:T(8,128)}, f32[72,1024]{1,0:T(8,128)S(1)}, u32[]{:S(2)}) copy-start(f32[72,1024]{1,0:T(8,128)S(1)} %collective-permute-done.3.refs_3_.refs_4_) | copy-start | bytes 884740
  41.1 1.6 collective-permute-start.4
  41.2 8.2 %copy-start.9 = (f32[72,1024]{1,0:T(8,128)}, f32[72,1024]{1,0:T(8,128)S(1)}, u32[]{:S(2)}) copy-start(f32[72,1024]{1,0:T(8,128)S(1)} %collective-permute-done.1.refs_1_.refs_2_) | copy-start | bytes 884740
  41.3 1.9 collective-permute-start.2
  41.8 7.6 %copy-start.10 = (f32[72,1024]{1,0:T(8,128)}, f32[72,1024]{1,0:T(8,128)S(1)}, u32[]{:S(2)}) copy-start(f32[72,1024]{1,0:T(8,128)S(1)} %collective-permute-done.refs_0_.refs_1_) | copy-start | bytes 884740
  42.2 7.2 %copy-start.11 = (f32[72,1024]{1,0:T(8,128)}, f32[72,1024]{1,0:T(8,128)S(1)}, u32[]{:S(2)}) copy-start(f32[72,1024]{1,0:T(8,128)S(1)} %collective-permute-done.6.refs_6_.refs_7_) | copy-start | bytes 884740
  42.7 6.7 %copy-start.12 = (f32[72,1024]{1,0:T(8,128)}, f32[72,1024]{1,0:T(8,128)S(1)}, u32[]{:S(2)}) copy-start(f32[72,1024]{1,0:T(8,128)S(1)} %collective-permute-done.4.refs_4_.refs_5_) | copy-start | bytes 884740
  43.1 6.3 %copy-start.13 = (f32[72,1024]{1,0:T(8,128)}, f32[72,1024]{1,0:T(8,128)S(1)}, u32[]{:S(2)}) copy-start(f32[72,1024]{1,0:T(8,128)S(1)} %collective-permute-done.2.refs_2_.refs_3_) | copy-start | bytes 884740
  43.4 8.8 %copy-start.22 = (f32[2]{0:T(128)}, f32[2]{0:T(128)S(1)}, u32[]{:S(2)}) copy-start(f32[2]{0:T(128)S(1)} %rsqrt.6.scale_ref) | copy-start | bytes 28
  52.1 13.2 %collective-permute-start.10 = (f32[32,3072]{1,0:T(8,128)}, f32[32,3072]{1,0:T(8,128)S(1)}, u32[]{:S(2)}, u32[]{:S(2)}) collective-permute-start(f32[32,3072]{1,0:T(8,128)} %entry_product.4.refs_0_.refs_8_), channel_id=1, source_target_pairs={{0,6},{1,7},{2,4},{3,5},{4,2},{5,3},{6,0},{7,1},{8,14},{9,15},{10,... | collective-permute-start | bytes 1179656 | tf_op jit(solution)/shard_map/ppermute | solution.py:594
  54.6 17.8 %collective-permute-start.9 = (f32[32,3072]{1,0:T(8,128)}, f32[32,3072]{1,0:T(8,128)S(1)}, u32[]{:S(2)}, u32[]{:S(2)}) collective-permute-start(f32[32,3072]{1,0:T(8,128)} %entry_product.4.refs_0_.refs_8_), channel_id=1, source_target_pairs={{0,4},{1,5},{2,6},{3,7},{4,0},{5,1},{6,2},{7,3},{8,12},{9,13},{10,... | collective-permute-start | bytes 1179656 | tf_op jit(solution)/shard_map/ppermute | solution.py:594
  55.1 17.5 %collective-permute-start.8 = (f32[32,3072]{1,0:T(8,128)}, f32[32,3072]{1,0:T(8,128)S(1)}, u32[]{:S(2)}, u32[]{:S(2)}) collective-permute-start(f32[32,3072]{1,0:T(8,128)} %entry_product.4.refs_0_.refs_8_), channel_id=1, source_target_pairs={{0,2},{1,3},{2,0},{3,1},{4,6},{5,7},{6,4},{7,5},{8,10},{9,11},{10,... | collective-permute-start | bytes 1179656 | tf_op jit(solution)/shard_map/ppermute | solution.py:594
  55.6 18.3 %collective-permute-start.7 = (f32[32,3072]{1,0:T(8,128)}, f32[32,3072]{1,0:T(8,128)S(1)}, u32[]{:S(2)}, u32[]{:S(2)}) collective-permute-start(f32[32,3072]{1,0:T(8,128)} %entry_product.4.refs_0_.refs_8_), channel_id=1, source_target_pairs={{0,1},{1,0},{2,3},{3,2},{4,5},{5,4},{6,7},{7,6},{8,9},{9,8},{10,11... | collective-permute-start | bytes 1179656 | tf_op jit(solution)/shard_map/ppermute | solution.py:594
  65.3 7.3 %copy-start.4 = (f32[32,3072]{1,0:T(8,128)}, f32[32,3072]{1,0:T(8,128)S(1)}, u32[]{:S(2)}) copy-start(f32[32,3072]{1,0:T(8,128)S(1)} %collective-permute-done.10.refs_2_) | copy-start | bytes 1179652
  72.4 0.8 copy-start.5
  72.6 0.8 copy-start.6
  73.4 1.9 %collective-permute-start.11 = (f32[32,3072]{1,0:T(8,128)}, f32[32,3072]{1,0:T(8,128)S(1)}, u32[]{:S(2)}, u32[]{:S(2)}) collective-permute-start(f32[32,3072]{1,0:T(8,128)} %get-tuple-element.40.refs_2_.refs_10_), channel_id=1, source_target_pairs={{0,1},{1,0},{2,3},{3,2},{4,5},{5,4},{6,7},{7,6},{8,9},{9,8},{10,11... | collective-permute-start | bytes 1179656 | tf_op jit(solution)/shard_map/ppermute | solution.py:594
  73.5 2.4 %collective-permute-start.12 = (f32[32,3072]{1,0:T(8,128)}, f32[32,3072]{1,0:T(8,128)S(1)}, u32[]{:S(2)}, u32[]{:S(2)}) collective-permute-start(f32[32,3072]{1,0:T(8,128)} %get-tuple-element.41.refs_4_.refs_12_), channel_id=1, source_target_pairs={{0,1},{1,0},{2,3},{3,2},{4,5},{5,4},{6,7},{7,6},{8,9},{9,8},{10,11... | collective-permute-start | bytes 1179656 | tf_op jit(solution)/shard_map/ppermute | solution.py:594
  73.9 2.5 %collective-permute-start.13 = (f32[32,3072]{1,0:T(8,128)}, f32[32,3072]{1,0:T(8,128)S(1)}, u32[]{:S(2)}, u32[]{:S(2)}) collective-permute-start(f32[32,3072]{1,0:T(8,128)} %get-tuple-element.42.refs_6_.refs_14_), channel_id=1, source_target_pairs={{0,1},{1,0},{2,3},{3,2},{4,5},{5,4},{6,7},{7,6},{8,9},{9,8},{10,11... | collective-permute-start | bytes 1179656 | tf_op jit(solution)/shard_map/ppermute | solution.py:594
  74.0 2.5 %copy-start.15 = (f32[32,3072]{1,0:T(8,128)}, f32[32,3072]{1,0:T(8,128)S(1)}, u32[]{:S(2)}) copy-start(f32[32,3072]{1,0:T(8,128)S(1)} %collective-permute-done.7.refs_1_.refs_9_) | copy-start | bytes 1179652
  75.3 1.1 copy-start.19
  75.9 0.7 copy-start.20
  76.5 0.7 copy-start.21
  77.2 52.5 %all-to-all-start = ((f32[8,640,128]{2,1,0:T(8,128)}), f32[8,640,128]{2,1,0:T(8,128)S(1)}, u32[]{:S(2)}, u32[]{:S(2)}) async-start(f32[8,640,128]{2,1,0:T(8,128)} %bitcast.29), calls=%async_computation | async-start | bytes 5242880 | tf_op jit(solution)/shard_map/all_to_all | solution.py:680
  100.9 21.1 %collective-permute-start.17 = (f32[32,3072]{1,0:T(8,128)}, f32[32,3072]{1,0:T(8,128)S(1)}, u32[]{:S(2)}, u32[]{:S(2)}) collective-permute-start(f32[32,3072]{1,0:T(8,128)} %entry_product.5.refs_0_.refs_8_), channel_id=1, source_target_pairs={{0,6},{1,7},{2,4},{3,5},{4,2},{5,3},{6,0},{7,1},{8,14},{9,15},{10,... | collective-permute-start | bytes 1179656 | tf_op jit(solution)/shard_map/ppermute | solution.py:594
  103.6 26.2 %collective-permute-start.16 = (f32[32,3072]{1,0:T(8,128)}, f32[32,3072]{1,0:T(8,128)S(1)}, u32[]{:S(2)}, u32[]{:S(2)}) collective-permute-start(f32[32,3072]{1,0:T(8,128)} %entry_product.5.refs_0_.refs_8_), channel_id=1, source_target_pairs={{0,4},{1,5},{2,6},{3,7},{4,0},{5,1},{6,2},{7,3},{8,12},{9,13},{10,... | collective-permute-start | bytes 1179656 | tf_op jit(solution)/shard_map/ppermute | solution.py:594
  104.1 25.6 %collective-permute-start.15 = (f32[32,3072]{1,0:T(8,128)}, f32[32,3072]{1,0:T(8,128)}, u32[]{:S(2)}, u32[]{:S(2)}) collective-permute-start(f32[32,3072]{1,0:T(8,128)} %entry_product.5.refs_0_.refs_8_), channel_id=1, source_target_pairs={{0,2},{1,3},{2,0},{3,1},{4,6},{5,7},{6,4},{7,5},{8,10},{9,11},{10,... | collective-permute-start | bytes 1179656 | tf_op jit(solution)/shard_map/ppermute | solution.py:594
  104.4 27.5 %collective-permute-start.14 = (f32[32,3072]{1,0:T(8,128)}, f32[32,3072]{1,0:T(8,128)}, u32[]{:S(2)}, u32[]{:S(2)}) collective-permute-start(f32[32,3072]{1,0:T(8,128)} %entry_product.5.refs_0_.refs_8_), channel_id=1, source_target_pairs={{0,1},{1,0},{2,3},{3,2},{4,5},{5,4},{6,7},{7,6},{8,9},{9,8},{10,11... | collective-permute-start | bytes 1179656 | tf_op jit(solution)/shard_map/ppermute | solution.py:594
  122.0 7.8 %copy-start.2 = (f32[32,3072]{1,0:T(8,128)}, f32[32,3072]{1,0:T(8,128)S(1)}, u32[]{:S(2)}) copy-start(f32[32,3072]{1,0:T(8,128)S(1)} %collective-permute-done.17.refs_2_) | copy-start | bytes 1179652
  129.7 0.7 copy-start.3
  129.7 1.6 copy-start
  131.4 1.9 %collective-permute-start.18 = (f32[32,3072]{1,0:T(8,128)}, f32[32,3072]{1,0:T(8,128)S(1)}, u32[]{:S(2)}, u32[]{:S(2)}) collective-permute-start(f32[32,3072]{1,0:T(8,128)} %get-tuple-element.51.refs_2_.refs_10_), channel_id=1, source_target_pairs={{0,1},{1,0},{2,3},{3,2},{4,5},{5,4},{6,7},{7,6},{8,9},{9,8},{10,11... | collective-permute-start | bytes 1179656 | tf_op jit(solution)/shard_map/ppermute | solution.py:594
  131.4 2.5 %collective-permute-start.19 = (f32[32,3072]{1,0:T(8,128)}, f32[32,3072]{1,0:T(8,128)S(1)}, u32[]{:S(2)}, u32[]{:S(2)}) collective-permute-start(f32[32,3072]{1,0:T(8,128)} %get-tuple-element.52.refs_4_.refs_12_), channel_id=1, source_target_pairs={{0,1},{1,0},{2,3},{3,2},{4,5},{5,4},{6,7},{7,6},{8,9},{9,8},{10,11... | collective-permute-start | bytes 1179656 | tf_op jit(solution)/shard_map/ppermute | solution.py:594
  131.9 2.5 %collective-permute-start.20 = (f32[32,3072]{1,0:T(8,128)}, f32[32,3072]{1,0:T(8,128)S(1)}, u32[]{:S(2)}, u32[]{:S(2)}) collective-permute-start(f32[32,3072]{1,0:T(8,128)} %get-tuple-element.53.refs_6_.refs_14_), channel_id=1, source_target_pairs={{0,1},{1,0},{2,3},{3,2},{4,5},{5,4},{6,7},{7,6},{8,9},{9,8},{10,11... | collective-permute-start | bytes 1179656 | tf_op jit(solution)/shard_map/ppermute | solution.py:594
  133.3 1.1 copy-start.16
  133.9 0.8 copy-start.17
  134.4 0.8 copy-start.18
  135.2 37.5 %all-to-all-start.1 = ((f32[8,640,128]{2,1,0:T(8,128)}), f32[8,640,128]{2,1,0:T(8,128)S(1)}, u32[]{:S(2)}, u32[]{:S(2)}) async-start(f32[8,640,128]{2,1,0:T(8,128)} %bitcast.28), calls=%async_computation.1 | async-start | bytes 5242880 | tf_op jit(solution)/shard_map/all_to_all | solution.py:680
  172.7 1.5 copy-start.1
Sparse Core Ops, SparseCore 0:
  9.6 39.7 all-gather.4
  55.8 35.9 all-gather.6

commit v12 on v11

--- a/solution.py
+++ b/solution.py
@@ -51,7 +51,7 @@
         angle = 2 * np.pi * (np.outer(n2, order) % N2) / N2
         cos, sin = np.cos(angle), np.sin(angle)
         blocks.append(np.block([[cos, -sin], [sin, cos]]))
-    return split_table(np.concatenate(blocks))
+    return np.concatenate([part for block in blocks for part in split_table(block)])
 
 
 def split(x):
@@ -116,6 +116,14 @@
         jnp.concatenate([rh, rl, rh], axis=0),
         preferred_element_type=F32,
     )
+
+
+def rows_dot3(left, right):
+    half = left.shape[0] // 2
+    high, low = right
+    both = jnp.dot(left, high, preferred_element_type=F32)
+    cross = jnp.dot(left[:half], low, preferred_element_type=F32)
+    return both[:half] + (both[half:] + cross)
 
 
 def products(tmpl, strain_ref, where, rows=slice(None)):
@@ -266,16 +274,16 @@
     )(which, templates, strain, *after)
 
 
-def second_points(x, w2h_ref, w2l_ref, use):
+def second_points(x, w2_ref, use):
     for a, (yr, yi) in enumerate(dft4(x)):
         y = jnp.concatenate([yr, yi], axis=0)
-        at = slice(a * 2 * LANES, (a + 1) * 2 * LANES)
-        z = dot3((w2h_ref[at, :], w2l_ref[at, :]), split(y))
+        table = w2_ref[a * 4 * LANES : (a + 1) * 4 * LANES, :]
+        z = rows_dot3(table, split(y))
         use(a, z[:LANES], z[LANES:])
 
 
 def second_kernel(freq, halves, info_ref, scale_ref, *refs):
-    part_refs, (w2h_ref, w2l_ref) = refs[:halves], refs[halves : halves + 2]
+    part_refs, w2_ref = refs[:halves], refs[halves]
     out_ref, hold, order = refs[-3:]
     place = info_ref[0]
     groups, cols = part_refs[0].shape[3:5]
@@ -300,7 +308,7 @@
             for g in range(groups):
                 hold[p, g, pl.ds(a, LANES, stride=FOUR), :] = value[:, tile(g)] * scale
 
-    second_points(x, w2h_ref, w2l_ref, keep)
+    second_points(x, w2_ref, keep)
     for p in range(2):
         for g in range(groups):
             turned = hold[p, g].T
@@ -319,7 +327,7 @@
     halves = len(parts)
     times = groups * LANES
     smem = pl.BlockSpec(memory_space=pltpu.SMEM)
-    table = pl.BlockSpec((FOUR * 2 * LANES, 2 * LANES), lambda i, n: (0, 0))
+    table = pl.BlockSpec((FOUR * 4 * LANES, 2 * LANES), lambda i, n: (0, 0))
     part = pl.BlockSpec(
         (freq, 1, 2, groups, cols, LANES), lambda i, n: (0, i, 0, 0, 0, 0)
     )
@@ -328,7 +336,7 @@
         grid_spec=pltpu.PrefetchScalarGridSpec(
             num_scalar_prefetch=1,
             grid=(series,),
-            in_specs=[smem] + [part] * halves + [table, table, ANY] + [ANY] * len(after),
+            in_specs=[smem] + [part] * halves + [table, ANY] + [ANY] * len(after),
             out_specs=pl.BlockSpec(
                 (1, 1, 2, times, N2), lambda i, n: (n[1 + 2 * i], n[2 + 2 * i], 0, 0, 0)
             ),
@@ -338,11 +346,11 @@
             ],
         ),
         out_shape=jax.ShapeDtypeStruct(snr.shape, F32),
-        input_output_aliases={4 + halves: 0},
+        input_output_aliases={3 + halves: 0},
         compiler_params=pltpu.CompilerParams(vmem_limit_bytes=VMEM_LIMIT),
         cost_estimate=COST,
         name="second_section",
-    )(info, scale, *parts, *second, snr, *after)
+    )(info, scale, *parts, second, snr, *after)
 
 
 BLOCKS = 4
@@ -386,8 +394,8 @@
 
 def bins_first_kernel(pieces, banks, place_ref, edge_ref, *refs):
     own_refs, rest_refs = refs[:pieces], refs[pieces : 2 * pieces]
-    table_refs, tw_ref = refs[2 * pieces : 2 * pieces + 2], refs[2 * pieces + 2]
-    level_ref, total_ref, xh, xl, acc, wh_ref, wl_ref, sems = refs[-8:]
+    wh_ref, wl_ref, tw_ref = refs[2 * pieces : 2 * pieces + 3]
+    level_ref, total_ref, x, acc = refs[-4:]
     times = total_ref.shape[-1]
     cols = own_refs[0].shape[0]
     length = 2 * N1 // banks
@@ -396,33 +404,26 @@
 
     @pl.when(step == 0)
     def _():
-        copies = [
-            pltpu.make_async_copy(source, target, sems.at[i])
-            for i, (source, target) in enumerate(zip(table_refs, (wh_ref, wl_ref)))
-        ]
-        for copy in copies:
-            copy.start()
         for k in range(pieces):
-            row = pl.ds(pl.multiple_of((place_ref[0] ^ k) * cols, cols), cols)
+            row = pl.multiple_of((place_ref[0] ^ k) * cols, cols)
+            low = pl.multiple_of(row + pieces * cols, cols)
             for n in range(banks):
                 ref = rest_refs[k] if n else own_refs[k]
                 start = lax.rem(place_ref[1] + n, banks) * length
 
                 def cut(i, carry):
                     lane = max(n - 1, 0) * length + i * chunk
-                    x = ref[:, pl.ds(pl.multiple_of(lane, chunk), chunk)]
+                    part = split(ref[:, pl.ds(pl.multiple_of(lane, chunk), chunk)])
                     to = pl.ds(pl.multiple_of(start + i * chunk, chunk), chunk)
-                    xh[row, to], xl[row, to] = split(x)
+                    x[pl.ds(row, cols), to], x[pl.ds(low, cols), to] = part
                     return carry
 
                 lax.fori_loop(0, length // chunk, cut, 0)
         total_ref[...] = jnp.zeros_like(total_ref)
-        for copy in copies:
-            copy.wait()
 
     def blocks_at(block, blocks):
         at = pl.ds(pl.multiple_of(block * LANES, LANES), blocks * LANES)
-        return dot3((xh[:, at], xl[:, at]), (wh_ref[at, :], wl_ref[at, :]))
+        return rows_dot3(x[:, at], (wh_ref[at, :], wl_ref[at, :]))
 
     for i in range(TOGETHER):
         start, end = edge_ref[step * TOGETHER + i], edge_ref[step * TOGETHER + i + 1]
@@ -467,7 +468,7 @@
         in_specs=[smem, smem]
         + [pl.BlockSpec((cols, 2 * N1 - length), lambda i: (half, 0))] * len(own)
         + [fixed((cols, length))] * len(rest)
-        + [ANY] * 2
+        + [fixed((2 * N1, 2 * times))] * 2
         + [fixed((2, rows, times))]
         + [ANY] * len(after),
         out_specs=[
@@ -479,12 +480,8 @@
             jax.ShapeDtypeStruct((2, rows, times), F32),
         ],
         scratch_shapes=[
-            pltpu.VMEM((rows, 2 * N1), BF16),
-            pltpu.VMEM((rows, 2 * N1), BF16),
+            pltpu.VMEM((2 * rows, 2 * N1), BF16),
             pltpu.VMEM((TOGETHER, rows, 2 * times), F32),
-            pltpu.VMEM((2 * N1, 2 * times), BF16),
-            pltpu.VMEM((2 * N1, 2 * times), BF16),
-            pltpu.SemaphoreType.DMA((2,)),
         ],
         compiler_params=pltpu.CompilerParams(vmem_limit_bytes=VMEM_LIMIT),
         cost_estimate=COST,
@@ -494,7 +491,7 @@
 
 def bins_second_kernel(halves, which_ref, scale_ref, gain_ref, share_ref, *refs):
     level_refs, total_refs = refs[:halves], refs[halves : 2 * halves]
-    w2h_ref, w2l_ref, out_ref, snr_ref, chi, hold = refs[2 * halves :]
+    w2_ref, out_ref, snr_ref, chi, hold = refs[2 * halves :]
     times = out_ref.shape[0]
     part_rows = LANES // halves
     step = pl.program_id(0)
@@ -519,7 +516,7 @@
             )
 
         x = [tuple(rows_of(deviation(p), u) for p in range(2)) for u in range(FOUR)]
-        second_points(x, w2h_ref, w2l_ref, keep)
+        second_points(x, w2_ref, keep)
 
     @pl.when(step == BINS // TOGETHER - 1)
     def _():
@@ -534,7 +531,7 @@
                     hold[p, g, pl.ds(a, LANES, stride=FOUR), :] = value[:, tile(g)]
 
         y = [tuple(rows_of(whole(p), u) for p in range(2)) for u in range(FOUR)]
-        second_points(y, w2h_ref, w2l_ref, put)
+        second_points(y, w2_ref, put)
         for g in range(times // LANES):
             for a in range(FOUR):
                 hold[2, g, pl.ds(a, LANES, stride=FOUR), :] = chi[a, :, tile(g)]
@@ -556,7 +553,7 @@
             in_specs=[smem, smem, smem]
             + [pl.BlockSpec((TOGETHER, 2, rows, times), lambda i, w: (i, 0, 0, 0))] * halves
             + [fixed((2, rows, times))] * halves
-            + [fixed((FOUR * 2 * LANES, 2 * LANES))] * 2,
+            + [fixed((FOUR * 4 * LANES, 2 * LANES))],
             out_specs=[
                 fixed((times, N2)),
                 pl.BlockSpec((1, 1, 2, times, N2), lambda i, w: (w[0], w[1], 0, 0, 0)),
@@ -573,7 +570,7 @@
         compiler_params=pltpu.CompilerParams(vmem_limit_bytes=VMEM_LIMIT),
         cost_estimate=COST,
         name="bins_second",
-    )(which, scale, gain, share, *levels, *totals, *second)
+    )(which, scale, gain, share, *levels, *totals, second)
 
 
 def handed_on(arrays, after):
@@ -614,7 +611,7 @@
     slices = [strain[:, :, h * part : (h + 1) * part] for h in range(HALVES)]
     strains = [lax.all_gather(x, "bank", axis=0, tiled=False) for x in slices]
     first = tuple(jnp.asarray(t) for t in first_table())
-    second = tuple(jnp.asarray(t) for t in second_table(cols, HALVES))
+    second = jnp.asarray(second_table(cols, HALVES))
     stage = jnp.asarray(stage_table())
 
     column = place * cols + jnp.arange(cols, dtype=jnp.int32)

time: 193 us -> 193 us (level)
  transfers between devices with their start and end apart: 25 -> 25, of which waited for: 15 -> 15; matrix products, arithmetic and copies ran while one was open for 9% -> 9% of each run, Pallas kernels for 41% -> 42%
where the time goes in v12:
time: 193 us; the launch traced here: 192 us
  Pallas kernels  93.2 us (48%)
  waiting for transfers between devices  36.9 us (19%)
  starting transfers between devices  21.3 us (11%)
  other arithmetic  16 us (8%)
  between operations  15.6 us (8%)
  local copies, waits for them, and re-layouts  9.31 us (5%)
    pallas_call x2, Pallas kernels, bins_first(): pl.pallas_call(functools.partial(bins_first_kernel, len(own), banks), gri...  35.1 us
    ppermute x21, waiting for transfers between devices, swap(): return lax.ppermute(x, 'freq', [(i, i ^ k) for i in range(freq)])  32.8 us
    pallas_call x1, Pallas kernels, bins_second(): pl.pallas_call(functools.partial(bins_second_kernel, halves), grid_spec=p...  16.7 us
    pallas_call x2, Pallas kernels, first_section(): pl.pallas_call(functools.partial(first_kernel, freq), grid_spec=pltpu.Pre...  15.2 us
    ppermute x21, starting transfers between devices, swap(): return lax.ppermute(x, 'freq', [(i, i ^ k) for i in range(freq)])  13.8 us
    pallas_call x1, Pallas kernels, second_section(): pl.pallas_call(functools.partial(second_kernel, freq, halves), grid_spec=...  10.7 us
    pallas_call x3, Pallas kernels, entry_product(): pl.pallas_call(functools.partial(entry_kernel, steps, banks), grid_spec=p...  9.43 us
    all_to_all x2, starting transfers between devices, per_device(): lax.all_to_all(ready.reshape(freq, -1, LANES), 'freq', split_axis=0, conc...  7.43 us
  transfers between devices with their start and end apart: 25, of which 15 were waited for; matrix products, arithmetic and copies ran while one was open for 9% of the time, Pallas kernels for 42%

profile of v12, /device:TPU:0, one launch (start us, length us, event | category | flops | bytes accessed | tf_op | source)
XLA Modules:
  0.0 192.2 jit_solution(10650519183553820897)
XLA Ops:
  7.2 2.1 %fusion.49 = (f32[3,2,32,512]{3,2,1,0:T(8,128)}, f32[3,2,32,512]{3,2,1,0:T(8,128)}) fusion(f32[3,2,64,512]{3,2,1,0:T(8,128)} %param.9), kind=kLoop, calls=%fused_computation.114 | loop fusion | bytes 1572864 | tf_op jit(solution)/shard_map/slice | solution.py:611
  10.7 1.7 add_reduce_fusion
  12.7 0.7 pad_add_fusion.1.which_ref
  13.3 4.0 %entry_product.3 = f32[64,1024]{1,0:T(8,128)} custom-call(s32[3]{0:T(128)} %pad_add_fusion.1.which_ref, f32[2,2,64,2048]{3,2,1,0:T(8,128)} %tmpl_ref.9, f32[1,3,2,64,512]{4,3,2,1,0:T(8,128)} %bitcast.31, f32[3,2,32,512]{3,2,1,0:T(8,128)} %get-tuple-element.67.refs_0_, f32[3,2,32,512]{3,2,1,0:T(8,128)} %get-tuple-element.66.refs_1_), custom_call_target="tpu_custom_call" | custom-call | flops 1048576 | bytes 1048576 | tf_op jit(solution)/shard_map/entry_product/pallas_call | solution.py:258
  17.4 1.0 select_maximum_fusion.refs_0_
  18.4 4.0 %collective-permute-start.5 = (f32[72,1024]{1,0:T(8,128)S(1)}, f32[72,1024]{1,0:T(8,128)S(1)}, u32[]{:S(2)}, u32[]{:S(2)}) collective-permute-start(f32[72,1024]{1,0:T(8,128)S(1)} %select_maximum_fusion.refs_0_), channel_id=1, source_target_pairs={{0,6},{1,7},{2,4},{3,5},{4,2},{5,3},{6,0},{7,1},{8,14},{9,15},{10,... | collective-permute-start | bytes 884744 | tf_op jit(solution)/shard_map/ppermute | solution.py:591
  22.3 0.5 collective-permute-start.3
  23.0 0.3 fusion.24
  23.3 0.7 pad_add_fusion.4.place_ref
  24.4 1.0 fusion.39
  25.4 0.7 pad_maximum_fusion.4.block_ref
  26.1 0.7 pad_maximum_fusion.3.inner_ref
  26.8 2.1 %fusion.12 = (f32[1,256,256]{2,1,0:T(8,128)S(1)}, f32[1,256,256]{2,1,0:T(8,128)S(1)}, f32[1,256,256]{2,1,0:T(8,128)S(1)}, f32[1,256,256]{2,1,0:T(8,128)S(1)}) fusion(s32[256]{0:T(256)S(1)} %iota_add_fusion, s32[256]{0:T(256)S(1)} %add_add_fusion, s32[256]{0:T(256)S(1)} %fusion.45), kind=kLoop, calls=%fused_computation.34 | loop fusion | flops 1835008 | bytes 1051648 | tf_op jit(solution)/shard_map/cos | solution.py:64
  28.9 6.1 %bank_table.1 = (bf16[4096,512]{1,0:T(8,128)(2,1)}, bf16[4096,512]{1,0:T(8,128)(2,1)}) custom-call(f32[32,2,256]{2,1,0:T(2,128)} %pad_maximum_fusion.4.block_ref, f32[2,64,256]{2,1,0:T(8,128)} %pad_maximum_fusion.3.inner_ref), custom_call_target="tpu_custom_call" | custom-call | flops 1048576 | bytes 1048576 | tf_op jit(solution)/shard_map/bank_table/pallas_call | solution.py:380
  34.9 1.0 pad_maximum_fusion.1
  36.0 2.1 %fusion.10 = (f32[1,64,2048]{2,1,0:T(8,128)S(1)}, f32[1,64,2048]{2,1,0:T(8,128)S(1)}) fusion(s32[2048]{0:T(1024)S(1)} %fusion.35, s32[64]{0:T(128)S(1)} %iota_add_fusion.1), kind=kLoop, calls=%fused_computation.31 | loop fusion | flops 1835008 | bytes 1057024 | tf_op jit(solution)/shard_map/cos | solution.py:64
  38.1 1.1 pad_maximum_fusion.tw_ref
  39.2 0.6 pad_add_fusion.2.info_ref
  39.8 0.6 pad_add_fusion.3.edge_ref
  40.5 0.5 collective-permute-start.6
  41.3 0.5 collective-permute-start.2
  41.9 0.4 collective-permute-done.6.refs_6_.refs_7_
  42.3 0.4 collective-permute-done.4.refs_4_.refs_5_
  42.8 0.3 collective-permute-done.2.refs_2_.refs_3_
  43.4 0.6 dynamic_slice.10
  44.1 1.2 bitcast_multiply_fusion
  45.4 4.0 %all-gather.5.cloned.1.call-done = f32[12,2,32,512]{3,2,1,0:T(8,128)} async-done(((f32[3,2,32,512]{3,2,1,0:T(8,128)}), f32[12,2,32,512]{3,2,1,0:T(8,128)}) %all-gather.5.cloned.1.call-update) | async-done | bytes 1572880 | tf_op jit(solution)/shard_map/all_gather | solution.py:612
  49.4 2.7 %entry_product.4.refs_0_.refs_8_ = f32[32,3072]{1,0:T(8,128)} custom-call(s32[3]{0:T(128)} %pad_add_fusion.1.which_ref, f32[2,2,64,2048]{3,2,1,0:T(8,128)} %tmpl_ref.9, f32[4,3,2,32,512]{4,3,2,1,0:T(8,128)} %bitcast.34, f32[72,1024]{1,0:T(8,128)} %copy-done.10, f32[72,1024]{1,0:T(8,128)} %copy-done.9, f32[72,1024]{1,0:T(8,128)} %copy-done.13, ...), custom_call_target="tpu_custom_call" | custom-call | flops 1048576 | bytes 1048576 | tf_op jit(solution)/shard_map/entry_product/pallas_call | solution.py:258
  52.1 2.4 %collective-permute-start.10 = (f32[32,3072]{1,0:T(8,128)}, f32[32,3072]{1,0:T(8,128)S(1)}, u32[]{:S(2)}, u32[]{:S(2)}) collective-permute-start(f32[32,3072]{1,0:T(8,128)} %entry_product.4.refs_0_.refs_8_), channel_id=1, source_target_pairs={{0,6},{1,7},{2,4},{3,5},{4,2},{5,3},{6,0},{7,1},{8,14},{9,15},{10,... | collective-permute-start | bytes 1179656 | tf_op jit(solution)/shard_map/ppermute | solution.py:591
  54.6 0.5 collective-permute-start.9
  55.1 0.5 collective-permute-start.8
  55.7 7.6 %first_section.2 = (f32[8,5,2,2,32,128]{5,4,3,2,1,0:T(8,128)}, f32[8,128]{1,0:T(8,128)}) custom-call(s32[11]{0:T(128)} %pad_add_fusion.2.info_ref, f32[2,2,64,2048]{3,2,1,0:T(8,128)} %tmpl_ref.9, f32[4,3,2,32,512]{4,3,2,1,0:T(8,128)} %bitcast.35, bf16[256,256]{1,0:T(8,128)(2,1)} %constant.173.clone.wh_ref, bf16[256,256]{1,0:T(8,128)(2,1)} %constant.174.clone.wl_ref, ...), custom_call_target="tpu_custom_call" | custom-call | flops 2516582400 | bytes 16777216 | tf_op jit(solution)/shard_map/first_section/pallas_call | solution.py:196
  63.3 2.0 %collective-permute-done.10.refs_2_ = f32[32,3072]{1,0:T(8,128)S(1)} collective-permute-done((f32[32,3072]{1,0:T(8,128)}, f32[32,3072]{1,0:T(8,128)S(1)}, u32[]{:S(2)}, u32[]{:S(2)}) %collective-permute-start.10) | collective-permute-done | bytes 393248 | tf_op jit(solution)/shard_map/ppermute | solution.py:591
  65.3 7.1 %collective-permute-done.9.refs_1_ = f32[32,3072]{1,0:T(8,128)S(1)} collective-permute-done((f32[32,3072]{1,0:T(8,128)}, f32[32,3072]{1,0:T(8,128)S(1)}, u32[]{:S(2)}, u32[]{:S(2)}) %collective-permute-start.9) | collective-permute-done | bytes 393248 | tf_op jit(solution)/shard_map/ppermute | solution.py:591
  72.4 0.2 collective-permute-done.8.refs_0_
  72.6 0.6 copy-done.5
  73.2 0.2 copy-done.6
  73.5 0.4 collective-permute-start.12
  74.0 1.3 collective-permute-done.11.refs_3_.refs_11_
  75.3 0.6 collective-permute-done.12.refs_5_.refs_13_
  75.9 0.6 collective-permute-done.13.refs_7_.refs_15_
  76.6 0.6 copy-done.21
  77.2 3.8 %all-to-all-start = ((f32[8,640,128]{2,1,0:T(8,128)}), f32[8,640,128]{2,1,0:T(8,128)S(1)}, u32[]{:S(2)}, u32[]{:S(2)}) async-start(f32[8,640,128]{2,1,0:T(8,128)} %bitcast.29), calls=%async_computation | async-start | bytes 5242880 | tf_op jit(solution)/shard_map/all_to_all | solution.py:677
  81.0 17.6 %bins_first.2 = (f32[16,2,256,256]{3,2,1,0:T(8,128)}, f32[2,256,256]{2,1,0:T(8,128)}) custom-call(s32[2]{0:T(128)} %pad_add_fusion.4.place_ref, s32[17]{0:T(128)} %pad_add_fusion.3.edge_ref, f32[72,1024]{1,0:T(8,128)} %copy-done.14, f32[72,1024]{1,0:T(8,128)} %copy-done.10, f32[72,1024]{1,0:T(8,128)} %copy-done.9, f32[72,1024]{1,0:T(8,128)} %copy-done.13, ...), custom_call_target="tpu_custom_call" | custom-call | flops 1048576 | bytes 1048576 | tf_op jit(solution)/shard_map/bins_first/pallas_call | solution.py:465
  98.6 2.7 %entry_product.5.refs_0_.refs_8_ = f32[32,3072]{1,0:T(8,128)} custom-call(s32[3]{0:T(128)} %pad_add_fusion.1.which_ref, f32[2,2,64,2048]{3,2,1,0:T(8,128)} %tmpl_ref.9, f32[4,3,2,32,512]{4,3,2,1,0:T(8,128)} %bitcast.32, f32[16,2,256,256]{3,2,1,0:T(8,128)} %get-tuple-element.48.refs_0_), custom_call_target="tpu_custom_call" | custom-call | flops 1048576 | bytes 1048576 | tf_op jit(solution)/shard_map/entry_product/pallas_call | solution.py:258
  101.3 2.7 %collective-permute-start.17 = (f32[32,3072]{1,0:T(8,128)}, f32[32,3072]{1,0:T(8,128)S(1)}, u32[]{:S(2)}, u32[]{:S(2)}) collective-permute-start(f32[32,3072]{1,0:T(8,128)} %entry_product.5.refs_0_.refs_8_), channel_id=1, source_target_pairs={{0,6},{1,7},{2,4},{3,5},{4,2},{5,3},{6,0},{7,1},{8,14},{9,15},{10,... | collective-permute-start | bytes 1179656 | tf_op jit(solution)/shard_map/ppermute | solution.py:591
  104.0 0.5 collective-permute-start.16
  104.5 0.3 collective-permute-start.15
  104.8 7.6 %first_section.3 = (f32[8,5,2,2,32,128]{5,4,3,2,1,0:T(8,128)}, f32[8,128]{1,0:T(8,128)}) custom-call(s32[11]{0:T(128)} %pad_add_fusion.2.info_ref, f32[2,2,64,2048]{3,2,1,0:T(8,128)} %tmpl_ref.9, f32[4,3,2,32,512]{4,3,2,1,0:T(8,128)} %bitcast.33, bf16[256,256]{1,0:T(8,128)(2,1)} %constant.173.clone.wh_ref, bf16[256,256]{1,0:T(8,128)(2,1)} %constant.174.clone.wl_ref, ...), custom_call_target="tpu_custom_call" | custom-call | flops 2516582400 | bytes 16777216 | tf_op jit(solution)/shard_map/first_section/pallas_call | solution.py:196
  112.4 9.6 %collective-permute-done.17.refs_2_ = f32[32,3072]{1,0:T(8,128)S(1)} collective-permute-done((f32[32,3072]{1,0:T(8,128)}, f32[32,3072]{1,0:T(8,128)S(1)}, u32[]{:S(2)}, u32[]{:S(2)}) %collective-permute-start.17) | collective-permute-done | bytes 393248 | tf_op jit(solution)/shard_map/ppermute | solution.py:591
  122.0 7.9 %collective-permute-done.16.refs_1_ = f32[32,3072]{1,0:T(8,128)S(1)} collective-permute-done((f32[32,3072]{1,0:T(8,128)}, f32[32,3072]{1,0:T(8,128)S(1)}, u32[]{:S(2)}, u32[]{:S(2)}) %collective-permute-start.16) | collective-permute-done | bytes 393248 | tf_op jit(solution)/shard_map/ppermute | solution.py:591
  129.9 0.7 copy-done.3
  130.6 0.9 copy-done
  131.5 0.5 collective-permute-start.19
  132.1 1.4 collective-permute-done.18.refs_3_.refs_11_
  133.5 0.6 collective-permute-done.19.refs_5_.refs_13_
  134.0 0.6 collective-permute-done.20.refs_7_.refs_15_
  134.6 0.2 copy-done.17
  134.8 0.6 copy-done.18
  135.4 3.6 %all-to-all-start.1 = ((f32[8,640,128]{2,1,0:T(8,128)}), f32[8,640,128]{2,1,0:T(8,128)S(1)}, u32[]{:S(2)}, u32[]{:S(2)}) async-start(f32[8,640,128]{2,1,0:T(8,128)} %bitcast.28), calls=%async_computation.1 | async-start | bytes 5242880 | tf_op jit(solution)/shard_map/all_to_all | solution.py:677
  139.0 17.5 %bins_first.3 = (f32[16,2,256,256]{3,2,1,0:T(8,128)}, f32[2,256,256]{2,1,0:T(8,128)}) custom-call(s32[2]{0:T(128)} %pad_add_fusion.4.place_ref, s32[17]{0:T(128)} %pad_add_fusion.3.edge_ref, f32[72,1024]{1,0:T(8,128)} %copy-done.14, f32[72,1024]{1,0:T(8,128)} %copy-done.10, f32[72,1024]{1,0:T(8,128)} %copy-done.9, f32[72,1024]{1,0:T(8,128)} %copy-done.13, ...), custom_call_target="tpu_custom_call" | custom-call | flops 1048576 | bytes 1048576 | tf_op jit(solution)/shard_map/bins_first/pallas_call | solution.py:465
  156.5 16.7 %bins_second.1 = (f32[256,512]{1,0:T(8,128)}, f32[2,3,2,256,512]{4,3,2,1,0:T(8,128)}) custom-call(s32[3]{0:T(128)} %pad_add_fusion.1.which_ref, f32[2]{0:T(128)} %copy-done.22, f32[16]{0:T(128)} %get-tuple-element.54.gain_ref, f32[16]{0:T(128)} %get-tuple-element.55.share_ref, f32[16,2,256,256]{3,2,1,0:T(8,128)} %get-tuple-element.48.refs_0_, ...), custom_call_target="tpu_custom_call" | custom-call | flops 1048576 | bytes 1048576 | tf_op jit(solution)/shard_map/bins_second/pallas_call | solution.py:548
  173.2 1.5 copy-done.1
  174.7 10.7 %second_section.1 = f32[2,3,2,256,512]{4,3,2,1,0:T(8,128)} custom-call(s32[11]{0:T(128)} %pad_add_fusion.2.info_ref, f32[2]{0:T(128)} %copy-done.22, f32[8,5,2,2,32,128]{5,4,3,2,1,0:T(8,128)} %bitcast.27, f32[8,5,2,2,32,128]{5,4,3,2,1,0:T(8,128)} %bitcast.30, bf16[2048,256]{1,0:T(8,128)(2,1)} %constant.175.clone.refs_4_.refs_2_, ...), custom_call_target="tpu_custom_call", output_to_operand_aliasing={{}: (5, {})} | custom-call | flops 1048576 | bytes 1048576 | tf_op jit(solution)/shard_map/second_section/pallas_call | solution.py:334
  (101 shorter events, 2.5 us)
Async XLA Ops:
  7.2 42.2 %all-gather.5.cloned.1.call-start = ((), (), s32[]{:S(2)}) async-start(), calls=%async_computation.2 | async-start | bytes 1966080 | tf_op jit(solution)/shard_map/all_gather | solution.py:612
  9.3 89.3 %all-gather.7.cloned.1.call-start = ((), (), s32[]{:S(2)}) async-start(), calls=%async_computation.3 | async-start | bytes 1966080 | tf_op jit(solution)/shard_map/all_gather | solution.py:612
  12.4 11.8 %copy-start.23 = (s32[2,15]{1,0:T(2,128)S(1)}, s32[2,15]{1,0:T(2,128)}, u32[]{:S(2)}) copy-start(s32[2,15]{1,0:T(2,128)} %param.13) | copy-start | bytes 364
  18.4 20.8 %copy-start.14 = (f32[72,1024]{1,0:T(8,128)}, f32[72,1024]{1,0:T(8,128)S(1)}, u32[]{:S(2)}) copy-start(f32[72,1024]{1,0:T(8,128)S(1)} %select_maximum_fusion.refs_0_) | copy-start | bytes 884740
  18.4 22.1 %collective-permute-start.5 = (f32[72,1024]{1,0:T(8,128)S(1)}, f32[72,1024]{1,0:T(8,128)S(1)}, u32[]{:S(2)}, u32[]{:S(2)}) collective-permute-start(f32[72,1024]{1,0:T(8,128)S(1)} %select_maximum_fusion.refs_0_), channel_id=1, source_target_pairs={{0,6},{1,7},{2,4},{3,5},{4,2},{5,3},{6,0},{7,1},{8,14},{9,15},{10,... | collective-permute-start | bytes 884744 | tf_op jit(solution)/shard_map/ppermute | solution.py:591
  22.3 18.7 %collective-permute-start.3 = (f32[72,1024]{1,0:T(8,128)S(1)}, f32[72,1024]{1,0:T(8,128)S(1)}, u32[]{:S(2)}, u32[]{:S(2)}) collective-permute-start(f32[72,1024]{1,0:T(8,128)S(1)} %select_maximum_fusion.refs_0_), channel_id=1, source_target_pairs={{0,4},{1,5},{2,6},{3,7},{4,0},{5,1},{6,2},{7,3},{8,12},{9,13},{10,... | collective-permute-start | bytes 884744 | tf_op jit(solution)/shard_map/ppermute | solution.py:591
  22.8 18.3 %collective-permute-start.1 = (f32[72,1024]{1,0:T(8,128)S(1)}, f32[72,1024]{1,0:T(8,128)S(1)}, u32[]{:S(2)}, u32[]{:S(2)}) collective-permute-start(f32[72,1024]{1,0:T(8,128)S(1)} %select_maximum_fusion.refs_0_), channel_id=1, source_target_pairs={{0,2},{1,3},{2,0},{3,1},{4,6},{5,7},{6,4},{7,5},{8,10},{9,11},{10,... | collective-permute-start | bytes 884744 | tf_op jit(solution)/shard_map/ppermute | solution.py:591
  23.0 18.8 %collective-permute-start = (f32[72,1024]{1,0:T(8,128)S(1)}, f32[72,1024]{1,0:T(8,128)S(1)}, u32[]{:S(2)}, u32[]{:S(2)}) collective-permute-start(f32[72,1024]{1,0:T(8,128)S(1)} %select_maximum_fusion.refs_0_), channel_id=1, source_target_pairs={{0,1},{1,0},{2,3},{3,2},{4,5},{5,4},{6,7},{7,6},{8,9},{9,8},{10,11... | collective-permute-start | bytes 884744 | tf_op jit(solution)/shard_map/ppermute | solution.py:591
  40.4 9.0 %copy-start.7 = (f32[72,1024]{1,0:T(8,128)}, f32[72,1024]{1,0:T(8,128)S(1)}, u32[]{:S(2)}) copy-start(f32[72,1024]{1,0:T(8,128)S(1)} %collective-permute-done.5.refs_5_.refs_6_) | copy-start | bytes 884740
  40.5 1.7 collective-permute-start.6
  41.0 8.4 %copy-start.8 = (f32[72,1024]{1,0:T(8,128)}, f32[72,1024]{1,0:T(8,128)S(1)}, u32[]{:S(2)}) copy-start(f32[72,1024]{1,0:T(8,128)S(1)} %collective-permute-done.3.refs_3_.refs_4_) | copy-start | bytes 884740
  41.1 1.6 collective-permute-start.4
  41.2 8.2 %copy-start.9 = (f32[72,1024]{1,0:T(8,128)}, f32[72,1024]{1,0:T(8,128)S(1)}, u32[]{:S(2)}) copy-start(f32[72,1024]{1,0:T(8,128)S(1)} %collective-permute-done.1.refs_1_.refs_2_) | copy-start | bytes 884740
  41.3 1.9 collective-permute-start.2
  41.8 7.6 %copy-start.10 = (f32[72,1024]{1,0:T(8,128)}, f32[72,1024]{1,0:T(8,128)S(1)}, u32[]{:S(2)}) copy-start(f32[72,1024]{1,0:T(8,128)S(1)} %collective-permute-done.refs_0_.refs_1_) | copy-start | bytes 884740
  42.2 7.2 %copy-start.11 = (f32[72,1024]{1,0:T(8,128)}, f32[72,1024]{1,0:T(8,128)S(1)}, u32[]{:S(2)}) copy-start(f32[72,1024]{1,0:T(8,128)S(1)} %collective-permute-done.6.refs_6_.refs_7_) | copy-start | bytes 884740
  42.7 6.7 %copy-start.12 = (f32[72,1024]{1,0:T(8,128)}, f32[72,1024]{1,0:T(8,128)S(1)}, u32[]{:S(2)}) copy-start(f32[72,1024]{1,0:T(8,128)S(1)} %collective-permute-done.4.refs_4_.refs_5_) | copy-start | bytes 884740
  43.1 6.3 %copy-start.13 = (f32[72,1024]{1,0:T(8,128)}, f32[72,1024]{1,0:T(8,128)S(1)}, u32[]{:S(2)}) copy-start(f32[72,1024]{1,0:T(8,128)S(1)} %collective-permute-done.2.refs_2_.refs_3_) | copy-start | bytes 884740
  43.4 8.8 %copy-start.22 = (f32[2]{0:T(128)}, f32[2]{0:T(128)S(1)}, u32[]{:S(2)}) copy-start(f32[2]{0:T(128)S(1)} %rsqrt.6.scale_ref) | copy-start | bytes 28
  52.1 13.2 %collective-permute-start.10 = (f32[32,3072]{1,0:T(8,128)}, f32[32,3072]{1,0:T(8,128)S(1)}, u32[]{:S(2)}, u32[]{:S(2)}) collective-permute-start(f32[32,3072]{1,0:T(8,128)} %entry_product.4.refs_0_.refs_8_), channel_id=1, source_target_pairs={{0,6},{1,7},{2,4},{3,5},{4,2},{5,3},{6,0},{7,1},{8,14},{9,15},{10,... | collective-permute-start | bytes 1179656 | tf_op jit(solution)/shard_map/ppermute | solution.py:591
  54.6 17.8 %collective-permute-start.9 = (f32[32,3072]{1,0:T(8,128)}, f32[32,3072]{1,0:T(8,128)S(1)}, u32[]{:S(2)}, u32[]{:S(2)}) collective-permute-start(f32[32,3072]{1,0:T(8,128)} %entry_product.4.refs_0_.refs_8_), channel_id=1, source_target_pairs={{0,4},{1,5},{2,6},{3,7},{4,0},{5,1},{6,2},{7,3},{8,12},{9,13},{10,... | collective-permute-start | bytes 1179656 | tf_op jit(solution)/shard_map/ppermute | solution.py:591
  55.1 17.5 %collective-permute-start.8 = (f32[32,3072]{1,0:T(8,128)}, f32[32,3072]{1,0:T(8,128)S(1)}, u32[]{:S(2)}, u32[]{:S(2)}) collective-permute-start(f32[32,3072]{1,0:T(8,128)} %entry_product.4.refs_0_.refs_8_), channel_id=1, source_target_pairs={{0,2},{1,3},{2,0},{3,1},{4,6},{5,7},{6,4},{7,5},{8,10},{9,11},{10,... | collective-permute-start | bytes 1179656 | tf_op jit(solution)/shard_map/ppermute | solution.py:591
  55.6 18.3 %collective-permute-start.7 = (f32[32,3072]{1,0:T(8,128)}, f32[32,3072]{1,0:T(8,128)S(1)}, u32[]{:S(2)}, u32[]{:S(2)}) collective-permute-start(f32[32,3072]{1,0:T(8,128)} %entry_product.4.refs_0_.refs_8_), channel_id=1, source_target_pairs={{0,1},{1,0},{2,3},{3,2},{4,5},{5,4},{6,7},{7,6},{8,9},{9,8},{10,11... | collective-permute-start | bytes 1179656 | tf_op jit(solution)/shard_map/ppermute | solution.py:591
  65.3 7.3 %copy-start.4 = (f32[32,3072]{1,0:T(8,128)}, f32[32,3072]{1,0:T(8,128)S(1)}, u32[]{:S(2)}) copy-start(f32[32,3072]{1,0:T(8,128)S(1)} %collective-permute-done.10.refs_2_) | copy-start | bytes 1179652
  72.4 0.8 copy-start.5
  72.6 0.8 copy-start.6
  73.4 1.9 %collective-permute-start.11 = (f32[32,3072]{1,0:T(8,128)}, f32[32,3072]{1,0:T(8,128)S(1)}, u32[]{:S(2)}, u32[]{:S(2)}) collective-permute-start(f32[32,3072]{1,0:T(8,128)} %get-tuple-element.40.refs_2_.refs_10_), channel_id=1, source_target_pairs={{0,1},{1,0},{2,3},{3,2},{4,5},{5,4},{6,7},{7,6},{8,9},{9,8},{10,11... | collective-permute-start | bytes 1179656 | tf_op jit(solution)/shard_map/ppermute | solution.py:591
  73.5 2.4 %collective-permute-start.12 = (f32[32,3072]{1,0:T(8,128)}, f32[32,3072]{1,0:T(8,128)S(1)}, u32[]{:S(2)}, u32[]{:S(2)}) collective-permute-start(f32[32,3072]{1,0:T(8,128)} %get-tuple-element.41.refs_4_.refs_12_), channel_id=1, source_target_pairs={{0,1},{1,0},{2,3},{3,2},{4,5},{5,4},{6,7},{7,6},{8,9},{9,8},{10,11... | collective-permute-start | bytes 1179656 | tf_op jit(solution)/shard_map/ppermute | solution.py:591
  73.9 2.5 %collective-permute-start.13 = (f32[32,3072]{1,0:T(8,128)}, f32[32,3072]{1,0:T(8,128)S(1)}, u32[]{:S(2)}, u32[]{:S(2)}) collective-permute-start(f32[32,3072]{1,0:T(8,128)} %get-tuple-element.42.refs_6_.refs_14_), channel_id=1, source_target_pairs={{0,1},{1,0},{2,3},{3,2},{4,5},{5,4},{6,7},{7,6},{8,9},{9,8},{10,11... | collective-permute-start | bytes 1179656 | tf_op jit(solution)/shard_map/ppermute | solution.py:591
  74.0 2.5 %copy-start.15 = (f32[32,3072]{1,0:T(8,128)}, f32[32,3072]{1,0:T(8,128)S(1)}, u32[]{:S(2)}) copy-start(f32[32,3072]{1,0:T(8,128)S(1)} %collective-permute-done.7.refs_1_.refs_9_) | copy-start | bytes 1179652
  75.3 1.1 copy-start.19
  75.9 0.7 copy-start.20
  76.5 0.7 copy-start.21
  77.2 52.7 %all-to-all-start = ((f32[8,640,128]{2,1,0:T(8,128)}), f32[8,640,128]{2,1,0:T(8,128)S(1)}, u32[]{:S(2)}, u32[]{:S(2)}) async-start(f32[8,640,128]{2,1,0:T(8,128)} %bitcast.29), calls=%async_computation | async-start | bytes 5242880 | tf_op jit(solution)/shard_map/all_to_all | solution.py:677
  101.3 20.6 %collective-permute-start.17 = (f32[32,3072]{1,0:T(8,128)}, f32[32,3072]{1,0:T(8,128)S(1)}, u32[]{:S(2)}, u32[]{:S(2)}) collective-permute-start(f32[32,3072]{1,0:T(8,128)} %entry_product.5.refs_0_.refs_8_), channel_id=1, source_target_pairs={{0,6},{1,7},{2,4},{3,5},{4,2},{5,3},{6,0},{7,1},{8,14},{9,15},{10,... | collective-permute-start | bytes 1179656 | tf_op jit(solution)/shard_map/ppermute | solution.py:591
  104.0 25.9 %collective-permute-start.16 = (f32[32,3072]{1,0:T(8,128)}, f32[32,3072]{1,0:T(8,128)S(1)}, u32[]{:S(2)}, u32[]{:S(2)}) collective-permute-start(f32[32,3072]{1,0:T(8,128)} %entry_product.5.refs_0_.refs_8_), channel_id=1, source_target_pairs={{0,4},{1,5},{2,6},{3,7},{4,0},{5,1},{6,2},{7,3},{8,12},{9,13},{10,... | collective-permute-start | bytes 1179656 | tf_op jit(solution)/shard_map/ppermute | solution.py:591
  104.5 25.4 %collective-permute-start.15 = (f32[32,3072]{1,0:T(8,128)}, f32[32,3072]{1,0:T(8,128)}, u32[]{:S(2)}, u32[]{:S(2)}) collective-permute-start(f32[32,3072]{1,0:T(8,128)} %entry_product.5.refs_0_.refs_8_), channel_id=1, source_target_pairs={{0,2},{1,3},{2,0},{3,1},{4,6},{5,7},{6,4},{7,5},{8,10},{9,11},{10,... | collective-permute-start | bytes 1179656 | tf_op jit(solution)/shard_map/ppermute | solution.py:591
  104.8 27.2 %collective-permute-start.14 = (f32[32,3072]{1,0:T(8,128)}, f32[32,3072]{1,0:T(8,128)}, u32[]{:S(2)}, u32[]{:S(2)}) collective-permute-start(f32[32,3072]{1,0:T(8,128)} %entry_product.5.refs_0_.refs_8_), channel_id=1, source_target_pairs={{0,1},{1,0},{2,3},{3,2},{4,5},{5,4},{6,7},{7,6},{8,9},{9,8},{10,11... | collective-permute-start | bytes 1179656 | tf_op jit(solution)/shard_map/ppermute | solution.py:591
  122.0 7.9 %copy-start.2 = (f32[32,3072]{1,0:T(8,128)}, f32[32,3072]{1,0:T(8,128)S(1)}, u32[]{:S(2)}) copy-start(f32[32,3072]{1,0:T(8,128)S(1)} %collective-permute-done.17.refs_2_) | copy-start | bytes 1179652
  129.9 0.7 copy-start.3
  129.9 1.6 copy-start
  131.5 1.9 %collective-permute-start.18 = (f32[32,3072]{1,0:T(8,128)}, f32[32,3072]{1,0:T(8,128)S(1)}, u32[]{:S(2)}, u32[]{:S(2)}) collective-permute-start(f32[32,3072]{1,0:T(8,128)} %get-tuple-element.51.refs_2_.refs_10_), channel_id=1, source_target_pairs={{0,1},{1,0},{2,3},{3,2},{4,5},{5,4},{6,7},{7,6},{8,9},{9,8},{10,11... | collective-permute-start | bytes 1179656 | tf_op jit(solution)/shard_map/ppermute | solution.py:591
  131.5 2.5 %collective-permute-start.19 = (f32[32,3072]{1,0:T(8,128)}, f32[32,3072]{1,0:T(8,128)S(1)}, u32[]{:S(2)}, u32[]{:S(2)}) collective-permute-start(f32[32,3072]{1,0:T(8,128)} %get-tuple-element.52.refs_4_.refs_12_), channel_id=1, source_target_pairs={{0,1},{1,0},{2,3},{3,2},{4,5},{5,4},{6,7},{7,6},{8,9},{9,8},{10,11... | collective-permute-start | bytes 1179656 | tf_op jit(solution)/shard_map/ppermute | solution.py:591
  132.0 2.5 %collective-permute-start.20 = (f32[32,3072]{1,0:T(8,128)}, f32[32,3072]{1,0:T(8,128)S(1)}, u32[]{:S(2)}, u32[]{:S(2)}) collective-permute-start(f32[32,3072]{1,0:T(8,128)} %get-tuple-element.53.refs_6_.refs_14_), channel_id=1, source_target_pairs={{0,1},{1,0},{2,3},{3,2},{4,5},{5,4},{6,7},{7,6},{8,9},{9,8},{10,11... | collective-permute-start | bytes 1179656 | tf_op jit(solution)/shard_map/ppermute | solution.py:591
  133.5 1.1 copy-start.16
  134.0 0.8 copy-start.17
  134.6 0.8 copy-start.18
  135.4 37.9 %all-to-all-start.1 = ((f32[8,640,128]{2,1,0:T(8,128)}), f32[8,640,128]{2,1,0:T(8,128)S(1)}, u32[]{:S(2)}, u32[]{:S(2)}) async-start(f32[8,640,128]{2,1,0:T(8,128)} %bitcast.28), calls=%async_computation.1 | async-start | bytes 5242880 | tf_op jit(solution)/shard_map/all_to_all | solution.py:677
  173.2 1.5 copy-start.1
Sparse Core Ops, SparseCore 0:
  9.6 39.7 all-gather.4
  55.8 35.9 all-gather.6

commit v13 on v12

--- a/solution.py
+++ b/solution.py
@@ -274,41 +274,40 @@
     )(which, templates, strain, *after)
 
 
-def second_points(x, w2_ref, use):
-    for a, (yr, yi) in enumerate(dft4(x)):
-        y = jnp.concatenate([yr, yi], axis=0)
+def second_points(get, w2_ref, y_ref, use):
+    for r in range(0, LANES, ROWS):
+        for g in range(y_ref.shape[-1] // LANES):
+            x = [(get(0, u, r, g), get(1, u, r, g)) for u in range(FOUR)]
+            for a, y in enumerate(dft4(x)):
+                for p in range(2):
+                    at = slice(p * LANES + r, p * LANES + r + ROWS)
+                    y_ref[a, 0, at, tile(g)], y_ref[a, 1, at, tile(g)] = split(y[p])
+    for a in range(FOUR):
         table = w2_ref[a * 4 * LANES : (a + 1) * 4 * LANES, :]
-        z = rows_dot3(table, split(y))
+        z = rows_dot3(table, (y_ref[a, 0], y_ref[a, 1]))
         use(a, z[:LANES], z[LANES:])
 
 
 def second_kernel(freq, halves, info_ref, scale_ref, *refs):
     part_refs, w2_ref = refs[:halves], refs[halves]
-    out_ref, hold, order = refs[-3:]
+    out_ref, hold, order, y_ref = refs[-4:]
     place = info_ref[0]
     groups, cols = part_refs[0].shape[3:5]
     per = LANES // (halves * cols)
     width = LANES // freq
     scale = scale_ref[info_ref[1 + 2 * pl.program_id(0)]]
 
-    def rows_of(p, u):
-        tiles = [
-            jnp.concatenate(
-                [ref[u * per + f, 0, p, g] for ref in part_refs for f in range(per)],
-                axis=0,
-            )
-            for g in range(groups)
-        ]
-        return jnp.concatenate(tiles, axis=1)
-
-    x = [(rows_of(0, u), rows_of(1, u)) for u in range(FOUR)]
+    def get(p, u, r, g):
+        half, row = divmod(r, per * cols)
+        device, row = divmod(row, cols)
+        return part_refs[half][u * per + device, 0, p, g, row : row + ROWS, :]
 
     def keep(a, re, im):
         for p, value in enumerate((re, im)):
             for g in range(groups):
                 hold[p, g, pl.ds(a, LANES, stride=FOUR), :] = value[:, tile(g)] * scale
 
-    second_points(x, w2_ref, keep)
+    second_points(get, w2_ref, y_ref, keep)
     for p in range(2):
         for g in range(groups):
             turned = hold[p, g].T
@@ -343,6 +342,7 @@
             scratch_shapes=[
                 pltpu.VMEM((2, groups, N2, LANES), F32),
                 pltpu.VMEM((2, FOUR, times, LANES), F32),
+                pltpu.VMEM((FOUR, 2, 2 * LANES, times), BF16),
             ],
         ),
         out_shape=jax.ShapeDtypeStruct(snr.shape, F32),
@@ -443,18 +443,19 @@
 
         lax.fori_loop(0, (end - start - 1) // 2, two, 0)
 
-    for u in range(pieces * cols // LANES):
-        at = tile(u)
-        cos, sin = tw_ref[0, at, :], tw_ref[1, at, :]
-        sum_r, sum_i = total_ref[0, at, :], total_ref[1, at, :]
-        for i in range(TOGETHER):
-            re, im = acc[i, at, :times], acc[i, at, times:]
-            vr, vi = re * cos - im * sin, re * sin + im * cos
-            level_ref[i, 0, at, :] = vr
-            level_ref[i, 1, at, :] = vi
-            sum_r, sum_i = sum_r + vr, sum_i + vi
-        total_ref[0, at, :] = sum_r
-        total_ref[1, at, :] = sum_i
+    for r in range(0, pieces * cols, ROWS):
+        at = slice(r, r + ROWS)
+        for g in range(times // LANES):
+            cos, sin = tw_ref[0, at, tile(g)], tw_ref[1, at, tile(g)]
+            sum_r, sum_i = total_ref[0, at, tile(g)], total_ref[1, at, tile(g)]
+            for i in range(TOGETHER):
+                re, im = acc[i, at, tile(g)], acc[i, at, tile(times // LANES + g)]
+                vr, vi = re * cos - im * sin, re * sin + im * cos
+                level_ref[i, 0, at, tile(g)] = vr
+                level_ref[i, 1, at, tile(g)] = vi
+                sum_r, sum_i = sum_r + vr, sum_i + vi
+            total_ref[0, at, tile(g)] = sum_r
+            total_ref[1, at, tile(g)] = sum_i
 
 
 def bins_first(half, banks, place, edges, own, rest, table, twist, after):
@@ -491,7 +492,7 @@
 
 def bins_second_kernel(halves, which_ref, scale_ref, gain_ref, share_ref, *refs):
     level_refs, total_refs = refs[:halves], refs[halves : 2 * halves]
-    w2_ref, out_ref, snr_ref, chi, hold = refs[2 * halves :]
+    w2_ref, out_ref, snr_ref, chi, hold, y_ref = refs[2 * halves :]
     times = out_ref.shape[0]
     part_rows = LANES // halves
     step = pl.program_id(0)
@@ -500,9 +501,10 @@
     def _():
         chi[...] = jnp.zeros_like(chi)
 
-    def rows_of(get, u):
-        at = slice(u * part_rows, (u + 1) * part_rows)
-        return jnp.concatenate([get(h, at) for h in range(halves)], axis=0)
+    def place_of(u, r):
+        half, row = divmod(r, part_rows)
+        row += u * part_rows
+        return half, slice(row, row + ROWS)
 
     def keep(a, re, im):
         chi[a] += re * re + im * im
@@ -510,28 +512,27 @@
     for i in range(TOGETHER):
         gain, share = gain_ref[step * TOGETHER + i], share_ref[step * TOGETHER + i]
 
-        def deviation(p):
-            return lambda h, at: (
-                level_refs[h][i, p, at, :] * gain - total_refs[h][p, at, :] * share
-            )
-
-        x = [tuple(rows_of(deviation(p), u) for p in range(2)) for u in range(FOUR)]
-        second_points(x, w2_ref, keep)
+        def deviation(p, u, r, g):
+            h, at = place_of(u, r)
+            whole = total_refs[h][p, at, tile(g)]
+            return level_refs[h][i, p, at, tile(g)] * gain - whole * share
+
+        second_points(deviation, w2_ref, y_ref.at[i], keep)
 
     @pl.when(step == BINS // TOGETHER - 1)
     def _():
         scale = scale_ref[which_ref[0]]
 
-        def whole(p):
-            return lambda h, at: total_refs[h][p, at, :] * scale
+        def whole(p, u, r, g):
+            h, at = place_of(u, r)
+            return total_refs[h][p, at, tile(g)] * scale
 
         def put(a, re, im):
             for p, value in enumerate((re, im)):
                 for g in range(times // LANES):
                     hold[p, g, pl.ds(a, LANES, stride=FOUR), :] = value[:, tile(g)]
 
-        y = [tuple(rows_of(whole(p), u) for p in range(2)) for u in range(FOUR)]
-        second_points(y, w2_ref, put)
+        second_points(whole, w2_ref, y_ref.at[0], put)
         for g in range(times // LANES):
             for a in range(FOUR):
                 hold[2, g, pl.ds(a, LANES, stride=FOUR), :] = chi[a, :, tile(g)]
@@ -561,6 +562,7 @@
             scratch_shapes=[
                 pltpu.VMEM((FOUR, LANES, times), F32),
                 pltpu.VMEM((3, times // LANES, N2, LANES), F32),
+                pltpu.VMEM((TOGETHER, FOUR, 2, 2 * LANES, times), BF16),
             ],
         ),
         out_shape=[

time: 193 us -> 194 us (level)
  transfers between devices with their start and end apart: 25 -> 25, of which waited for: 15 -> 15; matrix products, arithmetic and copies ran while one was open for 9% -> 9% of each run, Pallas kernels for 42% -> 41%
where the time goes in v13:
time: 194 us; the launch traced here: 192 us
  Pallas kernels  92.9 us (48%)
  waiting for transfers between devices  37.2 us (19%)
  starting transfers between devices  21.3 us (11%)
  other arithmetic  16 us (8%)
  between operations  15.6 us (8%)
  local copies, waits for them, and re-layouts  9.31 us (5%)
    pallas_call x2, Pallas kernels, bins_first(): pl.pallas_call(functools.partial(bins_first_kernel, len(own), banks), gri...  33.5 us
    ppermute x21, waiting for transfers between devices, swap(): return lax.ppermute(x, 'freq', [(i, i ^ k) for i in range(freq)])  33.1 us
    pallas_call x1, Pallas kernels, bins_second(): pl.pallas_call(functools.partial(bins_second_kernel, halves), grid_spec=p...  17.6 us
    pallas_call x2, Pallas kernels, first_section(): pl.pallas_call(functools.partial(first_kernel, freq), grid_spec=pltpu.Pre...  15.4 us
    ppermute x21, starting transfers between devices, swap(): return lax.ppermute(x, 'freq', [(i, i ^ k) for i in range(freq)])  13.8 us
    pallas_call x1, Pallas kernels, second_section(): pl.pallas_call(functools.partial(second_kernel, freq, halves), grid_spec=...  10.9 us
    pallas_call x3, Pallas kernels, entry_product(): pl.pallas_call(functools.partial(entry_kernel, steps, banks), grid_spec=p...  9.43 us
    all_to_all x2, starting transfers between devices, per_device(): lax.all_to_all(ready.reshape(freq, -1, LANES), 'freq', split_axis=0, conc...  7.43 us
  transfers between devices with their start and end apart: 25, of which 15 were waited for; matrix products, arithmetic and copies ran while one was open for 9% of the time, Pallas kernels for 41%

profile of v13, /device:TPU:0, one launch (start us, length us, event | category | flops | bytes accessed | tf_op | source)
XLA Modules:
  0.0 192.2 jit_solution(12964142622503168559)
XLA Ops:
  7.2 2.1 %fusion.49 = (f32[3,2,32,512]{3,2,1,0:T(8,128)}, f32[3,2,32,512]{3,2,1,0:T(8,128)}) fusion(f32[3,2,64,512]{3,2,1,0:T(8,128)} %param.9), kind=kLoop, calls=%fused_computation.114 | loop fusion | bytes 1572864 | tf_op jit(solution)/shard_map/slice | solution.py:613
  10.7 1.7 add_reduce_fusion
  12.7 0.7 pad_add_fusion.1.which_ref
  13.3 4.0 %entry_product.3 = f32[64,1024]{1,0:T(8,128)} custom-call(s32[3]{0:T(128)} %pad_add_fusion.1.which_ref, f32[2,2,64,2048]{3,2,1,0:T(8,128)} %tmpl_ref.9, f32[1,3,2,64,512]{4,3,2,1,0:T(8,128)} %bitcast.31, f32[3,2,32,512]{3,2,1,0:T(8,128)} %get-tuple-element.67.refs_0_, f32[3,2,32,512]{3,2,1,0:T(8,128)} %get-tuple-element.66.refs_1_), custom_call_target="tpu_custom_call" | custom-call | flops 1048576 | bytes 1048576 | tf_op jit(solution)/shard_map/entry_product/pallas_call | solution.py:258
  17.4 1.0 select_maximum_fusion.refs_0_
  18.4 4.0 %collective-permute-start.5 = (f32[72,1024]{1,0:T(8,128)S(1)}, f32[72,1024]{1,0:T(8,128)S(1)}, u32[]{:S(2)}, u32[]{:S(2)}) collective-permute-start(f32[72,1024]{1,0:T(8,128)S(1)} %select_maximum_fusion.refs_0_), channel_id=1, source_target_pairs={{0,6},{1,7},{2,4},{3,5},{4,2},{5,3},{6,0},{7,1},{8,14},{9,15},{10,... | collective-permute-start | bytes 884744 | tf_op jit(solution)/shard_map/ppermute | solution.py:593
  22.3 0.5 collective-permute-start.3
  23.0 0.3 fusion.24
  23.3 0.7 pad_add_fusion.4.place_ref
  24.4 1.0 fusion.39
  25.4 0.7 pad_maximum_fusion.4.block_ref
  26.1 0.7 pad_maximum_fusion.3.inner_ref
  26.8 2.1 %fusion.12 = (f32[1,256,256]{2,1,0:T(8,128)S(1)}, f32[1,256,256]{2,1,0:T(8,128)S(1)}, f32[1,256,256]{2,1,0:T(8,128)S(1)}, f32[1,256,256]{2,1,0:T(8,128)S(1)}) fusion(s32[256]{0:T(256)S(1)} %iota_add_fusion, s32[256]{0:T(256)S(1)} %add_add_fusion, s32[256]{0:T(256)S(1)} %fusion.45), kind=kLoop, calls=%fused_computation.34 | loop fusion | flops 1835008 | bytes 1051648 | tf_op jit(solution)/shard_map/cos | solution.py:64
  28.9 6.1 %bank_table.1 = (bf16[4096,512]{1,0:T(8,128)(2,1)}, bf16[4096,512]{1,0:T(8,128)(2,1)}) custom-call(f32[32,2,256]{2,1,0:T(2,128)} %pad_maximum_fusion.4.block_ref, f32[2,64,256]{2,1,0:T(8,128)} %pad_maximum_fusion.3.inner_ref), custom_call_target="tpu_custom_call" | custom-call | flops 1048576 | bytes 1048576 | tf_op jit(solution)/shard_map/bank_table/pallas_call | solution.py:380
  34.9 1.0 pad_maximum_fusion.1
  36.0 2.1 %fusion.10 = (f32[1,64,2048]{2,1,0:T(8,128)S(1)}, f32[1,64,2048]{2,1,0:T(8,128)S(1)}) fusion(s32[2048]{0:T(1024)S(1)} %fusion.35, s32[64]{0:T(128)S(1)} %iota_add_fusion.1), kind=kLoop, calls=%fused_computation.31 | loop fusion | flops 1835008 | bytes 1057024 | tf_op jit(solution)/shard_map/cos | solution.py:64
  38.1 1.1 pad_maximum_fusion.tw_ref
  39.2 0.6 pad_add_fusion.2.info_ref
  39.8 0.6 pad_add_fusion.3.edge_ref
  40.5 0.5 collective-permute-start.6
  41.3 0.5 collective-permute-start.2
  41.9 0.4 collective-permute-done.6.refs_6_.refs_7_
  42.3 0.4 collective-permute-done.4.refs_4_.refs_5_
  42.8 0.3 collective-permute-done.2.refs_2_.refs_3_
  43.4 0.6 dynamic_slice.10
  44.1 1.2 bitcast_multiply_fusion
  45.4 4.0 %all-gather.5.cloned.1.call-done = f32[12,2,32,512]{3,2,1,0:T(8,128)} async-done(((f32[3,2,32,512]{3,2,1,0:T(8,128)}), f32[12,2,32,512]{3,2,1,0:T(8,128)}) %all-gather.5.cloned.1.call-update) | async-done | bytes 1572880 | tf_op jit(solution)/shard_map/all_gather | solution.py:614
  49.4 2.7 %entry_product.4.refs_0_.refs_8_ = f32[32,3072]{1,0:T(8,128)} custom-call(s32[3]{0:T(128)} %pad_add_fusion.1.which_ref, f32[2,2,64,2048]{3,2,1,0:T(8,128)} %tmpl_ref.9, f32[4,3,2,32,512]{4,3,2,1,0:T(8,128)} %bitcast.34, f32[72,1024]{1,0:T(8,128)} %copy-done.10, f32[72,1024]{1,0:T(8,128)} %copy-done.9, f32[72,1024]{1,0:T(8,128)} %copy-done.13, ...), custom_call_target="tpu_custom_call" | custom-call | flops 1048576 | bytes 1048576 | tf_op jit(solution)/shard_map/entry_product/pallas_call | solution.py:258
  52.1 2.4 %collective-permute-start.10 = (f32[32,3072]{1,0:T(8,128)}, f32[32,3072]{1,0:T(8,128)S(1)}, u32[]{:S(2)}, u32[]{:S(2)}) collective-permute-start(f32[32,3072]{1,0:T(8,128)} %entry_product.4.refs_0_.refs_8_), channel_id=1, source_target_pairs={{0,6},{1,7},{2,4},{3,5},{4,2},{5,3},{6,0},{7,1},{8,14},{9,15},{10,... | collective-permute-start | bytes 1179656 | tf_op jit(solution)/shard_map/ppermute | solution.py:593
  54.6 0.5 collective-permute-start.9
  55.1 0.5 collective-permute-start.8
  55.7 7.7 %first_section.2 = (f32[8,5,2,2,32,128]{5,4,3,2,1,0:T(8,128)}, f32[8,128]{1,0:T(8,128)}) custom-call(s32[11]{0:T(128)} %pad_add_fusion.2.info_ref, f32[2,2,64,2048]{3,2,1,0:T(8,128)} %tmpl_ref.9, f32[4,3,2,32,512]{4,3,2,1,0:T(8,128)} %bitcast.35, bf16[256,256]{1,0:T(8,128)(2,1)} %constant.173.clone.wh_ref, bf16[256,256]{1,0:T(8,128)(2,1)} %constant.174.clone.wl_ref, ...), custom_call_target="tpu_custom_call" | custom-call | flops 2516582400 | bytes 16777216 | tf_op jit(solution)/shard_map/first_section/pallas_call | solution.py:196
  63.4 1.9 collective-permute-done.10.refs_2_
  65.3 7.1 %collective-permute-done.9.refs_1_ = f32[32,3072]{1,0:T(8,128)S(1)} collective-permute-done((f32[32,3072]{1,0:T(8,128)}, f32[32,3072]{1,0:T(8,128)S(1)}, u32[]{:S(2)}, u32[]{:S(2)}) %collective-permute-start.9) | collective-permute-done | bytes 393248 | tf_op jit(solution)/shard_map/ppermute | solution.py:593
  72.4 0.2 collective-permute-done.8.refs_0_
  72.6 0.6 copy-done.5
  73.2 0.2 copy-done.6
  73.5 0.4 collective-permute-start.12
  74.0 1.3 collective-permute-done.11.refs_3_.refs_11_
  75.3 0.6 collective-permute-done.12.refs_5_.refs_13_
  75.9 0.6 collective-permute-done.13.refs_7_.refs_15_
  76.6 0.6 copy-done.21
  77.2 3.8 %all-to-all-start = ((f32[8,640,128]{2,1,0:T(8,128)}), f32[8,640,128]{2,1,0:T(8,128)S(1)}, u32[]{:S(2)}, u32[]{:S(2)}) async-start(f32[8,640,128]{2,1,0:T(8,128)} %bitcast.29), calls=%async_computation | async-start | bytes 5242880 | tf_op jit(solution)/shard_map/all_to_all | solution.py:679
  81.0 16.8 %bins_first.2 = (f32[16,2,256,256]{3,2,1,0:T(8,128)}, f32[2,256,256]{2,1,0:T(8,128)}) custom-call(s32[2]{0:T(128)} %pad_add_fusion.4.place_ref, s32[17]{0:T(128)} %pad_add_fusion.3.edge_ref, f32[72,1024]{1,0:T(8,128)} %copy-done.14, f32[72,1024]{1,0:T(8,128)} %copy-done.10, f32[72,1024]{1,0:T(8,128)} %copy-done.9, f32[72,1024]{1,0:T(8,128)} %copy-done.13, ...), custom_call_target="tpu_custom_call" | custom-call | flops 1048576 | bytes 1048576 | tf_op jit(solution)/shard_map/bins_first/pallas_call | solution.py:466
  97.8 2.7 %entry_product.5.refs_0_.refs_8_ = f32[32,3072]{1,0:T(8,128)} custom-call(s32[3]{0:T(128)} %pad_add_fusion.1.which_ref, f32[2,2,64,2048]{3,2,1,0:T(8,128)} %tmpl_ref.9, f32[4,3,2,32,512]{4,3,2,1,0:T(8,128)} %bitcast.32, f32[16,2,256,256]{3,2,1,0:T(8,128)} %get-tuple-element.48.refs_0_), custom_call_target="tpu_custom_call" | custom-call | flops 1048576 | bytes 1048576 | tf_op jit(solution)/shard_map/entry_product/pallas_call | solution.py:258
  100.5 2.7 %collective-permute-start.17 = (f32[32,3072]{1,0:T(8,128)}, f32[32,3072]{1,0:T(8,128)S(1)}, u32[]{:S(2)}, u32[]{:S(2)}) collective-permute-start(f32[32,3072]{1,0:T(8,128)} %entry_product.5.refs_0_.refs_8_), channel_id=1, source_target_pairs={{0,6},{1,7},{2,4},{3,5},{4,2},{5,3},{6,0},{7,1},{8,14},{9,15},{10,... | collective-permute-start | bytes 1179656 | tf_op jit(solution)/shard_map/ppermute | solution.py:593
  103.2 0.5 collective-permute-start.16
  103.7 0.3 collective-permute-start.15
  104.0 7.7 %first_section.3 = (f32[8,5,2,2,32,128]{5,4,3,2,1,0:T(8,128)}, f32[8,128]{1,0:T(8,128)}) custom-call(s32[11]{0:T(128)} %pad_add_fusion.2.info_ref, f32[2,2,64,2048]{3,2,1,0:T(8,128)} %tmpl_ref.9, f32[4,3,2,32,512]{4,3,2,1,0:T(8,128)} %bitcast.33, bf16[256,256]{1,0:T(8,128)(2,1)} %constant.173.clone.wh_ref, bf16[256,256]{1,0:T(8,128)(2,1)} %constant.174.clone.wl_ref, ...), custom_call_target="tpu_custom_call" | custom-call | flops 2516582400 | bytes 16777216 | tf_op jit(solution)/shard_map/first_section/pallas_call | solution.py:196
  111.7 10.3 %collective-permute-done.17.refs_2_ = f32[32,3072]{1,0:T(8,128)S(1)} collective-permute-done((f32[32,3072]{1,0:T(8,128)}, f32[32,3072]{1,0:T(8,128)S(1)}, u32[]{:S(2)}, u32[]{:S(2)}) %collective-permute-start.17) | collective-permute-done | bytes 393248 | tf_op jit(solution)/shard_map/ppermute | solution.py:593
  122.0 7.6 %collective-permute-done.16.refs_1_ = f32[32,3072]{1,0:T(8,128)S(1)} collective-permute-done((f32[32,3072]{1,0:T(8,128)}, f32[32,3072]{1,0:T(8,128)S(1)}, u32[]{:S(2)}, u32[]{:S(2)}) %collective-permute-start.16) | collective-permute-done | bytes 393248 | tf_op jit(solution)/shard_map/ppermute | solution.py:593
  129.6 0.7 copy-done.3
  130.3 0.9 copy-done
  131.2 0.5 collective-permute-start.19
  131.7 1.4 collective-permute-done.18.refs_3_.refs_11_
  133.1 0.6 collective-permute-done.19.refs_5_.refs_13_
  133.7 0.6 collective-permute-done.20.refs_7_.refs_15_
  134.3 0.2 copy-done.17
  134.4 0.6 copy-done.18
  135.0 3.6 %all-to-all-start.1 = ((f32[8,640,128]{2,1,0:T(8,128)}), f32[8,640,128]{2,1,0:T(8,128)S(1)}, u32[]{:S(2)}, u32[]{:S(2)}) async-start(f32[8,640,128]{2,1,0:T(8,128)} %bitcast.28), calls=%async_computation.1 | async-start | bytes 5242880 | tf_op jit(solution)/shard_map/all_to_all | solution.py:679
  138.7 16.7 %bins_first.3 = (f32[16,2,256,256]{3,2,1,0:T(8,128)}, f32[2,256,256]{2,1,0:T(8,128)}) custom-call(s32[2]{0:T(128)} %pad_add_fusion.4.place_ref, s32[17]{0:T(128)} %pad_add_fusion.3.edge_ref, f32[72,1024]{1,0:T(8,128)} %copy-done.14, f32[72,1024]{1,0:T(8,128)} %copy-done.10, f32[72,1024]{1,0:T(8,128)} %copy-done.9, f32[72,1024]{1,0:T(8,128)} %copy-done.13, ...), custom_call_target="tpu_custom_call" | custom-call | flops 1048576 | bytes 1048576 | tf_op jit(solution)/shard_map/bins_first/pallas_call | solution.py:466
  155.4 17.6 %bins_second.1 = (f32[256,512]{1,0:T(8,128)}, f32[2,3,2,256,512]{4,3,2,1,0:T(8,128)}) custom-call(s32[3]{0:T(128)} %pad_add_fusion.1.which_ref, f32[2]{0:T(128)} %copy-done.22, f32[16]{0:T(128)} %get-tuple-element.54.gain_ref, f32[16]{0:T(128)} %get-tuple-element.55.share_ref, f32[16,2,256,256]{3,2,1,0:T(8,128)} %get-tuple-element.48.refs_0_, ...), custom_call_target="tpu_custom_call" | custom-call | flops 1048576 | bytes 1048576 | tf_op jit(solution)/shard_map/bins_second/pallas_call | solution.py:549
  173.0 1.5 copy-done.1
  174.5 10.9 %second_section.1 = f32[2,3,2,256,512]{4,3,2,1,0:T(8,128)} custom-call(s32[11]{0:T(128)} %pad_add_fusion.2.info_ref, f32[2]{0:T(128)} %copy-done.22, f32[8,5,2,2,32,128]{5,4,3,2,1,0:T(8,128)} %bitcast.27, f32[8,5,2,2,32,128]{5,4,3,2,1,0:T(8,128)} %bitcast.30, bf16[2048,256]{1,0:T(8,128)(2,1)} %constant.175.clone.refs_4_.refs_2_, ...), custom_call_target="tpu_custom_call", output_to_operand_aliasing={{}: (5, {})} | custom-call | flops 1048576 | bytes 1048576 | tf_op jit(solution)/shard_map/second_section/pallas_call | solution.py:333
  (101 shorter events, 2.5 us)
Async XLA Ops:
  7.2 42.2 %all-gather.5.cloned.1.call-start = ((), (), s32[]{:S(2)}) async-start(), calls=%async_computation.2 | async-start | bytes 1966080 | tf_op jit(solution)/shard_map/all_gather | solution.py:614
  9.3 88.5 %all-gather.7.cloned.1.call-start = ((), (), s32[]{:S(2)}) async-start(), calls=%async_computation.3 | async-start | bytes 1966080 | tf_op jit(solution)/shard_map/all_gather | solution.py:614
  12.4 11.8 %copy-start.23 = (s32[2,15]{1,0:T(2,128)S(1)}, s32[2,15]{1,0:T(2,128)}, u32[]{:S(2)}) copy-start(s32[2,15]{1,0:T(2,128)} %param.13) | copy-start | bytes 364
  18.4 20.8 %copy-start.14 = (f32[72,1024]{1,0:T(8,128)}, f32[72,1024]{1,0:T(8,128)S(1)}, u32[]{:S(2)}) copy-start(f32[72,1024]{1,0:T(8,128)S(1)} %select_maximum_fusion.refs_0_) | copy-start | bytes 884740
  18.4 22.1 %collective-permute-start.5 = (f32[72,1024]{1,0:T(8,128)S(1)}, f32[72,1024]{1,0:T(8,128)S(1)}, u32[]{:S(2)}, u32[]{:S(2)}) collective-permute-start(f32[72,1024]{1,0:T(8,128)S(1)} %select_maximum_fusion.refs_0_), channel_id=1, source_target_pairs={{0,6},{1,7},{2,4},{3,5},{4,2},{5,3},{6,0},{7,1},{8,14},{9,15},{10,... | collective-permute-start | bytes 884744 | tf_op jit(solution)/shard_map/ppermute | solution.py:593
  22.3 18.7 %collective-permute-start.3 = (f32[72,1024]{1,0:T(8,128)S(1)}, f32[72,1024]{1,0:T(8,128)S(1)}, u32[]{:S(2)}, u32[]{:S(2)}) collective-permute-start(f32[72,1024]{1,0:T(8,128)S(1)} %select_maximum_fusion.refs_0_), channel_id=1, source_target_pairs={{0,4},{1,5},{2,6},{3,7},{4,0},{5,1},{6,2},{7,3},{8,12},{9,13},{10,... | collective-permute-start | bytes 884744 | tf_op jit(solution)/shard_map/ppermute | solution.py:593
  22.8 18.3 %collective-permute-start.1 = (f32[72,1024]{1,0:T(8,128)S(1)}, f32[72,1024]{1,0:T(8,128)S(1)}, u32[]{:S(2)}, u32[]{:S(2)}) collective-permute-start(f32[72,1024]{1,0:T(8,128)S(1)} %select_maximum_fusion.refs_0_), channel_id=1, source_target_pairs={{0,2},{1,3},{2,0},{3,1},{4,6},{5,7},{6,4},{7,5},{8,10},{9,11},{10,... | collective-permute-start | bytes 884744 | tf_op jit(solution)/shard_map/ppermute | solution.py:593
  23.0 18.8 %collective-permute-start = (f32[72,1024]{1,0:T(8,128)S(1)}, f32[72,1024]{1,0:T(8,128)S(1)}, u32[]{:S(2)}, u32[]{:S(2)}) collective-permute-start(f32[72,1024]{1,0:T(8,128)S(1)} %select_maximum_fusion.refs_0_), channel_id=1, source_target_pairs={{0,1},{1,0},{2,3},{3,2},{4,5},{5,4},{6,7},{7,6},{8,9},{9,8},{10,11... | collective-permute-start | bytes 884744 | tf_op jit(solution)/shard_map/ppermute | solution.py:593
  40.4 9.0 %copy-start.7 = (f32[72,1024]{1,0:T(8,128)}, f32[72,1024]{1,0:T(8,128)S(1)}, u32[]{:S(2)}) copy-start(f32[72,1024]{1,0:T(8,128)S(1)} %collective-permute-done.5.refs_5_.refs_6_) | copy-start | bytes 884740
  40.5 1.7 collective-permute-start.6
  41.0 8.4 %copy-start.8 = (f32[72,1024]{1,0:T(8,128)}, f32[72,1024]{1,0:T(8,128)S(1)}, u32[]{:S(2)}) copy-start(f32[72,1024]{1,0:T(8,128)S(1)} %collective-permute-done.3.refs_3_.refs_4_) | copy-start | bytes 884740
  41.1 1.6 collective-permute-start.4
  41.2 8.2 %copy-start.9 = (f32[72,1024]{1,0:T(8,128)}, f32[72,1024]{1,0:T(8,128)S(1)}, u32[]{:S(2)}) copy-start(f32[72,1024]{1,0:T(8,128)S(1)} %collective-permute-done.1.refs_1_.refs_2_) | copy-start | bytes 884740
  41.3 1.9 collective-permute-start.2
  41.8 7.6 %copy-start.10 = (f32[72,1024]{1,0:T(8,128)}, f32[72,1024]{1,0:T(8,128)S(1)}, u32[]{:S(2)}) copy-start(f32[72,1024]{1,0:T(8,128)S(1)} %collective-permute-done.refs_0_.refs_1_) | copy-start | bytes 884740
  42.2 7.2 %copy-start.11 = (f32[72,1024]{1,0:T(8,128)}, f32[72,1024]{1,0:T(8,128)S(1)}, u32[]{:S(2)}) copy-start(f32[72,1024]{1,0:T(8,128)S(1)} %collective-permute-done.6.refs_6_.refs_7_) | copy-start | bytes 884740
  42.7 6.7 %copy-start.12 = (f32[72,1024]{1,0:T(8,128)}, f32[72,1024]{1,0:T(8,128)S(1)}, u32[]{:S(2)}) copy-start(f32[72,1024]{1,0:T(8,128)S(1)} %collective-permute-done.4.refs_4_.refs_5_) | copy-start | bytes 884740
  43.1 6.3 %copy-start.13 = (f32[72,1024]{1,0:T(8,128)}, f32[72,1024]{1,0:T(8,128)S(1)}, u32[]{:S(2)}) copy-start(f32[72,1024]{1,0:T(8,128)S(1)} %collective-permute-done.2.refs_2_.refs_3_) | copy-start | bytes 884740
  43.4 8.8 %copy-start.22 = (f32[2]{0:T(128)}, f32[2]{0:T(128)S(1)}, u32[]{:S(2)}) copy-start(f32[2]{0:T(128)S(1)} %rsqrt.6.scale_ref) | copy-start | bytes 28
  52.1 13.2 %collective-permute-start.10 = (f32[32,3072]{1,0:T(8,128)}, f32[32,3072]{1,0:T(8,128)S(1)}, u32[]{:S(2)}, u32[]{:S(2)}) collective-permute-start(f32[32,3072]{1,0:T(8,128)} %entry_product.4.refs_0_.refs_8_), channel_id=1, source_target_pairs={{0,6},{1,7},{2,4},{3,5},{4,2},{5,3},{6,0},{7,1},{8,14},{9,15},{10,... | collective-permute-start | bytes 1179656 | tf_op jit(solution)/shard_map/ppermute | solution.py:593
  54.6 17.8 %collective-permute-start.9 = (f32[32,3072]{1,0:T(8,128)}, f32[32,3072]{1,0:T(8,128)S(1)}, u32[]{:S(2)}, u32[]{:S(2)}) collective-permute-start(f32[32,3072]{1,0:T(8,128)} %entry_product.4.refs_0_.refs_8_), channel_id=1, source_target_pairs={{0,4},{1,5},{2,6},{3,7},{4,0},{5,1},{6,2},{7,3},{8,12},{9,13},{10,... | collective-permute-start | bytes 1179656 | tf_op jit(solution)/shard_map/ppermute | solution.py:593
  55.1 17.5 %collective-permute-start.8 = (f32[32,3072]{1,0:T(8,128)}, f32[32,3072]{1,0:T(8,128)S(1)}, u32[]{:S(2)}, u32[]{:S(2)}) collective-permute-start(f32[32,3072]{1,0:T(8,128)} %entry_product.4.refs_0_.refs_8_), channel_id=1, source_target_pairs={{0,2},{1,3},{2,0},{3,1},{4,6},{5,7},{6,4},{7,5},{8,10},{9,11},{10,... | collective-permute-start | bytes 1179656 | tf_op jit(solution)/shard_map/ppermute | solution.py:593
  55.6 18.3 %collective-permute-start.7 = (f32[32,3072]{1,0:T(8,128)}, f32[32,3072]{1,0:T(8,128)S(1)}, u32[]{:S(2)}, u32[]{:S(2)}) collective-permute-start(f32[32,3072]{1,0:T(8,128)} %entry_product.4.refs_0_.refs_8_), channel_id=1, source_target_pairs={{0,1},{1,0},{2,3},{3,2},{4,5},{5,4},{6,7},{7,6},{8,9},{9,8},{10,11... | collective-permute-start | bytes 1179656 | tf_op jit(solution)/shard_map/ppermute | solution.py:593
  65.3 7.3 %copy-start.4 = (f32[32,3072]{1,0:T(8,128)}, f32[32,3072]{1,0:T(8,128)S(1)}, u32[]{:S(2)}) copy-start(f32[32,3072]{1,0:T(8,128)S(1)} %collective-permute-done.10.refs_2_) | copy-start | bytes 1179652
  72.4 0.8 copy-start.5
  72.6 0.8 copy-start.6
  73.4 1.9 %collective-permute-start.11 = (f32[32,3072]{1,0:T(8,128)}, f32[32,3072]{1,0:T(8,128)S(1)}, u32[]{:S(2)}, u32[]{:S(2)}) collective-permute-start(f32[32,3072]{1,0:T(8,128)} %get-tuple-element.40.refs_2_.refs_10_), channel_id=1, source_target_pairs={{0,1},{1,0},{2,3},{3,2},{4,5},{5,4},{6,7},{7,6},{8,9},{9,8},{10,11... | collective-permute-start | bytes 1179656 | tf_op jit(solution)/shard_map/ppermute | solution.py:593
  73.5 2.4 %collective-permute-start.12 = (f32[32,3072]{1,0:T(8,128)}, f32[32,3072]{1,0:T(8,128)S(1)}, u32[]{:S(2)}, u32[]{:S(2)}) collective-permute-start(f32[32,3072]{1,0:T(8,128)} %get-tuple-element.41.refs_4_.refs_12_), channel_id=1, source_target_pairs={{0,1},{1,0},{2,3},{3,2},{4,5},{5,4},{6,7},{7,6},{8,9},{9,8},{10,11... | collective-permute-start | bytes 1179656 | tf_op jit(solution)/shard_map/ppermute | solution.py:593
  73.9 2.5 %collective-permute-start.13 = (f32[32,3072]{1,0:T(8,128)}, f32[32,3072]{1,0:T(8,128)S(1)}, u32[]{:S(2)}, u32[]{:S(2)}) collective-permute-start(f32[32,3072]{1,0:T(8,128)} %get-tuple-element.42.refs_6_.refs_14_), channel_id=1, source_target_pairs={{0,1},{1,0},{2,3},{3,2},{4,5},{5,4},{6,7},{7,6},{8,9},{9,8},{10,11... | collective-permute-start | bytes 1179656 | tf_op jit(solution)/shard_map/ppermute | solution.py:593
  74.0 2.5 %copy-start.15 = (f32[32,3072]{1,0:T(8,128)}, f32[32,3072]{1,0:T(8,128)S(1)}, u32[]{:S(2)}) copy-start(f32[32,3072]{1,0:T(8,128)S(1)} %collective-permute-done.7.refs_1_.refs_9_) | copy-start | bytes 1179652
  75.3 1.1 copy-start.19
  75.9 0.7 copy-start.20
  76.5 0.7 copy-start.21
  77.2 52.3 %all-to-all-start = ((f32[8,640,128]{2,1,0:T(8,128)}), f32[8,640,128]{2,1,0:T(8,128)S(1)}, u32[]{:S(2)}, u32[]{:S(2)}) async-start(f32[8,640,128]{2,1,0:T(8,128)} %bitcast.29), calls=%async_computation | async-start | bytes 5242880 | tf_op jit(solution)/shard_map/all_to_all | solution.py:679
  100.5 21.5 %collective-permute-start.17 = (f32[32,3072]{1,0:T(8,128)}, f32[32,3072]{1,0:T(8,128)S(1)}, u32[]{:S(2)}, u32[]{:S(2)}) collective-permute-start(f32[32,3072]{1,0:T(8,128)} %entry_product.5.refs_0_.refs_8_), channel_id=1, source_target_pairs={{0,6},{1,7},{2,4},{3,5},{4,2},{5,3},{6,0},{7,1},{8,14},{9,15},{10,... | collective-permute-start | bytes 1179656 | tf_op jit(solution)/shard_map/ppermute | solution.py:593
  103.2 26.4 %collective-permute-start.16 = (f32[32,3072]{1,0:T(8,128)}, f32[32,3072]{1,0:T(8,128)S(1)}, u32[]{:S(2)}, u32[]{:S(2)}) collective-permute-start(f32[32,3072]{1,0:T(8,128)} %entry_product.5.refs_0_.refs_8_), channel_id=1, source_target_pairs={{0,4},{1,5},{2,6},{3,7},{4,0},{5,1},{6,2},{7,3},{8,12},{9,13},{10,... | collective-permute-start | bytes 1179656 | tf_op jit(solution)/shard_map/ppermute | solution.py:593
  103.7 25.8 %collective-permute-start.15 = (f32[32,3072]{1,0:T(8,128)}, f32[32,3072]{1,0:T(8,128)}, u32[]{:S(2)}, u32[]{:S(2)}) collective-permute-start(f32[32,3072]{1,0:T(8,128)} %entry_product.5.refs_0_.refs_8_), channel_id=1, source_target_pairs={{0,2},{1,3},{2,0},{3,1},{4,6},{5,7},{6,4},{7,5},{8,10},{9,11},{10,... | collective-permute-start | bytes 1179656 | tf_op jit(solution)/shard_map/ppermute | solution.py:593
  104.0 27.7 %collective-permute-start.14 = (f32[32,3072]{1,0:T(8,128)}, f32[32,3072]{1,0:T(8,128)}, u32[]{:S(2)}, u32[]{:S(2)}) collective-permute-start(f32[32,3072]{1,0:T(8,128)} %entry_product.5.refs_0_.refs_8_), channel_id=1, source_target_pairs={{0,1},{1,0},{2,3},{3,2},{4,5},{5,4},{6,7},{7,6},{8,9},{9,8},{10,11... | collective-permute-start | bytes 1179656 | tf_op jit(solution)/shard_map/ppermute | solution.py:593
  122.0 7.6 %copy-start.2 = (f32[32,3072]{1,0:T(8,128)}, f32[32,3072]{1,0:T(8,128)S(1)}, u32[]{:S(2)}) copy-start(f32[32,3072]{1,0:T(8,128)S(1)} %collective-permute-done.17.refs_2_) | copy-start | bytes 1179652
  129.5 0.7 copy-start.3
  129.6 1.6 copy-start
  131.2 1.9 %collective-permute-start.18 = (f32[32,3072]{1,0:T(8,128)}, f32[32,3072]{1,0:T(8,128)S(1)}, u32[]{:S(2)}, u32[]{:S(2)}) collective-permute-start(f32[32,3072]{1,0:T(8,128)} %get-tuple-element.51.refs_2_.refs_10_), channel_id=1, source_target_pairs={{0,1},{1,0},{2,3},{3,2},{4,5},{5,4},{6,7},{7,6},{8,9},{9,8},{10,11... | collective-permute-start | bytes 1179656 | tf_op jit(solution)/shard_map/ppermute | solution.py:593
  131.2 2.5 %collective-permute-start.19 = (f32[32,3072]{1,0:T(8,128)}, f32[32,3072]{1,0:T(8,128)S(1)}, u32[]{:S(2)}, u32[]{:S(2)}) collective-permute-start(f32[32,3072]{1,0:T(8,128)} %get-tuple-element.52.refs_4_.refs_12_), channel_id=1, source_target_pairs={{0,1},{1,0},{2,3},{3,2},{4,5},{5,4},{6,7},{7,6},{8,9},{9,8},{10,11... | collective-permute-start | bytes 1179656 | tf_op jit(solution)/shard_map/ppermute | solution.py:593
  131.7 2.5 %collective-permute-start.20 = (f32[32,3072]{1,0:T(8,128)}, f32[32,3072]{1,0:T(8,128)S(1)}, u32[]{:S(2)}, u32[]{:S(2)}) collective-permute-start(f32[32,3072]{1,0:T(8,128)} %get-tuple-element.53.refs_6_.refs_14_), channel_id=1, source_target_pairs={{0,1},{1,0},{2,3},{3,2},{4,5},{5,4},{6,7},{7,6},{8,9},{9,8},{10,11... | collective-permute-start | bytes 1179656 | tf_op jit(solution)/shard_map/ppermute | solution.py:593
  133.1 1.1 copy-start.16
  133.7 0.8 copy-start.17
  134.2 0.8 copy-start.18
  135.0 38.0 %all-to-all-start.1 = ((f32[8,640,128]{2,1,0:T(8,128)}), f32[8,640,128]{2,1,0:T(8,128)S(1)}, u32[]{:S(2)}, u32[]{:S(2)}) async-start(f32[8,640,128]{2,1,0:T(8,128)} %bitcast.28), calls=%async_computation.1 | async-start | bytes 5242880 | tf_op jit(solution)/shard_map/all_to_all | solution.py:679
  173.0 1.5 copy-start.1
Sparse Core Ops, SparseCore 0:
  9.6 39.7 all-gather.4
  55.8 35.9 all-gather.6

commit v14 on v12

--- a/solution.py
+++ b/solution.py
@@ -662,30 +662,36 @@
         )
     )
 
-    parts, halves = [], []
+    def exchange(x):
+        got = lax.all_to_all(
+            x.reshape(freq, -1, LANES), "freq", split_axis=0, concat_axis=0, tiled=True
+        )
+        return got.reshape(x.shape)
+
+    def bins_of(h, rest, after):
+        return [
+            bins_first(h, banks, here, edges[j], own[j], rest[j], table, own_twist[h], after)
+            for j in range(slots)
+        ]
+
+    parts, halves, rest, after = [], [], [], gathered
     later = tuple(range(1, banks))
     for h in range(HALVES):
-        after = [x[0] for x in halves[-1]] if halves else gathered
         half = [entry_product(later, banks, h, w, templates, strains[h], after) for w in which]
         far = [far_pieces(x, freq) for x in half]
         sent, token = first_section(
             freq, h, info, templates, strains[h], first, stage, twist, half
         )
-        far = [x[:1] + list(handed_on(x[1:], [token] + parts)) for x in far]
+        if h:
+            halves.append(bins_of(h - 1, rest, [token]))
+        done = [token] + parts + [x[1] for one in halves for x in one]
+        far = [x[:1] + list(handed_on(x[1:], done)) for x in far]
         rest = [near_pieces(x, freq) for x in far]
-        (ready,) = handed_on([sent], [x for entry in rest for x in entry[1:]])
-        got = lax.all_to_all(
-            ready.reshape(freq, -1, LANES), "freq", split_axis=0, concat_axis=0, tiled=True
-        )
-        parts.append(got.reshape(ready.shape))
-        halves.append(
-            [
-                bins_first(
-                    h, banks, here, edges[j], own[j], rest[j], table, own_twist[h], [ready]
-                )
-                for j in range(slots)
-            ]
-        )
+        if h == HALVES - 1:
+            (sent,) = handed_on([sent], [x for entry in rest for x in entry[1:]])
+        parts.append(exchange(sent))
+        after = [token]
+    halves.append(bins_of(HALVES - 1, rest, [sent]))
 
     chi, snr = [], None
     for j in range(slots):

time: 193 us -> 208 us (1.078)
  waiting for transfers between devices: 36.9 us -> 51.9 us
    ppermute x21, waiting for transfers between devices: 32.8 us -> 47.8 us  [swap(): return lax.ppermute(x, 'freq', [(i, i ^ k) for i in range(freq)])]
    unnamed x49 -> x43, local copies, waits for them, and re-layouts: 5.55 us -> 4.99 us
  transfers between devices with their start and end apart: 25 -> 25, of which waited for: 15 -> 10; matrix products, arithmetic and copies ran while one was open for 9% -> 9% of each run, Pallas kernels for 42% -> 40%
where the time goes in v14:
time: 208 us; the launch traced here: 207 us
  Pallas kernels  92.7 us (45%)
  waiting for transfers between devices  51.9 us (25%)
  starting transfers between devices  21.9 us (11%)
  other arithmetic  15.9 us (8%)
  between operations  15.6 us (8%)
  local copies, waits for them, and re-layouts  8.72 us (4%)
    ppermute x21, waiting for transfers between devices, swap(): return lax.ppermute(x, 'freq', [(i, i ^ k) for i in range(freq)])  47.8 us
    pallas_call x2, Pallas kernels, bins_first(): pl.pallas_call(functools.partial(bins_first_kernel, len(own), banks), gri...  34.5 us
    pallas_call x1, Pallas kernels, bins_second(): pl.pallas_call(functools.partial(bins_second_kernel, halves), grid_spec=p...  16.7 us
    pallas_call x2, Pallas kernels, first_section(): pl.pallas_call(functools.partial(first_kernel, freq), grid_spec=pltpu.Pre...  15.4 us
    ppermute x21, starting transfers between devices, swap(): return lax.ppermute(x, 'freq', [(i, i ^ k) for i in range(freq)])  14.3 us
    pallas_call x1, Pallas kernels, second_section(): pl.pallas_call(functools.partial(second_kernel, freq, halves), grid_spec=...  10.7 us
    pallas_call x3, Pallas kernels, entry_product(): pl.pallas_call(functools.partial(entry_kernel, steps, banks), grid_spec=p...  9.41 us
    all_to_all x2, starting transfers between devices, exchange(): lax.all_to_all(x.reshape(freq, -1, LANES), 'freq', split_axis=0, concat_a...  7.57 us
  transfers between devices with their start and end apart: 25, of which 10 were waited for; matrix products, arithmetic and copies ran while one was open for 9% of the time, Pallas kernels for 40%

profile of v14, /device:TPU:0, one launch (start us, length us, event | category | flops | bytes accessed | tf_op | source)
XLA Modules:
  0.0 206.8 jit_solution(11661934678177817516)
XLA Ops:
  7.2 2.1 fusion.49
  10.6 1.7 add_reduce_fusion
  12.7 0.7 pad_add_fusion.1.which_ref
  13.3 4.0 %entry_product.3 = f32[64,1024]{1,0:T(8,128)} custom-call(s32[3]{0:T(128)} %pad_add_fusion.1.which_ref, f32[2,2,64,2048]{3,2,1,0:T(8,128)} %tmpl_ref.9, f32[1,3,2,64,512]{4,3,2,1,0:T(8,128)} %bitcast.30, f32[3,2,32,512]{3,2,1,0:T(8,128)} %get-tuple-element.67.refs_0_, f32[3,2,32,512]{3,2,1,0:T(8,128)} %get-tuple-element.66.refs_1_), custom_call_target="tpu_custom_call" | custom-call | flops 1048576 | bytes 1048576 | tf_op jit(solution)/shard_map/entry_product/pallas_call | solution.py:258
  17.4 1.0 select_maximum_fusion.refs_0_
  18.3 4.0 %collective-permute-start.5 = (f32[72,1024]{1,0:T(8,128)S(1)}, f32[72,1024]{1,0:T(8,128)S(1)}, u32[]{:S(2)}, u32[]{:S(2)}) collective-permute-start(f32[72,1024]{1,0:T(8,128)S(1)} %select_maximum_fusion.refs_0_), channel_id=1, source_target_pairs={{0,6},{1,7},{2,4},{3,5},{4,2},{5,3},{6,0},{7,1},{8,14},{9,15},{10,... | collective-permute-start | bytes 884744 | tf_op jit(solution)/shard_map/ppermute | solution.py:591
  22.3 0.5 collective-permute-start.3
  22.8 0.1 collective-permute-start.1
  23.1 0.3 fusion.24
  23.4 0.7 pad_add_fusion.4.place_ref
  24.0 0.1 copy.23
  24.2 0.1 copy.22
  24.3 0.1 fusion.32
  24.4 1.0 fusion.39
  25.4 0.7 pad_maximum_fusion.4.block_ref
  26.1 0.7 pad_maximum_fusion.3.inner_ref
  26.8 2.1 %fusion.10 = (f32[1,64,2048]{2,1,0:T(8,128)S(1)}, f32[1,64,2048]{2,1,0:T(8,128)S(1)}) fusion(s32[2048]{0:T(1024)S(1)} %fusion.35, s32[64]{0:T(128)S(1)} %iota_add_fusion.1), kind=kLoop, calls=%fused_computation.31 | loop fusion | flops 1835008 | bytes 1057024 | tf_op jit(solution)/shard_map/cos | solution.py:64
  28.9 1.1 pad_maximum_fusion.tw_ref
  30.0 2.1 %fusion.12 = (f32[1,256,256]{2,1,0:T(8,128)S(1)}, f32[1,256,256]{2,1,0:T(8,128)S(1)}, f32[1,256,256]{2,1,0:T(8,128)S(1)}, f32[1,256,256]{2,1,0:T(8,128)S(1)}) fusion(s32[256]{0:T(256)S(1)} %iota_add_fusion, s32[256]{0:T(256)S(1)} %add_add_fusion, s32[256]{0:T(256)S(1)} %fusion.45), kind=kLoop, calls=%fused_computation.34 | loop fusion | flops 1835008 | bytes 1051648 | tf_op jit(solution)/shard_map/cos | solution.py:64
  32.1 6.0 %bank_table.1 = (bf16[4096,512]{1,0:T(8,128)(2,1)}, bf16[4096,512]{1,0:T(8,128)(2,1)}) custom-call(f32[32,2,256]{2,1,0:T(2,128)} %pad_maximum_fusion.4.block_ref, f32[2,64,256]{2,1,0:T(8,128)} %pad_maximum_fusion.3.inner_ref), custom_call_target="tpu_custom_call" | custom-call | flops 1048576 | bytes 1048576 | tf_op jit(solution)/shard_map/bank_table/pallas_call | solution.py:380
  38.2 1.0 pad_maximum_fusion.1
  39.2 0.7 pad_add_fusion.2.info_ref
  39.8 0.7 pad_add_fusion.3.edge_ref
  40.6 0.5 collective-permute-start.6
  41.4 0.5 collective-permute-start.2
  42.0 0.4 collective-permute-done.6.refs_6_.refs_7_
  42.4 0.4 collective-permute-done.4.refs_4_.refs_5_
  42.9 0.3 collective-permute-done.2.refs_2_.refs_3_
  43.3 0.1 fusion.48
  43.6 0.6 dynamic_slice.10
  44.2 1.1 bitcast_multiply_fusion
  45.3 4.1 %all-gather.5.cloned.1.call-done = f32[12,2,32,512]{3,2,1,0:T(8,128)} async-done(((f32[3,2,32,512]{3,2,1,0:T(8,128)}), f32[12,2,32,512]{3,2,1,0:T(8,128)}) %all-gather.5.cloned.1.call-update) | async-done | bytes 1572880 | tf_op jit(solution)/shard_map/all_gather | solution.py:612
  49.4 2.7 %entry_product.4.refs_0_.refs_8_ = f32[32,3072]{1,0:T(8,128)} custom-call(s32[3]{0:T(128)} %pad_add_fusion.1.which_ref, f32[2,2,64,2048]{3,2,1,0:T(8,128)} %tmpl_ref.9, f32[4,3,2,32,512]{4,3,2,1,0:T(8,128)} %bitcast.34, f32[72,1024]{1,0:T(8,128)} %copy-done.7, f32[72,1024]{1,0:T(8,128)} %copy-done.6, f32[72,1024]{1,0:T(8,128)} %copy-done.10, ...), custom_call_target="tpu_custom_call" | custom-call | flops 1048576 | bytes 1048576 | tf_op jit(solution)/shard_map/entry_product/pallas_call | solution.py:258
  52.1 7.7 %first_section.2 = (f32[8,5,2,2,32,128]{5,4,3,2,1,0:T(8,128)}, f32[8,128]{1,0:T(8,128)}) custom-call(s32[11]{0:T(128)} %pad_add_fusion.2.info_ref, f32[2,2,64,2048]{3,2,1,0:T(8,128)} %tmpl_ref.9, f32[4,3,2,32,512]{4,3,2,1,0:T(8,128)} %bitcast.35, bf16[256,256]{1,0:T(8,128)(2,1)} %constant.173.clone.wh_ref, bf16[256,256]{1,0:T(8,128)(2,1)} %constant.174.clone.wl_ref, ...), custom_call_target="tpu_custom_call" | custom-call | flops 2516582400 | bytes 16777216 | tf_op jit(solution)/shard_map/first_section/pallas_call | solution.py:196
  59.8 3.9 %all-to-all-start = ((f32[8,640,128]{2,1,0:T(8,128)}), f32[8,640,128]{2,1,0:T(8,128)S(1)}, u32[]{:S(2)}, u32[]{:S(2)}) async-start(f32[8,640,128]{2,1,0:T(8,128)} %bitcast.31), calls=%async_computation | async-start | bytes 5242880 | tf_op jit(solution)/shard_map/all_to_all | solution.py:666
  63.8 2.8 %collective-permute-start.14 = (f32[32,3072]{1,0:T(8,128)S(1)}, f32[32,3072]{1,0:T(8,128)S(1)}, u32[]{:S(2)}, u32[]{:S(2)}) collective-permute-start(f32[32,3072]{1,0:T(8,128)S(1)} %copy-done.15), channel_id=1, source_target_pairs={{0,6},{1,7},{2,4},{3,5},{4,2},{5,3},{6,0},{7,1},{8,14},{9,15},{10,... | collective-permute-start | bytes 1179656 | tf_op jit(solution)/shard_map/ppermute | solution.py:591
  66.6 0.6 collective-permute-start.13
  67.1 0.2 collective-permute-start.12
  67.4 37.5 %collective-permute-done.14.refs_2_ = f32[32,3072]{1,0:T(8,128)S(1)} collective-permute-done((f32[32,3072]{1,0:T(8,128)S(1)}, f32[32,3072]{1,0:T(8,128)S(1)}, u32[]{:S(2)}, u32[]{:S(2)}) %collective-permute-start.14) | collective-permute-done | bytes 393248 | tf_op jit(solution)/shard_map/ppermute | solution.py:591
  104.9 7.0 %collective-permute-done.13.refs_1_ = f32[32,3072]{1,0:T(8,128)S(1)} collective-permute-done((f32[32,3072]{1,0:T(8,128)S(1)}, f32[32,3072]{1,0:T(8,128)S(1)}, u32[]{:S(2)}, u32[]{:S(2)}) %collective-permute-start.13) | collective-permute-done | bytes 393248 | tf_op jit(solution)/shard_map/ppermute | solution.py:591
  111.9 0.7 copy-done.17
  112.6 0.2 copy-done.18
  112.8 0.5 collective-permute-start.16
  113.3 2.7 %entry_product.5.refs_0_.refs_8_ = f32[32,3072]{1,0:T(8,128)} custom-call(s32[3]{0:T(128)} %pad_add_fusion.1.which_ref, f32[2,2,64,2048]{3,2,1,0:T(8,128)} %tmpl_ref.9, f32[4,3,2,32,512]{4,3,2,1,0:T(8,128)} %bitcast.32, f32[8,128]{1,0:T(8,128)} %get-tuple-element.39.refs_0_.refs_3_), custom_call_target="tpu_custom_call" | custom-call | flops 1048576 | bytes 1048576 | tf_op jit(solution)/shard_map/entry_product/pallas_call | solution.py:258
  116.0 1.4 collective-permute-start.10
  117.4 1.6 collective-permute-start.9
  118.9 0.5 collective-permute-start.8
  119.4 7.7 %first_section.3 = (f32[8,5,2,2,32,128]{5,4,3,2,1,0:T(8,128)}, f32[8,128]{1,0:T(8,128)}) custom-call(s32[11]{0:T(128)} %pad_add_fusion.2.info_ref, f32[2,2,64,2048]{3,2,1,0:T(8,128)} %tmpl_ref.9, f32[4,3,2,32,512]{4,3,2,1,0:T(8,128)} %bitcast.33, bf16[256,256]{1,0:T(8,128)(2,1)} %constant.173.clone.wh_ref, bf16[256,256]{1,0:T(8,128)(2,1)} %constant.174.clone.wl_ref, ...), custom_call_target="tpu_custom_call" | custom-call | flops 2516582400 | bytes 16777216 | tf_op jit(solution)/shard_map/first_section/pallas_call | solution.py:196
  127.2 17.3 %bins_first.2 = (f32[16,2,256,256]{3,2,1,0:T(8,128)}, f32[2,256,256]{2,1,0:T(8,128)}) custom-call(s32[2]{0:T(128)} %pad_add_fusion.4.place_ref, s32[17]{0:T(128)} %pad_add_fusion.3.edge_ref, f32[72,1024]{1,0:T(8,128)} %copy-done.11, f32[72,1024]{1,0:T(8,128)} %copy-done.7, f32[72,1024]{1,0:T(8,128)} %copy-done.6, f32[72,1024]{1,0:T(8,128)} %copy-done.10, ...), custom_call_target="tpu_custom_call" | custom-call | flops 1048576 | bytes 1048576 | tf_op jit(solution)/shard_map/bins_first/pallas_call | solution.py:465
  144.6 0.7 copy-done.2
  145.3 0.1 copy-done.3
  145.4 0.9 copy-done
  146.3 0.5 collective-permute-start.18
  146.8 0.5 collective-permute-start.20
  147.3 1.0 collective-permute-done.18.refs_3_.refs_11_
  148.3 0.6 collective-permute-done.19.refs_5_.refs_13_
  148.9 0.6 collective-permute-done.20.refs_7_.refs_15_
  149.4 0.2 copy-done.13
  149.7 0.6 copy-done.14
  150.2 3.6 %all-to-all-start.1 = ((f32[8,640,128]{2,1,0:T(8,128)}), f32[8,640,128]{2,1,0:T(8,128)S(1)}, u32[]{:S(2)}, u32[]{:S(2)}) async-start(f32[8,640,128]{2,1,0:T(8,128)} %bitcast.28), calls=%async_computation.1 | async-start | bytes 5242880 | tf_op jit(solution)/shard_map/all_to_all | solution.py:666
  153.9 17.2 %bins_first.3 = (f32[16,2,256,256]{3,2,1,0:T(8,128)}, f32[2,256,256]{2,1,0:T(8,128)}) custom-call(s32[2]{0:T(128)} %pad_add_fusion.4.place_ref, s32[17]{0:T(128)} %pad_add_fusion.3.edge_ref, f32[72,1024]{1,0:T(8,128)} %copy-done.11, f32[72,1024]{1,0:T(8,128)} %copy-done.7, f32[72,1024]{1,0:T(8,128)} %copy-done.6, f32[72,1024]{1,0:T(8,128)} %copy-done.10, ...), custom_call_target="tpu_custom_call" | custom-call | flops 1048576 | bytes 1048576 | tf_op jit(solution)/shard_map/bins_first/pallas_call | solution.py:465
  171.1 16.7 %bins_second.1 = (f32[256,512]{1,0:T(8,128)}, f32[2,3,2,256,512]{4,3,2,1,0:T(8,128)}) custom-call(s32[3]{0:T(128)} %pad_add_fusion.1.which_ref, f32[2]{0:T(128)} %copy-done.19, f32[16]{0:T(128)} %get-tuple-element.54.gain_ref, f32[16]{0:T(128)} %get-tuple-element.55.share_ref, f32[16,2,256,256]{3,2,1,0:T(8,128)} %get-tuple-element.56.refs_0_, ...), custom_call_target="tpu_custom_call" | custom-call | flops 1048576 | bytes 1048576 | tf_op jit(solution)/shard_map/bins_second/pallas_call | solution.py:548
  187.8 1.5 copy-done.1
  189.3 10.7 %second_section.1 = f32[2,3,2,256,512]{4,3,2,1,0:T(8,128)} custom-call(s32[11]{0:T(128)} %pad_add_fusion.2.info_ref, f32[2]{0:T(128)} %copy-done.19, f32[8,5,2,2,32,128]{5,4,3,2,1,0:T(8,128)} %bitcast.27, f32[8,5,2,2,32,128]{5,4,3,2,1,0:T(8,128)} %bitcast.29, bf16[2048,256]{1,0:T(8,128)(2,1)} %constant.175.clone.refs_4_.refs_2_, ...), custom_call_target="tpu_custom_call", output_to_operand_aliasing={{}: (5, {})} | custom-call | flops 1048576 | bytes 1048576 | tf_op jit(solution)/shard_map/second_section/pallas_call | solution.py:334
  (94 shorter events, 1.7 us)
Async XLA Ops:
  7.2 42.2 %all-gather.5.cloned.1.call-start = ((), (), s32[]{:S(2)}) async-start(), calls=%async_computation.2 | async-start | bytes 1966080 | tf_op jit(solution)/shard_map/all_gather | solution.py:612
  9.3 104.0 %all-gather.7.cloned.1.call-start = ((), (), s32[]{:S(2)}) async-start(), calls=%async_computation.3 | async-start | bytes 1966080 | tf_op jit(solution)/shard_map/all_gather | solution.py:612
  12.4 11.8 %copy-start.20 = (s32[2,15]{1,0:T(2,128)S(1)}, s32[2,15]{1,0:T(2,128)}, u32[]{:S(2)}) copy-start(s32[2,15]{1,0:T(2,128)} %param.13) | copy-start | bytes 364
  18.3 13.8 %copy-start.11 = (f32[72,1024]{1,0:T(8,128)}, f32[72,1024]{1,0:T(8,128)S(1)}, u32[]{:S(2)}) copy-start(f32[72,1024]{1,0:T(8,128)S(1)} %select_maximum_fusion.refs_0_) | copy-start | bytes 884740
  18.3 22.2 %collective-permute-start.5 = (f32[72,1024]{1,0:T(8,128)S(1)}, f32[72,1024]{1,0:T(8,128)S(1)}, u32[]{:S(2)}, u32[]{:S(2)}) collective-permute-start(f32[72,1024]{1,0:T(8,128)S(1)} %select_maximum_fusion.refs_0_), channel_id=1, source_target_pairs={{0,6},{1,7},{2,4},{3,5},{4,2},{5,3},{6,0},{7,1},{8,14},{9,15},{10,... | collective-permute-start | bytes 884744 | tf_op jit(solution)/shard_map/ppermute | solution.py:591
  22.3 18.8 %collective-permute-start.3 = (f32[72,1024]{1,0:T(8,128)S(1)}, f32[72,1024]{1,0:T(8,128)S(1)}, u32[]{:S(2)}, u32[]{:S(2)}) collective-permute-start(f32[72,1024]{1,0:T(8,128)S(1)} %select_maximum_fusion.refs_0_), channel_id=1, source_target_pairs={{0,4},{1,5},{2,6},{3,7},{4,0},{5,1},{6,2},{7,3},{8,12},{9,13},{10,... | collective-permute-start | bytes 884744 | tf_op jit(solution)/shard_map/ppermute | solution.py:591
  22.8 18.4 %collective-permute-start.1 = (f32[72,1024]{1,0:T(8,128)S(1)}, f32[72,1024]{1,0:T(8,128)S(1)}, u32[]{:S(2)}, u32[]{:S(2)}) collective-permute-start(f32[72,1024]{1,0:T(8,128)S(1)} %select_maximum_fusion.refs_0_), channel_id=1, source_target_pairs={{0,2},{1,3},{2,0},{3,1},{4,6},{5,7},{6,4},{7,5},{8,10},{9,11},{10,... | collective-permute-start | bytes 884744 | tf_op jit(solution)/shard_map/ppermute | solution.py:591
  23.0 18.9 %collective-permute-start = (f32[72,1024]{1,0:T(8,128)S(1)}, f32[72,1024]{1,0:T(8,128)S(1)}, u32[]{:S(2)}, u32[]{:S(2)}) collective-permute-start(f32[72,1024]{1,0:T(8,128)S(1)} %select_maximum_fusion.refs_0_), channel_id=1, source_target_pairs={{0,1},{1,0},{2,3},{3,2},{4,5},{5,4},{6,7},{7,6},{8,9},{9,8},{10,11... | collective-permute-start | bytes 884744 | tf_op jit(solution)/shard_map/ppermute | solution.py:591
  40.5 8.9 %copy-start.4 = (f32[72,1024]{1,0:T(8,128)}, f32[72,1024]{1,0:T(8,128)S(1)}, u32[]{:S(2)}) copy-start(f32[72,1024]{1,0:T(8,128)S(1)} %collective-permute-done.5.refs_5_.refs_6_) | copy-start | bytes 884740
  40.6 1.7 collective-permute-start.6
  41.1 8.3 %copy-start.5 = (f32[72,1024]{1,0:T(8,128)}, f32[72,1024]{1,0:T(8,128)S(1)}, u32[]{:S(2)}) copy-start(f32[72,1024]{1,0:T(8,128)S(1)} %collective-permute-done.3.refs_3_.refs_4_) | copy-start | bytes 884740
  41.2 1.6 collective-permute-start.4
  41.3 8.1 %copy-start.6 = (f32[72,1024]{1,0:T(8,128)}, f32[72,1024]{1,0:T(8,128)S(1)}, u32[]{:S(2)}) copy-start(f32[72,1024]{1,0:T(8,128)S(1)} %collective-permute-done.1.refs_1_.refs_2_) | copy-start | bytes 884740
  41.4 1.9 collective-permute-start.2
  41.9 7.5 %copy-start.7 = (f32[72,1024]{1,0:T(8,128)}, f32[72,1024]{1,0:T(8,128)S(1)}, u32[]{:S(2)}) copy-start(f32[72,1024]{1,0:T(8,128)S(1)} %collective-permute-done.refs_0_.refs_1_) | copy-start | bytes 884740
  42.3 7.1 %copy-start.8 = (f32[72,1024]{1,0:T(8,128)}, f32[72,1024]{1,0:T(8,128)S(1)}, u32[]{:S(2)}) copy-start(f32[72,1024]{1,0:T(8,128)S(1)} %collective-permute-done.6.refs_6_.refs_7_) | copy-start | bytes 884740
  42.8 6.6 %copy-start.9 = (f32[72,1024]{1,0:T(8,128)}, f32[72,1024]{1,0:T(8,128)S(1)}, u32[]{:S(2)}) copy-start(f32[72,1024]{1,0:T(8,128)S(1)} %collective-permute-done.4.refs_4_.refs_5_) | copy-start | bytes 884740
  43.2 6.2 %copy-start.10 = (f32[72,1024]{1,0:T(8,128)}, f32[72,1024]{1,0:T(8,128)S(1)}, u32[]{:S(2)}) copy-start(f32[72,1024]{1,0:T(8,128)S(1)} %collective-permute-done.2.refs_2_.refs_3_) | copy-start | bytes 884740
  43.6 8.5 %copy-start.19 = (f32[2]{0:T(128)}, f32[2]{0:T(128)S(1)}, u32[]{:S(2)}) copy-start(f32[2]{0:T(128)S(1)} %rsqrt.6.scale_ref) | copy-start | bytes 28
  59.8 4.0 %copy-start.15 = (f32[32,3072]{1,0:T(8,128)S(1)}, f32[32,3072]{1,0:T(8,128)}, u32[]{:S(2)}) copy-start(f32[32,3072]{1,0:T(8,128)} %entry_product.4.refs_0_.refs_8_) | copy-start | bytes 1179652
  59.8 84.7 %all-to-all-start = ((f32[8,640,128]{2,1,0:T(8,128)}), f32[8,640,128]{2,1,0:T(8,128)S(1)}, u32[]{:S(2)}, u32[]{:S(2)}) async-start(f32[8,640,128]{2,1,0:T(8,128)} %bitcast.31), calls=%async_computation | async-start | bytes 5242880 | tf_op jit(solution)/shard_map/all_to_all | solution.py:666
  63.8 41.1 %collective-permute-start.14 = (f32[32,3072]{1,0:T(8,128)S(1)}, f32[32,3072]{1,0:T(8,128)S(1)}, u32[]{:S(2)}, u32[]{:S(2)}) collective-permute-start(f32[32,3072]{1,0:T(8,128)S(1)} %copy-done.15), channel_id=1, source_target_pairs={{0,6},{1,7},{2,4},{3,5},{4,2},{5,3},{6,0},{7,1},{8,14},{9,15},{10,... | collective-permute-start | bytes 1179656 | tf_op jit(solution)/shard_map/ppermute | solution.py:591
  66.6 45.2 %collective-permute-start.13 = (f32[32,3072]{1,0:T(8,128)S(1)}, f32[32,3072]{1,0:T(8,128)S(1)}, u32[]{:S(2)}, u32[]{:S(2)}) collective-permute-start(f32[32,3072]{1,0:T(8,128)S(1)} %copy-done.15), channel_id=1, source_target_pairs={{0,4},{1,5},{2,6},{3,7},{4,0},{5,1},{6,2},{7,3},{8,12},{9,13},{10,... | collective-permute-start | bytes 1179656 | tf_op jit(solution)/shard_map/ppermute | solution.py:591
  67.1 44.8 %collective-permute-start.12 = (f32[32,3072]{1,0:T(8,128)S(1)}, f32[32,3072]{1,0:T(8,128)S(1)}, u32[]{:S(2)}, u32[]{:S(2)}) collective-permute-start(f32[32,3072]{1,0:T(8,128)S(1)} %copy-done.15), channel_id=1, source_target_pairs={{0,2},{1,3},{2,0},{3,1},{4,6},{5,7},{6,4},{7,5},{8,10},{9,11},{10,... | collective-permute-start | bytes 1179656 | tf_op jit(solution)/shard_map/ppermute | solution.py:591
  67.4 50.0 %collective-permute-start.11 = (f32[32,3072]{1,0:T(8,128)S(1)}, f32[32,3072]{1,0:T(8,128)}, u32[]{:S(2)}, u32[]{:S(2)}) collective-permute-start(f32[32,3072]{1,0:T(8,128)S(1)} %copy-done.15), channel_id=1, source_target_pairs={{0,1},{1,0},{2,3},{3,2},{4,5},{5,4},{6,7},{7,6},{8,9},{9,8},{10,11... | collective-permute-start | bytes 1179656 | tf_op jit(solution)/shard_map/ppermute | solution.py:591
  104.9 7.1 %copy-start.16 = (f32[32,3072]{1,0:T(8,128)}, f32[32,3072]{1,0:T(8,128)S(1)}, u32[]{:S(2)}) copy-start(f32[32,3072]{1,0:T(8,128)S(1)} %collective-permute-done.14.refs_2_) | copy-start | bytes 1179652
  111.8 0.8 copy-start.17
  111.9 0.8 copy-start.18
  112.7 6.2 %collective-permute-start.15 = (f32[32,3072]{1,0:T(8,128)}, f32[32,3072]{1,0:T(8,128)}, u32[]{:S(2)}, u32[]{:S(2)}) collective-permute-start(f32[32,3072]{1,0:T(8,128)} %get-tuple-element.44.refs_10_), channel_id=1, source_target_pairs={{0,1},{1,0},{2,3},{3,2},{4,5},{5,4},{6,7},{7,6},{8,9},{9,8},{10,11... | collective-permute-start | bytes 1179656 | tf_op jit(solution)/shard_map/ppermute | solution.py:591
  112.8 14.4 %collective-permute-start.16 = (f32[32,3072]{1,0:T(8,128)}, f32[32,3072]{1,0:T(8,128)}, u32[]{:S(2)}, u32[]{:S(2)}) collective-permute-start(f32[32,3072]{1,0:T(8,128)} %get-tuple-element.45.refs_12_), channel_id=1, source_target_pairs={{0,1},{1,0},{2,3},{3,2},{4,5},{5,4},{6,7},{7,6},{8,9},{9,8},{10,11... | collective-permute-start | bytes 1179656 | tf_op jit(solution)/shard_map/ppermute | solution.py:591
  113.3 14.0 %collective-permute-start.17 = (f32[32,3072]{1,0:T(8,128)}, f32[32,3072]{1,0:T(8,128)}, u32[]{:S(2)}, u32[]{:S(2)}) collective-permute-start(f32[32,3072]{1,0:T(8,128)} %get-tuple-element.46.refs_14_), channel_id=1, source_target_pairs={{0,1},{1,0},{2,3},{3,2},{4,5},{5,4},{6,7},{7,6},{8,9},{9,8},{10,11... | collective-permute-start | bytes 1179656 | tf_op jit(solution)/shard_map/ppermute | solution.py:591
  116.0 28.5 %collective-permute-start.10 = (f32[32,3072]{1,0:T(8,128)}, f32[32,3072]{1,0:T(8,128)S(1)}, u32[]{:S(2)}, u32[]{:S(2)}) collective-permute-start(f32[32,3072]{1,0:T(8,128)} %entry_product.5.refs_0_.refs_8_), channel_id=1, source_target_pairs={{0,6},{1,7},{2,4},{3,5},{4,2},{5,3},{6,0},{7,1},{8,14},{9,15},{10,... | collective-permute-start | bytes 1179656 | tf_op jit(solution)/shard_map/ppermute | solution.py:591
  117.4 27.1 %collective-permute-start.9 = (f32[32,3072]{1,0:T(8,128)}, f32[32,3072]{1,0:T(8,128)S(1)}, u32[]{:S(2)}, u32[]{:S(2)}) collective-permute-start(f32[32,3072]{1,0:T(8,128)} %entry_product.5.refs_0_.refs_8_), channel_id=1, source_target_pairs={{0,4},{1,5},{2,6},{3,7},{4,0},{5,1},{6,2},{7,3},{8,12},{9,13},{10,... | collective-permute-start | bytes 1179656 | tf_op jit(solution)/shard_map/ppermute | solution.py:591
  118.9 25.6 %collective-permute-start.8 = (f32[32,3072]{1,0:T(8,128)}, f32[32,3072]{1,0:T(8,128)}, u32[]{:S(2)}, u32[]{:S(2)}) collective-permute-start(f32[32,3072]{1,0:T(8,128)} %entry_product.5.refs_0_.refs_8_), channel_id=1, source_target_pairs={{0,2},{1,3},{2,0},{3,1},{4,6},{5,7},{6,4},{7,5},{8,10},{9,11},{10,... | collective-permute-start | bytes 1179656 | tf_op jit(solution)/shard_map/ppermute | solution.py:591
  127.1 20.1 %collective-permute-start.7 = (f32[32,3072]{1,0:T(8,128)}, f32[32,3072]{1,0:T(8,128)}, u32[]{:S(2)}, u32[]{:S(2)}) collective-permute-start(f32[32,3072]{1,0:T(8,128)} %entry_product.5.refs_0_.refs_8_), channel_id=1, source_target_pairs={{0,1},{1,0},{2,3},{3,2},{4,5},{5,4},{6,7},{7,6},{8,9},{9,8},{10,11... | collective-permute-start | bytes 1179656 | tf_op jit(solution)/shard_map/ppermute | solution.py:591
  144.5 0.8 copy-start.2
  144.5 0.9 copy-start.3
  144.5 1.7 copy-start
  146.3 2.0 collective-permute-start.18
  146.8 2.1 %collective-permute-start.19 = (f32[32,3072]{1,0:T(8,128)}, f32[32,3072]{1,0:T(8,128)S(1)}, u32[]{:S(2)}, u32[]{:S(2)}) collective-permute-start(f32[32,3072]{1,0:T(8,128)} %get-tuple-element.52.refs_4_.refs_12_), channel_id=1, source_target_pairs={{0,1},{1,0},{2,3},{3,2},{4,5},{5,4},{6,7},{7,6},{8,9},{9,8},{10,11... | collective-permute-start | bytes 1179656 | tf_op jit(solution)/shard_map/ppermute | solution.py:591
  146.8 2.7 %collective-permute-start.20 = (f32[32,3072]{1,0:T(8,128)}, f32[32,3072]{1,0:T(8,128)S(1)}, u32[]{:S(2)}, u32[]{:S(2)}) collective-permute-start(f32[32,3072]{1,0:T(8,128)} %get-tuple-element.53.refs_6_.refs_14_), channel_id=1, source_target_pairs={{0,1},{1,0},{2,3},{3,2},{4,5},{5,4},{6,7},{7,6},{8,9},{9,8},{10,11... | collective-permute-start | bytes 1179656 | tf_op jit(solution)/shard_map/ppermute | solution.py:591
  148.3 1.1 copy-start.12
  148.9 0.8 copy-start.13
  149.4 0.8 copy-start.14
  150.2 37.6 %all-to-all-start.1 = ((f32[8,640,128]{2,1,0:T(8,128)}), f32[8,640,128]{2,1,0:T(8,128)S(1)}, u32[]{:S(2)}, u32[]{:S(2)}) async-start(f32[8,640,128]{2,1,0:T(8,128)} %bitcast.28), calls=%async_computation.1 | async-start | bytes 5242880 | tf_op jit(solution)/shard_map/all_to_all | solution.py:666
  187.8 1.5 copy-start.1
Sparse Core Ops, SparseCore 0:
  9.6 39.7 all-gather.4
  51.0 35.9 all-gather.6

commit v15 on v14

--- a/solution.py
+++ b/solution.py
@@ -682,6 +682,8 @@
         sent, token = first_section(
             freq, h, info, templates, strains[h], first, stage, twist, half
         )
+        if h < HALVES - 1:
+            (sent,) = handed_on([sent], [x[-1] for x in far])
         if h:
             halves.append(bins_of(h - 1, rest, [token]))
         done = [token] + parts + [x[1] for one in halves for x in one]

time: 208 us -> 205 us (0.986)
  waiting for transfers between devices: 51.9 us -> 45.3 us
  starting transfers between devices: 21.9 us -> 24.2 us
    ppermute x21, waiting for transfers between devices: 47.8 us -> 41.2 us  [swap(): return lax.ppermute(x, 'freq', [(i, i ^ k) for i in range(freq)])]
    ppermute x21, starting transfers between devices: 14.3 us -> 16.6 us  [swap(): return lax.ppermute(x, 'freq', [(i, i ^ k) for i in range(freq)])]
  transfers between devices with their start and end apart: 25 -> 25, of which waited for: 10 -> 10; matrix products, arithmetic and copies ran while one was open for 9% -> 9% of each run, Pallas kernels for 40% -> 41%
where the time goes in v15:
time: 205 us; the launch traced here: 204 us
  Pallas kernels  93.4 us (46%)
  waiting for transfers between devices  45.3 us (22%)
  starting transfers between devices  24.2 us (12%)
  other arithmetic  15.9 us (8%)
  between operations  15.6 us (8%)
  local copies, waits for them, and re-layouts  9.48 us (5%)
    ppermute x21, waiting for transfers between devices, swap(): return lax.ppermute(x, 'freq', [(i, i ^ k) for i in range(freq)])  41.2 us
    pallas_call x2, Pallas kernels, bins_first(): pl.pallas_call(functools.partial(bins_first_kernel, len(own), banks), gri...  35.1 us
    pallas_call x1, Pallas kernels, bins_second(): pl.pallas_call(functools.partial(bins_second_kernel, halves), grid_spec=p...  16.7 us
    ppermute x21, starting transfers between devices, swap(): return lax.ppermute(x, 'freq', [(i, i ^ k) for i in range(freq)])  16.6 us
    pallas_call x2, Pallas kernels, first_section(): pl.pallas_call(functools.partial(first_kernel, freq), grid_spec=pltpu.Pre...  15.5 us
    pallas_call x1, Pallas kernels, second_section(): pl.pallas_call(functools.partial(second_kernel, freq, halves), grid_spec=...  10.7 us
    pallas_call x3, Pallas kernels, entry_product(): pl.pallas_call(functools.partial(entry_kernel, steps, banks), grid_spec=p...  9.41 us
    all_to_all x2, starting transfers between devices, exchange(): lax.all_to_all(x.reshape(freq, -1, LANES), 'freq', split_axis=0, concat_a...  7.57 us
  transfers between devices with their start and end apart: 25, of which 10 were waited for; matrix products, arithmetic and copies ran while one was open for 9% of the time, Pallas kernels for 41%

profile of v15, /device:TPU:0, one launch (start us, length us, event | category | flops | bytes accessed | tf_op | source)
XLA Modules:
  0.0 204.0 jit_solution(5615391856498930835)
XLA Ops:
  7.2 2.1 %fusion.49 = (f32[3,2,32,512]{3,2,1,0:T(8,128)}, f32[3,2,32,512]{3,2,1,0:T(8,128)}) fusion(f32[3,2,64,512]{3,2,1,0:T(8,128)} %param.9), kind=kLoop, calls=%fused_computation.114 | loop fusion | bytes 1572864 | tf_op jit(solution)/shard_map/slice | solution.py:611
  10.6 1.7 add_reduce_fusion
  12.7 0.7 pad_add_fusion.1.which_ref
  13.3 4.0 %entry_product.3 = f32[64,1024]{1,0:T(8,128)} custom-call(s32[3]{0:T(128)} %pad_add_fusion.1.which_ref, f32[2,2,64,2048]{3,2,1,0:T(8,128)} %tmpl_ref.9, f32[1,3,2,64,512]{4,3,2,1,0:T(8,128)} %bitcast.31, f32[3,2,32,512]{3,2,1,0:T(8,128)} %get-tuple-element.67.refs_0_, f32[3,2,32,512]{3,2,1,0:T(8,128)} %get-tuple-element.66.refs_1_), custom_call_target="tpu_custom_call" | custom-call | flops 1048576 | bytes 1048576 | tf_op jit(solution)/shard_map/entry_product/pallas_call | solution.py:258
  17.4 1.0 select_maximum_fusion.refs_0_
  18.3 4.0 %collective-permute-start.5 = (f32[72,1024]{1,0:T(8,128)S(1)}, f32[72,1024]{1,0:T(8,128)S(1)}, u32[]{:S(2)}, u32[]{:S(2)}) collective-permute-start(f32[72,1024]{1,0:T(8,128)S(1)} %select_maximum_fusion.refs_0_), channel_id=1, source_target_pairs={{0,6},{1,7},{2,4},{3,5},{4,2},{5,3},{6,0},{7,1},{8,14},{9,15},{10,... | collective-permute-start | bytes 884744 | tf_op jit(solution)/shard_map/ppermute | solution.py:591
  22.3 0.5 collective-permute-start.3
  22.8 0.1 collective-permute-start.1
  23.1 0.3 fusion.24
  23.4 0.7 pad_add_fusion.4.place_ref
  24.0 0.1 copy.24
  24.2 0.1 copy.23
  24.4 1.0 fusion.39
  25.4 0.7 pad_maximum_fusion.4.block_ref
  26.1 0.7 pad_maximum_fusion.3.inner_ref
  26.8 2.1 %fusion.10 = (f32[1,64,2048]{2,1,0:T(8,128)S(1)}, f32[1,64,2048]{2,1,0:T(8,128)S(1)}) fusion(s32[2048]{0:T(1024)S(1)} %fusion.35, s32[64]{0:T(128)S(1)} %iota_add_fusion.1), kind=kLoop, calls=%fused_computation.31 | loop fusion | flops 1835008 | bytes 1057024 | tf_op jit(solution)/shard_map/cos | solution.py:64
  28.9 1.1 pad_maximum_fusion.tw_ref
  29.9 2.1 %fusion.12 = (f32[1,256,256]{2,1,0:T(8,128)S(1)}, f32[1,256,256]{2,1,0:T(8,128)S(1)}, f32[1,256,256]{2,1,0:T(8,128)S(1)}, f32[1,256,256]{2,1,0:T(8,128)S(1)}) fusion(s32[256]{0:T(256)S(1)} %iota_add_fusion, s32[256]{0:T(256)S(1)} %add_add_fusion, s32[256]{0:T(256)S(1)} %fusion.45), kind=kLoop, calls=%fused_computation.34 | loop fusion | flops 1835008 | bytes 1051648 | tf_op jit(solution)/shard_map/cos | solution.py:64
  32.1 6.0 %bank_table.1 = (bf16[4096,512]{1,0:T(8,128)(2,1)}, bf16[4096,512]{1,0:T(8,128)(2,1)}) custom-call(f32[32,2,256]{2,1,0:T(2,128)} %pad_maximum_fusion.4.block_ref, f32[2,64,256]{2,1,0:T(8,128)} %pad_maximum_fusion.3.inner_ref), custom_call_target="tpu_custom_call" | custom-call | flops 1048576 | bytes 1048576 | tf_op jit(solution)/shard_map/bank_table/pallas_call | solution.py:380
  38.1 1.0 pad_maximum_fusion.1
  39.2 0.7 pad_add_fusion.2.info_ref
  39.8 0.7 pad_add_fusion.3.edge_ref
  40.6 0.5 collective-permute-start.6
  41.3 0.5 collective-permute-start.2
  41.9 0.4 collective-permute-done.6.refs_6_.refs_7_
  42.4 0.4 collective-permute-done.4.refs_4_.refs_5_
  42.9 0.3 collective-permute-done.2.refs_2_.refs_3_
  43.3 0.1 fusion.48
  43.6 0.6 dynamic_slice.10
  44.2 1.1 bitcast_multiply_fusion
  45.3 4.1 %all-gather.5.cloned.1.call-done = f32[12,2,32,512]{3,2,1,0:T(8,128)} async-done(((f32[3,2,32,512]{3,2,1,0:T(8,128)}), f32[12,2,32,512]{3,2,1,0:T(8,128)}) %all-gather.5.cloned.1.call-update) | async-done | bytes 1572880 | tf_op jit(solution)/shard_map/all_gather | solution.py:612
  49.4 2.7 %entry_product.4.refs_0_.refs_8_ = f32[32,3072]{1,0:T(8,128)} custom-call(s32[3]{0:T(128)} %pad_add_fusion.1.which_ref, f32[2,2,64,2048]{3,2,1,0:T(8,128)} %tmpl_ref.9, f32[4,3,2,32,512]{4,3,2,1,0:T(8,128)} %bitcast.34, f32[72,1024]{1,0:T(8,128)} %copy-done.8, f32[72,1024]{1,0:T(8,128)} %copy-done.7, f32[72,1024]{1,0:T(8,128)} %copy-done.11, ...), custom_call_target="tpu_custom_call" | custom-call | flops 1048576 | bytes 1048576 | tf_op jit(solution)/shard_map/entry_product/pallas_call | solution.py:258
  52.1 2.4 %collective-permute-start.7 = (f32[32,3072]{1,0:T(8,128)}, f32[32,3072]{1,0:T(8,128)S(1)}, u32[]{:S(2)}, u32[]{:S(2)}) collective-permute-start(f32[32,3072]{1,0:T(8,128)} %entry_product.4.refs_0_.refs_8_), channel_id=1, source_target_pairs={{0,6},{1,7},{2,4},{3,5},{4,2},{5,3},{6,0},{7,1},{8,14},{9,15},{10,... | collective-permute-start | bytes 1179656 | tf_op jit(solution)/shard_map/ppermute | solution.py:591
  54.6 7.8 %first_section.2 = (f32[8,5,2,2,32,128]{5,4,3,2,1,0:T(8,128)}, f32[8,128]{1,0:T(8,128)}) custom-call(s32[11]{0:T(128)} %pad_add_fusion.2.info_ref, f32[2,2,64,2048]{3,2,1,0:T(8,128)} %tmpl_ref.9, f32[4,3,2,32,512]{4,3,2,1,0:T(8,128)} %bitcast.35, bf16[256,256]{1,0:T(8,128)(2,1)} %constant.173.clone.wh_ref, bf16[256,256]{1,0:T(8,128)(2,1)} %constant.174.clone.wl_ref, ...), custom_call_target="tpu_custom_call" | custom-call | flops 2516582400 | bytes 16777216 | tf_op jit(solution)/shard_map/first_section/pallas_call | solution.py:196
  62.4 1.6 collective-permute-done.7.refs_1_.refs_2_
  64.0 0.8 copy-done.4
  64.7 3.9 %all-to-all-start = ((f32[8,640,128]{2,1,0:T(8,128)}), f32[8,640,128]{2,1,0:T(8,128)S(1)}, u32[]{:S(2)}, u32[]{:S(2)}) async-start(f32[8,640,128]{2,1,0:T(8,128)} %bitcast.30), calls=%async_computation | async-start | bytes 5242880 | tf_op jit(solution)/shard_map/all_to_all | solution.py:666
  68.7 2.0 collective-permute-start.14
  70.7 1.5 collective-permute-start.13
  72.2 36.2 %collective-permute-done.14.refs_1_ = f32[32,3072]{1,0:T(8,128)S(1)} collective-permute-done((f32[32,3072]{1,0:T(8,128)S(1)}, f32[32,3072]{1,0:T(8,128)S(1)}, u32[]{:S(2)}, u32[]{:S(2)}) %collective-permute-start.14) | collective-permute-done | bytes 393248 | tf_op jit(solution)/shard_map/ppermute | solution.py:591
  108.5 0.7 copy-done.17
  109.2 0.2 copy-done.18
  109.3 0.5 collective-permute-start.16
  109.9 2.7 %entry_product.5.refs_0_.refs_8_ = f32[32,3072]{1,0:T(8,128)} custom-call(s32[3]{0:T(128)} %pad_add_fusion.1.which_ref, f32[2,2,64,2048]{3,2,1,0:T(8,128)} %tmpl_ref.9, f32[4,3,2,32,512]{4,3,2,1,0:T(8,128)} %bitcast.32, f32[8,128]{1,0:T(8,128)} %get-tuple-element.39.refs_0_.refs_3_), custom_call_target="tpu_custom_call" | custom-call | flops 1048576 | bytes 1048576 | tf_op jit(solution)/shard_map/entry_product/pallas_call | solution.py:258
  112.6 1.4 collective-permute-start.11
  113.9 1.6 collective-permute-start.10
  115.5 0.5 collective-permute-start.9
  116.0 7.7 %first_section.3 = (f32[8,5,2,2,32,128]{5,4,3,2,1,0:T(8,128)}, f32[8,128]{1,0:T(8,128)}) custom-call(s32[11]{0:T(128)} %pad_add_fusion.2.info_ref, f32[2,2,64,2048]{3,2,1,0:T(8,128)} %tmpl_ref.9, f32[4,3,2,32,512]{4,3,2,1,0:T(8,128)} %bitcast.33, bf16[256,256]{1,0:T(8,128)(2,1)} %constant.173.clone.wh_ref, bf16[256,256]{1,0:T(8,128)(2,1)} %constant.174.clone.wl_ref, ...), custom_call_target="tpu_custom_call" | custom-call | flops 2516582400 | bytes 16777216 | tf_op jit(solution)/shard_map/first_section/pallas_call | solution.py:196
  123.8 17.5 %bins_first.2 = (f32[16,2,256,256]{3,2,1,0:T(8,128)}, f32[2,256,256]{2,1,0:T(8,128)}) custom-call(s32[2]{0:T(128)} %pad_add_fusion.4.place_ref, s32[17]{0:T(128)} %pad_add_fusion.3.edge_ref, f32[72,1024]{1,0:T(8,128)} %copy-done.12, f32[72,1024]{1,0:T(8,128)} %copy-done.8, f32[72,1024]{1,0:T(8,128)} %copy-done.7, f32[72,1024]{1,0:T(8,128)} %copy-done.11, ...), custom_call_target="tpu_custom_call" | custom-call | flops 1048576 | bytes 1048576 | tf_op jit(solution)/shard_map/bins_first/pallas_call | solution.py:465
  141.4 0.7 copy-done.2
  142.1 0.1 copy-done.3
  142.3 0.9 copy-done
  143.2 0.5 collective-permute-start.18
  143.7 0.5 collective-permute-start.20
  144.2 1.0 collective-permute-done.18.refs_3_.refs_11_
  145.2 0.6 collective-permute-done.19.refs_5_.refs_13_
  145.8 0.6 collective-permute-done.20.refs_7_.refs_15_
  146.3 0.2 copy-done.14
  146.5 0.6 copy-done.15
  147.1 3.6 %all-to-all-start.1 = ((f32[8,640,128]{2,1,0:T(8,128)}), f32[8,640,128]{2,1,0:T(8,128)S(1)}, u32[]{:S(2)}, u32[]{:S(2)}) async-start(f32[8,640,128]{2,1,0:T(8,128)} %bitcast.28), calls=%async_computation.1 | async-start | bytes 5242880 | tf_op jit(solution)/shard_map/all_to_all | solution.py:666
  150.8 17.5 %bins_first.3 = (f32[16,2,256,256]{3,2,1,0:T(8,128)}, f32[2,256,256]{2,1,0:T(8,128)}) custom-call(s32[2]{0:T(128)} %pad_add_fusion.4.place_ref, s32[17]{0:T(128)} %pad_add_fusion.3.edge_ref, f32[72,1024]{1,0:T(8,128)} %copy-done.12, f32[72,1024]{1,0:T(8,128)} %copy-done.8, f32[72,1024]{1,0:T(8,128)} %copy-done.7, f32[72,1024]{1,0:T(8,128)} %copy-done.11, ...), custom_call_target="tpu_custom_call" | custom-call | flops 1048576 | bytes 1048576 | tf_op jit(solution)/shard_map/bins_first/pallas_call | solution.py:465
  168.3 16.7 %bins_second.1 = (f32[256,512]{1,0:T(8,128)}, f32[2,3,2,256,512]{4,3,2,1,0:T(8,128)}) custom-call(s32[3]{0:T(128)} %pad_add_fusion.1.which_ref, f32[2]{0:T(128)} %copy-done.19, f32[16]{0:T(128)} %get-tuple-element.54.gain_ref, f32[16]{0:T(128)} %get-tuple-element.55.share_ref, f32[16,2,256,256]{3,2,1,0:T(8,128)} %get-tuple-element.56.refs_0_, ...), custom_call_target="tpu_custom_call" | custom-call | flops 1048576 | bytes 1048576 | tf_op jit(solution)/shard_map/bins_second/pallas_call | solution.py:548
  185.0 1.5 copy-done.1
  186.5 10.7 %second_section.1 = f32[2,3,2,256,512]{4,3,2,1,0:T(8,128)} custom-call(s32[11]{0:T(128)} %pad_add_fusion.2.info_ref, f32[2]{0:T(128)} %copy-done.19, f32[8,5,2,2,32,128]{5,4,3,2,1,0:T(8,128)} %bitcast.27, f32[8,5,2,2,32,128]{5,4,3,2,1,0:T(8,128)} %bitcast.29, bf16[2048,256]{1,0:T(8,128)(2,1)} %constant.175.clone.refs_4_.refs_2_, ...), custom_call_target="tpu_custom_call", output_to_operand_aliasing={{}: (5, {})} | custom-call | flops 1048576 | bytes 1048576 | tf_op jit(solution)/shard_map/second_section/pallas_call | solution.py:334
  (95 shorter events, 1.8 us)
Async XLA Ops:
  7.2 42.2 %all-gather.5.cloned.1.call-start = ((), (), s32[]{:S(2)}) async-start(), calls=%async_computation.2 | async-start | bytes 1966080 | tf_op jit(solution)/shard_map/all_gather | solution.py:612
  9.3 100.6 %all-gather.7.cloned.1.call-start = ((), (), s32[]{:S(2)}) async-start(), calls=%async_computation.3 | async-start | bytes 1966080 | tf_op jit(solution)/shard_map/all_gather | solution.py:612
  12.4 11.8 %copy-start.20 = (s32[2,15]{1,0:T(2,128)S(1)}, s32[2,15]{1,0:T(2,128)}, u32[]{:S(2)}) copy-start(s32[2,15]{1,0:T(2,128)} %param.13) | copy-start | bytes 364
  18.3 13.7 %copy-start.12 = (f32[72,1024]{1,0:T(8,128)}, f32[72,1024]{1,0:T(8,128)S(1)}, u32[]{:S(2)}) copy-start(f32[72,1024]{1,0:T(8,128)S(1)} %select_maximum_fusion.refs_0_) | copy-start | bytes 884740
  18.3 22.1 %collective-permute-start.5 = (f32[72,1024]{1,0:T(8,128)S(1)}, f32[72,1024]{1,0:T(8,128)S(1)}, u32[]{:S(2)}, u32[]{:S(2)}) collective-permute-start(f32[72,1024]{1,0:T(8,128)S(1)} %select_maximum_fusion.refs_0_), channel_id=1, source_target_pairs={{0,6},{1,7},{2,4},{3,5},{4,2},{5,3},{6,0},{7,1},{8,14},{9,15},{10,... | collective-permute-start | bytes 884744 | tf_op jit(solution)/shard_map/ppermute | solution.py:591
  22.3 18.8 %collective-permute-start.3 = (f32[72,1024]{1,0:T(8,128)S(1)}, f32[72,1024]{1,0:T(8,128)S(1)}, u32[]{:S(2)}, u32[]{:S(2)}) collective-permute-start(f32[72,1024]{1,0:T(8,128)S(1)} %select_maximum_fusion.refs_0_), channel_id=1, source_target_pairs={{0,4},{1,5},{2,6},{3,7},{4,0},{5,1},{6,2},{7,3},{8,12},{9,13},{10,... | collective-permute-start | bytes 884744 | tf_op jit(solution)/shard_map/ppermute | solution.py:591
  22.8 18.4 %collective-permute-start.1 = (f32[72,1024]{1,0:T(8,128)S(1)}, f32[72,1024]{1,0:T(8,128)S(1)}, u32[]{:S(2)}, u32[]{:S(2)}) collective-permute-start(f32[72,1024]{1,0:T(8,128)S(1)} %select_maximum_fusion.refs_0_), channel_id=1, source_target_pairs={{0,2},{1,3},{2,0},{3,1},{4,6},{5,7},{6,4},{7,5},{8,10},{9,11},{10,... | collective-permute-start | bytes 884744 | tf_op jit(solution)/shard_map/ppermute | solution.py:591
  23.0 18.9 %collective-permute-start = (f32[72,1024]{1,0:T(8,128)S(1)}, f32[72,1024]{1,0:T(8,128)S(1)}, u32[]{:S(2)}, u32[]{:S(2)}) collective-permute-start(f32[72,1024]{1,0:T(8,128)S(1)} %select_maximum_fusion.refs_0_), channel_id=1, source_target_pairs={{0,1},{1,0},{2,3},{3,2},{4,5},{5,4},{6,7},{7,6},{8,9},{9,8},{10,11... | collective-permute-start | bytes 884744 | tf_op jit(solution)/shard_map/ppermute | solution.py:591
  40.5 8.9 %copy-start.5 = (f32[72,1024]{1,0:T(8,128)}, f32[72,1024]{1,0:T(8,128)S(1)}, u32[]{:S(2)}) copy-start(f32[72,1024]{1,0:T(8,128)S(1)} %collective-permute-done.5.refs_5_.refs_6_) | copy-start | bytes 884740
  40.6 1.7 collective-permute-start.6
  41.1 8.3 %copy-start.6 = (f32[72,1024]{1,0:T(8,128)}, f32[72,1024]{1,0:T(8,128)S(1)}, u32[]{:S(2)}) copy-start(f32[72,1024]{1,0:T(8,128)S(1)} %collective-permute-done.3.refs_3_.refs_4_) | copy-start | bytes 884740
  41.2 1.6 collective-permute-start.4
  41.2 8.2 %copy-start.7 = (f32[72,1024]{1,0:T(8,128)}, f32[72,1024]{1,0:T(8,128)S(1)}, u32[]{:S(2)}) copy-start(f32[72,1024]{1,0:T(8,128)S(1)} %collective-permute-done.1.refs_1_.refs_2_) | copy-start | bytes 884740
  41.3 1.9 collective-permute-start.2
  41.8 7.6 %copy-start.8 = (f32[72,1024]{1,0:T(8,128)}, f32[72,1024]{1,0:T(8,128)S(1)}, u32[]{:S(2)}) copy-start(f32[72,1024]{1,0:T(8,128)S(1)} %collective-permute-done.refs_0_.refs_1_) | copy-start | bytes 884740
  42.3 7.1 %copy-start.9 = (f32[72,1024]{1,0:T(8,128)}, f32[72,1024]{1,0:T(8,128)S(1)}, u32[]{:S(2)}) copy-start(f32[72,1024]{1,0:T(8,128)S(1)} %collective-permute-done.6.refs_6_.refs_7_) | copy-start | bytes 884740
  42.8 6.6 %copy-start.10 = (f32[72,1024]{1,0:T(8,128)}, f32[72,1024]{1,0:T(8,128)S(1)}, u32[]{:S(2)}) copy-start(f32[72,1024]{1,0:T(8,128)S(1)} %collective-permute-done.4.refs_4_.refs_5_) | copy-start | bytes 884740
  43.2 6.2 %copy-start.11 = (f32[72,1024]{1,0:T(8,128)}, f32[72,1024]{1,0:T(8,128)S(1)}, u32[]{:S(2)}) copy-start(f32[72,1024]{1,0:T(8,128)S(1)} %collective-permute-done.2.refs_2_.refs_3_) | copy-start | bytes 884740
  43.4 8.7 %copy-start.19 = (f32[2]{0:T(128)}, f32[2]{0:T(128)S(1)}, u32[]{:S(2)}) copy-start(f32[2]{0:T(128)S(1)} %rsqrt.6.scale_ref) | copy-start | bytes 28
  52.1 11.8 %collective-permute-start.7 = (f32[32,3072]{1,0:T(8,128)}, f32[32,3072]{1,0:T(8,128)S(1)}, u32[]{:S(2)}, u32[]{:S(2)}) collective-permute-start(f32[32,3072]{1,0:T(8,128)} %entry_product.4.refs_0_.refs_8_), channel_id=1, source_target_pairs={{0,6},{1,7},{2,4},{3,5},{4,2},{5,3},{6,0},{7,1},{8,14},{9,15},{10,... | collective-permute-start | bytes 1179656 | tf_op jit(solution)/shard_map/ppermute | solution.py:591
  64.0 0.8 copy-start.4
  64.7 4.0 %copy-start.16 = (f32[32,3072]{1,0:T(8,128)S(1)}, f32[32,3072]{1,0:T(8,128)}, u32[]{:S(2)}) copy-start(f32[32,3072]{1,0:T(8,128)} %entry_product.4.refs_0_.refs_8_) | copy-start | bytes 1179652
  64.7 76.7 %all-to-all-start = ((f32[8,640,128]{2,1,0:T(8,128)}), f32[8,640,128]{2,1,0:T(8,128)S(1)}, u32[]{:S(2)}, u32[]{:S(2)}) async-start(f32[8,640,128]{2,1,0:T(8,128)} %bitcast.30), calls=%async_computation | async-start | bytes 5242880 | tf_op jit(solution)/shard_map/all_to_all | solution.py:666
  68.7 39.7 %collective-permute-start.14 = (f32[32,3072]{1,0:T(8,128)S(1)}, f32[32,3072]{1,0:T(8,128)S(1)}, u32[]{:S(2)}, u32[]{:S(2)}) collective-permute-start(f32[32,3072]{1,0:T(8,128)S(1)} %copy-done.16), channel_id=1, source_target_pairs={{0,4},{1,5},{2,6},{3,7},{4,0},{5,1},{6,2},{7,3},{8,12},{9,13},{10,... | collective-permute-start | bytes 1179656 | tf_op jit(solution)/shard_map/ppermute | solution.py:591
  70.7 37.8 %collective-permute-start.13 = (f32[32,3072]{1,0:T(8,128)S(1)}, f32[32,3072]{1,0:T(8,128)S(1)}, u32[]{:S(2)}, u32[]{:S(2)}) collective-permute-start(f32[32,3072]{1,0:T(8,128)S(1)} %copy-done.16), channel_id=1, source_target_pairs={{0,2},{1,3},{2,0},{3,1},{4,6},{5,7},{6,4},{7,5},{8,10},{9,11},{10,... | collective-permute-start | bytes 1179656 | tf_op jit(solution)/shard_map/ppermute | solution.py:591
  72.2 41.8 %collective-permute-start.12 = (f32[32,3072]{1,0:T(8,128)S(1)}, f32[32,3072]{1,0:T(8,128)}, u32[]{:S(2)}, u32[]{:S(2)}) collective-permute-start(f32[32,3072]{1,0:T(8,128)S(1)} %copy-done.16), channel_id=1, source_target_pairs={{0,1},{1,0},{2,3},{3,2},{4,5},{5,4},{6,7},{7,6},{8,9},{9,8},{10,11... | collective-permute-start | bytes 1179656 | tf_op jit(solution)/shard_map/ppermute | solution.py:591
  108.4 0.7 copy-start.17
  108.5 0.8 copy-start.18
  109.3 6.2 %collective-permute-start.15 = (f32[32,3072]{1,0:T(8,128)}, f32[32,3072]{1,0:T(8,128)}, u32[]{:S(2)}, u32[]{:S(2)}) collective-permute-start(f32[32,3072]{1,0:T(8,128)} %get-tuple-element.44.refs_10_), channel_id=1, source_target_pairs={{0,1},{1,0},{2,3},{3,2},{4,5},{5,4},{6,7},{7,6},{8,9},{9,8},{10,11... | collective-permute-start | bytes 1179656 | tf_op jit(solution)/shard_map/ppermute | solution.py:591
  109.3 14.4 %collective-permute-start.16 = (f32[32,3072]{1,0:T(8,128)}, f32[32,3072]{1,0:T(8,128)}, u32[]{:S(2)}, u32[]{:S(2)}) collective-permute-start(f32[32,3072]{1,0:T(8,128)} %get-tuple-element.45.refs_12_), channel_id=1, source_target_pairs={{0,1},{1,0},{2,3},{3,2},{4,5},{5,4},{6,7},{7,6},{8,9},{9,8},{10,11... | collective-permute-start | bytes 1179656 | tf_op jit(solution)/shard_map/ppermute | solution.py:591
  109.9 14.0 %collective-permute-start.17 = (f32[32,3072]{1,0:T(8,128)}, f32[32,3072]{1,0:T(8,128)}, u32[]{:S(2)}, u32[]{:S(2)}) collective-permute-start(f32[32,3072]{1,0:T(8,128)} %get-tuple-element.46.refs_14_), channel_id=1, source_target_pairs={{0,1},{1,0},{2,3},{3,2},{4,5},{5,4},{6,7},{7,6},{8,9},{9,8},{10,11... | collective-permute-start | bytes 1179656 | tf_op jit(solution)/shard_map/ppermute | solution.py:591
  112.6 28.8 %collective-permute-start.11 = (f32[32,3072]{1,0:T(8,128)}, f32[32,3072]{1,0:T(8,128)S(1)}, u32[]{:S(2)}, u32[]{:S(2)}) collective-permute-start(f32[32,3072]{1,0:T(8,128)} %entry_product.5.refs_0_.refs_8_), channel_id=1, source_target_pairs={{0,6},{1,7},{2,4},{3,5},{4,2},{5,3},{6,0},{7,1},{8,14},{9,15},{10,... | collective-permute-start | bytes 1179656 | tf_op jit(solution)/shard_map/ppermute | solution.py:591
  113.9 27.4 %collective-permute-start.10 = (f32[32,3072]{1,0:T(8,128)}, f32[32,3072]{1,0:T(8,128)S(1)}, u32[]{:S(2)}, u32[]{:S(2)}) collective-permute-start(f32[32,3072]{1,0:T(8,128)} %entry_product.5.refs_0_.refs_8_), channel_id=1, source_target_pairs={{0,4},{1,5},{2,6},{3,7},{4,0},{5,1},{6,2},{7,3},{8,12},{9,13},{10,... | collective-permute-start | bytes 1179656 | tf_op jit(solution)/shard_map/ppermute | solution.py:591
  115.5 25.9 %collective-permute-start.9 = (f32[32,3072]{1,0:T(8,128)}, f32[32,3072]{1,0:T(8,128)}, u32[]{:S(2)}, u32[]{:S(2)}) collective-permute-start(f32[32,3072]{1,0:T(8,128)} %entry_product.5.refs_0_.refs_8_), channel_id=1, source_target_pairs={{0,2},{1,3},{2,0},{3,1},{4,6},{5,7},{6,4},{7,5},{8,10},{9,11},{10,... | collective-permute-start | bytes 1179656 | tf_op jit(solution)/shard_map/ppermute | solution.py:591
  123.7 20.4 %collective-permute-start.8 = (f32[32,3072]{1,0:T(8,128)}, f32[32,3072]{1,0:T(8,128)}, u32[]{:S(2)}, u32[]{:S(2)}) collective-permute-start(f32[32,3072]{1,0:T(8,128)} %entry_product.5.refs_0_.refs_8_), channel_id=1, source_target_pairs={{0,1},{1,0},{2,3},{3,2},{4,5},{5,4},{6,7},{7,6},{8,9},{9,8},{10,11... | collective-permute-start | bytes 1179656 | tf_op jit(solution)/shard_map/ppermute | solution.py:591
  141.4 0.8 copy-start.2
  141.4 0.9 copy-start.3
  141.4 1.7 copy-start
  143.2 2.0 collective-permute-start.18
  143.6 2.1 %collective-permute-start.19 = (f32[32,3072]{1,0:T(8,128)}, f32[32,3072]{1,0:T(8,128)S(1)}, u32[]{:S(2)}, u32[]{:S(2)}) collective-permute-start(f32[32,3072]{1,0:T(8,128)} %get-tuple-element.52.refs_4_.refs_12_), channel_id=1, source_target_pairs={{0,1},{1,0},{2,3},{3,2},{4,5},{5,4},{6,7},{7,6},{8,9},{9,8},{10,11... | collective-permute-start | bytes 1179656 | tf_op jit(solution)/shard_map/ppermute | solution.py:591
  143.7 2.7 %collective-permute-start.20 = (f32[32,3072]{1,0:T(8,128)}, f32[32,3072]{1,0:T(8,128)S(1)}, u32[]{:S(2)}, u32[]{:S(2)}) collective-permute-start(f32[32,3072]{1,0:T(8,128)} %get-tuple-element.53.refs_6_.refs_14_), channel_id=1, source_target_pairs={{0,1},{1,0},{2,3},{3,2},{4,5},{5,4},{6,7},{7,6},{8,9},{9,8},{10,11... | collective-permute-start | bytes 1179656 | tf_op jit(solution)/shard_map/ppermute | solution.py:591
  145.2 1.1 copy-start.13
  145.8 0.8 copy-start.14
  146.3 0.8 copy-start.15
  147.1 37.9 %all-to-all-start.1 = ((f32[8,640,128]{2,1,0:T(8,128)}), f32[8,640,128]{2,1,0:T(8,128)S(1)}, u32[]{:S(2)}, u32[]{:S(2)}) async-start(f32[8,640,128]{2,1,0:T(8,128)} %bitcast.28), calls=%async_computation.1 | async-start | bytes 5242880 | tf_op jit(solution)/shard_map/all_to_all | solution.py:666
  185.0 1.5 copy-start.1
Sparse Core Ops, SparseCore 0:
  9.6 39.7 all-gather.4
  51.0 35.9 all-gather.6

commit v16 on v15

--- a/solution.py
+++ b/solution.py
@@ -683,7 +683,7 @@
             freq, h, info, templates, strains[h], first, stage, twist, half
         )
         if h < HALVES - 1:
-            (sent,) = handed_on([sent], [x[-1] for x in far])
+            (sent,) = handed_on([sent], [piece for x in far for piece in x[1:]])
         if h:
             halves.append(bins_of(h - 1, rest, [token]))
         done = [token] + parts + [x[1] for one in halves for x in one]

time: 205 us -> 188 us (0.917)
  waiting for transfers between devices: 45.3 us -> 33 us
  starting transfers between devices: 24.2 us -> 21.9 us
    ppermute x21, waiting for transfers between devices: 41.2 us -> 20.2 us  [swap(): return lax.ppermute(x, 'freq', [(i, i ^ k) for i in range(freq)])]
    all_gather x2, waiting for transfers between devices: 4.1 us -> 12.7 us  [per_device(): strains = [lax.all_gather(x, 'bank', axis=0, tiled=False) for x in slices]]
    ppermute x21, starting transfers between devices: 16.6 us -> 14.3 us  [swap(): return lax.ppermute(x, 'freq', [(i, i ^ k) for i in range(freq)])]
  transfers between devices with their start and end apart: 25 -> 25, of which waited for: 10 -> 14; matrix products, arithmetic and copies ran while one was open for 9% -> 9% of each run, Pallas kernels for 41% -> 44%
where the time goes in v16:
time: 188 us; the launch traced here: 187 us
  Pallas kernels  92.1 us (49%)
  waiting for transfers between devices  33 us (18%)
  starting transfers between devices  21.9 us (12%)
  other arithmetic  15.9 us (8%)
  between operations  15.6 us (8%)
  local copies, waits for them, and re-layouts  8.45 us (4%)
    pallas_call x2, Pallas kernels, bins_first(): pl.pallas_call(functools.partial(bins_first_kernel, len(own), banks), gri...  33.8 us
    ppermute x21, waiting for transfers between devices, swap(): return lax.ppermute(x, 'freq', [(i, i ^ k) for i in range(freq)])  20.2 us
    pallas_call x1, Pallas kernels, bins_second(): pl.pallas_call(functools.partial(bins_second_kernel, halves), grid_spec=p...  16.7 us
    pallas_call x2, Pallas kernels, first_section(): pl.pallas_call(functools.partial(first_kernel, freq), grid_spec=pltpu.Pre...  15.5 us
    ppermute x21, starting transfers between devices, swap(): return lax.ppermute(x, 'freq', [(i, i ^ k) for i in range(freq)])  14.3 us
    all_gather x2, waiting for transfers between devices, per_device(): strains = [lax.all_gather(x, 'bank', axis=0, tiled=False) for x in slices]  12.7 us
    pallas_call x1, Pallas kernels, second_section(): pl.pallas_call(functools.partial(second_kernel, freq, halves), grid_spec=...  10.7 us
    pallas_call x3, Pallas kernels, entry_product(): pl.pallas_call(functools.partial(entry_kernel, steps, banks), grid_spec=p...  9.41 us
  transfers between devices with their start and end apart: 25, of which 14 were waited for; matrix products, arithmetic and copies ran while one was open for 9% of the time, Pallas kernels for 44%

profile of v16, /device:TPU:0, one launch (start us, length us, event | category | flops | bytes accessed | tf_op | source)
XLA Modules:
  0.0 187.0 jit_solution(5487338874674949746)
XLA Ops:
  7.2 2.1 %fusion.49 = (f32[3,2,32,512]{3,2,1,0:T(8,128)}, f32[3,2,32,512]{3,2,1,0:T(8,128)}) fusion(f32[3,2,64,512]{3,2,1,0:T(8,128)} %param.9), kind=kLoop, calls=%fused_computation.114 | loop fusion | bytes 1572864 | tf_op jit(solution)/shard_map/slice | solution.py:611
  10.6 1.7 add_reduce_fusion
  12.7 0.7 pad_add_fusion.1.which_ref
  13.3 4.0 %entry_product.3 = f32[64,1024]{1,0:T(8,128)} custom-call(s32[3]{0:T(128)} %pad_add_fusion.1.which_ref, f32[2,2,64,2048]{3,2,1,0:T(8,128)} %tmpl_ref.9, f32[1,3,2,64,512]{4,3,2,1,0:T(8,128)} %bitcast.31, f32[3,2,32,512]{3,2,1,0:T(8,128)} %get-tuple-element.67.refs_0_, f32[3,2,32,512]{3,2,1,0:T(8,128)} %get-tuple-element.66.refs_1_), custom_call_target="tpu_custom_call" | custom-call | flops 1048576 | bytes 1048576 | tf_op jit(solution)/shard_map/entry_product/pallas_call | solution.py:258
  17.4 1.0 select_maximum_fusion.refs_0_
  18.3 4.0 %collective-permute-start.5 = (f32[72,1024]{1,0:T(8,128)S(1)}, f32[72,1024]{1,0:T(8,128)S(1)}, u32[]{:S(2)}, u32[]{:S(2)}) collective-permute-start(f32[72,1024]{1,0:T(8,128)S(1)} %select_maximum_fusion.refs_0_), channel_id=1, source_target_pairs={{0,6},{1,7},{2,4},{3,5},{4,2},{5,3},{6,0},{7,1},{8,14},{9,15},{10,... | collective-permute-start | bytes 884744 | tf_op jit(solution)/shard_map/ppermute | solution.py:591
  22.3 0.5 collective-permute-start.3
  22.8 0.1 collective-permute-start.1
  23.1 0.3 fusion.24
  23.4 0.7 pad_add_fusion.4.place_ref
  24.4 1.0 fusion.39
  25.4 0.7 pad_maximum_fusion.4.block_ref
  26.1 0.7 pad_maximum_fusion.3.inner_ref
  26.8 2.1 %fusion.10 = (f32[1,64,2048]{2,1,0:T(8,128)S(1)}, f32[1,64,2048]{2,1,0:T(8,128)S(1)}) fusion(s32[2048]{0:T(1024)S(1)} %fusion.35, s32[64]{0:T(128)S(1)} %iota_add_fusion.1), kind=kLoop, calls=%fused_computation.31 | loop fusion | flops 1835008 | bytes 1057024 | tf_op jit(solution)/shard_map/cos | solution.py:64
  28.9 1.1 pad_maximum_fusion.tw_ref
  29.9 2.1 %fusion.12 = (f32[1,256,256]{2,1,0:T(8,128)S(1)}, f32[1,256,256]{2,1,0:T(8,128)S(1)}, f32[1,256,256]{2,1,0:T(8,128)S(1)}, f32[1,256,256]{2,1,0:T(8,128)S(1)}) fusion(s32[256]{0:T(256)S(1)} %iota_add_fusion, s32[256]{0:T(256)S(1)} %add_add_fusion, s32[256]{0:T(256)S(1)} %fusion.45), kind=kLoop, calls=%fused_computation.34 | loop fusion | flops 1835008 | bytes 1051648 | tf_op jit(solution)/shard_map/cos | solution.py:64
  32.1 6.0 %bank_table.1 = (bf16[4096,512]{1,0:T(8,128)(2,1)}, bf16[4096,512]{1,0:T(8,128)(2,1)}) custom-call(f32[32,2,256]{2,1,0:T(2,128)} %pad_maximum_fusion.4.block_ref, f32[2,64,256]{2,1,0:T(8,128)} %pad_maximum_fusion.3.inner_ref), custom_call_target="tpu_custom_call" | custom-call | flops 1048576 | bytes 1048576 | tf_op jit(solution)/shard_map/bank_table/pallas_call | solution.py:380
  38.1 1.0 pad_maximum_fusion.1
  39.2 0.7 pad_add_fusion.2.info_ref
  39.8 0.7 pad_add_fusion.3.edge_ref
  40.6 0.5 collective-permute-start.6
  41.3 0.5 collective-permute-start.2
  41.9 0.4 collective-permute-done.6.refs_6_.refs_7_
  42.4 0.4 collective-permute-done.4.refs_4_.refs_5_
  42.9 0.3 collective-permute-done.2.refs_2_.refs_3_
  43.6 0.6 dynamic_slice.10
  44.2 1.1 bitcast_multiply_fusion
  45.3 4.1 %all-gather.5.cloned.1.call-done = f32[12,2,32,512]{3,2,1,0:T(8,128)} async-done(((f32[3,2,32,512]{3,2,1,0:T(8,128)}), f32[12,2,32,512]{3,2,1,0:T(8,128)}) %all-gather.5.cloned.1.call-update) | async-done | bytes 1572880 | tf_op jit(solution)/shard_map/all_gather | solution.py:612
  49.4 2.7 %entry_product.4.refs_0_.refs_8_ = f32[32,3072]{1,0:T(8,128)} custom-call(s32[3]{0:T(128)} %pad_add_fusion.1.which_ref, f32[2,2,64,2048]{3,2,1,0:T(8,128)} %tmpl_ref.9, f32[4,3,2,32,512]{4,3,2,1,0:T(8,128)} %bitcast.34, f32[72,1024]{1,0:T(8,128)} %copy-done.10, f32[72,1024]{1,0:T(8,128)} %copy-done.9, f32[72,1024]{1,0:T(8,128)} %copy-done.13, ...), custom_call_target="tpu_custom_call" | custom-call | flops 1048576 | bytes 1048576 | tf_op jit(solution)/shard_map/entry_product/pallas_call | solution.py:258
  52.1 2.4 %collective-permute-start.9 = (f32[32,3072]{1,0:T(8,128)}, f32[32,3072]{1,0:T(8,128)S(1)}, u32[]{:S(2)}, u32[]{:S(2)}) collective-permute-start(f32[32,3072]{1,0:T(8,128)} %entry_product.4.refs_0_.refs_8_), channel_id=1, source_target_pairs={{0,6},{1,7},{2,4},{3,5},{4,2},{5,3},{6,0},{7,1},{8,14},{9,15},{10,... | collective-permute-start | bytes 1179656 | tf_op jit(solution)/shard_map/ppermute | solution.py:591
  54.6 0.5 collective-permute-start.8
  55.0 0.6 collective-permute-start.7
  55.6 7.8 %first_section.2 = (f32[8,5,2,2,32,128]{5,4,3,2,1,0:T(8,128)}, f32[8,128]{1,0:T(8,128)}) custom-call(s32[11]{0:T(128)} %pad_add_fusion.2.info_ref, f32[2,2,64,2048]{3,2,1,0:T(8,128)} %tmpl_ref.9, f32[4,3,2,32,512]{4,3,2,1,0:T(8,128)} %bitcast.35, bf16[256,256]{1,0:T(8,128)(2,1)} %constant.173.clone.wh_ref, bf16[256,256]{1,0:T(8,128)(2,1)} %constant.174.clone.wl_ref, ...), custom_call_target="tpu_custom_call" | custom-call | flops 2516582400 | bytes 16777216 | tf_op jit(solution)/shard_map/first_section/pallas_call | solution.py:196
  63.4 1.9 %collective-permute-done.9.refs_3_.refs_2_ = f32[32,3072]{1,0:T(8,128)S(1)} collective-permute-done((f32[32,3072]{1,0:T(8,128)}, f32[32,3072]{1,0:T(8,128)S(1)}, u32[]{:S(2)}, u32[]{:S(2)}) %collective-permute-start.9) | collective-permute-done | bytes 393248 | tf_op jit(solution)/shard_map/ppermute | solution.py:591
  65.3 7.1 %collective-permute-done.8.refs_2_.refs_1_ = f32[32,3072]{1,0:T(8,128)S(1)} collective-permute-done((f32[32,3072]{1,0:T(8,128)}, f32[32,3072]{1,0:T(8,128)S(1)}, u32[]{:S(2)}, u32[]{:S(2)}) %collective-permute-start.8) | collective-permute-done | bytes 393248 | tf_op jit(solution)/shard_map/ppermute | solution.py:591
  72.5 0.6 copy-done.5
  73.3 3.9 %all-to-all-start = ((f32[8,640,128]{2,1,0:T(8,128)}), f32[8,640,128]{2,1,0:T(8,128)S(1)}, u32[]{:S(2)}, u32[]{:S(2)}) async-start(f32[8,640,128]{2,1,0:T(8,128)} %bitcast.30), calls=%async_computation | async-start | bytes 5242880 | tf_op jit(solution)/shard_map/all_to_all | solution.py:666
  77.2 0.2 collective-permute-start.14
  77.5 0.4 collective-permute-start.15
  77.8 0.2 collective-permute-start.16
  78.0 0.4 collective-permute-start.17
  78.3 8.6 %all-gather.7.cloned.1.call-done = f32[12,2,32,512]{3,2,1,0:T(8,128)} async-done(((f32[3,2,32,512]{3,2,1,0:T(8,128)}), f32[12,2,32,512]{3,2,1,0:T(8,128)}) %all-gather.7.cloned.1.call-update) | async-done | bytes 1572880 | tf_op jit(solution)/shard_map/all_gather | solution.py:612
  87.0 2.7 %entry_product.5.refs_0_.refs_8_ = f32[32,3072]{1,0:T(8,128)} custom-call(s32[3]{0:T(128)} %pad_add_fusion.1.which_ref, f32[2,2,64,2048]{3,2,1,0:T(8,128)} %tmpl_ref.9, f32[4,3,2,32,512]{4,3,2,1,0:T(8,128)} %bitcast.32, f32[8,128]{1,0:T(8,128)} %get-tuple-element.39.refs_0_.refs_3_), custom_call_target="tpu_custom_call" | custom-call | flops 1048576 | bytes 1048576 | tf_op jit(solution)/shard_map/entry_product/pallas_call | solution.py:258
  89.6 2.4 %collective-permute-start.13 = (f32[32,3072]{1,0:T(8,128)}, f32[32,3072]{1,0:T(8,128)S(1)}, u32[]{:S(2)}, u32[]{:S(2)}) collective-permute-start(f32[32,3072]{1,0:T(8,128)} %entry_product.5.refs_0_.refs_8_), channel_id=1, source_target_pairs={{0,6},{1,7},{2,4},{3,5},{4,2},{5,3},{6,0},{7,1},{8,14},{9,15},{10,... | collective-permute-start | bytes 1179656 | tf_op jit(solution)/shard_map/ppermute | solution.py:591
  92.0 0.6 collective-permute-start.12
  92.6 0.6 collective-permute-start.11
  93.1 7.7 %first_section.3 = (f32[8,5,2,2,32,128]{5,4,3,2,1,0:T(8,128)}, f32[8,128]{1,0:T(8,128)}) custom-call(s32[11]{0:T(128)} %pad_add_fusion.2.info_ref, f32[2,2,64,2048]{3,2,1,0:T(8,128)} %tmpl_ref.9, f32[4,3,2,32,512]{4,3,2,1,0:T(8,128)} %bitcast.33, bf16[256,256]{1,0:T(8,128)(2,1)} %constant.173.clone.wh_ref, bf16[256,256]{1,0:T(8,128)(2,1)} %constant.174.clone.wl_ref, ...), custom_call_target="tpu_custom_call" | custom-call | flops 2516582400 | bytes 16777216 | tf_op jit(solution)/shard_map/first_section/pallas_call | solution.py:196
  100.9 16.9 %bins_first.2 = (f32[16,2,256,256]{3,2,1,0:T(8,128)}, f32[2,256,256]{2,1,0:T(8,128)}) custom-call(s32[2]{0:T(128)} %pad_add_fusion.4.place_ref, s32[17]{0:T(128)} %pad_add_fusion.3.edge_ref, f32[72,1024]{1,0:T(8,128)} %copy-done.14, f32[72,1024]{1,0:T(8,128)} %copy-done.10, f32[72,1024]{1,0:T(8,128)} %copy-done.9, f32[72,1024]{1,0:T(8,128)} %copy-done.13, ...), custom_call_target="tpu_custom_call" | custom-call | flops 1048576 | bytes 1048576 | tf_op jit(solution)/shard_map/bins_first/pallas_call | solution.py:465
  117.8 0.4 collective-permute-done.13.refs_2_
  118.2 6.9 %collective-permute-done.12.refs_1_ = f32[32,3072]{1,0:T(8,128)S(1)} collective-permute-done((f32[32,3072]{1,0:T(8,128)}, f32[32,3072]{1,0:T(8,128)S(1)}, u32[]{:S(2)}, u32[]{:S(2)}) %collective-permute-start.12) | collective-permute-done | bytes 393248 | tf_op jit(solution)/shard_map/ppermute | solution.py:591
  125.1 0.2 collective-permute-done.11.refs_0_
  125.3 0.6 copy-done.3
  125.9 1.0 copy-done
  126.9 0.5 collective-permute-start.19
  127.4 1.4 collective-permute-done.18.refs_3_.refs_11_
  128.8 0.6 collective-permute-done.19.refs_5_.refs_13_
  129.4 0.6 collective-permute-done.20.refs_7_.refs_15_
  129.9 0.2 copy-done.16
  130.1 0.6 copy-done.17
  130.7 3.6 %all-to-all-start.1 = ((f32[8,640,128]{2,1,0:T(8,128)}), f32[8,640,128]{2,1,0:T(8,128)S(1)}, u32[]{:S(2)}, u32[]{:S(2)}) async-start(f32[8,640,128]{2,1,0:T(8,128)} %bitcast.28), calls=%async_computation.1 | async-start | bytes 5242880 | tf_op jit(solution)/shard_map/all_to_all | solution.py:666
  134.3 16.9 %bins_first.3 = (f32[16,2,256,256]{3,2,1,0:T(8,128)}, f32[2,256,256]{2,1,0:T(8,128)}) custom-call(s32[2]{0:T(128)} %pad_add_fusion.4.place_ref, s32[17]{0:T(128)} %pad_add_fusion.3.edge_ref, f32[72,1024]{1,0:T(8,128)} %copy-done.14, f32[72,1024]{1,0:T(8,128)} %copy-done.10, f32[72,1024]{1,0:T(8,128)} %copy-done.9, f32[72,1024]{1,0:T(8,128)} %copy-done.13, ...), custom_call_target="tpu_custom_call" | custom-call | flops 1048576 | bytes 1048576 | tf_op jit(solution)/shard_map/bins_first/pallas_call | solution.py:465
  151.3 16.7 %bins_second.1 = (f32[256,512]{1,0:T(8,128)}, f32[2,3,2,256,512]{4,3,2,1,0:T(8,128)}) custom-call(s32[3]{0:T(128)} %pad_add_fusion.1.which_ref, f32[2]{0:T(128)} %copy-done.19, f32[16]{0:T(128)} %get-tuple-element.54.gain_ref, f32[16]{0:T(128)} %get-tuple-element.55.share_ref, f32[16,2,256,256]{3,2,1,0:T(8,128)} %get-tuple-element.56.refs_0_, ...), custom_call_target="tpu_custom_call" | custom-call | flops 1048576 | bytes 1048576 | tf_op jit(solution)/shard_map/bins_second/pallas_call | solution.py:548
  168.0 1.5 copy-done.1
  169.5 10.7 %second_section.1 = f32[2,3,2,256,512]{4,3,2,1,0:T(8,128)} custom-call(s32[11]{0:T(128)} %pad_add_fusion.2.info_ref, f32[2]{0:T(128)} %copy-done.19, f32[8,5,2,2,32,128]{5,4,3,2,1,0:T(8,128)} %bitcast.27, f32[8,5,2,2,32,128]{5,4,3,2,1,0:T(8,128)} %bitcast.29, bf16[2048,256]{1,0:T(8,128)(2,1)} %constant.175.clone.refs_4_.refs_2_, ...), custom_call_target="tpu_custom_call", output_to_operand_aliasing={{}: (5, {})} | custom-call | flops 1048576 | bytes 1048576 | tf_op jit(solution)/shard_map/second_section/pallas_call | solution.py:334
  (95 shorter events, 2.3 us)
Async XLA Ops:
  7.2 42.2 %all-gather.5.cloned.1.call-start = ((), (), s32[]{:S(2)}) async-start(), calls=%async_computation.2 | async-start | bytes 1966080 | tf_op jit(solution)/shard_map/all_gather | solution.py:612
  9.3 77.7 %all-gather.7.cloned.1.call-start = ((), (), s32[]{:S(2)}) async-start(), calls=%async_computation.3 | async-start | bytes 1966080 | tf_op jit(solution)/shard_map/all_gather | solution.py:612
  12.4 11.8 %copy-start.20 = (s32[2,15]{1,0:T(2,128)S(1)}, s32[2,15]{1,0:T(2,128)}, u32[]{:S(2)}) copy-start(s32[2,15]{1,0:T(2,128)} %param.13) | copy-start | bytes 364
  18.3 13.7 %copy-start.14 = (f32[72,1024]{1,0:T(8,128)}, f32[72,1024]{1,0:T(8,128)S(1)}, u32[]{:S(2)}) copy-start(f32[72,1024]{1,0:T(8,128)S(1)} %select_maximum_fusion.refs_0_) | copy-start | bytes 884740
  18.3 22.1 %collective-permute-start.5 = (f32[72,1024]{1,0:T(8,128)S(1)}, f32[72,1024]{1,0:T(8,128)S(1)}, u32[]{:S(2)}, u32[]{:S(2)}) collective-permute-start(f32[72,1024]{1,0:T(8,128)S(1)} %select_maximum_fusion.refs_0_), channel_id=1, source_target_pairs={{0,6},{1,7},{2,4},{3,5},{4,2},{5,3},{6,0},{7,1},{8,14},{9,15},{10,... | collective-permute-start | bytes 884744 | tf_op jit(solution)/shard_map/ppermute | solution.py:591
  22.3 18.8 %collective-permute-start.3 = (f32[72,1024]{1,0:T(8,128)S(1)}, f32[72,1024]{1,0:T(8,128)S(1)}, u32[]{:S(2)}, u32[]{:S(2)}) collective-permute-start(f32[72,1024]{1,0:T(8,128)S(1)} %select_maximum_fusion.refs_0_), channel_id=1, source_target_pairs={{0,4},{1,5},{2,6},{3,7},{4,0},{5,1},{6,2},{7,3},{8,12},{9,13},{10,... | collective-permute-start | bytes 884744 | tf_op jit(solution)/shard_map/ppermute | solution.py:591
  22.8 18.4 %collective-permute-start.1 = (f32[72,1024]{1,0:T(8,128)S(1)}, f32[72,1024]{1,0:T(8,128)S(1)}, u32[]{:S(2)}, u32[]{:S(2)}) collective-permute-start(f32[72,1024]{1,0:T(8,128)S(1)} %select_maximum_fusion.refs_0_), channel_id=1, source_target_pairs={{0,2},{1,3},{2,0},{3,1},{4,6},{5,7},{6,4},{7,5},{8,10},{9,11},{10,... | collective-permute-start | bytes 884744 | tf_op jit(solution)/shard_map/ppermute | solution.py:591
  23.0 18.9 %collective-permute-start = (f32[72,1024]{1,0:T(8,128)S(1)}, f32[72,1024]{1,0:T(8,128)S(1)}, u32[]{:S(2)}, u32[]{:S(2)}) collective-permute-start(f32[72,1024]{1,0:T(8,128)S(1)} %select_maximum_fusion.refs_0_), channel_id=1, source_target_pairs={{0,1},{1,0},{2,3},{3,2},{4,5},{5,4},{6,7},{7,6},{8,9},{9,8},{10,11... | collective-permute-start | bytes 884744 | tf_op jit(solution)/shard_map/ppermute | solution.py:591
  40.5 8.9 %copy-start.7 = (f32[72,1024]{1,0:T(8,128)}, f32[72,1024]{1,0:T(8,128)S(1)}, u32[]{:S(2)}) copy-start(f32[72,1024]{1,0:T(8,128)S(1)} %collective-permute-done.5.refs_5_.refs_6_) | copy-start | bytes 884740
  40.6 1.7 collective-permute-start.6
  41.1 8.3 %copy-start.8 = (f32[72,1024]{1,0:T(8,128)}, f32[72,1024]{1,0:T(8,128)S(1)}, u32[]{:S(2)}) copy-start(f32[72,1024]{1,0:T(8,128)S(1)} %collective-permute-done.3.refs_3_.refs_4_) | copy-start | bytes 884740
  41.2 1.6 collective-permute-start.4
  41.2 8.2 %copy-start.9 = (f32[72,1024]{1,0:T(8,128)}, f32[72,1024]{1,0:T(8,128)S(1)}, u32[]{:S(2)}) copy-start(f32[72,1024]{1,0:T(8,128)S(1)} %collective-permute-done.1.refs_1_.refs_2_) | copy-start | bytes 884740
  41.3 1.9 %collective-permute-start.2 = (f32[72,1024]{1,0:T(8,128)S(1)}, f32[72,1024]{1,0:T(8,128)S(1)}, u32[]{:S(2)}, u32[]{:S(2)}) collective-permute-start(f32[72,1024]{1,0:T(8,128)S(1)} %collective-permute-done.1.refs_1_.refs_2_), channel_id=1, source_target_pairs={{0,1},{1,0},{2,3},{3,2},{4,5},{5,4},{6,7},{7,6},{8,9},{9,8},{10,11... | collective-permute-start | bytes 884744 | tf_op jit(solution)/shard_map/ppermute | solution.py:591
  41.8 7.6 %copy-start.10 = (f32[72,1024]{1,0:T(8,128)}, f32[72,1024]{1,0:T(8,128)S(1)}, u32[]{:S(2)}) copy-start(f32[72,1024]{1,0:T(8,128)S(1)} %collective-permute-done.refs_0_.refs_1_) | copy-start | bytes 884740
  42.3 7.1 %copy-start.11 = (f32[72,1024]{1,0:T(8,128)}, f32[72,1024]{1,0:T(8,128)S(1)}, u32[]{:S(2)}) copy-start(f32[72,1024]{1,0:T(8,128)S(1)} %collective-permute-done.6.refs_6_.refs_7_) | copy-start | bytes 884740
  42.8 6.6 %copy-start.12 = (f32[72,1024]{1,0:T(8,128)}, f32[72,1024]{1,0:T(8,128)S(1)}, u32[]{:S(2)}) copy-start(f32[72,1024]{1,0:T(8,128)S(1)} %collective-permute-done.4.refs_4_.refs_5_) | copy-start | bytes 884740
  43.2 6.2 %copy-start.13 = (f32[72,1024]{1,0:T(8,128)}, f32[72,1024]{1,0:T(8,128)S(1)}, u32[]{:S(2)}) copy-start(f32[72,1024]{1,0:T(8,128)S(1)} %collective-permute-done.2.refs_2_.refs_3_) | copy-start | bytes 884740
  43.4 8.7 %copy-start.19 = (f32[2]{0:T(128)}, f32[2]{0:T(128)S(1)}, u32[]{:S(2)}) copy-start(f32[2]{0:T(128)S(1)} %rsqrt.6.scale_ref) | copy-start | bytes 28
  52.1 13.2 %collective-permute-start.9 = (f32[32,3072]{1,0:T(8,128)}, f32[32,3072]{1,0:T(8,128)S(1)}, u32[]{:S(2)}, u32[]{:S(2)}) collective-permute-start(f32[32,3072]{1,0:T(8,128)} %entry_product.4.refs_0_.refs_8_), channel_id=1, source_target_pairs={{0,6},{1,7},{2,4},{3,5},{4,2},{5,3},{6,0},{7,1},{8,14},{9,15},{10,... | collective-permute-start | bytes 1179656 | tf_op jit(solution)/shard_map/ppermute | solution.py:591
  54.6 17.8 %collective-permute-start.8 = (f32[32,3072]{1,0:T(8,128)}, f32[32,3072]{1,0:T(8,128)S(1)}, u32[]{:S(2)}, u32[]{:S(2)}) collective-permute-start(f32[32,3072]{1,0:T(8,128)} %entry_product.4.refs_0_.refs_8_), channel_id=1, source_target_pairs={{0,4},{1,5},{2,6},{3,7},{4,0},{5,1},{6,2},{7,3},{8,12},{9,13},{10,... | collective-permute-start | bytes 1179656 | tf_op jit(solution)/shard_map/ppermute | solution.py:591
  55.0 17.5 %collective-permute-start.7 = (f32[32,3072]{1,0:T(8,128)}, f32[32,3072]{1,0:T(8,128)S(1)}, u32[]{:S(2)}, u32[]{:S(2)}) collective-permute-start(f32[32,3072]{1,0:T(8,128)} %entry_product.4.refs_0_.refs_8_), channel_id=1, source_target_pairs={{0,2},{1,3},{2,0},{3,1},{4,6},{5,7},{6,4},{7,5},{8,10},{9,11},{10,... | collective-permute-start | bytes 1179656 | tf_op jit(solution)/shard_map/ppermute | solution.py:591
  65.3 7.2 %copy-start.4 = (f32[32,3072]{1,0:T(8,128)}, f32[32,3072]{1,0:T(8,128)S(1)}, u32[]{:S(2)}) copy-start(f32[32,3072]{1,0:T(8,128)S(1)} %collective-permute-done.9.refs_3_.refs_2_) | copy-start | bytes 1179652
  72.4 0.8 copy-start.5
  72.5 0.8 copy-start.6
  73.3 4.0 %copy-start.18 = (f32[32,3072]{1,0:T(8,128)S(1)}, f32[32,3072]{1,0:T(8,128)}, u32[]{:S(2)}) copy-start(f32[32,3072]{1,0:T(8,128)} %entry_product.4.refs_0_.refs_8_) | copy-start | bytes 1179652
  73.3 52.0 %all-to-all-start = ((f32[8,640,128]{2,1,0:T(8,128)}), f32[8,640,128]{2,1,0:T(8,128)S(1)}, u32[]{:S(2)}, u32[]{:S(2)}) async-start(f32[8,640,128]{2,1,0:T(8,128)} %bitcast.30), calls=%async_computation | async-start | bytes 5242880 | tf_op jit(solution)/shard_map/all_to_all | solution.py:666
  77.2 14.8 %collective-permute-start.14 = (f32[32,3072]{1,0:T(8,128)S(1)}, f32[32,3072]{1,0:T(8,128)}, u32[]{:S(2)}, u32[]{:S(2)}) collective-permute-start(f32[32,3072]{1,0:T(8,128)S(1)} %copy-done.18), channel_id=1, source_target_pairs={{0,1},{1,0},{2,3},{3,2},{4,5},{5,4},{6,7},{7,6},{8,9},{9,8},{10,11... | collective-permute-start | bytes 1179656 | tf_op jit(solution)/shard_map/ppermute | solution.py:591
  77.5 15.1 %collective-permute-start.15 = (f32[32,3072]{1,0:T(8,128)}, f32[32,3072]{1,0:T(8,128)}, u32[]{:S(2)}, u32[]{:S(2)}) collective-permute-start(f32[32,3072]{1,0:T(8,128)} %get-tuple-element.44.refs_10_), channel_id=1, source_target_pairs={{0,1},{1,0},{2,3},{3,2},{4,5},{5,4},{6,7},{7,6},{8,9},{9,8},{10,11... | collective-permute-start | bytes 1179656 | tf_op jit(solution)/shard_map/ppermute | solution.py:591
  77.8 23.0 %collective-permute-start.16 = (f32[32,3072]{1,0:T(8,128)}, f32[32,3072]{1,0:T(8,128)}, u32[]{:S(2)}, u32[]{:S(2)}) collective-permute-start(f32[32,3072]{1,0:T(8,128)} %get-tuple-element.45.refs_12_), channel_id=1, source_target_pairs={{0,1},{1,0},{2,3},{3,2},{4,5},{5,4},{6,7},{7,6},{8,9},{9,8},{10,11... | collective-permute-start | bytes 1179656 | tf_op jit(solution)/shard_map/ppermute | solution.py:591
  78.0 22.9 %collective-permute-start.17 = (f32[32,3072]{1,0:T(8,128)}, f32[32,3072]{1,0:T(8,128)}, u32[]{:S(2)}, u32[]{:S(2)}) collective-permute-start(f32[32,3072]{1,0:T(8,128)} %get-tuple-element.46.refs_14_), channel_id=1, source_target_pairs={{0,1},{1,0},{2,3},{3,2},{4,5},{5,4},{6,7},{7,6},{8,9},{9,8},{10,11... | collective-permute-start | bytes 1179656 | tf_op jit(solution)/shard_map/ppermute | solution.py:591
  89.6 28.5 %collective-permute-start.13 = (f32[32,3072]{1,0:T(8,128)}, f32[32,3072]{1,0:T(8,128)S(1)}, u32[]{:S(2)}, u32[]{:S(2)}) collective-permute-start(f32[32,3072]{1,0:T(8,128)} %entry_product.5.refs_0_.refs_8_), channel_id=1, source_target_pairs={{0,6},{1,7},{2,4},{3,5},{4,2},{5,3},{6,0},{7,1},{8,14},{9,15},{10,... | collective-permute-start | bytes 1179656 | tf_op jit(solution)/shard_map/ppermute | solution.py:591
  92.0 33.1 %collective-permute-start.12 = (f32[32,3072]{1,0:T(8,128)}, f32[32,3072]{1,0:T(8,128)S(1)}, u32[]{:S(2)}, u32[]{:S(2)}) collective-permute-start(f32[32,3072]{1,0:T(8,128)} %entry_product.5.refs_0_.refs_8_), channel_id=1, source_target_pairs={{0,4},{1,5},{2,6},{3,7},{4,0},{5,1},{6,2},{7,3},{8,12},{9,13},{10,... | collective-permute-start | bytes 1179656 | tf_op jit(solution)/shard_map/ppermute | solution.py:591
  92.6 32.7 %collective-permute-start.11 = (f32[32,3072]{1,0:T(8,128)}, f32[32,3072]{1,0:T(8,128)}, u32[]{:S(2)}, u32[]{:S(2)}) collective-permute-start(f32[32,3072]{1,0:T(8,128)} %entry_product.5.refs_0_.refs_8_), channel_id=1, source_target_pairs={{0,2},{1,3},{2,0},{3,1},{4,6},{5,7},{6,4},{7,5},{8,10},{9,11},{10,... | collective-permute-start | bytes 1179656 | tf_op jit(solution)/shard_map/ppermute | solution.py:591
  100.8 26.6 %collective-permute-start.10 = (f32[32,3072]{1,0:T(8,128)}, f32[32,3072]{1,0:T(8,128)}, u32[]{:S(2)}, u32[]{:S(2)}) collective-permute-start(f32[32,3072]{1,0:T(8,128)} %entry_product.5.refs_0_.refs_8_), channel_id=1, source_target_pairs={{0,1},{1,0},{2,3},{3,2},{4,5},{5,4},{6,7},{7,6},{8,9},{9,8},{10,11... | collective-permute-start | bytes 1179656 | tf_op jit(solution)/shard_map/ppermute | solution.py:591
  118.2 7.1 %copy-start.2 = (f32[32,3072]{1,0:T(8,128)}, f32[32,3072]{1,0:T(8,128)S(1)}, u32[]{:S(2)}) copy-start(f32[32,3072]{1,0:T(8,128)S(1)} %collective-permute-done.13.refs_2_) | copy-start | bytes 1179652
  125.1 0.7 copy-start.3
  125.3 1.5 copy-start
  126.9 1.9 %collective-permute-start.18 = (f32[32,3072]{1,0:T(8,128)}, f32[32,3072]{1,0:T(8,128)S(1)}, u32[]{:S(2)}, u32[]{:S(2)}) collective-permute-start(f32[32,3072]{1,0:T(8,128)} %get-tuple-element.51.refs_2_.refs_10_), channel_id=1, source_target_pairs={{0,1},{1,0},{2,3},{3,2},{4,5},{5,4},{6,7},{7,6},{8,9},{9,8},{10,11... | collective-permute-start | bytes 1179656 | tf_op jit(solution)/shard_map/ppermute | solution.py:591
  126.9 2.5 %collective-permute-start.19 = (f32[32,3072]{1,0:T(8,128)}, f32[32,3072]{1,0:T(8,128)S(1)}, u32[]{:S(2)}, u32[]{:S(2)}) collective-permute-start(f32[32,3072]{1,0:T(8,128)} %get-tuple-element.52.refs_4_.refs_12_), channel_id=1, source_target_pairs={{0,1},{1,0},{2,3},{3,2},{4,5},{5,4},{6,7},{7,6},{8,9},{9,8},{10,11... | collective-permute-start | bytes 1179656 | tf_op jit(solution)/shard_map/ppermute | solution.py:591
  127.4 2.5 %collective-permute-start.20 = (f32[32,3072]{1,0:T(8,128)}, f32[32,3072]{1,0:T(8,128)S(1)}, u32[]{:S(2)}, u32[]{:S(2)}) collective-permute-start(f32[32,3072]{1,0:T(8,128)} %get-tuple-element.53.refs_6_.refs_14_), channel_id=1, source_target_pairs={{0,1},{1,0},{2,3},{3,2},{4,5},{5,4},{6,7},{7,6},{8,9},{9,8},{10,11... | collective-permute-start | bytes 1179656 | tf_op jit(solution)/shard_map/ppermute | solution.py:591
  128.8 1.1 copy-start.15
  129.4 0.8 copy-start.16
  129.9 0.8 copy-start.17
  130.7 37.2 %all-to-all-start.1 = ((f32[8,640,128]{2,1,0:T(8,128)}), f32[8,640,128]{2,1,0:T(8,128)S(1)}, u32[]{:S(2)}, u32[]{:S(2)}) async-start(f32[8,640,128]{2,1,0:T(8,128)} %bitcast.28), calls=%async_computation.1 | async-start | bytes 5242880 | tf_op jit(solution)/shard_map/all_to_all | solution.py:666
  168.0 1.5 copy-start.1
Sparse Core Ops, SparseCore 0:
  9.6 39.7 all-gather.4
  51.0 35.9 all-gather.6

commit v17 on v16

--- a/solution.py
+++ b/solution.py
@@ -347,7 +347,7 @@
         ),
         out_shape=jax.ShapeDtypeStruct(snr.shape, F32),
         input_output_aliases={3 + halves: 0},
-        compiler_params=pltpu.CompilerParams(vmem_limit_bytes=VMEM_LIMIT),
+        compiler_params=pltpu.CompilerParams(vmem_limit_bytes=24 * MIB),
         cost_estimate=COST,
         name="second_section",
     )(info, scale, *parts, second, snr, *after)

time: 188 us -> 190 us (1.011)
    unnamed x43 -> x51, local copies, waits for them, and re-layouts: 4.73 us -> 5.43 us
where the time goes in v17:
time: 190 us; the launch traced here: 188 us
  Pallas kernels  91.9 us (48%)
  waiting for transfers between devices  32.6 us (17%)
  starting transfers between devices  22.7 us (12%)
  other arithmetic  16 us (8%)
  between operations  15.6 us (8%)
  local copies, waits for them, and re-layouts  9.24 us (5%)
    pallas_call x2, Pallas kernels, bins_first(): pl.pallas_call(functools.partial(bins_first_kernel, len(own), banks), gri...  34.5 us
    ppermute x21, waiting for transfers between devices, swap(): return lax.ppermute(x, 'freq', [(i, i ^ k) for i in range(freq)])  20 us
    pallas_call x1, Pallas kernels, bins_second(): pl.pallas_call(functools.partial(bins_second_kernel, halves), grid_spec=p...  16.8 us
    pallas_call x2, Pallas kernels, first_section(): pl.pallas_call(functools.partial(first_kernel, freq), grid_spec=pltpu.Pre...  15.2 us
    ppermute x21, starting transfers between devices, swap(): return lax.ppermute(x, 'freq', [(i, i ^ k) for i in range(freq)])  14.3 us
    all_gather x2, waiting for transfers between devices, per_device(): strains = [lax.all_gather(x, 'bank', axis=0, tiled=False) for x in slices]  12.6 us
    pallas_call x1, Pallas kernels, second_section(): pl.pallas_call(functools.partial(second_kernel, freq, halves), grid_spec=...  9.9 us
    pallas_call x3, Pallas kernels, entry_product(): pl.pallas_call(functools.partial(entry_kernel, steps, banks), grid_spec=p...  9.42 us
  transfers between devices with their start and end apart: 25, of which 14 were waited for; matrix products, arithmetic and copies ran while one was open for 9% of the time, Pallas kernels for 44%

profile of v17, /device:TPU:0, one launch (start us, length us, event | category | flops | bytes accessed | tf_op | source)
XLA Modules:
  0.0 188.1 jit_solution(16056281238379310115)
XLA Ops:
  7.2 2.1 %fusion.49 = (f32[3,2,32,512]{3,2,1,0:T(8,128)}, f32[3,2,32,512]{3,2,1,0:T(8,128)}) fusion(f32[3,2,64,512]{3,2,1,0:T(8,128)} %param.9), kind=kLoop, calls=%fused_computation.114 | loop fusion | bytes 1572864 | tf_op jit(solution)/shard_map/slice | solution.py:611
  10.7 1.7 add_reduce_fusion
  12.7 0.6 pad_add_fusion.1.which_ref
  13.3 4.0 %entry_product.3 = f32[64,1024]{1,0:T(8,128)} custom-call(s32[3]{0:T(128)} %pad_add_fusion.1.which_ref, f32[2,2,64,2048]{3,2,1,0:T(8,128)} %tmpl_ref.9, f32[1,3,2,64,512]{4,3,2,1,0:T(8,128)} %bitcast.31, f32[3,2,32,512]{3,2,1,0:T(8,128)} %get-tuple-element.67.refs_0_, f32[3,2,32,512]{3,2,1,0:T(8,128)} %get-tuple-element.66.refs_1_), custom_call_target="tpu_custom_call" | custom-call | flops 1048576 | bytes 1048576 | tf_op jit(solution)/shard_map/entry_product/pallas_call | solution.py:258
  17.4 1.0 select_maximum_fusion.refs_0_
  18.3 4.0 %collective-permute-start.5 = (f32[72,1024]{1,0:T(8,128)S(1)}, f32[72,1024]{1,0:T(8,128)S(1)}, u32[]{:S(2)}, u32[]{:S(2)}) collective-permute-start(f32[72,1024]{1,0:T(8,128)S(1)} %select_maximum_fusion.refs_0_), channel_id=1, source_target_pairs={{0,6},{1,7},{2,4},{3,5},{4,2},{5,3},{6,0},{7,1},{8,14},{9,15},{10,... | collective-permute-start | bytes 884744 | tf_op jit(solution)/shard_map/ppermute | solution.py:591
  22.3 0.5 collective-permute-start.3
  23.1 0.3 fusion.24
  23.4 0.7 pad_add_fusion.4.place_ref
  24.4 1.0 fusion.39
  25.4 0.7 pad_maximum_fusion.4.block_ref
  26.1 0.7 pad_maximum_fusion.3.inner_ref
  26.8 2.1 %fusion.10 = (f32[1,64,2048]{2,1,0:T(8,128)S(1)}, f32[1,64,2048]{2,1,0:T(8,128)S(1)}) fusion(s32[2048]{0:T(1024)S(1)} %fusion.35, s32[64]{0:T(128)S(1)} %iota_add_fusion.1), kind=kLoop, calls=%fused_computation.31 | loop fusion | flops 1835008 | bytes 1057024 | tf_op jit(solution)/shard_map/cos | solution.py:64
  28.9 1.1 pad_maximum_fusion.tw_ref
  30.0 2.1 %fusion.12 = (f32[1,256,256]{2,1,0:T(8,128)S(1)}, f32[1,256,256]{2,1,0:T(8,128)S(1)}, f32[1,256,256]{2,1,0:T(8,128)S(1)}, f32[1,256,256]{2,1,0:T(8,128)S(1)}) fusion(s32[256]{0:T(256)S(1)} %iota_add_fusion, s32[256]{0:T(256)S(1)} %add_add_fusion, s32[256]{0:T(256)S(1)} %fusion.45), kind=kLoop, calls=%fused_computation.34 | loop fusion | flops 1835008 | bytes 1051648 | tf_op jit(solution)/shard_map/cos | solution.py:64
  32.1 6.0 %bank_table.1 = (bf16[4096,512]{1,0:T(8,128)(2,1)}, bf16[4096,512]{1,0:T(8,128)(2,1)}) custom-call(f32[32,2,256]{2,1,0:T(2,128)} %pad_maximum_fusion.4.block_ref, f32[2,64,256]{2,1,0:T(8,128)} %pad_maximum_fusion.3.inner_ref), custom_call_target="tpu_custom_call" | custom-call | flops 1048576 | bytes 1048576 | tf_op jit(solution)/shard_map/bank_table/pallas_call | solution.py:380
  38.2 1.1 pad_maximum_fusion.1
  39.2 0.7 pad_add_fusion.2.info_ref
  39.9 0.6 pad_add_fusion.3.edge_ref
  40.6 0.5 collective-permute-start.6
  41.4 0.5 collective-permute-start.2
  42.0 0.4 collective-permute-done.6.refs_6_.refs_7_
  42.4 0.4 collective-permute-done.4.refs_4_.refs_5_
  42.9 0.3 collective-permute-done.2.refs_2_.refs_3_
  43.7 0.6 dynamic_slice.10
  44.3 1.2 bitcast_multiply_fusion
  45.5 3.9 %all-gather.5.cloned.1.call-done = f32[12,2,32,512]{3,2,1,0:T(8,128)} async-done(((f32[3,2,32,512]{3,2,1,0:T(8,128)}), f32[12,2,32,512]{3,2,1,0:T(8,128)}) %all-gather.5.cloned.1.call-update) | async-done | bytes 1572880 | tf_op jit(solution)/shard_map/all_gather | solution.py:612
  49.4 2.7 %entry_product.4.refs_0_.refs_8_ = f32[32,3072]{1,0:T(8,128)} custom-call(s32[3]{0:T(128)} %pad_add_fusion.1.which_ref, f32[2,2,64,2048]{3,2,1,0:T(8,128)} %tmpl_ref.9, f32[4,3,2,32,512]{4,3,2,1,0:T(8,128)} %bitcast.34, f32[72,1024]{1,0:T(8,128)} %copy-done.15, f32[72,1024]{1,0:T(8,128)} %copy-done.14, f32[72,1024]{1,0:T(8,128)} %copy-done.18, ...), custom_call_target="tpu_custom_call" | custom-call | flops 1048576 | bytes 1048576 | tf_op jit(solution)/shard_map/entry_product/pallas_call | solution.py:258
  52.1 2.4 %collective-permute-start.9 = (f32[32,3072]{1,0:T(8,128)}, f32[32,3072]{1,0:T(8,128)S(1)}, u32[]{:S(2)}, u32[]{:S(2)}) collective-permute-start(f32[32,3072]{1,0:T(8,128)} %entry_product.4.refs_0_.refs_8_), channel_id=1, source_target_pairs={{0,6},{1,7},{2,4},{3,5},{4,2},{5,3},{6,0},{7,1},{8,14},{9,15},{10,... | collective-permute-start | bytes 1179656 | tf_op jit(solution)/shard_map/ppermute | solution.py:591
  54.5 0.5 collective-permute-start.8
  55.0 0.6 collective-permute-start.7
  55.6 7.7 %first_section.2 = (f32[8,5,2,2,32,128]{5,4,3,2,1,0:T(8,128)}, f32[8,128]{1,0:T(8,128)}) custom-call(s32[11]{0:T(128)} %pad_add_fusion.2.info_ref, f32[2,2,64,2048]{3,2,1,0:T(8,128)} %tmpl_ref.9, f32[4,3,2,32,512]{4,3,2,1,0:T(8,128)} %bitcast.35, bf16[256,256]{1,0:T(8,128)(2,1)} %constant.173.clone.wh_ref, bf16[256,256]{1,0:T(8,128)(2,1)} %constant.174.clone.wl_ref, ...), custom_call_target="tpu_custom_call" | custom-call | flops 2516582400 | bytes 16777216 | tf_op jit(solution)/shard_map/first_section/pallas_call | solution.py:196
  63.3 2.0 %collective-permute-done.9.refs_3_.refs_2_ = f32[32,3072]{1,0:T(8,128)S(1)} collective-permute-done((f32[32,3072]{1,0:T(8,128)}, f32[32,3072]{1,0:T(8,128)S(1)}, u32[]{:S(2)}, u32[]{:S(2)}) %collective-permute-start.9) | collective-permute-done | bytes 393248 | tf_op jit(solution)/shard_map/ppermute | solution.py:591
  65.3 6.9 %collective-permute-done.8.refs_2_.refs_1_ = f32[32,3072]{1,0:T(8,128)S(1)} collective-permute-done((f32[32,3072]{1,0:T(8,128)}, f32[32,3072]{1,0:T(8,128)S(1)}, u32[]{:S(2)}, u32[]{:S(2)}) %collective-permute-start.8) | collective-permute-done | bytes 393248 | tf_op jit(solution)/shard_map/ppermute | solution.py:591
  72.3 0.2 collective-permute-done.7.refs_1_.refs_0_
  72.5 0.5 copy-done.10
  73.0 0.2 copy-done.11
  73.2 3.9 %all-to-all-start = ((f32[8,640,128]{2,1,0:T(8,128)}), f32[8,640,128]{2,1,0:T(8,128)S(1)}, u32[]{:S(2)}, u32[]{:S(2)}) async-start(f32[8,640,128]{2,1,0:T(8,128)} %bitcast.30), calls=%async_computation | async-start | bytes 5242880 | tf_op jit(solution)/shard_map/all_to_all | solution.py:666
  77.2 0.2 collective-permute-start.14
  77.4 0.4 collective-permute-start.15
  77.9 0.4 collective-permute-start.17
  78.3 8.7 %all-gather.7.cloned.1.call-done = f32[12,2,32,512]{3,2,1,0:T(8,128)} async-done(((f32[3,2,32,512]{3,2,1,0:T(8,128)}), f32[12,2,32,512]{3,2,1,0:T(8,128)}) %all-gather.7.cloned.1.call-update) | async-done | bytes 1572880 | tf_op jit(solution)/shard_map/all_gather | solution.py:612
  87.0 2.7 %entry_product.5.refs_0_.refs_8_ = f32[32,3072]{1,0:T(8,128)} custom-call(s32[3]{0:T(128)} %pad_add_fusion.1.which_ref, f32[2,2,64,2048]{3,2,1,0:T(8,128)} %tmpl_ref.9, f32[4,3,2,32,512]{4,3,2,1,0:T(8,128)} %bitcast.32, f32[8,128]{1,0:T(8,128)} %get-tuple-element.39.refs_0_.refs_3_), custom_call_target="tpu_custom_call" | custom-call | flops 1048576 | bytes 1048576 | tf_op jit(solution)/shard_map/entry_product/pallas_call | solution.py:258
  89.7 2.4 %collective-permute-start.13 = (f32[32,3072]{1,0:T(8,128)}, f32[32,3072]{1,0:T(8,128)S(1)}, u32[]{:S(2)}, u32[]{:S(2)}) collective-permute-start(f32[32,3072]{1,0:T(8,128)} %entry_product.5.refs_0_.refs_8_), channel_id=1, source_target_pairs={{0,6},{1,7},{2,4},{3,5},{4,2},{5,3},{6,0},{7,1},{8,14},{9,15},{10,... | collective-permute-start | bytes 1179656 | tf_op jit(solution)/shard_map/ppermute | solution.py:591
  92.0 0.6 collective-permute-start.12
  92.6 0.6 collective-permute-start.11
  93.2 7.6 %first_section.3 = (f32[8,5,2,2,32,128]{5,4,3,2,1,0:T(8,128)}, f32[8,128]{1,0:T(8,128)}) custom-call(s32[11]{0:T(128)} %pad_add_fusion.2.info_ref, f32[2,2,64,2048]{3,2,1,0:T(8,128)} %tmpl_ref.9, f32[4,3,2,32,512]{4,3,2,1,0:T(8,128)} %bitcast.33, bf16[256,256]{1,0:T(8,128)(2,1)} %constant.173.clone.wh_ref, bf16[256,256]{1,0:T(8,128)(2,1)} %constant.174.clone.wl_ref, ...), custom_call_target="tpu_custom_call" | custom-call | flops 2516582400 | bytes 16777216 | tf_op jit(solution)/shard_map/first_section/pallas_call | solution.py:196
  100.8 17.3 %bins_first.2 = (f32[16,2,256,256]{3,2,1,0:T(8,128)}, f32[2,256,256]{2,1,0:T(8,128)}) custom-call(s32[2]{0:T(128)} %pad_add_fusion.4.place_ref, s32[17]{0:T(128)} %pad_add_fusion.3.edge_ref, f32[72,1024]{1,0:T(8,128)} %copy-done.19, f32[72,1024]{1,0:T(8,128)} %copy-done.15, f32[72,1024]{1,0:T(8,128)} %copy-done.14, f32[72,1024]{1,0:T(8,128)} %copy-done.18, ...), custom_call_target="tpu_custom_call" | custom-call | flops 1048576 | bytes 1048576 | tf_op jit(solution)/shard_map/bins_first/pallas_call | solution.py:465
  118.1 6.9 %collective-permute-done.12.refs_1_ = f32[32,3072]{1,0:T(8,128)S(1)} collective-permute-done((f32[32,3072]{1,0:T(8,128)}, f32[32,3072]{1,0:T(8,128)S(1)}, u32[]{:S(2)}, u32[]{:S(2)}) %collective-permute-start.12) | collective-permute-done | bytes 393248 | tf_op jit(solution)/shard_map/ppermute | solution.py:591
  125.1 0.2 collective-permute-done.11.refs_0_
  125.3 0.6 copy-done.8
  125.8 1.0 copy-done
  126.8 0.5 collective-permute-start.19
  127.3 1.4 collective-permute-done.18.refs_3_.refs_11_
  128.7 0.6 collective-permute-done.19.refs_5_.refs_13_
  129.3 0.6 collective-permute-done.20.refs_7_.refs_15_
  129.9 0.2 copy-done.21
  130.1 0.5 copy-done.22
  130.6 4.4 %all-to-all-start.1 = ((f32[8,640,128]{2,1,0:T(8,128)}), f32[8,640,128]{2,1,0:T(8,128)}, u32[]{:S(2)}, u32[]{:S(2)}) async-start(f32[8,640,128]{2,1,0:T(8,128)} %bitcast.29), calls=%async_computation.1 | async-start | bytes 5242880 | tf_op jit(solution)/shard_map/all_to_all | solution.py:666
  135.0 17.2 %bins_first.3 = (f32[16,2,256,256]{3,2,1,0:T(8,128)}, f32[2,256,256]{2,1,0:T(8,128)}) custom-call(s32[2]{0:T(128)} %pad_add_fusion.4.place_ref, s32[17]{0:T(128)} %pad_add_fusion.3.edge_ref, f32[72,1024]{1,0:T(8,128)} %copy-done.19, f32[72,1024]{1,0:T(8,128)} %copy-done.15, f32[72,1024]{1,0:T(8,128)} %copy-done.14, f32[72,1024]{1,0:T(8,128)} %copy-done.18, ...), custom_call_target="tpu_custom_call" | custom-call | flops 1048576 | bytes 1048576 | tf_op jit(solution)/shard_map/bins_first/pallas_call | solution.py:465
  152.2 16.8 %bins_second.1 = (f32[256,512]{1,0:T(8,128)}, f32[2,3,2,256,512]{4,3,2,1,0:T(8,128)}) custom-call(s32[3]{0:T(128)} %pad_add_fusion.1.which_ref, f32[2]{0:T(128)} %copy-done.4, f32[16]{0:T(128)} %get-tuple-element.54.gain_ref, f32[16]{0:T(128)} %get-tuple-element.55.share_ref, f32[16,2,256,256]{3,2,1,0:T(8,128)} %get-tuple-element.56.refs_0_, ...), custom_call_target="tpu_custom_call" | custom-call | flops 1048576 | bytes 1048576 | tf_op jit(solution)/shard_map/bins_second/pallas_call | solution.py:548
  169.1 1.2 copy-done.2
  170.3 1.0 copy-done.3
  171.4 9.9 %second_section.1 = f32[2,3,2,256,512]{4,3,2,1,0:T(8,128)} custom-call(s32[11]{0:T(128)S(1)} %copy-done.6, f32[2]{0:T(128)S(1)} %copy-done.5, f32[8,5,2,2,32,128]{5,4,3,2,1,0:T(8,128)S(1)} %bitcast.27, f32[8,5,2,2,32,128]{5,4,3,2,1,0:T(8,128)} %bitcast.13.refs_1_, bf16[2048,256]{1,0:T(8,128)(2,1)S(1)} %copy-done.2, ...), custom_call_target="tpu_custom_call", output_to_operand_aliasing={{}: (5, {})} | custom-call | flops 1048576 | bytes 1048576 | tf_op jit(solution)/shard_map/second_section/pallas_call | solution.py:334
  (103 shorter events, 2.4 us)
Async XLA Ops:
  7.2 42.2 %all-gather.5.cloned.1.call-start = ((), (), s32[]{:S(2)}) async-start(), calls=%async_computation.2 | async-start | bytes 1966080 | tf_op jit(solution)/shard_map/all_gather | solution.py:612
  9.3 77.6 %all-gather.7.cloned.1.call-start = ((), (), s32[]{:S(2)}) async-start(), calls=%async_computation.3 | async-start | bytes 1966080 | tf_op jit(solution)/shard_map/all_gather | solution.py:612
  12.4 11.8 %copy-start.24 = (s32[2,15]{1,0:T(2,128)S(1)}, s32[2,15]{1,0:T(2,128)}, u32[]{:S(2)}) copy-start(s32[2,15]{1,0:T(2,128)} %param.13) | copy-start | bytes 364
  18.3 13.8 %copy-start.19 = (f32[72,1024]{1,0:T(8,128)}, f32[72,1024]{1,0:T(8,128)S(1)}, u32[]{:S(2)}) copy-start(f32[72,1024]{1,0:T(8,128)S(1)} %select_maximum_fusion.refs_0_) | copy-start | bytes 884740
  18.3 22.2 %collective-permute-start.5 = (f32[72,1024]{1,0:T(8,128)S(1)}, f32[72,1024]{1,0:T(8,128)S(1)}, u32[]{:S(2)}, u32[]{:S(2)}) collective-permute-start(f32[72,1024]{1,0:T(8,128)S(1)} %select_maximum_fusion.refs_0_), channel_id=1, source_target_pairs={{0,6},{1,7},{2,4},{3,5},{4,2},{5,3},{6,0},{7,1},{8,14},{9,15},{10,... | collective-permute-start | bytes 884744 | tf_op jit(solution)/shard_map/ppermute | solution.py:591
  22.3 18.8 %collective-permute-start.3 = (f32[72,1024]{1,0:T(8,128)S(1)}, f32[72,1024]{1,0:T(8,128)S(1)}, u32[]{:S(2)}, u32[]{:S(2)}) collective-permute-start(f32[72,1024]{1,0:T(8,128)S(1)} %select_maximum_fusion.refs_0_), channel_id=1, source_target_pairs={{0,4},{1,5},{2,6},{3,7},{4,0},{5,1},{6,2},{7,3},{8,12},{9,13},{10,... | collective-permute-start | bytes 884744 | tf_op jit(solution)/shard_map/ppermute | solution.py:591
  22.8 18.4 %collective-permute-start.1 = (f32[72,1024]{1,0:T(8,128)S(1)}, f32[72,1024]{1,0:T(8,128)S(1)}, u32[]{:S(2)}, u32[]{:S(2)}) collective-permute-start(f32[72,1024]{1,0:T(8,128)S(1)} %select_maximum_fusion.refs_0_), channel_id=1, source_target_pairs={{0,2},{1,3},{2,0},{3,1},{4,6},{5,7},{6,4},{7,5},{8,10},{9,11},{10,... | collective-permute-start | bytes 884744 | tf_op jit(solution)/shard_map/ppermute | solution.py:591
  23.0 18.9 %collective-permute-start = (f32[72,1024]{1,0:T(8,128)S(1)}, f32[72,1024]{1,0:T(8,128)S(1)}, u32[]{:S(2)}, u32[]{:S(2)}) collective-permute-start(f32[72,1024]{1,0:T(8,128)S(1)} %select_maximum_fusion.refs_0_), channel_id=1, source_target_pairs={{0,1},{1,0},{2,3},{3,2},{4,5},{5,4},{6,7},{7,6},{8,9},{9,8},{10,11... | collective-permute-start | bytes 884744 | tf_op jit(solution)/shard_map/ppermute | solution.py:591
  40.5 8.9 %copy-start.12 = (f32[72,1024]{1,0:T(8,128)}, f32[72,1024]{1,0:T(8,128)S(1)}, u32[]{:S(2)}) copy-start(f32[72,1024]{1,0:T(8,128)S(1)} %collective-permute-done.5.refs_5_.refs_6_) | copy-start | bytes 884740
  40.6 1.7 collective-permute-start.6
  41.1 8.3 %copy-start.13 = (f32[72,1024]{1,0:T(8,128)}, f32[72,1024]{1,0:T(8,128)S(1)}, u32[]{:S(2)}) copy-start(f32[72,1024]{1,0:T(8,128)S(1)} %collective-permute-done.3.refs_3_.refs_4_) | copy-start | bytes 884740
  41.2 1.6 collective-permute-start.4
  41.3 8.1 %copy-start.14 = (f32[72,1024]{1,0:T(8,128)}, f32[72,1024]{1,0:T(8,128)S(1)}, u32[]{:S(2)}) copy-start(f32[72,1024]{1,0:T(8,128)S(1)} %collective-permute-done.1.refs_1_.refs_2_) | copy-start | bytes 884740
  41.4 1.9 collective-permute-start.2
  41.9 7.5 %copy-start.15 = (f32[72,1024]{1,0:T(8,128)}, f32[72,1024]{1,0:T(8,128)S(1)}, u32[]{:S(2)}) copy-start(f32[72,1024]{1,0:T(8,128)S(1)} %collective-permute-done.refs_0_.refs_1_) | copy-start | bytes 884740
  42.3 7.1 %copy-start.16 = (f32[72,1024]{1,0:T(8,128)}, f32[72,1024]{1,0:T(8,128)S(1)}, u32[]{:S(2)}) copy-start(f32[72,1024]{1,0:T(8,128)S(1)} %collective-permute-done.6.refs_6_.refs_7_) | copy-start | bytes 884740
  42.8 6.6 %copy-start.17 = (f32[72,1024]{1,0:T(8,128)}, f32[72,1024]{1,0:T(8,128)S(1)}, u32[]{:S(2)}) copy-start(f32[72,1024]{1,0:T(8,128)S(1)} %collective-permute-done.4.refs_4_.refs_5_) | copy-start | bytes 884740
  43.2 6.2 %copy-start.18 = (f32[72,1024]{1,0:T(8,128)}, f32[72,1024]{1,0:T(8,128)S(1)}, u32[]{:S(2)}) copy-start(f32[72,1024]{1,0:T(8,128)S(1)} %collective-permute-done.2.refs_2_.refs_3_) | copy-start | bytes 884740
  43.5 8.6 %copy-start.4 = (f32[2]{0:T(128)}, f32[2]{0:T(128)S(1)}, u32[]{:S(2)}) copy-start(f32[2]{0:T(128)S(1)} %rsqrt.6.scale_ref) | copy-start | bytes 28
  52.1 13.2 %collective-permute-start.9 = (f32[32,3072]{1,0:T(8,128)}, f32[32,3072]{1,0:T(8,128)S(1)}, u32[]{:S(2)}, u32[]{:S(2)}) collective-permute-start(f32[32,3072]{1,0:T(8,128)} %entry_product.4.refs_0_.refs_8_), channel_id=1, source_target_pairs={{0,6},{1,7},{2,4},{3,5},{4,2},{5,3},{6,0},{7,1},{8,14},{9,15},{10,... | collective-permute-start | bytes 1179656 | tf_op jit(solution)/shard_map/ppermute | solution.py:591
  54.5 17.7 %collective-permute-start.8 = (f32[32,3072]{1,0:T(8,128)}, f32[32,3072]{1,0:T(8,128)S(1)}, u32[]{:S(2)}, u32[]{:S(2)}) collective-permute-start(f32[32,3072]{1,0:T(8,128)} %entry_product.4.refs_0_.refs_8_), channel_id=1, source_target_pairs={{0,4},{1,5},{2,6},{3,7},{4,0},{5,1},{6,2},{7,3},{8,12},{9,13},{10,... | collective-permute-start | bytes 1179656 | tf_op jit(solution)/shard_map/ppermute | solution.py:591
  55.0 17.4 %collective-permute-start.7 = (f32[32,3072]{1,0:T(8,128)}, f32[32,3072]{1,0:T(8,128)S(1)}, u32[]{:S(2)}, u32[]{:S(2)}) collective-permute-start(f32[32,3072]{1,0:T(8,128)} %entry_product.4.refs_0_.refs_8_), channel_id=1, source_target_pairs={{0,2},{1,3},{2,0},{3,1},{4,6},{5,7},{6,4},{7,5},{8,10},{9,11},{10,... | collective-permute-start | bytes 1179656 | tf_op jit(solution)/shard_map/ppermute | solution.py:591
  65.3 7.2 %copy-start.9 = (f32[32,3072]{1,0:T(8,128)}, f32[32,3072]{1,0:T(8,128)S(1)}, u32[]{:S(2)}) copy-start(f32[32,3072]{1,0:T(8,128)S(1)} %collective-permute-done.9.refs_3_.refs_2_) | copy-start | bytes 1179652
  72.2 0.8 copy-start.10
  72.5 0.8 copy-start.11
  73.2 4.0 %copy-start.23 = (f32[32,3072]{1,0:T(8,128)S(1)}, f32[32,3072]{1,0:T(8,128)}, u32[]{:S(2)}) copy-start(f32[32,3072]{1,0:T(8,128)} %entry_product.4.refs_0_.refs_8_) | copy-start | bytes 1179652
  73.2 52.0 %all-to-all-start = ((f32[8,640,128]{2,1,0:T(8,128)}), f32[8,640,128]{2,1,0:T(8,128)S(1)}, u32[]{:S(2)}, u32[]{:S(2)}) async-start(f32[8,640,128]{2,1,0:T(8,128)} %bitcast.30), calls=%async_computation | async-start | bytes 5242880 | tf_op jit(solution)/shard_map/all_to_all | solution.py:666
  77.2 14.9 %collective-permute-start.14 = (f32[32,3072]{1,0:T(8,128)S(1)}, f32[32,3072]{1,0:T(8,128)}, u32[]{:S(2)}, u32[]{:S(2)}) collective-permute-start(f32[32,3072]{1,0:T(8,128)S(1)} %copy-done.23), channel_id=1, source_target_pairs={{0,1},{1,0},{2,3},{3,2},{4,5},{5,4},{6,7},{7,6},{8,9},{9,8},{10,11... | collective-permute-start | bytes 1179656 | tf_op jit(solution)/shard_map/ppermute | solution.py:591
  77.4 15.2 %collective-permute-start.15 = (f32[32,3072]{1,0:T(8,128)}, f32[32,3072]{1,0:T(8,128)}, u32[]{:S(2)}, u32[]{:S(2)}) collective-permute-start(f32[32,3072]{1,0:T(8,128)} %get-tuple-element.44.refs_10_), channel_id=1, source_target_pairs={{0,1},{1,0},{2,3},{3,2},{4,5},{5,4},{6,7},{7,6},{8,9},{9,8},{10,11... | collective-permute-start | bytes 1179656 | tf_op jit(solution)/shard_map/ppermute | solution.py:591
  77.8 23.0 %collective-permute-start.16 = (f32[32,3072]{1,0:T(8,128)}, f32[32,3072]{1,0:T(8,128)}, u32[]{:S(2)}, u32[]{:S(2)}) collective-permute-start(f32[32,3072]{1,0:T(8,128)} %get-tuple-element.45.refs_12_), channel_id=1, source_target_pairs={{0,1},{1,0},{2,3},{3,2},{4,5},{5,4},{6,7},{7,6},{8,9},{9,8},{10,11... | collective-permute-start | bytes 1179656 | tf_op jit(solution)/shard_map/ppermute | solution.py:591
  77.9 22.9 %collective-permute-start.17 = (f32[32,3072]{1,0:T(8,128)}, f32[32,3072]{1,0:T(8,128)}, u32[]{:S(2)}, u32[]{:S(2)}) collective-permute-start(f32[32,3072]{1,0:T(8,128)} %get-tuple-element.46.refs_14_), channel_id=1, source_target_pairs={{0,1},{1,0},{2,3},{3,2},{4,5},{5,4},{6,7},{7,6},{8,9},{9,8},{10,11... | collective-permute-start | bytes 1179656 | tf_op jit(solution)/shard_map/ppermute | solution.py:591
  89.7 28.5 %collective-permute-start.13 = (f32[32,3072]{1,0:T(8,128)}, f32[32,3072]{1,0:T(8,128)S(1)}, u32[]{:S(2)}, u32[]{:S(2)}) collective-permute-start(f32[32,3072]{1,0:T(8,128)} %entry_product.5.refs_0_.refs_8_), channel_id=1, source_target_pairs={{0,6},{1,7},{2,4},{3,5},{4,2},{5,3},{6,0},{7,1},{8,14},{9,15},{10,... | collective-permute-start | bytes 1179656 | tf_op jit(solution)/shard_map/ppermute | solution.py:591
  92.0 33.0 %collective-permute-start.12 = (f32[32,3072]{1,0:T(8,128)}, f32[32,3072]{1,0:T(8,128)S(1)}, u32[]{:S(2)}, u32[]{:S(2)}) collective-permute-start(f32[32,3072]{1,0:T(8,128)} %entry_product.5.refs_0_.refs_8_), channel_id=1, source_target_pairs={{0,4},{1,5},{2,6},{3,7},{4,0},{5,1},{6,2},{7,3},{8,12},{9,13},{10,... | collective-permute-start | bytes 1179656 | tf_op jit(solution)/shard_map/ppermute | solution.py:591
  92.6 32.7 %collective-permute-start.11 = (f32[32,3072]{1,0:T(8,128)}, f32[32,3072]{1,0:T(8,128)}, u32[]{:S(2)}, u32[]{:S(2)}) collective-permute-start(f32[32,3072]{1,0:T(8,128)} %entry_product.5.refs_0_.refs_8_), channel_id=1, source_target_pairs={{0,2},{1,3},{2,0},{3,1},{4,6},{5,7},{6,4},{7,5},{8,10},{9,11},{10,... | collective-permute-start | bytes 1179656 | tf_op jit(solution)/shard_map/ppermute | solution.py:591
  100.7 26.6 %collective-permute-start.10 = (f32[32,3072]{1,0:T(8,128)}, f32[32,3072]{1,0:T(8,128)}, u32[]{:S(2)}, u32[]{:S(2)}) collective-permute-start(f32[32,3072]{1,0:T(8,128)} %entry_product.5.refs_0_.refs_8_), channel_id=1, source_target_pairs={{0,1},{1,0},{2,3},{3,2},{4,5},{5,4},{6,7},{7,6},{8,9},{9,8},{10,11... | collective-permute-start | bytes 1179656 | tf_op jit(solution)/shard_map/ppermute | solution.py:591
  118.1 7.1 %copy-start.7 = (f32[32,3072]{1,0:T(8,128)}, f32[32,3072]{1,0:T(8,128)S(1)}, u32[]{:S(2)}) copy-start(f32[32,3072]{1,0:T(8,128)S(1)} %collective-permute-done.13.refs_2_) | copy-start | bytes 1179652
  125.1 0.7 copy-start.8
  125.3 1.5 copy-start
  126.8 1.9 %collective-permute-start.18 = (f32[32,3072]{1,0:T(8,128)}, f32[32,3072]{1,0:T(8,128)S(1)}, u32[]{:S(2)}, u32[]{:S(2)}) collective-permute-start(f32[32,3072]{1,0:T(8,128)} %get-tuple-element.51.refs_2_.refs_10_), channel_id=1, source_target_pairs={{0,1},{1,0},{2,3},{3,2},{4,5},{5,4},{6,7},{7,6},{8,9},{9,8},{10,11... | collective-permute-start | bytes 1179656 | tf_op jit(solution)/shard_map/ppermute | solution.py:591
  126.8 2.5 %collective-permute-start.19 = (f32[32,3072]{1,0:T(8,128)}, f32[32,3072]{1,0:T(8,128)S(1)}, u32[]{:S(2)}, u32[]{:S(2)}) collective-permute-start(f32[32,3072]{1,0:T(8,128)} %get-tuple-element.52.refs_4_.refs_12_), channel_id=1, source_target_pairs={{0,1},{1,0},{2,3},{3,2},{4,5},{5,4},{6,7},{7,6},{8,9},{9,8},{10,11... | collective-permute-start | bytes 1179656 | tf_op jit(solution)/shard_map/ppermute | solution.py:591
  127.3 2.5 %collective-permute-start.20 = (f32[32,3072]{1,0:T(8,128)}, f32[32,3072]{1,0:T(8,128)S(1)}, u32[]{:S(2)}, u32[]{:S(2)}) collective-permute-start(f32[32,3072]{1,0:T(8,128)} %get-tuple-element.53.refs_6_.refs_14_), channel_id=1, source_target_pairs={{0,1},{1,0},{2,3},{3,2},{4,5},{5,4},{6,7},{7,6},{8,9},{9,8},{10,11... | collective-permute-start | bytes 1179656 | tf_op jit(solution)/shard_map/ppermute | solution.py:591
  128.7 1.1 copy-start.20
  129.3 0.8 copy-start.21
  129.9 0.7 copy-start.22
  130.6 38.5 %all-to-all-start.1 = ((f32[8,640,128]{2,1,0:T(8,128)}), f32[8,640,128]{2,1,0:T(8,128)}, u32[]{:S(2)}, u32[]{:S(2)}) async-start(f32[8,640,128]{2,1,0:T(8,128)} %bitcast.29), calls=%async_computation.1 | async-start | bytes 5242880 | tf_op jit(solution)/shard_map/all_to_all | solution.py:666
  152.2 16.9 %copy-start.1 = (f32[8,640,128]{2,1,0:T(8,128)S(1)}, f32[8,640,128]{2,1,0:T(8,128)}, u32[]{:S(2)}) copy-start(f32[8,640,128]{2,1,0:T(8,128)} %copy-done) | copy-start | bytes 7864324
  152.2 16.9 %copy-start.5 = (f32[2]{0:T(128)S(1)}, f32[2]{0:T(128)}, u32[]{:S(2)}) copy-start(f32[2]{0:T(128)} %copy-done.4) | copy-start | bytes 28
  152.2 16.9 %copy-start.6 = (s32[11]{0:T(128)S(1)}, s32[11]{0:T(128)}, u32[]{:S(2)}) copy-start(s32[11]{0:T(128)} %pad_add_fusion.2.info_ref) | copy-start | bytes 136
  169.1 1.2 copy-start.2
  170.3 1.0 copy-start.3
Sparse Core Ops, SparseCore 0:
  9.6 39.7 all-gather.4
  51.0 35.9 all-gather.6
